TPU v7x, 32 devices: a whole 2x2x4 slice. The times are simulated.
32 devices in a mesh: dp: 4 (over y, x), filt: 8 (over z, core).
Axes of the slice: x: 2, y: 2, z: 4, core: 2. Of those that a mesh axis runs over, the one named last changes fastest.
Arguments:
- images: bfloat16 [576, 3, 1024], P('filt'), may hold values from -4 to 4
- labels: int32 [576], P('filt'), may hold values from 0 to 9
- corners: int32 [576, 2], P('filt'), may hold values from -8 to 24
- partners: int32 [576], P('filt'), may hold values from 0 to 575, each once
- stem_w: float32 [27, 16], replicated, may hold values from -1.25 to 1.25
- stem_w_m: float32 [27, 16], replicated, may hold values from -1.1444092e-05 to 1.1444092e-05
- stem_w_v: float32 [27, 16], replicated, may hold values from 3.271381e-13 to 1.3085524e-12
- proj_a: float32 [16, 160], replicated, may hold values from -1.5 to 1.5
- proj_a_m: float32 [16, 160], replicated, may hold values from -1.1444092e-05 to 1.1444092e-05
- proj_a_v: float32 [16, 160], replicated, may hold values from 3.271381e-13 to 1.3085524e-12
- proj_b: float32 [160, 320], replicated, may hold values from -0.5 to 0.5
- proj_b_m: float32 [160, 320], replicated, may hold values from -1.1444092e-05 to 1.1444092e-05
- proj_b_v: float32 [160, 320], replicated, may hold values from 3.271381e-13 to 1.3085524e-12
- proj_c: float32 [320, 640], P(None, 'dp'), may hold values from -0.3125 to 0.3125
- proj_c_m: float32 [320, 640], P(None, 'dp'), may hold values from -1.1444092e-05 to 1.1444092e-05
- proj_c_v: float32 [320, 640], P(None, 'dp'), may hold values from 3.271381e-13 to 1.3085524e-12
- conv_w: float32 [2, 640, 5760], P(None, 'dp'), may hold values from -0.078125 to 0.078125
- conv_w_m: float32 [2, 640, 5760], P(None, 'dp'), may hold values from -1.1444092e-05 to 1.1444092e-05
- conv_w_v: float32 [2, 640, 5760], P(None, 'dp'), may hold values from 3.271381e-13 to 1.3085524e-12
- head_w: float32 [640, 10], P('dp'), may hold values from -0.625 to 0.625
- head_w_m: float32 [640, 10], P('dp'), may hold values from -0.00015258789 to 0.00015258789
- head_w_v: float32 [640, 10], P('dp'), may hold values from 9.375e-11 to 3.75e-10
- norm_p: float32 [6, 640], P(None, 'dp'), may hold values from -0.5 to 7, as said below
- norm_p_m: float32 [6, 640], P(None, 'dp'), may hold values from -4.5776367e-05 to 4.5776367e-05
- norm_p_v: float32 [6, 640], P(None, 'dp'), may hold values from 5.2342098e-12 to 2.0936839e-11
Outputs:
- stem_w_mom: float32 [27, 16], replicated
- stem_w_sq: float32 [27, 16], replicated
- stem_w_new: float32 [27, 16], replicated
- proj_a_mom: float32 [16, 160], replicated
- proj_a_sq: float32 [16, 160], replicated
- proj_a_new: float32 [16, 160], replicated
- proj_b_mom: float32 [160, 320], replicated
- proj_b_sq: float32 [160, 320], replicated
- proj_b_new: float32 [160, 320], replicated
- proj_c_mom: float32 [320, 640], P(None, 'dp')
- proj_c_sq: float32 [320, 640], P(None, 'dp')
- proj_c_new: float32 [320, 640], P(None, 'dp')
- conv_w_mom: float32 [2, 640, 5760], P(None, 'dp')
- conv_w_sq: float32 [2, 640, 5760], P(None, 'dp')
- conv_w_new: float32 [2, 640, 5760], P(None, 'dp')
- head_w_mom: float32 [640, 10], P('dp')
- head_w_sq: float32 [640, 10], P('dp')
- head_w_new: float32 [640, 10], P('dp')
- norm_p_mom: float32 [6, 640], P(None, 'dp')
- norm_p_sq: float32 [6, 640], P(None, 'dp')
- norm_p_new: float32 [6, 640], P(None, 'dp')
- loss_sum: float32 [], replicated
- grad_norm: float32 [], replicated
Inputs may be any that keep to these rules, and one draw needn't show every extreme that they name: `partners`: a permutation of the 576 images. `corners`: a square may reach past the image's border. `norm_p`: rows 0, 2 and 4 are positive gains, rows 1, 3 and 5 biases.
All inputs are finite; a program needn't handle non-finite values.
Results may differ from a plain program's by a relative error of at most 0.03.
Values may be sent and summed in bfloat16 or wider, within the bound.
No kernel may reach another device: no remote copies, remote signals or barrier semaphores. Data moves between devices by JAX's collectives and lax.ppermute only.
A program may use at most 256 MiB of HBM per device.

v0:
```python
import math

import jax
import jax.numpy as jnp
from jax import lax
from jax.sharding import PartitionSpec as P

C0 = 16
C1 = 160
C2 = 320
C3 = 640
SIDE = 32
CUT = 16
STEP = 10


beta_one = 0.9
beta_two = 0.999
adam_eps = 1e-08
weight_decay = 0.0005
clip_limit = 0.05
norm_eps = 1e-05


def blend_planes(planes, corners, partners, source_planes, source_labels):
    partner_planes = jnp.take(source_planes, partners, axis=0)
    partner_labels = jnp.take(source_labels, partners, axis=0)
    places = jnp.arange(SIDE, dtype=jnp.int32)
    inside_rows = (places[None, :] >= corners[:, 0:1]) & (places[None, :] < corners[:, 0:1] + CUT)
    inside_cols = (places[None, :] >= corners[:, 1:2]) & (places[None, :] < corners[:, 1:2] + CUT)
    square = inside_rows[:, :, None] & inside_cols[:, None, :]
    blended = jnp.where(square[:, None, :, :], partner_planes, planes)
    area = jnp.sum(inside_rows.astype(jnp.int32), axis=1) * jnp.sum(
        inside_cols.astype(jnp.int32), axis=1
    )
    own_share = 1.0 - area.astype(jnp.float32) / float(SIDE * SIDE)
    return (blended, partner_labels, own_share)


def dot_plain(left, right):
    return jnp.dot(left, right, preferred_element_type=jnp.float32)


def dot_left_t(left, right):
    return jnp.einsum("rc,ro->co", left, right, preferred_element_type=jnp.float32)


def dot_right_t(left, right):
    return jnp.einsum("ro,co->rc", left, right, preferred_element_type=jnp.float32)


def conv_general(left, right, strides, padding, specs, dilation=(1, 1)):
    return lax.conv_general_dilated(
        left,
        right,
        strides,
        padding,
        rhs_dilation=dilation,
        dimension_numbers=specs,
        preferred_element_type=jnp.float32,
    )


def conv_forward(field, kernel):
    result = conv_general(field, kernel, (1, 1), ((1, 1), (1, 1)), ("NHWC", "OHWI", "NHWC"))
    return result.reshape(-1, result.shape[3])


def conv_weight_grad(field, gradient_rows):
    gradient = gradient_rows.reshape(field.shape[0], field.shape[1], field.shape[2], -1)
    return conv_general(field, gradient, (1, 1), ((1, 1), (1, 1)), ("CHWN", "IHWO", "CHWN"))


def conv_input_grad(gradient_rows, kernel, count, side_cells):
    gradient = gradient_rows.reshape(count, side_cells, side_cells, -1)
    flipped = jnp.flip(kernel, (1, 2))
    return conv_general(gradient, flipped, (1, 1), ((1, 1), (1, 1)), ("NHWC", "IHWO", "NHWC"))


def layer_input_grad(gradient_rows, kernel, count, side_cells):
    partial_grad = conv_input_grad(gradient_rows, kernel, count, side_cells)
    result = lax.psum_scatter(
        partial_grad.astype(jnp.bfloat16), "dp", scatter_dimension=3, tiled=True
    ).astype(jnp.float32)
    return result.reshape(-1, result.shape[3])


def conv_layer(activation, kernel, count, side_cells):
    whole = lax.all_gather(activation, "dp", axis=1, tiled=True)
    field = whole.reshape(count, side_cells, side_cells, -1)
    return (conv_forward(field, kernel), field)


def norm_forward(values, gain, bias, row_total):
    totals = lax.psum((jnp.sum(values, axis=0), jnp.sum(values * values, axis=0)), "filt")
    mean = totals[0] / row_total
    rstd = lax.rsqrt(totals[1] / row_total - mean * mean + norm_eps)
    normal_part = (values - mean) * rstd
    return (normal_part * gain + bias, normal_part, rstd)


def norm_backward(gradient, normal_part, rstd, gain, row_total):
    totals = lax.psum((jnp.sum(gradient, axis=0), jnp.sum(gradient * normal_part, axis=0)), "filt")
    result = rstd * (
        gradient * gain - gain * totals[0] / row_total - normal_part * gain * totals[1] / row_total
    )
    return (result, totals[1], totals[0])


def gelu_back(values, gradient):
    return jax.vjp(jax.nn.gelu, values)[1](gradient)[0]


def adamw(weight, gradient, first, second, step_rate):
    first_new = beta_one * first + (1.0 - beta_one) * gradient
    second_new = beta_two * second + (1.0 - beta_two) * gradient * gradient
    first_hat = first_new / (1.0 - beta_one**STEP)
    second_hat = second_new / (1.0 - beta_two**STEP)
    weight_new = weight - step_rate * (
        first_hat / (jnp.sqrt(second_hat) + adam_eps) + weight_decay * weight
    )
    return (first_new, second_new, weight_new)


def shards(
    images,
    labels,
    corners,
    partners,
    stem_w,
    stem_w_m,
    stem_w_v,
    proj_a,
    proj_a_m,
    proj_a_v,
    proj_b,
    proj_b_m,
    proj_b_v,
    proj_c,
    proj_c_m,
    proj_c_v,
    conv_w,
    conv_w_m,
    conv_w_v,
    head_w,
    head_w_m,
    head_w_v,
    norm_p,
    norm_p_m,
    norm_p_v,
):
    half = jnp.bfloat16
    gelu = jax.nn.gelu
    count = images.shape[0]
    side_cells = SIDE // 4
    out_local = conv_w.shape[1]
    total_images = count * lax.axis_size("filt")
    row_total = float(total_images * side_cells * side_cells)
    every_image, every_label = (
        lax.all_gather(images, "filt", axis=0, tiled=True),
        lax.all_gather(labels, "filt", axis=0, tiled=True),
    )
    blended, partner_labels, own_share = blend_planes(
        images.reshape(count, 3, SIDE, SIDE),
        corners,
        partners,
        every_image.reshape(-1, 3, SIDE, SIDE),
        every_label,
    )
    stem_kernel = stem_w.astype(half).reshape(3, 3, 3, stem_w.shape[1])
    proj_a_half = proj_a.astype(half)
    proj_b_half = proj_b.astype(half)
    proj_c_half = proj_c.astype(half)
    head_half = head_w.astype(half)
    kernels = conv_w.astype(half).reshape(2, out_local, 3, 3, C3)
    stem_field = conv_general(
        blended, stem_kernel, (4, 4), ((1, 1), (1, 1)), ("NCHW", "HWIO", "NHWC")
    )
    stem_out = stem_field.reshape(-1, stem_field.shape[3])
    act_one = gelu(stem_out).astype(half)
    mid_one = dot_plain(act_one, proj_a_half)
    act_two = gelu(mid_one).astype(half)
    mid_two = dot_plain(act_two, proj_b_half)
    act_three = gelu(mid_two).astype(half)
    trunk = dot_plain(act_three, proj_c_half)
    normed_one, unit_one, rstd_one = norm_forward(trunk, norm_p[0], norm_p[1], row_total)
    conv_one, field_one = conv_layer(gelu(normed_one).astype(half), kernels[0], count, side_cells)
    normed_two, unit_two, rstd_two = norm_forward(conv_one, norm_p[2], norm_p[3], row_total)
    conv_two, field_two = conv_layer(gelu(normed_two).astype(half), kernels[1], count, side_cells)
    summed = trunk + conv_two
    normed_three, unit_three, rstd_three = norm_forward(summed, norm_p[4], norm_p[5], row_total)
    pooled = jnp.mean(gelu(normed_three).reshape(count, side_cells * side_cells, -1), axis=1)
    pooled_half = pooled.astype(half)
    logits = lax.psum(dot_plain(pooled_half, head_half), "dp")
    classes = jnp.arange(logits.shape[1], dtype=jnp.int32)
    own_hot = (labels[:, None] == classes[None, :]).astype(jnp.float32)
    other_hot = (partner_labels[:, None] == classes[None, :]).astype(jnp.float32)
    target = own_share[:, None] * own_hot + (1.0 - own_share[:, None]) * other_hot
    lse = jax.nn.logsumexp(logits, axis=1)
    local_loss = jnp.sum(lse - jnp.sum(target * logits, axis=1))
    grad_logits = ((jnp.exp(logits - lse[:, None]) - target) / total_images).astype(half)
    grad_head = dot_left_t(pooled_half, grad_logits)
    grad_pooled = dot_right_t(grad_logits, head_half)
    spread_pool = jnp.broadcast_to(
        grad_pooled[:, None, :] / (side_cells * side_cells),
        (count, side_cells * side_cells, grad_pooled.shape[1]),
    )
    grad_normed_three = gelu_back(normed_three, spread_pool.reshape(-1, grad_pooled.shape[1]))
    grad_summed, gain_three, bias_three = norm_backward(
        grad_normed_three, unit_three, rstd_three, norm_p[4], row_total
    )
    grad_conv_two = grad_summed.astype(half)
    weight_grad_two = conv_weight_grad(field_two, grad_conv_two)
    grad_field_two = layer_input_grad(grad_conv_two, kernels[1], count, side_cells)
    grad_conv_one_f, gain_two, bias_two = norm_backward(
        gelu_back(normed_two, grad_field_two), unit_two, rstd_two, norm_p[2], row_total
    )
    grad_conv_one = grad_conv_one_f.astype(half)
    weight_grad_one = conv_weight_grad(field_one, grad_conv_one)
    grad_field_one = layer_input_grad(grad_conv_one, kernels[0], count, side_cells)
    grad_trunk_norm, gain_one, bias_one = norm_backward(
        gelu_back(normed_one, grad_field_one), unit_one, rstd_one, norm_p[0], row_total
    )
    grad_trunk = (grad_summed + grad_trunk_norm).astype(half)
    grad_proj_c = dot_left_t(act_three, grad_trunk)
    grad_act_three = lax.psum(
        dot_right_t(grad_trunk, proj_c_half).astype(jnp.bfloat16), "dp"
    ).astype(jnp.float32)
    grad_mid_two = gelu_back(mid_two, grad_act_three).astype(half)
    grad_proj_b = dot_left_t(act_two, grad_mid_two)
    grad_mid_one = gelu_back(mid_one, dot_right_t(grad_mid_two, proj_b_half)).astype(half)
    grad_proj_a = dot_left_t(act_one, grad_mid_one)
    grad_stem_out = gelu_back(stem_out, dot_right_t(grad_mid_one, proj_a_half)).astype(half)
    grad_stem_field = grad_stem_out.reshape(count, side_cells, side_cells, -1)
    grad_stem = conv_general(
        blended,
        grad_stem_field,
        (1, 1),
        ((1, -2), (1, -2)),
        ("CNHW", "IHWO", "HWNC"),
        dilation=(4, 4),
    ).reshape(27, -1)
    grad_conv = jnp.stack([weight_grad_one, weight_grad_two]).reshape(2, out_local, 9 * C3)
    grad_norm_p = jnp.stack([gain_one, bias_one, gain_two, bias_two, gain_three, bias_three])
    reduced = (
        lax.psum(grad_stem.astype(jnp.bfloat16), "filt").astype(jnp.float32),
        lax.psum(grad_proj_a.astype(jnp.bfloat16), "filt").astype(jnp.float32),
        lax.psum(grad_proj_b.astype(jnp.bfloat16), "filt").astype(jnp.float32),
        lax.psum(grad_proj_c.astype(jnp.bfloat16), "filt").astype(jnp.float32),
        lax.psum(grad_conv.astype(jnp.bfloat16), "filt").astype(jnp.float32),
        lax.psum(grad_head.astype(jnp.bfloat16), "filt").astype(jnp.float32),
        lax.psum(local_loss.astype(jnp.bfloat16), "filt").astype(jnp.float32),
    )
    grad_stem, grad_proj_a, grad_proj_b, grad_proj_c, grad_conv, grad_head, total_loss = reduced
    split_squares = (
        jnp.sum(grad_proj_c * grad_proj_c)
        + jnp.sum(grad_conv * grad_conv)
        + jnp.sum(grad_head * grad_head)
        + jnp.sum(grad_norm_p * grad_norm_p)
    )
    shared_squares = (
        jnp.sum(grad_stem * grad_stem)
        + jnp.sum(grad_proj_a * grad_proj_a)
        + jnp.sum(grad_proj_b * grad_proj_b)
    )
    grad_norm = jnp.sqrt(lax.psum(split_squares, "dp") + shared_squares)
    scale = jnp.minimum(1.0, clip_limit / grad_norm)
    params = (stem_w, proj_a, proj_b, proj_c, conv_w, head_w, norm_p)
    gradients = (
        grad_stem,
        grad_proj_a,
        grad_proj_b,
        grad_proj_c,
        grad_conv,
        grad_head,
        grad_norm_p,
    )
    firsts = (stem_w_m, proj_a_m, proj_b_m, proj_c_m, conv_w_m, head_w_m, norm_p_m)
    seconds = (stem_w_v, proj_a_v, proj_b_v, proj_c_v, conv_w_v, head_w_v, norm_p_v)
    step_rates = (
        0.7 / math.sqrt(27.0),
        0.7 / math.sqrt(C0),
        0.7 / math.sqrt(C1),
        0.7 / math.sqrt(C2),
        0.7 / math.sqrt(9.0 * C3),
        0.7 / math.sqrt(C3 / 8.0),
        0.8,
    )
    updated = [
        adamw(
            params[index],
            gradients[index] * scale,
            firsts[index],
            seconds[index],
            step_rates[index],
        )
        for index in range(7)
    ]
    return (
        updated[0][0],
        updated[0][1],
        updated[0][2],
        updated[1][0],
        updated[1][1],
        updated[1][2],
        updated[2][0],
        updated[2][1],
        updated[2][2],
        updated[3][0],
        updated[3][1],
        updated[3][2],
        updated[4][0],
        updated[4][1],
        updated[4][2],
        updated[5][0],
        updated[5][1],
        updated[5][2],
        updated[6][0],
        updated[6][1],
        updated[6][2],
        total_loss,
        grad_norm,
    )


def solution(mesh):
    placed = (
        P("filt", None, None),
        P("filt"),
        P("filt", None),
        P("filt"),
        P(),
        P(),
        P(),
        P(),
        P(),
        P(),
        P(),
        P(),
        P(),
        P(None, "dp"),
        P(None, "dp"),
        P(None, "dp"),
        P(None, "dp", None),
        P(None, "dp", None),
        P(None, "dp", None),
        P("dp", None),
        P("dp", None),
        P("dp", None),
        P(None, "dp"),
        P(None, "dp"),
        P(None, "dp"),
    )
    return jax.shard_map(
        shards,
        mesh=mesh,
        in_specs=placed,
        out_specs=(
            P(),
            P(),
            P(),
            P(),
            P(),
            P(),
            P(),
            P(),
            P(),
            P(None, "dp"),
            P(None, "dp"),
            P(None, "dp"),
            P(None, "dp", None),
            P(None, "dp", None),
            P(None, "dp", None),
            P("dp", None),
            P("dp", None),
            P("dp", None),
            P(None, "dp"),
            P(None, "dp"),
            P(None, "dp"),
            P(),
            P(),
        ),
        check_vma=False,
    )
```

profile of v0, /device:TPU:0, one launch (start us, length us, event | category | flops | bytes accessed | tf_op | source)
XLA Modules:
  0.0 977.1 jit_solution(4757748983357669079)
XLA Ops:
  13.3 10.7 %all-reduce = s32[576]{0:T(1024)S(1)} all-reduce(s32[576]{0:T(1024)S(1)} %dynamic-update-slice), channel_id=1, replica_groups=mesh['dp'=4,'filt'=8] {'filt'}, use_global_device_ids=true, to_apply=%add | all-reduce | flops 576 | bytes 4608
  27.7 26.3 %all-gather.4.cloned.1.call-done = bf16[576,3,1024]{2,0,1:T(8,128)(2,1)} async-done(((bf16[72,3,1024]{2,0,1:T(8,128)(2,1)}), bf16[576,3,1024]{2,0,1:T(8,128)(2,1)}) %all-gather.4.cloned.1.call-update) | async-done | bytes 3538960 | tf_op jit(solution)/shard_map/all_gather | solution.py:160
  54.0 5.9 copy.155
  59.9 14.2 %copy.156 = bf16[576,3,32,32]{3,2,1,0:T(8,128)(2,1)} copy(bf16[576,3,32,32]{0,3,2,1:T(8,128)(2,1)} %bitcast.61) | data formatting | bytes 7077888 | tf_op jit(solution)/shard_map/reshape | solution.py:167
  74.0 6.0 gather_fusion
  95.2 15.0 %all-reduce.6 = (f32[160]{0:T(256)S(1)}, f32[160]{0:T(256)S(1)}) all-reduce(f32[160]{0:T(256)S(1)} %get-tuple-element.80, f32[160]{0:T(256)S(1)} %get-tuple-element.79), channel_id=1, replica_groups=mesh['dp'=4,'filt'=8] {'filt'}, use_global_device_ids=true, to_apply=%region_3.4 | all-reduce | flops 320 | bytes 2560 | tf_op jit(solution)/shard_map/psum | solution.py:95
  118.4 4.6 squeeze.4
  123.0 54.7 %all-gather.6.cloned.1.call-done = bf16[4608,640]{0,1:T(8,128)(2,1)} async-done(((bf16[4608,160]{0,1:T(8,128)(2,1)}), bf16[4608,640]{0,1:T(8,128)(2,1)}) %all-gather.6.cloned.1.call-update) | async-done | bytes 5898256 | tf_op jit(solution)/shard_map/all_gather | solution.py:89
  177.7 8.9 copy.167
  186.6 18.5 %fusion.128 = (f32[160]{0:T(256)S(1)}, f32[160]{0:T(256)S(1)}, f32[72,8,8,160]{3,0,2,1:T(8,128)S(1)}) fusion(bf16[160,3,3,640]{3,2,1,0:T(4,128)(2,1)} %squeeze.4, bf16[72,8,8,640]{3,2,1,0:T(8,128)(2,1)} %bitcast.65), kind=kOutput, calls=%fused_computation.228 | convolution fusion | flops 7139082240 | bytes 10691840 | tf_op jit(solution)/shard_map/conv_general_dilated | solution.py:53
  205.1 3.7 copy.170
  208.8 5.4 copy.171
  214.2 16.3 %all-reduce.5 = (f32[160]{0:T(256)S(1)}, f32[160]{0:T(256)S(1)}) all-reduce(f32[160]{0:T(256)S(1)} %get-tuple-element.72, f32[160]{0:T(256)S(1)} %get-tuple-element.71), channel_id=1, replica_groups=mesh['dp'=4,'filt'=8] {'filt'}, use_global_device_ids=true, to_apply=%region_7.8 | all-reduce | flops 320 | bytes 2560 | tf_op jit(solution)/shard_map/psum | solution.py:95
  230.6 4.4 fusion.57
  235.5 4.6 squeeze.5
  240.3 59.0 %all-gather.8.cloned.1.call-done = bf16[4608,640]{0,1:T(8,128)(2,1)} async-done(((bf16[4608,160]{0,1:T(8,128)(2,1)}), bf16[4608,640]{0,1:T(8,128)(2,1)}) %all-gather.8.cloned.1.call-update) | async-done | bytes 5898256 | tf_op jit(solution)/shard_map/all_gather | solution.py:89
  299.3 8.9 copy.172
  308.2 18.3 %fusion.16 = f32[72,8,8,160]{3,0,2,1:T(8,128)S(1)} fusion(bf16[72,8,8,640]{3,2,1,0:T(8,128)(2,1)} %bitcast.67, bf16[160,3,3,640]{3,2,1,0:T(4,128)(2,1)} %squeeze.5), kind=kOutput, calls=%fused_computation.32 | convolution fusion | flops 7136870400 | bytes 10690560 | tf_op jit(solution)/shard_map/conv_general_dilated | solution.py:53
  326.4 3.6 copy.175
  330.1 5.4 copy.176
  335.5 3.9 multiply_reduce_fusion.4
  339.3 16.3 %all-reduce.4 = (f32[160]{0:T(256)S(1)}, f32[160]{0:T(256)S(1)}) all-reduce(f32[160]{0:T(256)S(1)} %get-tuple-element.78, f32[160]{0:T(256)S(1)} %get-tuple-element.77), channel_id=1, replica_groups=mesh['dp'=4,'filt'=8] {'filt'}, use_global_device_ids=true, to_apply=%region_11.12 | all-reduce | flops 320 | bytes 2560 | tf_op jit(solution)/shard_map/psum | solution.py:95
  355.7 4.8 multiply_multiply_fusion.12
  360.5 5.3 reshape.318
  365.8 5.5 reduce_sum.231
  371.5 9.2 psum.160
  381.8 3.6 broadcast_in_dim.42
  385.4 5.4 reshape.319
  390.8 5.7 fusion.130
  396.5 13.6 %all-reduce.3 = (f32[160]{0:T(256)S(1)}, f32[160]{0:T(256)S(1)}) all-reduce(f32[160]{0:T(256)S(1)} %get-tuple-element.76, f32[160]{0:T(256)S(1)} %get-tuple-element.75), channel_id=1, replica_groups=mesh['dp'=4,'filt'=8] {'filt'}, use_global_device_ids=true, to_apply=%region_21.22 | all-reduce | flops 320 | bytes 2560 | tf_op jit(solution)/shard_map/psum | solution.py:103
  410.1 6.1 fusion.146
  416.1 3.8 copy.179
  420.0 19.0 %convolution_convert_fusion.2 = bf16[72,8,8,640]{3,0,2,1:T(8,128)(2,1)} fusion(bf16[72,8,8,160]{3,2,1,0:T(8,128)(2,1)} %bitcast.70, bf16[160,3,3,640]{3,2,1,0:T(4,128)(2,1)} %squeeze.5), kind=kOutput, calls=%fused_computation.60 | convolution fusion | flops 7139819520 | bytes 9216000 | tf_op jit(solution)/shard_map/conv_general_dilated | solution.py:53
  439.0 13.6 %copy.196 = bf16[72,8,8,640]{0,2,1,3:T(8,128)(2,1)} copy(bf16[72,8,8,640]{3,0,2,1:T(8,128)(2,1)} %convolution_convert_fusion.2) | data formatting | bytes 11796480
  452.6 17.8 %reshape.349 = bf16[640,4608]{1,0:T(8,128)(2,1)} reshape(bf16[640,8,8,72]{3,2,1,0:T(8,128)(2,1)} %bitcast.56) | data formatting | bytes 11796480
  470.8 63.8 %reduce-scatter.7.cloned.1.call-done = bf16[160,4608]{1,0:T(8,128)(2,1)} async-done(((bf16[640,4608]{1,0:T(8,128)(2,1)}), bf16[160,4608]{1,0:T(8,128)(2,1)}) %reduce-scatter.7.cloned.1.call-update) | async-done | bytes 1474576
  534.7 7.6 reshape.350
  542.3 4.9 copy.197
  547.2 6.6 fusion.127
  553.8 16.4 %all-reduce.2 = (f32[160]{0:T(256)S(1)}, f32[160]{0:T(256)S(1)}) all-reduce(f32[160]{0:T(256)S(1)} %get-tuple-element.70, f32[160]{0:T(256)S(1)} %get-tuple-element.69), channel_id=1, replica_groups=mesh['dp'=4,'filt'=8] {'filt'}, use_global_device_ids=true, to_apply=%region_26.27 | all-reduce | flops 320 | bytes 2560 | tf_op jit(solution)/shard_map/psum | solution.py:103
  570.2 7.1 multiply_convert_fusion.1
  578.7 13.8 %convolution_convert_fusion.1 = bf16[72,8,8,640]{3,0,2,1:T(8,128)(2,1)} fusion(bf16[72,8,8,160]{3,0,2,1:T(8,128)(2,1)S(1)} %multiply_convert_fusion.1, bf16[160,3,3,640]{3,2,1,0:T(4,128)(2,1)S(1)} %copy-done.9), kind=kOutput, calls=%fused_computation.59 | convolution fusion | flops 7139819520 | bytes 9216000 | tf_op jit(solution)/shard_map/conv_general_dilated | solution.py:53
  592.5 13.6 %copy.198 = bf16[72,8,8,640]{0,2,1,3:T(8,128)(2,1)} copy(bf16[72,8,8,640]{3,0,2,1:T(8,128)(2,1)} %convolution_convert_fusion.1) | data formatting | bytes 11796480
  606.1 17.8 %reshape.351 = bf16[640,4608]{1,0:T(8,128)(2,1)} reshape(bf16[640,8,8,72]{3,2,1,0:T(8,128)(2,1)} %bitcast.57) | data formatting | bytes 11796480
  624.1 15.4 %fusion.63 = bf16[160,3,3,640]{3,0,2,1:T(8,128)(2,1)} fusion(bf16[72,8,8,160]{3,2,1,0:T(8,128)(2,1)} %bitcast.71, bf16[72,8,8,640]{3,2,1,0:T(8,128)(2,1)} %bitcast.68), kind=kOutput, calls=%fused_computation.104 | convolution fusion | flops 7137792000 | bytes 9216000 | tf_op jit(solution)/shard_map/conv_general_dilated | solution.py:53
  639.5 48.7 %reduce-scatter.9.cloned.1.call-done = bf16[160,4608]{1,0:T(8,128)(2,1)} async-done(((bf16[640,4608]{1,0:T(8,128)(2,1)}), bf16[160,4608]{1,0:T(8,128)(2,1)}) %reduce-scatter.9.cloned.1.call-update) | async-done | bytes 1474576
  688.2 7.8 reshape.352
  696.0 4.9 copy.199
  700.9 4.5 copy.183
  705.4 5.4 copy.184
  710.8 5.2 fusion.129
  716.0 16.3 %all-reduce.1 = (f32[160]{0:T(256)S(1)}, f32[160]{0:T(256)S(1)}) all-reduce(f32[160]{0:T(256)S(1)} %get-tuple-element.74, f32[160]{0:T(256)S(1)} %get-tuple-element.73), channel_id=1, replica_groups=mesh['dp'=4,'filt'=8] {'filt'}, use_global_device_ids=true, to_apply=%region_31.32 | all-reduce | flops 320 | bytes 2560 | tf_op jit(solution)/shard_map/psum | solution.py:103
  732.4 4.2 add_convert_fusion
  746.9 13.1 %fusion.60 = bf16[160,3,3,640]{3,0,2,1:T(8,128)(2,1)S(1)} fusion(bf16[72,8,8,160]{3,0,2,1:T(8,128)(2,1)} %copy-done.10, bf16[72,8,8,640]{3,2,1,0:T(8,128)(2,1)} %bitcast.66), kind=kOutput, calls=%fused_computation.103 | convolution fusion | flops 7137792000 | bytes 9216000 | tf_op jit(solution)/shard_map/conv_general_dilated | solution.py:53
  764.6 4.4 pad_maximum_fusion
  769.0 5.5 convolution_convert_fusion.4
  774.5 47.1 %all-reduce.12.cloned.1.call-done = bf16[4608,320]{0,1:T(8,128)(2,1)} async-done(((bf16[4608,320]{0,1:T(8,128)(2,1)}), bf16[4608,320]{0,1:T(8,128)(2,1)}) %all-reduce.12.cloned.1.call-update) | async-done | bytes 2949136 | tf_op jit(solution)/shard_map/psum | solution.py:226
  821.6 6.4 fusion.6
  832.3 4.4 fusion.37
  842.0 32.0 %all-reduce.7 = (bf16[27,16]{0,1:T(8,128)(2,1)S(1)}, bf16[160,10]{0,1:T(8,128)(2,1)S(1)}, bf16[16,160]{1,0:T(8,128)(2,1)S(1)}, bf16[]{:T(256)}) all-reduce(bf16[27,16]{0,1:T(8,128)(2,1)S(1)} %copy.190, bf16[160,10]{0,1:T(8,128)(2,1)S(1)} %convolution_convert_fusion.6, ...), channel_id=1, replica_groups=mesh['dp'=4,'filt'=8] {'filt'}, use_global_device_ids=true, to_apply=%region_33.34 | all-reduce | flops 4593 | bytes 18372 | tf_op jit(solution)/shard_map/psum | solution.py:246
  877.8 47.0 %all-reduce.14.cloned.1.call-done = (bf16[320,160]{0,1:T(8,128)(2,1)}, bf16[2,160,5760]{2,1,0:T(8,128)(2,1)}, bf16[160,320]{1,0:T(8,128)(2,1)}) async-done(((bf16[320,160]{0,1:T(8,128)(2,1)}, bf16[2,160,5760]{2,1,0:T(8,128)(2,1)}, bf16[160,320]{1,0:T(8,128)(2,1)}), (bf16[320,160]{0,1:T(8,128)(2,1)}, bf16[2,160,5760]{2,1,0:T(8,128)(2,1)}, bf16[160,320]{1,0:T(8,128)(2,1)})) %all-reduce.14.cloned.1.call-update) | async-done | bytes 3891216 | tf_op jit(solution)/shard_map/psum | solution.py:249
  924.8 4.6 fusion.2
  933.3 10.3 %psum.172 = f32[]{:T(128)} all-reduce(f32[]{:T(128)S(6)} %add.356), channel_id=1, replica_groups=mesh['dp'=4,'filt'=8] {'dp'}, use_global_device_ids=true, to_apply=%region_41.42 | all-reduce | flops 1 | bytes 8 | tf_op jit(solution)/shard_map/psum | solution.py:266
  949.5 18.2 %multiply_subtract_fusion = (f32[2,160,5760]{2,1,0:T(8,128)}, f32[2,160,5760]{2,1,0:T(8,128)}, f32[2,160,5760]{2,1,0:T(8,128)}) fusion(f32[2,160,5760]{2,1,0:T(8,128)} %param.41, f32[]{:T(128)S(6)} %min.3, bf16[2,160,5760]{2,1,0:T(8,128)(2,1)} %get-tuple-element.100, f32[2,160,5760]{2,1,0:T(8,128)} %param.43, f32[2,160,5760]{2,1,0:T(8,128)} %param.42), kind=kLoop, calls=%fused_computation.11 | loop fusion | flops 31334400 | bytes 47923204 | tf_op jit(solution)/shard_map/sub | solution.py:119
  (199 shorter events, 68.3 us)
Async XLA Ops:
  7.2 4.6 copy-start.57
  7.2 5.9 copy-start.45
  7.2 16.8 %copy-start.56 = (s32[72]{0:T(128)S(1)}, s32[72]{0:T(128)}, u32[]{:S(2)}) copy-start(s32[72]{0:T(128)} %param.28) | copy-start | bytes 868
  7.2 18.3 %copy-start.55 = (s32[72,2]{0,1:T(2,128)S(1)}, s32[72,2]{0,1:T(2,128)}, u32[]{:S(2)}) copy-start(s32[72,2]{0,1:T(2,128)} %param.27) | copy-start | bytes 1732
  7.2 18.3 %copy-start.30 = (f32[6,160]{1,0:T(8,128)S(1)}, f32[6,160]{1,0:T(8,128)}, u32[]{:S(2)}) copy-start(f32[6,160]{1,0:T(8,128)} %param.47) | copy-start | bytes 11524
  7.2 46.7 %all-gather.4.cloned.1.call-start = ((), (), s32[]{:S(2)}) async-start(), calls=%async_computation.2 | async-start | bytes 3981312 | tf_op jit(solution)/shard_map/all_gather | solution.py:160
  8.0 169.8 %all-gather.6.cloned.1.call-start = ((), (), s32[]{:S(2)}) async-start(), calls=%async_computation.3 | async-start | bytes 7372800 | tf_op jit(solution)/shard_map/all_gather | solution.py:89
  24.1 35.8 %copy-start.44 = (s32[1024]{0:T(1024)}, s32[1024]{0:T(1024)S(1)}, u32[]{:S(2)}) copy-start(s32[1024]{0:T(1024)S(1)} %pad_clamp_fusion) | copy-start | bytes 12292
  25.6 34.3 %copy-start.47 = (s32[72]{0:T(128)}, s32[72]{0:T(128)S(1)}, u32[]{:S(2)}) copy-start(s32[72]{0:T(128)S(1)} %get-tuple-element.148) | copy-start | bytes 868
  25.6 34.3 %copy-start.49 = (s32[72]{0:T(128)}, s32[72]{0:T(128)S(1)}, u32[]{:S(2)}) copy-start(s32[72]{0:T(128)S(1)} %get-tuple-element.149) | copy-start | bytes 868
  25.6 34.3 %copy-start.51 = (s32[72]{0:T(128)}, s32[72]{0:T(128)S(1)}, u32[]{:S(2)}) copy-start(s32[72]{0:T(128)S(1)} %get-tuple-element.150) | copy-start | bytes 868
  25.6 34.3 %copy-start.53 = (s32[72]{0:T(128)}, s32[72]{0:T(128)S(1)}, u32[]{:S(2)}) copy-start(s32[72]{0:T(128)S(1)} %get-tuple-element.151) | copy-start | bytes 868
  86.0 1.0 copy-start.13
  87.0 3.2 copy-start.24
  89.5 1.4 copy-start.15
  90.9 1.6 copy-start.2
  90.9 1.6 copy-start.14
  92.5 2.7 copy-start.1
  92.5 17.7 %copy-start.27 = (f32[1,160]{1,0:T(1,128)S(1)}, f32[1,160]{1,0:T(1,128)}, u32[]{:S(2)}) copy-start(f32[1,160]{1,0:T(1,128)} %get-tuple-element.140) | copy-start | bytes 1924
  92.5 17.7 %copy-start.37 = (f32[1,160]{1,0:T(1,128)S(1)}, f32[1,160]{1,0:T(1,128)}, u32[]{:S(2)}) copy-start(f32[1,160]{1,0:T(1,128)} %get-tuple-element.139) | copy-start | bytes 1924
  112.8 186.5 %all-gather.8.cloned.1.call-start = ((), (), s32[]{:S(2)}) async-start(), calls=%async_computation.4 | async-start | bytes 7372800 | tf_op jit(solution)/shard_map/all_gather | solution.py:89
  205.1 3.7 copy-start
  208.8 21.7 %copy-start.28 = (f32[1,160]{1,0:T(1,128)S(1)}, f32[1,160]{1,0:T(1,128)}, u32[]{:S(2)}) copy-start(f32[1,160]{1,0:T(1,128)} %get-tuple-element.138) | copy-start | bytes 1924
  208.8 21.7 %copy-start.32 = (f32[1,160]{1,0:T(1,128)S(1)}, f32[1,160]{1,0:T(1,128)}, u32[]{:S(2)}) copy-start(f32[1,160]{1,0:T(1,128)} %get-tuple-element.137) | copy-start | bytes 1924
  235.0 5.1 copy-start.48
  235.0 5.1 copy-start.50
  235.0 5.1 copy-start.52
  235.0 5.1 copy-start.54
  235.0 299.6 %reduce-scatter.7.cloned.1.call-start = ((), (), s32[]{:S(2)}) async-start(), calls=%async_computation.6 | async-start | bytes 7372800
  335.5 20.2 %copy-start.29 = (f32[1,160]{1,0:T(1,128)S(1)}, f32[1,160]{1,0:T(1,128)}, u32[]{:S(2)}) copy-start(f32[1,160]{1,0:T(1,128)} %get-tuple-element.136) | copy-start | bytes 1924
  335.5 20.2 %copy-start.38 = (f32[1,160]{1,0:T(1,128)S(1)}, f32[1,160]{1,0:T(1,128)}, u32[]{:S(2)}) copy-start(f32[1,160]{1,0:T(1,128)} %get-tuple-element.141) | copy-start | bytes 1924
  365.8 5.6 copy-start.23
  365.8 15.0 %copy-start.39 = (s32[72]{0:T(128)S(1)}, s32[72]{0:T(128)}, u32[]{:S(2)}) copy-start(s32[72]{0:T(128)} %get-tuple-element.129) | copy-start | bytes 868
  365.8 15.0 %copy-start.46 = (s32[72]{0:T(128)S(1)}, s32[72]{0:T(128)}, u32[]{:S(2)}) copy-start(s32[72]{0:T(128)} %param.26) | copy-start | bytes 868
  470.4 217.8 %reduce-scatter.9.cloned.1.call-start = ((), (), s32[]{:S(2)}) async-start(), calls=%async_computation.7 | async-start | bytes 7372800
  570.2 8.5 copy-start.9
  577.2 1.4 copy-start.10
  623.9 197.7 %all-reduce.12.cloned.1.call-start = ((), (), s32[]{:S(2)}) async-start(), calls=%async_computation.5 | async-start | bytes 5898240 | tf_op jit(solution)/shard_map/psum | solution.py:226
  736.6 1.2 copy-start.4
  740.3 184.4 %all-reduce.14.cloned.1.call-start = ((), (), s32[]{:S(2)}) async-start(), calls=%async_computation.8 | async-start | bytes 7864320 | tf_op jit(solution)/shard_map/psum | solution.py:249
  764.6 4.4 copy-start.5
  774.5 55.1 %copy-start.3 = (f32[4608,160]{0,1:T(8,128)S(1)}, f32[4608,160]{0,1:T(8,128)}, u32[]{:S(2)}) copy-start(f32[4608,160]{0,1:T(8,128)} %copy-done.2) | copy-start | bytes 8847364
  828.0 1.6 copy-start.6
  832.3 5.5 copy-start.8
  832.3 5.5 copy-start.25
  836.7 1.1 copy-start.11
  838.2 3.4 copy-start.12
  841.3 103.6 %copy-start.31 = (f32[6,160]{1,0:T(8,128)S(1)}, f32[6,160]{1,0:T(8,128)}, u32[]{:S(2)}) copy-start(f32[6,160]{1,0:T(8,128)} %param.47) | copy-start | bytes 11524
  841.3 103.6 %copy-start.40 = (f32[6,160]{1,0:T(8,128)S(1)}, f32[6,160]{1,0:T(8,128)}, u32[]{:S(2)}) copy-start(f32[6,160]{1,0:T(8,128)} %param.49) | copy-start | bytes 11524
  841.4 103.6 %copy-start.41 = (f32[6,160]{1,0:T(8,128)S(1)}, f32[6,160]{1,0:T(8,128)}, u32[]{:S(2)}) copy-start(f32[6,160]{1,0:T(8,128)} %param.48) | copy-start | bytes 11524
  841.4 104.3 %copy-start.26 = (f32[27,16]{0,1:T(8,128)S(1)}, f32[27,16]{0,1:T(8,128)}, u32[]{:S(2)}) copy-start(f32[27,16]{0,1:T(8,128)} %param.29) | copy-start | bytes 5188
  841.4 104.3 %copy-start.42 = (f32[27,16]{0,1:T(8,128)S(1)}, f32[27,16]{0,1:T(8,128)}, u32[]{:S(2)}) copy-start(f32[27,16]{0,1:T(8,128)} %param.31) | copy-start | bytes 5188
  841.4 104.3 %copy-start.43 = (f32[27,16]{0,1:T(8,128)S(1)}, f32[27,16]{0,1:T(8,128)}, u32[]{:S(2)}) copy-start(f32[27,16]{0,1:T(8,128)} %param.30) | copy-start | bytes 5188
  841.5 104.8 %copy-start.33 = (f32[16,160]{1,0:T(8,128)S(1)}, f32[16,160]{1,0:T(8,128)}, u32[]{:S(2)}) copy-start(f32[16,160]{1,0:T(8,128)} %param.34) | copy-start | bytes 30724
  841.5 104.8 %copy-start.34 = (f32[16,160]{1,0:T(8,128)S(1)}, f32[16,160]{1,0:T(8,128)}, u32[]{:S(2)}) copy-start(f32[16,160]{1,0:T(8,128)} %param.33) | copy-start | bytes 30724
  841.5 105.4 %copy-start.35 = (f32[160,10]{0,1:T(8,128)S(1)}, f32[160,10]{0,1:T(8,128)}, u32[]{:S(2)}) copy-start(f32[160,10]{0,1:T(8,128)} %param.46) | copy-start | bytes 19204
  841.5 105.4 %copy-start.36 = (f32[160,10]{0,1:T(8,128)S(1)}, f32[160,10]{0,1:T(8,128)}, u32[]{:S(2)}) copy-start(f32[160,10]{0,1:T(8,128)} %param.45) | copy-start | bytes 19204
  841.5 106.0 %copy-start.16 = (f32[160,320]{1,0:T(8,128)S(1)}, f32[160,320]{1,0:T(8,128)}, u32[]{:S(2)}) copy-start(f32[160,320]{1,0:T(8,128)} %param.35) | copy-start | bytes 614404
  841.6 106.0 %copy-start.19 = (f32[160,320]{1,0:T(8,128)S(1)}, f32[160,320]{1,0:T(8,128)}, u32[]{:S(2)}) copy-start(f32[160,320]{1,0:T(8,128)} %param.37) | copy-start | bytes 614404
  841.6 106.0 %copy-start.20 = (f32[160,320]{1,0:T(8,128)S(1)}, f32[160,320]{1,0:T(8,128)}, u32[]{:S(2)}) copy-start(f32[160,320]{1,0:T(8,128)} %param.36) | copy-start | bytes 614404
  875.3 73.3 %copy-start.21 = (f32[320,160]{0,1:T(8,128)S(1)}, f32[320,160]{0,1:T(8,128)}, u32[]{:S(2)}) copy-start(f32[320,160]{0,1:T(8,128)} %param.40) | copy-start | bytes 614404
  875.3 73.3 %copy-start.22 = (f32[320,160]{0,1:T(8,128)S(1)}, f32[320,160]{0,1:T(8,128)}, u32[]{:S(2)}) copy-start(f32[320,160]{0,1:T(8,128)} %param.39) | copy-start | bytes 614404
  924.8 4.6 copy-start.17
  924.8 7.8 copy-start.18
  (1 other events, 0.7 us)
Sparse Core Ops, SparseCore 0:
  9.7 44.2 all-gather.3
  112.9 64.7 all-gather.5
  235.1 64.1 all-gather.7
  470.5 64.1 reduce-scatter.6
  624.0 64.1 reduce-scatter.8
  740.5 81.1 all-reduce.11
  831.8 92.9 all-reduce.13
where the time goes:
time: 988 us; the launch traced here: 977 us
  waiting for transfers between devices  347 us (35%)
  local copies, waits for them, and re-layouts  220 us (22%)
  blocking collectives  156 us (16%)
  matrix products  121 us (12%)
  other arithmetic  107 us (11%)
  between operations  23.9 us (2%)
    all_gather x2, waiting for transfers between devices, conv_layer(): whole = lax.all_gather(activation, 'dp', axis=1, tiled=True)  114 us
    unnamed x9, waiting for transfers between devices  113 us
    conv_general_dilated x8, matrix products, conv_general(): lax.conv_general_dilated(left, right, strides, padding, rhs_dilation=dila...  101 us
    unnamed x128, local copies, waits for them, and re-layouts  97.3 us
    psum x3, blocking collectives, norm_forward(): lax.psum((jnp.sum(values, axis=0), jnp.sum(values * values, axis=0)), 'fi...  47.7 us
    psum x1, waiting for transfers between devices, shards(): lax.psum(dot_right_t(grad_trunk, proj_c_half).astype(jnp.bfloat16), 'dp')  47.1 us
    psum x1, waiting for transfers between devices, shards(): lax.psum(grad_proj_c.astype(jnp.bfloat16), 'filt').astype(jnp.float32)  47 us
    psum x3, blocking collectives, norm_backward(): lax.psum((jnp.sum(gradient, axis=0), jnp.sum(gradient * normal_part, axis...  46.3 us
  transfers between devices with their start and end apart: 7, of which 7 were waited for; matrix products, arithmetic and copies ran while one was open for 9% of the time, Pallas kernels for 0%

commit v1 on v0

v1 whole, which is shorter than its diff:
```python
import functools
import math

import jax
import jax.numpy as jnp
from jax import lax
from jax.experimental import pallas as pl
from jax.experimental.pallas import tpu as pltpu
from jax.sharding import PartitionSpec as P

C0 = 16
C1 = 160
C2 = 320
C3 = 640
WIDE = 384
TRIPLE = 3 * C3
SIDE = 32
CUT = 16
STEP = 10
PLANE = 640
META = 576
CHUNK = 48

beta_one = 0.9
beta_two = 0.999
adam_eps = 1e-08
weight_decay = 0.0005
clip_limit = 0.05
norm_eps = 1e-05
gelu_one = math.sqrt(2.0 / math.pi)
gelu_three = 0.044715 * gelu_one

half = jnp.bfloat16
full = jnp.float32
NT = (((1,), (1,)), ((), ()))
NN = (((1,), (0,)), ((), ()))
TN = (((0,), (0,)), ((), ()))
VMEM = pl.BlockSpec(memory_space=pltpu.VMEM)
SMEM = pl.BlockSpec(memory_space=pltpu.SMEM)
ANY = pl.BlockSpec(memory_space=pl.ANY)
MIB = 2**20


def shape(dims, kind=full):
    return jax.ShapeDtypeStruct(dims, kind)


def dot(left, right, dims=NN):
    return lax.dot_general(left, right, dims, preferred_element_type=full)


def iota(dims, axis):
    return lax.broadcasted_iota(jnp.int32, dims, axis)


def hot(condition):
    return condition.astype(full).astype(half)


def call(kernel, ins, outs, scratch, flops, bytes_moved, limit):
    return pl.pallas_call(
        kernel,
        out_shape=[item[0] for item in outs],
        in_specs=ins,
        out_specs=[item[1] for item in outs],
        scratch_shapes=scratch,
        cost_estimate=pl.CostEstimate(flops=flops, bytes_accessed=bytes_moved, transcendentals=0),
        compiler_params=pltpu.CompilerParams(vmem_limit_bytes=limit * MIB),
    )


def gelu_pair(values):
    square = values * values
    bent = jnp.tanh(values * (gelu_one + gelu_three * square))
    gate = 0.5 + 0.5 * bent
    slope = gate + (0.5 * values) * (1.0 - bent * bent) * (gelu_one + (3.0 * gelu_three) * square)
    return (values * gate, slope)


def adamw(weight, gradient, first, second, step_rate):
    first_new = beta_one * first + (1.0 - beta_one) * gradient
    second_new = beta_two * second + (1.0 - beta_two) * gradient * gradient
    first_hat = first_new / (1.0 - beta_one**STEP)
    second_hat = second_new / (1.0 - beta_two**STEP)
    weight_new = weight - step_rate * (
        first_hat / (jnp.sqrt(second_hat) + adam_eps) + weight_decay * weight
    )
    return (first_new, second_new, weight_new)


def lane_pixel(lanes):
    tap = lanes // 64
    cell = lanes % 64
    row = 4 * (cell // 8) + tap // 3 - 1
    col = 4 * (cell % 8) + tap % 3 - 1
    return (tap, row, col)


def image_kernel(planes, numbers, out):
    tap, row, col = lane_pixel(iota((1, PLANE), 1))
    pixel = jnp.where((row >= 0) & (col >= 0) & (tap < 9), row * SIDE + col, -1)
    pick = hot(iota((SIDE * SIDE, PLANE), 0) == pixel)
    lanes = iota((1, PLANE), 1)
    for colour in range(3):
        taken = dot(planes[colour], pick)
        if colour == 0:
            for item in range(5):
                value = numbers[:, item : item + 1].astype(full)
                taken = jnp.where(lanes == META + item, value, taken)
        out[:, colour * PLANE : (colour + 1) * PLANE] = taken.astype(half)


def pack_kernel(proj_c, head, norm, out):
    width = proj_c.shape[1]
    place = hot(iota((C2, WIDE), 0) == iota((C2, WIDE), 1))
    total = dot(proj_c[...].astype(half), place, TN)
    classes = head.shape[1]
    place = hot(iota((classes, WIDE), 0) + C2 == iota((classes, WIDE), 1))
    total = total + dot(head[...].astype(half), place)
    rest = norm[...]
    for part in range(3):
        piece = rest.astype(half)
        rest = rest - piece.astype(full)
        place = hot(iota((6, WIDE), 0) + (C2 + 16 + 8 * part) == iota((6, WIDE), 1))
        total = total + dot(piece, place, TN)
    out[...] = total.astype(half)


def cast_kernel(ids, weights, out):
    out[...] = weights[0].astype(half)


def cast_half(ids, conv_w, layer):
    rows = conv_w.shape[1] // 2
    cols = conv_w.shape[2]
    wide = cols // 5
    return pl.pallas_call(
        cast_kernel,
        grid_spec=pltpu.PrefetchScalarGridSpec(
            num_scalar_prefetch=1,
            grid=(5,),
            in_specs=[pl.BlockSpec((1, rows, wide), lambda step, ids: (layer, ids[2], step))],
            out_specs=pl.BlockSpec((rows, wide), lambda step, ids: (0, step)),
        ),
        out_shape=shape((rows, cols), half),
        compiler_params=pltpu.CompilerParams(vmem_limit_bytes=16 * MIB),
        cost_estimate=pl.CostEstimate(
            flops=rows * cols, bytes_accessed=6 * rows * cols, transcendentals=0
        ),
    )(ids, conv_w)


def front_kernel(sizes, *refs):
    per, count, groups, devices, split = sizes
    rows = per * 64
    band = per * 8
    ids = refs[0]
    images = refs[1 : 1 + groups]
    packs = refs[1 + groups : 1 + groups + split]
    stem_w, proj_a, proj_b = refs[1 + groups + split : 4 + groups + split]
    (
        patches,
        stem_out,
        mid_one,
        mid_two,
        act_three,
        base,
        stats,
        norm_rows,
        head_all,
        proj_t,
        facts,
        gathered,
        tiles,
        loose,
        stem_pad,
        proj_b_pad,
        totals,
        sems,
    ) = refs[4 + groups + split :]
    quarter = gathered.shape[0] // split
    copies = []
    for turn in range(split):
        spot = pl.multiple_of((ids[0] ^ turn) * quarter, 16)
        copy = pltpu.make_async_copy(
            packs[turn], gathered.at[pl.ds(spot, quarter)], sems.at[turn]
        )
        copy.start()
        copies.append(copy)
    slot = iota((per, count), 0)
    column = iota((per, count), 1)
    own = dot(hot(column == slot + ids[0] * per), images[0][...])
    group_of = own[:, META + 3 : META + 4].astype(jnp.int32)
    local_of = own[:, META + 4 : META + 5].astype(jnp.int32)
    turn_of = group_of ^ ids[1]
    other = jnp.zeros((per, 3 * PLANE), full)
    for turn in range(groups):
        other = other + dot(hot((turn_of == turn) & (column == local_of)), images[turn][...])
    top = own[:, META + 1 : META + 2]
    left = own[:, META + 2 : META + 3]
    tap, row, col = lane_pixel(iota((1, 3 * PLANE), 1) % PLANE)
    row = row.astype(full)
    col = col.astype(full)
    inside = (row >= top) & (row < top + CUT) & (col >= left) & (col < left + CUT) & (tap < 9)
    blended = jnp.where(inside, other, own)
    tall = jnp.maximum(jnp.minimum(top + CUT, float(SIDE)) - jnp.maximum(top, 0.0), 0.0)
    broad = jnp.maximum(jnp.minimum(left + CUT, float(SIDE)) - jnp.maximum(left, 0.0), 0.0)
    share = 1.0 - tall * broad / float(SIDE * SIDE)
    lanes = iota((per, 128), 1)
    facts[...] = jnp.where(
        lanes == 0,
        own[:, META : META + 1],
        jnp.where(lanes == 1, other[:, META : META + 1], share),
    )
    tiles[...] = jnp.zeros(tiles.shape, full)
    for piece in range(15):
        tiles[:, piece, :] = blended[:, piece * 128 : (piece + 1) * 128]
    tiles[:, 16:32, :] = pltpu.roll(tiles[:, 0:16, :], 64, 2)
    spot = iota((32, 32), 0)
    tap_at = ((spot % 16) % 5) * 2 + spot // 16
    colour_at = (spot % 16) // 5
    order = hot(
        (iota((32, 32), 1) == tap_at * 3 + colour_at) & (tap_at < 9) & (spot % 16 < 15)
    )
    for image in range(per):
        cells = dot(tiles[image].astype(half), order, TN)
        for line in range(8):
            loose[line * band + image * 8 : line * band + image * 8 + 8, :] = cells[
                line * 8 : line * 8 + 8
            ]
    patches[...] = loose[...].astype(half)
    stem_pad[...] = jnp.zeros(stem_pad.shape, full)
    stem_pad[0:27, :] = stem_w[...]
    proj_b_pad[...] = jnp.zeros(proj_b_pad.shape, half)
    proj_b_pad[:, 0:C2] = proj_b[...].astype(half)
    for copy in copies:
        copy.wait()
    lanes = iota((1, WIDE), 1)
    packed = gathered[...]
    proj_t[...] = jnp.where(lanes < C2, packed.astype(full), 0.0).astype(half)
    place = hot(iota((WIDE, 16), 0) == iota((WIDE, 16), 1) + C2)
    head_all[...] = dot(packed, place).astype(half)
    column = iota((8, WIDE), 1)
    name = iota((8, WIDE), 0)
    pieces = [
        dot(hot((column == name + (C2 + 16 + 8 * part)) & (name < 6)), packed, NT)
        for part in range(3)
    ]
    norm_rows[...] = pieces[0] + (pieces[1] + pieces[2])
    stem_half = stem_pad[...].astype(half)
    proj_a_half = proj_a[...].astype(half)
    totals[...] = jnp.zeros(totals.shape, full)
    tall_chunk = 2 * band

    def step(index, carry):
        at = pl.ds(pl.multiple_of(index * tall_chunk, 16), tall_chunk)
        stem = dot(patches[at], stem_half)
        stem_out[at] = stem
        one = dot(gelu_pair(stem)[0].astype(half), proj_a_half)
        mid_one[at] = one
        two = dot(gelu_pair(one)[0].astype(half), proj_b_pad[...])
        mid_two[at] = two
        three = gelu_pair(two)[0].astype(half)
        act_three[at] = three
        result = dot(three, proj_t[...], NT)
        base[at] = result
        totals[0:1] += jnp.sum(result, axis=0, keepdims=True)
        totals[1:2] += jnp.sum(result * result, axis=0, keepdims=True)
        return carry

    lax.fori_loop(0, rows // tall_chunk, step, 0)
    spread_stats(stats, [totals[0:1], totals[1:2]])


def spread_stats(out, parts):
    line = jnp.concatenate(parts, axis=1)
    out[...] = jnp.broadcast_to(line[None], out.shape)


def moments(stats, row_total):
    line = jnp.sum(stats[...], axis=0)
    mean = line[:, 0:C3] / row_total
    rstd = lax.rsqrt(line[:, C3 : 2 * C3] / row_total - mean * mean + norm_eps)
    return (mean, rstd)


def start_weights(ids, pieces, weights, sems):
    count = len(pieces) // 2
    rows = pieces[0].shape[0]
    copies = []
    for turn in range(count):
        for side in range(2):
            spot = pl.multiple_of(
                (ids[0] ^ turn) * (2 * rows) + (ids[2] ^ side) * rows, 16
            )
            copy = pltpu.make_async_copy(
                pieces[2 * turn + side],
                weights.at[pl.ds(spot, rows)],
                sems.at[2 * turn + side],
            )
            copy.start()
            copies.append(copy)
    return copies


def shifted(values, by):
    block = values.reshape(CHUNK // 8, 8, C3)
    place = iota((1, 8, 1), 1)
    if by == 1:
        moved = jnp.where(place == 0, 0.0, pltpu.roll(block, 1, 1))
    else:
        moved = jnp.where(place == 7, 0.0, pltpu.roll(block, 7, 1))
    return moved.reshape(CHUNK, C3)


def conv_kernel(sizes, layer, *refs):
    per, row_total, split = sizes
    rows = per * 64
    band = per * 8
    ids, source, stats_in, norm_rows = refs[0:4]
    offset = 4
    if layer == 1:
        base = refs[4]
        offset = 5
    pieces = refs[offset : offset + 2 * split]
    (result, field_out, slope_out, stats, weights, field, slope, sems, out_sems) = refs[
        offset + 2 * split :
    ]
    copies = start_weights(ids, pieces, weights, sems)
    mean, rstd = moments(stats_in, row_total)
    factor = rstd * norm_rows[2 * layer : 2 * layer + 1]
    shift = norm_rows[2 * layer + 1 : 2 * layer + 2] - mean * factor

    def prepare(index, carry):
        at = pl.ds(pl.multiple_of(index * CHUNK, 16), CHUNK)
        value, gradient = gelu_pair(source[at] * factor + shift)
        slope[at] = gradient
        field[at, 0:C3] = shifted(value, 1).astype(half)
        field[at, C3 : 2 * C3] = value.astype(half)
        field[at, 2 * C3 : TRIPLE] = shifted(value, -1).astype(half)
        return carry

    lax.fori_loop(0, rows // CHUNK, prepare, 0)
    keep_field = pltpu.make_async_copy(field, field_out, out_sems.at[0])
    keep_field.start()
    keep_slope = pltpu.make_async_copy(slope, slope_out, out_sems.at[1])
    keep_slope.start()
    for copy in copies:
        copy.wait()
    inner = rows - band
    result[...] = dot(field[...], weights[:, TRIPLE : 2 * TRIPLE], NT)
    result[band:rows] += dot(field[0:inner], weights[:, 0:TRIPLE], NT)
    result[0:inner] += dot(field[band:rows], weights[:, 2 * TRIPLE : 3 * TRIPLE], NT)

    def count(index, carry):
        at = pl.ds(pl.multiple_of(index * CHUNK, 16), CHUNK)
        value = result[at]
        if layer == 1:
            value = value + base[at]
            result[at] = value
        return (
            carry[0] + jnp.sum(value.reshape(CHUNK // 8, 8, C3), axis=0),
            carry[1] + jnp.sum((value * value).reshape(CHUNK // 8, 8, C3), axis=0),
        )

    zero = jnp.zeros((8, C3), full)
    sums = lax.fori_loop(0, rows // CHUNK, count, (zero, zero))
    spread_stats(stats, [jnp.sum(item, axis=0, keepdims=True) for item in sums])
    keep_field.wait()
    keep_slope.wait()


def head_kernel(sizes, *refs):
    per, row_total, image_total, classes = sizes
    rows = per * 64
    band = per * 8
    (
        summed,
        stats_in,
        norm_rows,
        head_all,
        facts,
        slope,
        spread,
        stats,
        grad_head,
        sum_value,
        sum_slope,
        sum_cross,
    ) = refs
    mean, rstd = moments(stats_in, row_total)
    gain = norm_rows[4:5]
    bias = norm_rows[5:6]
    sum_value[...] = jnp.zeros((band, C3), full)
    sum_slope[...] = jnp.zeros((band, C3), full)
    sum_cross[...] = jnp.zeros((band, C3), full)

    def walk(index, carry):
        for part in range(band // CHUNK):
            at = pl.ds(pl.multiple_of(index * band + part * CHUNK, 16), CHUNK)
            here = slice(part * CHUNK, part * CHUNK + CHUNK)
            unit = (summed[at] - mean) * rstd
            value, gradient = gelu_pair(unit * gain + bias)
            slope[at] = gradient
            sum_value[here] += value
            sum_slope[here] += gradient
            sum_cross[here] += gradient * unit
        return carry

    lax.fori_loop(0, 8, walk, 0)

    def by_image(ref):
        return jnp.sum(ref[...].reshape(per, 8, C3), axis=1)

    pooled = (by_image(sum_value) / 64.0).astype(half)
    logits = dot(pooled, head_all[...])
    lanes = iota((per, 16), 1)
    inside = lanes < classes
    own = facts[:, 0:1].astype(jnp.int32)
    other = facts[:, 1:2].astype(jnp.int32)
    share = facts[:, 2:3]
    target = jnp.where(lanes == own, share, 0.0) + jnp.where(lanes == other, 1.0 - share, 0.0)
    top = jnp.max(jnp.where(inside, logits, -3e38), axis=1, keepdims=True)
    powers = jnp.where(inside, jnp.exp(jnp.where(inside, logits - top, 0.0)), 0.0)
    lse = top + jnp.log(jnp.sum(powers, axis=1, keepdims=True))
    losses = lse - jnp.sum(target * logits, axis=1, keepdims=True)
    loss = jnp.sum(losses, axis=0, keepdims=True)
    soft = jnp.where(inside, jnp.exp(jnp.where(inside, logits - lse, 0.0)), 0.0)
    grad_logits = ((soft - target) / image_total).astype(half)
    grad_head[...] = dot(pooled, grad_logits, TN)
    pull = dot(grad_logits, head_all[...], NT) / 64.0
    spread[...] = jnp.broadcast_to(pull[:, None, :], (per, 8, C3)).reshape(band, C3)
    bias_sum = jnp.sum(pull * by_image(sum_slope), axis=0, keepdims=True)
    gain_sum = jnp.sum(pull * by_image(sum_cross), axis=0, keepdims=True)
    spread_stats(stats, [bias_sum, gain_sum, jnp.broadcast_to(loss, (1, 128))])


def grad_moments(stats, row_total):
    line = jnp.sum(stats[...], axis=0)
    return (line[:, 0:C3] / row_total, line[:, C3 : 2 * C3] / row_total)


def input_grad(gradient, weights, out, band):
    rows = gradient.shape[0]
    inner = rows - band
    spans = (
        (1, slice(0, rows), slice(0, rows)),
        (0, slice(0, inner), slice(band, rows)),
        (2, slice(band, rows), slice(0, inner)),
    )
    for line, to, of in spans:
        for col in range(3):
            tap = 3 * line + col
            part = dot(
                gradient[of, col * C3 : (col + 1) * C3], weights[:, tap * C3 : (tap + 1) * C3]
            )
            if line == 1 and col == 0:
                out[to] = part
            else:
                out[to] += part


def close_input_grad(out, slope, source, mean, rstd, stats, rows):
    def finish(index, carry):
        at = pl.ds(pl.multiple_of(index * CHUNK, 16), CHUNK)
        value = out[at] * slope[at]
        out[at] = value
        unit = (source[at] - mean) * rstd
        return (
            carry[0] + jnp.sum(value.reshape(CHUNK // 8, 8, C3), axis=0),
            carry[1] + jnp.sum((value * unit).reshape(CHUNK // 8, 8, C3), axis=0),
        )

    zero = jnp.zeros((8, C3), full)
    sums = lax.fori_loop(0, rows // CHUNK, finish, (zero, zero))
    spread_stats(stats, [jnp.sum(item, axis=0, keepdims=True) for item in sums])


def put_shifted(gradient, at, value):
    gradient[at, 0:C3] = shifted(value, -1).astype(half)
    gradient[at, C3 : 2 * C3] = value.astype(half)
    gradient[at, 2 * C3 : TRIPLE] = shifted(value, 1).astype(half)


def back_two_kernel(sizes, *refs):
    per, row_total, split = sizes
    rows = per * 64
    band = per * 8
    (
        ids,
        summed,
        slope_three,
        spread,
        stats_three,
        stats_four,
        norm_rows,
        conv_one,
        slope_two,
        stats_two,
    ) = refs[0:10]
    pieces = refs[10 : 10 + 2 * split]
    (result, grad_summed, grad_half, stats, weights, gradient, sems) = refs[10 + 2 * split :]
    copies = start_weights(ids, pieces, weights, sems)
    mean, rstd = moments(stats_three, row_total)
    low, high = grad_moments(stats_four, row_total)
    factor = rstd * norm_rows[4:5]

    def prepare(index, carry):
        for part in range(band // CHUNK):
            at = pl.ds(pl.multiple_of(index * band + part * CHUNK, 16), CHUNK)
            here = slice(part * CHUNK, part * CHUNK + CHUNK)
            unit = (summed[at] - mean) * rstd
            value = factor * (slope_three[at] * spread[here] - low - unit * high)
            grad_summed[at] = value
            grad_half[at] = value.astype(half)
            put_shifted(gradient, at, value)
        return carry

    lax.fori_loop(0, 8, prepare, 0)
    for copy in copies:
        copy.wait()
    input_grad(gradient, weights, result, band)
    mean, rstd = moments(stats_two, row_total)
    close_input_grad(result, slope_two, conv_one, mean, rstd, stats, rows)


def norm_back_kernel(sizes, *refs):
    row_total = sizes
    (incoming, source, stats_two, stats_five, norm_rows, grad_half) = refs
    rows = incoming.shape[0]
    mean, rstd = moments(stats_two, row_total)
    low, high = grad_moments(stats_five, row_total)
    factor = rstd * norm_rows[2:3]

    def prepare(index, carry):
        at = pl.ds(pl.multiple_of(index * CHUNK, 16), CHUNK)
        unit = (source[at] - mean) * rstd
        grad_half[at] = (factor * (incoming[at] - low - unit * high)).astype(half)
        return carry

    lax.fori_loop(0, rows // CHUNK, prepare, 0)


def back_one_kernel(sizes, *refs):
    per, row_total, split = sizes
    rows = per * 64
    band = per * 8
    (ids, grad_half, base, slope_one, stats_one) = refs[0:5]
    pieces = refs[5 : 5 + 2 * split]
    (result, stats, weights, gradient, sems) = refs[5 + 2 * split :]
    copies = start_weights(ids, pieces, weights, sems)

    def prepare(index, carry):
        at = pl.ds(pl.multiple_of(index * CHUNK, 16), CHUNK)
        put_shifted(gradient, at, grad_half[at].astype(full))
        return carry

    lax.fori_loop(0, rows // CHUNK, prepare, 0)
    for copy in copies:
        copy.wait()
    input_grad(gradient, weights, result, band)
    mean, rstd = moments(stats_one, row_total)
    close_input_grad(result, slope_one, base, mean, rstd, stats, rows)


def weight_grad_kernel(sizes, *refs):
    lines, split, band, blocks = sizes
    (ids, grad_half, field, mine, other, held, sems) = refs
    rows = field.shape[0]
    inner = rows - band
    spans = {
        0: (slice(band, rows), slice(0, inner)),
        1: (slice(0, rows), slice(0, rows)),
        2: (slice(0, inner), slice(band, rows)),
    }
    used = 15 * len(lines)
    for spare in range(used, blocks):
        held[spare] = jnp.zeros(held.shape[1:], half)
    for place, line in enumerate(lines):
        left, right = spans[line]
        part = dot(grad_half[left], field[right], TN).astype(half)
        for block in range(15):
            held[place * 15 + block] = part[:, block * 128 : (block + 1) * 128]
    tall = mine.shape[2]
    copies = []
    for turn in range(split):
        for side, target in ((0, mine), (1, other)):
            spot = pl.multiple_of(
                (ids[0] ^ turn) * (2 * tall) + (ids[2] ^ side) * tall, 16
            )
            copy = pltpu.make_async_copy(
                held.at[:, pl.ds(spot, tall), :], target.at[turn], sems.at[2 * turn + side]
            )
            copy.start()
            copies.append(copy)
    for copy in copies:
        copy.wait()


def trunk_kernel(sizes, *refs):
    per, row_total, split = sizes
    rows = per * 64
    band = per * 8
    (
        ids,
        incoming,
        grad_summed,
        base,
        stats_one,
        stats_six,
        norm_rows,
        proj_t,
        act_three,
        mid_two,
        mid_one,
        stem_out,
        patches,
        proj_a,
        proj_b,
        grad_head,
        mine,
        other,
        trunk,
        grad_two,
        act_two,
        grad_one,
        act_one,
        grad_stem,
        proj_b_pad,
        split_part,
        shared_part,
        sems,
    ) = refs
    mean, rstd = moments(stats_one, row_total)
    low, high = grad_moments(stats_six, row_total)
    factor = rstd * norm_rows[0:1]
    proj_b_pad[...] = jnp.zeros(proj_b_pad.shape, half)
    proj_b_pad[:, 0:C2] = proj_b[...].astype(half)
    proj_a_half = proj_a[...].astype(half)

    def prepare(index, carry):
        at = pl.ds(pl.multiple_of(index * CHUNK, 16), CHUNK)
        unit = (base[at] - mean) * rstd
        value = grad_summed[at] + factor * (incoming[at] - low - unit * high)
        trunk[at] = value.astype(half)
        return carry

    lax.fori_loop(0, rows // CHUNK, prepare, 0)
    tall_chunk = 2 * band

    def step(index, carry):
        at = pl.ds(pl.multiple_of(index * tall_chunk, 16), tall_chunk)
        three = dot(trunk[at], proj_t[...])
        two = (three * gelu_pair(mid_two[at])[1]).astype(half)
        grad_two[at] = two
        value, slope = gelu_pair(mid_one[at])
        act_two[at] = value.astype(half)
        one = (dot(two, proj_b_pad[...], NT) * slope).astype(half)
        grad_one[at] = one
        value, slope = gelu_pair(stem_out[at])
        act_one[at] = value.astype(half)
        grad_stem[at] = (dot(one, proj_a_half, NT) * slope).astype(half)
        return carry

    lax.fori_loop(0, rows // tall_chunk, step, 0)
    place = hot(iota((16, WIDE), 0) + C2 == iota((16, WIDE), 1))
    split_part[...] = (
        dot(trunk[...], act_three[...], TN) + dot(grad_head[...].astype(half), place)
    ).astype(half)
    shared = dot(act_two[...], grad_two[...], TN)
    shared = shared + dot(dot(grad_one[...], act_one[...], TN).astype(half), place)
    stem = dot(patches[...], grad_stem[...], TN).astype(half)
    tall = split_part.shape[0] // (2 * split)
    spot = iota((C1, 32), 0)
    twice = hot((spot % tall == iota((C1, 32), 1)) & (spot % tall < 27))
    place = hot(iota((16, WIDE), 0) + (C2 + 16) == iota((16, WIDE), 1))
    shared = shared + dot(dot(twice, stem).astype(half), place)
    shared_part[...] = shared.astype(half)
    copies = []
    for turn in range(split):
        for side, target in ((0, mine), (1, other)):
            place = pl.multiple_of((ids[2] ^ side) * tall, 16)
            spot = pl.multiple_of((ids[0] ^ turn) * (2 * tall) + (ids[2] ^ side) * tall, 16)
            number = 2 * (2 * turn + side)
            copy = pltpu.make_async_copy(
                split_part.at[pl.ds(spot, tall)], target.at[turn, 0:tall], sems.at[number]
            )
            copy.start()
            copies.append(copy)
            copy = pltpu.make_async_copy(
                shared_part.at[pl.ds(place, tall)],
                target.at[turn, tall : 2 * tall],
                sems.at[number + 1],
            )
            copy.start()
            copies.append(copy)
    for copy in copies:
        copy.wait()


def clip_scale(squares):
    total = jnp.sum(jnp.sum(squares[...], axis=0), axis=1, keepdims=True)
    size = jnp.sqrt(total[:, 0:1] / 128.0)
    return (size, jnp.minimum(1.0, clip_limit / size))


def conv_update_kernel(sizes, *refs):
    pieces_count, places, blocks, step_rate = sizes
    ids = refs[0]
    squares, weight, first, second = refs[1:5]
    pieces = refs[5 : 5 + pieces_count]
    (first_new, second_new, weight_new, held, sems) = refs[5 + pieces_count :]
    layer = pl.program_id(0)
    line = pl.program_id(1)

    def copies():
        made = []
        for number, (owner, start, per_piece, turn, side) in enumerate(places):
            tall = pieces[number].shape[1]
            spot = start + (ids[3] ^ turn) * per_piece
            row = pl.multiple_of((ids[2] ^ side) * tall, 16)
            made.append(
                pltpu.make_async_copy(
                    pieces[number],
                    held.at[owner, pl.ds(spot, per_piece), pl.ds(row, tall), :],
                    sems.at[number],
                )
            )
        return made

    @pl.when((layer == 0) & (line == 0))
    def _():
        made = copies()
        for copy in made:
            copy.start()
        for copy in made:
            copy.wait()

    size, scale = clip_scale(squares)
    for part in range(5):
        lanes = slice(part * 128, part * 128 + 128)
        block = line * 5 + part + line // 3 * (blocks - 15)
        gradient = held[layer, block].astype(full) * scale
        results = adamw(
            weight[0, :, lanes], gradient, first[0, :, lanes], second[0, :, lanes], step_rate
        )
        first_new[0, :, lanes] = results[0]
        second_new[0, :, lanes] = results[1]
        weight_new[0, :, lanes] = results[2]


def small_update_kernel(rates, *refs):
    ids, squares, mine, other, grad_norm_p = refs[0:5]
    states = refs[5:23]
    outs = refs[23:41]
    size_out = refs[41]
    size, scale = clip_scale(squares)
    size_out[...] = jnp.broadcast_to(size, size_out.shape)
    first_core = ids[2] == 0
    tall = mine.shape[0] // 2
    here = mine[...].astype(full)
    there = other[...].astype(full)
    even = jnp.where(first_core, here, there)
    odd = jnp.where(first_core, there, here)
    split_part = jnp.concatenate([even[0:tall], odd[0:tall]], axis=0).astype(half)
    shared = jnp.concatenate([even[tall:], odd[tall:]], axis=0).astype(half)
    eye = hot(iota((2 * tall, 2 * tall), 0) == iota((2 * tall, 2 * tall), 1))
    grad_c = dot(split_part, eye, TN)[0:C2]
    classes = states[12].shape[1]
    pick = hot(iota((WIDE, classes), 0) == iota((WIDE, classes), 1) + C2)
    grad_head = dot(split_part, pick)
    grad_b = shared[:, 0:C2].astype(full)
    pick = hot(iota((C0, WIDE), 0) + C2 == iota((C0, WIDE), 1))
    grad_a = dot(pick, shared, NT)
    pick = hot(iota((WIDE, C0), 0) == iota((WIDE, C0), 1) + (C2 + 16))
    grad_stem = dot(shared[0:32], pick)[0:27]
    gradients = (grad_stem, grad_a, grad_b, grad_c, grad_head, grad_norm_p[...])
    for index in range(6):
        weight, first, second = states[3 * index : 3 * index + 3]
        results = adamw(
            weight[...], gradients[index] * scale, first[...], second[...], rates[index]
        )
        for item in range(3):
            outs[3 * index + item][...] = results[item]


def xor_pairs(size, turn):
    return [(index, index ^ turn) for index in range(size)]


def shards(
    images,
    labels,
    corners,
    partners,
    stem_w,
    stem_w_m,
    stem_w_v,
    proj_a,
    proj_a_m,
    proj_a_v,
    proj_b,
    proj_b_m,
    proj_b_v,
    proj_c,
    proj_c_m,
    proj_c_v,
    conv_w,
    conv_w_m,
    conv_w_v,
    head_w,
    head_w_m,
    head_w_v,
    norm_p,
    norm_p_m,
    norm_p_v,
):
    split = lax.axis_size("dp")
    groups = lax.axis_size("filt")
    chips = groups // 2
    devices = split * groups
    count = images.shape[0]
    per = count // split
    rows = per * 64
    band = per * 8
    image_total = float(count * groups)
    row_total = image_total * 64.0
    tall = conv_w.shape[1] // 2
    spot_d = lax.axis_index("dp")
    spot_f = lax.axis_index("filt")
    ids = jnp.stack([spot_d, spot_f, spot_f % 2, spot_f // 2]).astype(jnp.int32)

    def over_dp(value, turn):
        return lax.ppermute(value, "dp", xor_pairs(split, turn))

    def over_filt(value, turn):
        return lax.ppermute(value, "filt", xor_pairs(groups, turn))

    def exchange(stats):
        return lax.all_to_all(stats, ("dp", "filt"), 0, 0)

    numbers = jnp.stack(
        [labels, corners[:, 0], corners[:, 1], partners // count, partners % count], axis=1
    )
    (own_images,) = call(
        image_kernel,
        [VMEM, VMEM],
        [(shape((count, 3 * PLANE), half), VMEM)],
        [],
        2 * 3 * count * 1024 * PLANE,
        2**20,
        24,
    )(images.transpose(1, 0, 2), numbers)
    (own_pack,) = call(
        pack_kernel, [VMEM] * 3, [(shape((2 * tall, WIDE), half), VMEM)], [], 10**8, 2**19, 16
    )(proj_c, head_w, norm_p)
    packs = [own_pack] + [over_dp(own_pack, turn) for turn in range(1, split)]
    far_images = [own_images] + [over_filt(own_images, 2 * turn) for turn in range(1, chips)]
    all_images = []
    for piece in far_images:
        all_images += [piece, over_filt(piece, 1)]
    kernels = []
    for layer in range(2):
        own = cast_half(ids, conv_w, layer)
        pieces = []
        for turn in range(split):
            piece = own if turn == 0 else over_dp(own, turn)
            pieces += [piece, over_filt(piece, 1)]
        kernels.append(pieces)

    line = shape((devices, 1, 2 * C3))
    (
        patches,
        stem_out,
        mid_one,
        mid_two,
        act_three,
        base,
        stats,
        norm_rows,
        head_all,
        proj_t,
        facts,
    ) = call(
        functools.partial(front_kernel, (per, count, groups, devices, split)),
        [SMEM] + [VMEM] * groups + [ANY] * split + [VMEM] * 3,
        [
            (shape((rows, 32), half), VMEM),
            (shape((rows, C0)), VMEM),
            (shape((rows, C1)), VMEM),
            (shape((rows, WIDE)), VMEM),
            (shape((rows, WIDE), half), VMEM),
            (shape((rows, C3)), VMEM),
            (line, VMEM),
            (shape((8, C3)), VMEM),
            (shape((C3, 16), half), VMEM),
            (shape((C3, WIDE), half), VMEM),
            (shape((per, 128)), VMEM),
        ],
        [
            pltpu.VMEM((C3, WIDE), half),
            pltpu.VMEM((per, 32, 128), full),
            pltpu.VMEM((rows, 32), full),
            pltpu.VMEM((32, C0), full),
            pltpu.VMEM((C1, WIDE), half),
            pltpu.VMEM((8, C3), full),
            pltpu.SemaphoreType.DMA((split,)),
        ],
        2 * rows * (32 * 16 + 16 * 160 + 160 * 320 + 320 * 640) * 8,
        10**7,
        48,
    )(ids, *all_images, *packs, stem_w, proj_a, proj_b)
    stats_one = exchange(stats)

    conv_flops = 2 * rows * 9 * C3 * C3
    weight_scratch = [pltpu.VMEM((C3, 9 * C3), half)]
    conv_outs = [
        (shape((rows, C3)), VMEM),
        (shape((rows, TRIPLE), half), ANY),
        (shape((rows, C3)), ANY),
        (line, VMEM),
    ]
    conv_scratch = weight_scratch + [
        pltpu.VMEM((rows, TRIPLE), half),
        pltpu.VMEM((rows, C3), full),
        pltpu.SemaphoreType.DMA((2 * split,)),
        pltpu.SemaphoreType.DMA((2,)),
    ]
    conv_one, field_one, slope_one, stats = call(
        functools.partial(conv_kernel, (per, row_total, split), 0),
        [SMEM] + [VMEM] * 3 + [ANY] * (2 * split),
        conv_outs,
        conv_scratch,
        conv_flops,
        2 * 10**7,
        48,
    )(ids, base, stats_one, norm_rows, *kernels[0])
    stats_two = exchange(stats)
    summed, field_two, slope_two, stats = call(
        functools.partial(conv_kernel, (per, row_total, split), 1),
        [SMEM] + [VMEM] * 4 + [ANY] * (2 * split),
        conv_outs,
        conv_scratch,
        conv_flops,
        2 * 10**7,
        48,
    )(ids, conv_one, stats_two, norm_rows, base, *kernels[1])
    stats_three = exchange(stats)
    slope_three, spread, stats, grad_head = call(
        functools.partial(head_kernel, (per, row_total, image_total, head_w.shape[1])),
        [VMEM] * 5,
        [
            (shape((rows, C3)), VMEM),
            (shape((band, C3)), VMEM),
            (shape((devices, 1, 2 * C3 + 128)), VMEM),
            (shape((C3, 16)), VMEM),
        ],
        [pltpu.VMEM((band, C3), full)] * 3,
        20 * rows * C3,
        8 * 10**6,
        32,
    )(summed, stats_three, norm_rows, head_all, facts)
    stats_four = exchange(stats)
    loss = jnp.sum(stats_four[:, 0, 2 * C3])

    back_scratch = weight_scratch + [
        pltpu.VMEM((rows, TRIPLE), half),
        pltpu.SemaphoreType.DMA((2 * split,)),
    ]
    grad_conv_one, grad_summed, grad_two_half, stats = call(
        functools.partial(back_two_kernel, (per, row_total, split)),
        [SMEM] + [VMEM] * 9 + [ANY] * (2 * split),
        [
            (shape((rows, C3)), VMEM),
            (shape((rows, C3)), VMEM),
            (shape((rows, C3), half), VMEM),
            (line, VMEM),
        ],
        back_scratch,
        conv_flops,
        2 * 10**7,
        52,
    )(
        ids,
        summed,
        slope_three,
        spread,
        stats_three,
        stats_four,
        norm_rows,
        conv_one,
        slope_two,
        stats_two,
        *kernels[1],
    )
    stats_five = exchange(stats)

    def weight_grad(grad_half, field, lines):
        blocks = -(-15 * len(lines) // chips) * chips
        piece = shape((split, blocks, tall, 128), half)
        return call(
            functools.partial(weight_grad_kernel, (lines, split, band, blocks)),
            [SMEM, VMEM, VMEM],
            [(piece, ANY), (piece, ANY)],
            [pltpu.VMEM((blocks, C3, 128), half), pltpu.SemaphoreType.DMA((2 * split,))],
            conv_flops * len(lines) // 3,
            10**7 * len(lines) // 3,
            40,
        )(ids, grad_half, field)

    def add(values):
        return sum(value.astype(full) for value in values).astype(half)

    def reduce_grad(mine, other):
        crossed = over_filt(other, 1)
        pair = [add([mine[turn], crossed[turn]]) for turn in range(split)]
        parts = [pair[0]] + [over_dp(pair[turn], turn) for turn in range(1, split)]
        wide = pair[0].shape[0] // chips
        pieces = []
        for turn in range(chips):
            start = (ids[3] ^ turn) * wide
            pieces.append(
                add([lax.dynamic_slice_in_dim(part, start, wide, axis=0) for part in parts])
            )
        return add(
            [pieces[0]] + [over_filt(pieces[turn], 2 * turn) for turn in range(1, chips)]
        )

    def share_grad(mine):
        pieces = []
        for turn in range(chips):
            piece = mine if turn == 0 else over_filt(mine, 2 * turn)
            pieces += [piece, over_filt(piece, 1)]
        return pieces

    def square_sum(value):
        wide = value.astype(full)
        return jnp.sum(wide * wide)

    mine, other = weight_grad(grad_two_half, field_two, (0, 1, 2))
    reduced_two = reduce_grad(mine, other)

    (grad_one_half,) = call(
        functools.partial(norm_back_kernel, row_total),
        [VMEM] * 5,
        [(shape((rows, C3), half), VMEM)],
        [],
        8 * rows * C3,
        8 * 10**6,
        24,
    )(grad_conv_one, conv_one, stats_two, stats_five, norm_rows)
    mine, other = weight_grad(grad_one_half, field_one, (0, 1, 2))
    reduced_one = reduce_grad(mine, other)
    grad_base, stats = call(
        functools.partial(back_one_kernel, (per, row_total, split)),
        [SMEM] + [VMEM] * 4 + [ANY] * (2 * split),
        [(shape((rows, C3)), VMEM), (line, VMEM)],
        back_scratch,
        conv_flops,
        2 * 10**7,
        48,
    )(ids, grad_one_half, base, slope_one, stats_one, *kernels[0])
    stats_six = exchange(stats)
    small = shape((split, 2 * tall, WIDE), half)
    small_mine, small_other = call(
        functools.partial(trunk_kernel, (per, row_total, split)),
        [SMEM] + [VMEM] * 15,
        [(small, ANY), (small, ANY)],
        [
            pltpu.VMEM((rows, C3), half),
            pltpu.VMEM((rows, WIDE), half),
            pltpu.VMEM((rows, C1), half),
            pltpu.VMEM((rows, C1), half),
            pltpu.VMEM((rows, C0), half),
            pltpu.VMEM((rows, C0), half),
            pltpu.VMEM((C1, WIDE), half),
            pltpu.VMEM((C3, WIDE), half),
            pltpu.VMEM((C1, WIDE), half),
            pltpu.SemaphoreType.DMA((4 * split,)),
        ],
        4 * rows * 320 * 640,
        2 * 10**7,
        48,
    )(
        ids,
        grad_base,
        grad_summed,
        base,
        stats_one,
        stats_six,
        norm_rows,
        proj_t,
        act_three,
        mid_two,
        mid_one,
        stem_out,
        patches,
        proj_a,
        proj_b,
        grad_head,
    )
    crossed = over_filt(small_other, 1)
    pair = [add([small_mine[turn], crossed[turn]]) for turn in range(split)]
    small_sum = add([pair[0]] + [over_dp(pair[turn], turn) for turn in range(1, split)])
    small_sum = add(
        [small_sum] + [over_filt(small_sum, 2 * turn) for turn in range(1, chips)]
    )
    small_far = over_filt(small_sum, 1)

    norm_sums = []
    for stats in (stats_six, stats_five, stats_four):
        sums = jnp.sum(stats[:, 0, :], axis=0)
        norm_sums += [sums[C3 : 2 * C3], sums[0:C3]]
    grad_norm_all = jnp.stack(norm_sums)
    grad_norm_p = lax.dynamic_slice_in_dim(grad_norm_all, spot_d * 2 * tall, 2 * tall, axis=1)
    squares = (
        square_sum(reduced_one)
        + square_sum(reduced_two)
        + square_sum(small_sum[0:tall, 0 : C2 + 16]) / chips
        + square_sum(small_sum[tall:, 0 : C2 + 16]) / (chips * split)
        + square_sum(small_sum[tall:, C2 + 16 :]) / (2 * chips * split)
        + jnp.sum(grad_norm_all * grad_norm_all) / devices
    )
    squares = exchange(jnp.broadcast_to(squares, (devices, 1, 128)))

    pieces = share_grad(reduced_one) + share_grad(reduced_two)
    wide = reduced_one.shape[0]
    places = [
        (owner, 0, wide, turn, side) for owner in range(2) for turn in range(chips) for side in range(2)
    ]
    whole_spec = pl.BlockSpec((1, 2 * tall, C3), lambda layer, line: (layer, 0, line))
    conv_shape = shape(conv_w.shape)
    conv_new = pl.pallas_call(
        functools.partial(
            conv_update_kernel, (len(pieces), places, 15, 0.7 / math.sqrt(9.0 * C3))
        ),
        grid=(2, 9),
        in_specs=[SMEM, VMEM, whole_spec, whole_spec, whole_spec] + [ANY] * len(pieces),
        out_specs=[whole_spec] * 3,
        out_shape=[conv_shape] * 3,
        scratch_shapes=[
            pltpu.VMEM((2, wide * chips, 2 * tall, 128), half),
            pltpu.SemaphoreType.DMA((len(pieces),)),
        ],
        compiler_params=pltpu.CompilerParams(vmem_limit_bytes=40 * MIB),
        cost_estimate=pl.CostEstimate(
            flops=20 * conv_w.size, bytes_accessed=26 * conv_w.size, transcendentals=0
        ),
    )(ids, squares, conv_w, conv_w_m, conv_w_v, *pieces)
    states = (
        (stem_w, stem_w_m, stem_w_v),
        (proj_a, proj_a_m, proj_a_v),
        (proj_b, proj_b_m, proj_b_v),
        (proj_c, proj_c_m, proj_c_v),
        (head_w, head_w_m, head_w_v),
        (norm_p, norm_p_m, norm_p_v),
    )
    rates = (
        0.7 / math.sqrt(27.0),
        0.7 / math.sqrt(C0),
        0.7 / math.sqrt(C1),
        0.7 / math.sqrt(C2),
        0.7 / math.sqrt(C3 / 8.0),
        0.8,
    )
    flat = [item for group in states for item in group]
    small_new = call(
        functools.partial(small_update_kernel, rates),
        [SMEM] + [VMEM] * 22,
        [(shape(item.shape), VMEM) for item in flat] + [(shape((1, 128)), VMEM)],
        [],
        10**7,
        4 * 10**6,
        32,
    )(ids, squares, small_sum, small_far, grad_norm_p, *flat)
    size = small_new[18][0, 0]
    return (
        *small_new[0:12],
        *conv_new,
        *small_new[12:18],
        loss,
        size,
    )


def solution(mesh):
    placed = (
        P("filt", None, None),
        P("filt"),
        P("filt", None),
        P("filt"),
        *([P()] * 9),
        *([P(None, "dp")] * 3),
        *([P(None, "dp", None)] * 3),
        *([P("dp", None)] * 3),
        *([P(None, "dp")] * 3),
    )
    return jax.shard_map(
        shards,
        mesh=mesh,
        in_specs=placed,
        out_specs=(
            *([P()] * 9),
            *([P(None, "dp")] * 3),
            *([P(None, "dp", None)] * 3),
            *([P("dp", None)] * 3),
            *([P(None, "dp")] * 3),
            P(),
            P(),
        ),
        check_vma=False,
    )
```

time: 988 us -> 595 us (0.60)
  local copies, waits for them, and re-layouts: 220 us -> 61.1 us
  Pallas kernels: 0 us -> 157 us
  waiting for transfers between devices: 347 us -> 217 us
  matrix products: 121 us -> 0 us
  blocking collectives: 156 us -> 36.4 us
  starting transfers between devices: 1.27 us -> 82.6 us
  other arithmetic: 107 us -> 28.5 us
  between operations: 23.9 us -> 5.67 us
    ppermute x0 -> x60, waiting for transfers between devices: none -> 195 us  [the longest x18 128 us: over_dp(): return lax.ppermute(value, 'dp', xor_pairs(split, turn))]
    pallas_call x0 -> x16, Pallas kernels: none -> 157 us  [the longest x2 23.3 us: weight_grad(): call(functools.partial(weight_grad_kernel, (lines, split, band, blocks)),...]
    psum x9 -> x0, blocking collectives: 146 us -> none  [the longest x3 47.7 us: norm_forward(): lax.psum((jnp.sum(values, axis=0), jnp.sum(values * values, axis=0)), 'fi...]
    all_gather x3 -> x0, waiting for transfers between devices: 140 us -> none  [the longest x2 114 us: conv_layer(): whole = lax.all_gather(activation, 'dp', axis=1, tiled=True)]
    unnamed x9 -> x0, waiting for transfers between devices: 113 us -> none
    conv_general_dilated x8 -> x0, matrix products: 101 us -> none  [conv_general(): lax.conv_general_dilated(left, right, strides, padding, rhs_dilation=dila...]
    psum x2 -> x0, waiting for transfers between devices: 94.1 us -> none  [the longest x1 47.1 us: shards(): lax.psum(dot_right_t(grad_trunk, proj_c_half).astype(jnp.bfloat16), 'dp')]
    ppermute x0 -> x60, starting transfers between devices: none -> 62.8 us  [the longest x42 41.4 us: over_filt(): return lax.ppermute(value, 'filt', xor_pairs(groups, turn))]
  transfers between devices with their start and end apart: 7 -> 64, of which waited for: 7 -> 19; matrix products, arithmetic and copies ran while one was open for 9% -> 7% of each run, Pallas kernels for 0% -> 15%
where the time goes in v1:
time: 595 us; the launch traced here: 589 us
  waiting for transfers between devices  217 us (36%)
  Pallas kernels  157 us (26%)
  starting transfers between devices  82.6 us (14%)
  local copies, waits for them, and re-layouts  61.1 us (10%)
  blocking collectives  36.4 us (6%)
  other arithmetic  28.5 us (5%)
    ppermute x18, waiting for transfers between devices, over_dp(): return lax.ppermute(value, 'dp', xor_pairs(split, turn))  128 us
    ppermute x42, waiting for transfers between devices, over_filt(): return lax.ppermute(value, 'filt', xor_pairs(groups, turn))  67.1 us
    unnamed x206, local copies, waits for them, and re-layouts  60.2 us
    ppermute x42, starting transfers between devices, over_filt(): return lax.ppermute(value, 'filt', xor_pairs(groups, turn))  41.4 us
    all_to_all x3, blocking collectives, exchange(): return lax.all_to_all(stats, ('dp', 'filt'), 0, 0)  36.4 us
    pallas_call x2, Pallas kernels, weight_grad(): call(functools.partial(weight_grad_kernel, (lines, split, band, blocks)),...  23.3 us
    pallas_call x1, Pallas kernels, shards(): call(functools.partial(back_two_kernel, (per, row_total, split)), [SMEM]...  22.8 us
    all_to_all x4, waiting for transfers between devices, exchange(): return lax.all_to_all(stats, ('dp', 'filt'), 0, 0)  22.8 us
  transfers between devices with their start and end apart: 64, of which 19 were waited for; matrix products, arithmetic and copies ran while one was open for 7% of the time, Pallas kernels for 15%

profile of v1, /device:TPU:0, one launch (start us, length us, event | category | flops | bytes accessed | tf_op | source)
XLA Modules:
  0.0 588.9 jit_solution(7679760201298333013)
XLA Ops:
  3.9 3.1 collective-permute-start.1
  7.0 2.6 collective-permute-start.3
  14.4 4.4 collective-permute-done.1.refs_3_
  18.8 10.5 %collective-permute-done.3.refs_5_ = bf16[72,1920]{1,0:T(8,128)(2,1)S(1)} collective-permute-done((bf16[72,1920]{1,0:T(8,128)(2,1)S(1)}, bf16[72,1920]{1,0:T(8,128)(2,1)S(1)}, u32[]{:S(2)}, u32[]{:S(2)}) %collective-permute-start.3) | collective-permute-done | bytes 276512 | tf_op jit(solution)/shard_map/ppermute | solution.py:837
  32.0 3.8 collective-permute-done.8.refs_11_
  36.4 2.4 collective-permute-start.9
  39.0 3.1 copy-done
  50.5 16.1 %collective-permute-done.11.refs_6_.refs_7_ = bf16[80,5760]{1,0:T(8,128)(2,1)} collective-permute-done((bf16[80,5760]{1,0:T(8,128)(2,1)S(1)}, bf16[80,5760]{1,0:T(8,128)(2,1)}, u32[]{:S(2)}, u32[]{:S(2)}) %collective-permute-start.11) | collective-permute-done | bytes 921632 | tf_op jit(solution)/shard_map/ppermute | solution.py:834
  67.3 19.6 %collective-permute-done.13.refs_8_.refs_9_ = bf16[80,5760]{1,0:T(8,128)(2,1)} collective-permute-done((bf16[80,5760]{1,0:T(8,128)(2,1)S(1)}, bf16[80,5760]{1,0:T(8,128)(2,1)}, u32[]{:S(2)}, u32[]{:S(2)}) %collective-permute-start.13) | collective-permute-done | bytes 921632 | tf_op jit(solution)/shard_map/ppermute | solution.py:834
  87.0 2.0 collective-permute-start.22
  90.5 15.7 %collective-permute-done.18.refs_7_.refs_12_ = bf16[80,5760]{1,0:T(8,128)(2,1)} collective-permute-done((bf16[80,5760]{1,0:T(8,128)(2,1)S(1)}, bf16[80,5760]{1,0:T(8,128)(2,1)}, u32[]{:S(2)}, u32[]{:S(2)}) %collective-permute-start.18) | collective-permute-done | bytes 921632 | tf_op jit(solution)/shard_map/ppermute | solution.py:834
  111.9 9.7 %shard_map.418 = (bf16[1152,32]{1,0:T(8,128)(2,1)S(1)}, f32[1152,16]{1,0:T(8,128)S(1)}, f32[1152,160]{1,0:T(8,128)}, f32[1152,384]{1,0:T(8,128)}, bf16[1152,384]...) custom-call(s32[4]{0:T(128)S(1)} %pad_add_fusion.1.refs_0_.ids, ...), custom_call_target="tpu_custom_call" | custom-call | flops 4775215104 | bytes 10000000 | tf_op jit(solution)/shard_map/pallas_call | solution.py:884
  125.6 8.0 %all-to-all-start = ((f32[32,1,1280]{2,1,0:T(1,128)}), f32[32,1,1280]{2,1,0:T(1,128)S(1)}, u32[]{:S(2)}, u32[]{:S(2)}) async-start(f32[32,1,1280]{2,1,0:T(1,128)} %get-tuple-element.81), calls=%async_computation | async-start | bytes 327680 | tf_op jit(solution)/shard_map/all_to_all | solution.py:840
  134.7 7.3 %all-to-all-done.refs_2_.refs_4_ = f32[32,1,1280]{2,1,0:T(1,128)S(1)} async-done(((f32[32,1,1280]{2,1,0:T(1,128)}), f32[32,1,1280]{2,1,0:T(1,128)S(1)}, u32[]{:S(2)}, u32[]{:S(2)}) %all-to-all-start) | async-done | bytes 163872 | tf_op jit(solution)/shard_map/all_to_all | solution.py:840
  143.2 17.3 %shard_map.420 = (f32[1152,640]{1,0:T(8,128)}, bf16[1152,1920]{1,0:T(8,128)(2,1)}, f32[1152,640]{1,0:T(8,128)}, f32[32,1,1280]{2,1,0:T(1,128)}) custom-call(s32[4]{0:T(128)S(1)} %pad_add_fusion.1.refs_0_.ids, f32[1152,640]{1,0:T(8,128)} %get-tuple-element.80.refs_1_.refs_4_.refs_2_.refs_3_, f32[32,1,1280]{2,1,0:T(1,128)S(1)} %all-to-all-done.refs_2_.refs_4_, ...), custom_call_target="tpu_custom_call" | custom-call | flops 8493465600 | bytes 20000000 | tf_op jit(solution)/shard_map/pallas_call | solution.py:929
  160.6 2.9 all-to-all-start.1
  163.6 8.4 %all-to-all-done.1.refs_2_.refs_9_ = f32[32,1,1280]{2,1,0:T(1,128)S(1)} async-done(((f32[32,1,1280]{2,1,0:T(1,128)}), f32[32,1,1280]{2,1,0:T(1,128)S(1)}, u32[]{:S(2)}, u32[]{:S(2)}) %all-to-all-start.1) | async-done | bytes 163872 | tf_op jit(solution)/shard_map/all_to_all | solution.py:840
  172.0 18.4 %shard_map.422 = (f32[1152,640]{1,0:T(8,128)}, bf16[1152,1920]{1,0:T(8,128)(2,1)}, f32[1152,640]{1,0:T(8,128)}, f32[32,1,1280]{2,1,0:T(1,128)S(1)}) custom-call(s32[4]{0:T(128)S(1)} %pad_add_fusion.1.refs_0_.ids, f32[1152,640]{1,0:T(8,128)} %get-tuple-element.83.refs_1_.refs_7_, f32[32,1,1280]{2,1,0:T(1,128)S(1)} %all-to-all-done.1.refs_2_.refs_9_, ...), custom_call_target="tpu_custom_call" | custom-call | flops 8493465600 | bytes 20000000 | tf_op jit(solution)/shard_map/pallas_call | solution.py:939
  190.4 10.5 %all_to_all.35.refs_1_.refs_4_ = f32[32,1,1280]{2,1,0:T(1,128)S(1)} all-to-all(f32[32,1,1280]{2,1,0:T(1,128)S(1)} %get-tuple-element.86), channel_id=1, replica_groups=mesh['dp'=4,'filt'=8] {'dp','filt'}, dimensions={0} | all-to-all | bytes 327680 | tf_op jit(solution)/shard_map/all_to_all | solution.py:840
  200.9 1.8 copy-done.7
  202.7 3.9 shard_map.423
  208.3 11.3 %all_to_all.36.refs_5_ = f32[32,1,1408]{2,1,0:T(1,128)S(1)} all-to-all(f32[32,1,1408]{2,1,0:T(1,128)S(1)} %get-tuple-element.91), channel_id=1, replica_groups=mesh['dp'=4,'filt'=8] {'dp','filt'}, dimensions={0} | all-to-all | bytes 360448 | tf_op jit(solution)/shard_map/all_to_all | solution.py:840
  219.5 22.8 %shard_map.424 = (f32[1152,640]{1,0:T(8,128)}, f32[1152,640]{1,0:T(8,128)}, bf16[1152,640]{1,0:T(8,128)(2,1)}, f32[32,1,1280]{2,1,0:T(1,128)}) custom-call(s32[4]{0:T(128)S(1)} %pad_add_fusion.1.refs_0_.ids, f32[1152,640]{1,0:T(8,128)} %get-tuple-element.85.refs_0_.refs_1_, f32[1152,640]{1,0:T(8,128)} %copy-done.62, ...), custom_call_target="tpu_custom_call" | custom-call | flops 8493465600 | bytes 20000000 | tf_op jit(solution)/shard_map/pallas_call | solution.py:970
  242.4 2.8 all-to-all-start.4
  245.2 2.2 copy-done.79
  248.8 11.6 %shard_map.427 = (bf16[4,48,80,128]{3,2,1,0:T(8,128)(2,1)S(1)}, bf16[4,48,80,128]{3,2,1,0:T(8,128)(2,1)}) custom-call(s32[4]{0:T(128)S(1)} %pad_add_fusion.1.refs_0_.ids, bf16[1152,640]{1,0:T(8,128)(2,1)S(1)} %copy-done.80, bf16[1152,1920]{1,0:T(8,128)(2,1)S(1)} %copy-done.79), custom_call_target="tpu_custom_call" | custom-call | flops 8493465600 | bytes 10000000 | tf_op jit(solution)/shard_map/pallas_call | solution.py:1001
  260.4 2.0 copy-done.3
  262.8 1.8 copy-done.6
  267.1 2.8 copy-done.81
  269.9 11.7 %shard_map.426 = (bf16[4,48,80,128]{3,2,1,0:T(8,128)(2,1)S(1)}, bf16[4,48,80,128]{3,2,1,0:T(8,128)(2,1)}) custom-call(s32[4]{0:T(128)S(1)} %pad_add_fusion.1.refs_0_.ids, bf16[1152,640]{1,0:T(8,128)(2,1)S(1)} %shard_map.425.refs_1_, bf16[1152,1920]{1,0:T(8,128)(2,1)S(1)} %copy-done.81), custom_call_target="tpu_custom_call" | custom-call | flops 8493465600 | bytes 10000000 | tf_op jit(solution)/shard_map/pallas_call | solution.py:1001
  281.5 1.9 copy-done.2
  283.6 20.2 %shard_map.428 = (f32[1152,640]{1,0:T(8,128)}, f32[32,1,1280]{2,1,0:T(1,128)S(1)}) custom-call(s32[4]{0:T(128)S(1)} %pad_add_fusion.1.refs_0_.ids, bf16[1152,640]{1,0:T(8,128)(2,1)} %copy-done.8, f32[1152,640]{1,0:T(8,128)} %get-tuple-element.80.refs_1_.refs_4_.refs_2_.refs_3_, f32[1152,640]{1,0:T(8,128)} %get-tuple-element.102.refs_3_, ...), custom_call_target="tpu_custom_call" | custom-call | flops 8493465600 | bytes 20000000 | tf_op jit(solution)/shard_map/pallas_call | solution.py:1054
  303.8 14.7 %all_to_all.37.refs_5_ = f32[32,1,1280]{2,1,0:T(1,128)S(1)} all-to-all(f32[32,1,1280]{2,1,0:T(1,128)S(1)} %get-tuple-element.105), channel_id=1, replica_groups=mesh['dp'=4,'filt'=8] {'dp','filt'}, dimensions={0} | all-to-all | bytes 327680 | tf_op jit(solution)/shard_map/all_to_all | solution.py:840
  318.6 12.2 %shard_map.429 = (bf16[4,160,384]{2,1,0:T(8,128)(2,1)S(1)}, bf16[4,160,384]{2,1,0:T(8,128)(2,1)}) custom-call(s32[4]{0:T(128)S(1)} %pad_add_fusion.1.refs_0_.ids, f32[1152,640]{1,0:T(8,128)} %get-tuple-element.103.refs_1_, f32[1152,640]{1,0:T(8,128)} %get-tuple-element.104.refs_2_, f32[1152,640]{1,0:T(8,128)} %get-tuple-element.80.refs_1_.refs_4_.refs_2_.refs_3_, ...), custom_call_target="tpu_custom_call" | custom-call | flops 943718400 | bytes 20000000 | tf_op jit(solution)/shard_map/pallas_call | solution.py:1065
  331.4 4.7 add_convert_fusion.3
  337.4 2.3 collective-permute-start.34
  341.6 6.0 %add_convert_fusion.7 = (bf16[1,48,80,128]{3,2,1,0:T(8,128)(2,1)}, bf16[48,80,128]{2,1,0:T(8,128)(2,1)}, bf16[48,80,128]{2,1,0:T(8,128)(2,1)}, bf16[48,80,128]{2,1,0:T(8,128)(2,1)}) fusion(bf16[4,48,80,128]{3,2,1,0:T(8,128)(2,1)} %collective-permute-done.24, bf16[4,48,80,128]{3,2,1,0:T(8,128)(2,1)} %copy-done.2), kind=kLoop, calls=%fused_computation.7 | loop fusion | flops 7864320 | bytes 11796480 | tf_op jit(solution)/shard_map/convert_element_type | solution.py:1012
  347.6 13.5 %collective-permute-done.32 = bf16[48,80,128]{2,1,0:T(8,128)(2,1)} collective-permute-done((bf16[48,80,128]{2,1,0:T(8,128)(2,1)}, bf16[48,80,128]{2,1,0:T(8,128)(2,1)}, u32[]{:S(2)}, u32[]{:S(2)}) %collective-permute-start.32) | collective-permute-done | bytes 983072 | tf_op jit(solution)/shard_map/ppermute | solution.py:834
  361.5 21.0 %collective-permute-done.33 = bf16[48,80,128]{2,1,0:T(8,128)(2,1)S(1)} collective-permute-done((bf16[48,80,128]{2,1,0:T(8,128)(2,1)}, bf16[48,80,128]{2,1,0:T(8,128)(2,1)S(1)}, u32[]{:S(2)}, u32[]{:S(2)}) %collective-permute-start.33) | collective-permute-done | bytes 983072 | tf_op jit(solution)/shard_map/ppermute | solution.py:834
  382.9 2.6 collective-permute-start.27
  385.6 3.0 fusion.14
  391.2 37.8 %collective-permute-done.41 = bf16[160,384]{1,0:T(8,128)(2,1)S(1)} collective-permute-done((bf16[160,384]{1,0:T(8,128)(2,1)}, bf16[160,384]{1,0:T(8,128)(2,1)S(1)}, u32[]{:S(2)}, u32[]{:S(2)}) %collective-permute-start.41) | collective-permute-done | bytes 122912 | tf_op jit(solution)/shard_map/ppermute | solution.py:834
  430.3 2.0 collective-permute-start.37
  434.1 14.3 %collective-permute-done.36 = bf16[12,80,128]{2,1,0:T(8,128)(2,1)S(1)} collective-permute-done((bf16[12,80,128]{2,1,0:T(8,128)(2,1)}, bf16[12,80,128]{2,1,0:T(8,128)(2,1)S(1)}, u32[]{:S(2)}, u32[]{:S(2)}) %collective-permute-start.36) | collective-permute-done | bytes 245792 | tf_op jit(solution)/shard_map/ppermute | solution.py:837
  448.4 5.6 collective-permute-start.43
  454.0 2.3 multiply_reduce_fusion
  456.3 2.6 collective-permute-start.44
  458.9 1.8 collective-permute-start.56
  460.7 3.0 fusion.26
  464.0 2.9 collective-permute-start.29
  471.8 3.9 collective-permute-done.56.refs_17_
  475.8 3.1 collective-permute-start.58
  478.9 2.2 collective-permute-done.28
  481.1 15.8 %collective-permute-done.29 = bf16[12,80,128]{2,1,0:T(8,128)(2,1)} collective-permute-done((bf16[12,80,128]{2,1,0:T(8,128)(2,1)S(1)}, bf16[12,80,128]{2,1,0:T(8,128)(2,1)}, u32[]{:S(2)}, u32[]{:S(2)}) %collective-permute-start.29) | collective-permute-done | bytes 245792 | tf_op jit(solution)/shard_map/ppermute | solution.py:837
  497.4 2.4 multiply_reduce_fusion.1
  499.8 5.3 collective-permute-start.47
  505.1 4.3 collective-permute-start.49
  512.8 3.6 collective-permute-done.47.refs_7_
  516.4 10.5 %collective-permute-done.49.refs_9_ = bf16[12,80,128]{2,1,0:T(8,128)(2,1)} collective-permute-done((bf16[12,80,128]{2,1,0:T(8,128)(2,1)S(1)}, bf16[12,80,128]{2,1,0:T(8,128)(2,1)}, u32[]{:S(2)}, u32[]{:S(2)}) %collective-permute-start.49) | collective-permute-done | bytes 245792 | tf_op jit(solution)/shard_map/ppermute | solution.py:837
  532.5 6.1 %all-to-all-start.6 = ((f32[32,1,128]{2,1,0:T(1,128)}), f32[32,1,128]{2,1,0:T(1,128)S(1)}, u32[]{:S(2)}, u32[]{:S(2)}) async-start(f32[32,1,128]{2,1,0:T(1,128)} %broadcast_in_dim.3), calls=%async_computation.6 | async-start | bytes 32768 | tf_op jit(solution)/shard_map/all_to_all | solution.py:840
  538.7 7.0 %all-to-all-done.6.refs_1_ = f32[32,1,128]{2,1,0:T(1,128)S(1)} async-done(((f32[32,1,128]{2,1,0:T(1,128)}), f32[32,1,128]{2,1,0:T(1,128)S(1)}, u32[]{:S(2)}, u32[]{:S(2)}) %all-to-all-start.6) | async-done | bytes 16416 | tf_op jit(solution)/shard_map/all_to_all | solution.py:840
  547.7 2.1 shard_map.430
  562.0 3.1 copy-done.1
  566.0 22.7 %shard_map.431 = (f32[2,160,5760]{2,1,0:T(8,128)}, f32[2,160,5760]{2,1,0:T(8,128)}, f32[2,160,5760]{2,1,0:T(8,128)}) custom-call(s32[4]{0:T(128)S(1)} %pad_add_fusion.1.refs_0_.ids, f32[32,1,128]{2,1,0:T(1,128)S(1)} %all-to-all-done.6.refs_1_, f32[2,160,5760]{2,1,0:T(8,128)S(1)} %copy-done.1, f32[2,160,5760]{2,1,0:T(8,128)} %refs_3_.1, ...), custom_call_target="tpu_custom_call" | custom-call | flops 36864000 | bytes 47923200 | tf_op jit(solution)/shard_map/pallas_call | solution.py:1133
  (321 shorter events, 76.1 us)
Async XLA Ops:
  3.9 14.9 %collective-permute-start.1 = (bf16[72,1920]{1,0:T(8,128)(2,1)S(1)}, bf16[72,1920]{1,0:T(8,128)(2,1)S(1)}, u32[]{:S(2)}, u32[]{:S(2)}) collective-permute-start(bf16[72,1920]{1,0:T(8,128)(2,1)S(1)} %shard_map.416.refs_1_), channel_id=1, source_target_pairs={{0,2},{1,3},{2,0},{3,1},{4,6},{5,7},{6,4},{7,5},{8,10},{9,11},{10,... | collective-permute-start | bytes 829448 | tf_op jit(solution)/shard_map/ppermute | solution.py:837
  7.0 22.3 %collective-permute-start.3 = (bf16[72,1920]{1,0:T(8,128)(2,1)S(1)}, bf16[72,1920]{1,0:T(8,128)(2,1)S(1)}, u32[]{:S(2)}, u32[]{:S(2)}) collective-permute-start(bf16[72,1920]{1,0:T(8,128)(2,1)S(1)} %shard_map.416.refs_1_), channel_id=1, source_target_pairs={{0,4},{1,5},{2,6},{3,7},{4,0},{5,1},{6,2},{7,3},{8,12},{9,13},{10,... | collective-permute-start | bytes 829448 | tf_op jit(solution)/shard_map/ppermute | solution.py:837
  9.6 19.7 %collective-permute-start.5 = (bf16[72,1920]{1,0:T(8,128)(2,1)S(1)}, bf16[72,1920]{1,0:T(8,128)(2,1)}, u32[]{:S(2)}, u32[]{:S(2)}) collective-permute-start(bf16[72,1920]{1,0:T(8,128)(2,1)S(1)} %shard_map.416.refs_1_), channel_id=1, source_target_pairs={{0,6},{1,7},{2,4},{3,5},{4,2},{5,3},{6,0},{7,1},{8,14},{9,15},{10,... | collective-permute-start | bytes 829448 | tf_op jit(solution)/shard_map/ppermute | solution.py:837
  12.6 17.3 %collective-permute-start.7 = (bf16[160,384]{1,0:T(8,128)(2,1)S(1)}, bf16[160,384]{1,0:T(8,128)(2,1)S(1)}, u32[]{:S(2)}, u32[]{:S(2)}) collective-permute-start(bf16[160,384]{1,0:T(8,128)(2,1)S(1)} %shard_map.417.refs_9_), channel_id=1, source_target_pairs={{0,8},{8,0},{16,24},{24,16},{1,9},{9,1},{17,25},{25,17},{2,10},{10... | collective-permute-start | bytes 368648 | tf_op jit(solution)/shard_map/ppermute | solution.py:834
  14.3 29.5 %collective-permute-start = (bf16[72,1920]{1,0:T(8,128)(2,1)S(1)}, bf16[72,1920]{1,0:T(8,128)(2,1)S(1)}, u32[]{:S(2)}, u32[]{:S(2)}) collective-permute-start(bf16[72,1920]{1,0:T(8,128)(2,1)S(1)} %shard_map.416.refs_1_), channel_id=1, source_target_pairs={{0,1},{1,0},{2,3},{3,2},{4,5},{5,4},{6,7},{7,6},{8,9},{9,8},{10,11... | collective-permute-start | bytes 829448 | tf_op jit(solution)/shard_map/ppermute | solution.py:837
  18.8 27.2 %collective-permute-start.2 = (bf16[72,1920]{1,0:T(8,128)(2,1)S(1)}, bf16[72,1920]{1,0:T(8,128)(2,1)S(1)}, u32[]{:S(2)}, u32[]{:S(2)}) collective-permute-start(bf16[72,1920]{1,0:T(8,128)(2,1)S(1)} %collective-permute-done.1.refs_3_), channel_id=1, source_target_pairs={{0,1},{1,0},{2,3},{3,2},{4,5},{5,4},{6,7},{7,6},{8,9},{9,8},{10,11... | collective-permute-start | bytes 829448 | tf_op jit(solution)/shard_map/ppermute | solution.py:837
  29.3 18.8 %collective-permute-start.4 = (bf16[72,1920]{1,0:T(8,128)(2,1)S(1)}, bf16[72,1920]{1,0:T(8,128)(2,1)S(1)}, u32[]{:S(2)}, u32[]{:S(2)}) collective-permute-start(bf16[72,1920]{1,0:T(8,128)(2,1)S(1)} %collective-permute-done.3.refs_5_), channel_id=1, source_target_pairs={{0,1},{1,0},{2,3},{3,2},{4,5},{5,4},{6,7},{7,6},{8,9},{9,8},{10,11... | collective-permute-start | bytes 829448 | tf_op jit(solution)/shard_map/ppermute | solution.py:837
  29.3 20.5 %collective-permute-start.6 = (bf16[72,1920]{1,0:T(8,128)(2,1)}, bf16[72,1920]{1,0:T(8,128)(2,1)}, u32[]{:S(2)}, u32[]{:S(2)}) collective-permute-start(bf16[72,1920]{1,0:T(8,128)(2,1)} %collective-permute-done.5.refs_7_), channel_id=1, source_target_pairs={{0,1},{1,0},{2,3},{3,2},{4,5},{5,4},{6,7},{7,6},{8,9},{9,8},{10,11... | collective-permute-start | bytes 829448 | tf_op jit(solution)/shard_map/ppermute | solution.py:837
  30.5 5.3 collective-permute-start.8
  36.4 6.7 %collective-permute-start.9 = (bf16[160,384]{1,0:T(8,128)(2,1)S(1)}, bf16[160,384]{1,0:T(8,128)(2,1)}, u32[]{:S(2)}, u32[]{:S(2)}) collective-permute-start(bf16[160,384]{1,0:T(8,128)(2,1)S(1)} %shard_map.417.refs_9_), channel_id=1, source_target_pairs={{0,24},{8,16},{16,8},{24,0},{1,25},{9,17},{17,9},{25,1},{2,26},{10... | collective-permute-start | bytes 368648 | tf_op jit(solution)/shard_map/ppermute | solution.py:834
  43.1 23.5 %collective-permute-start.11 = (bf16[80,5760]{1,0:T(8,128)(2,1)S(1)}, bf16[80,5760]{1,0:T(8,128)(2,1)}, u32[]{:S(2)}, u32[]{:S(2)}) collective-permute-start(bf16[80,5760]{1,0:T(8,128)(2,1)S(1)} %shard_map.419.refs_4_.refs_5_), channel_id=1, source_target_pairs={{0,8},{8,0},{16,24},{24,16},{1,9},{9,1},{17,25},{25,17},{2,10},{10... | collective-permute-start | bytes 2764808 | tf_op jit(solution)/shard_map/ppermute | solution.py:834
  44.5 42.4 %collective-permute-start.13 = (bf16[80,5760]{1,0:T(8,128)(2,1)S(1)}, bf16[80,5760]{1,0:T(8,128)(2,1)}, u32[]{:S(2)}, u32[]{:S(2)}) collective-permute-start(bf16[80,5760]{1,0:T(8,128)(2,1)S(1)} %shard_map.419.refs_4_.refs_5_), channel_id=1, source_target_pairs={{0,16},{8,24},{16,0},{24,8},{1,17},{9,25},{17,1},{25,9},{2,18},{10... | collective-permute-start | bytes 2764808 | tf_op jit(solution)/shard_map/ppermute | solution.py:834
  46.7 42.2 %collective-permute-start.15 = (bf16[80,5760]{1,0:T(8,128)(2,1)S(1)}, bf16[80,5760]{1,0:T(8,128)(2,1)}, u32[]{:S(2)}, u32[]{:S(2)}) collective-permute-start(bf16[80,5760]{1,0:T(8,128)(2,1)S(1)} %shard_map.419.refs_4_.refs_5_), channel_id=1, source_target_pairs={{0,24},{8,16},{16,8},{24,0},{1,25},{9,17},{17,9},{25,1},{2,26},{10... | collective-permute-start | bytes 2764808 | tf_op jit(solution)/shard_map/ppermute | solution.py:834
  48.8 40.2 %collective-permute-start.10 = (bf16[80,5760]{1,0:T(8,128)(2,1)S(1)}, bf16[80,5760]{1,0:T(8,128)(2,1)S(1)}, u32[]{:S(2)}, u32[]{:S(2)}) collective-permute-start(bf16[80,5760]{1,0:T(8,128)(2,1)S(1)} %shard_map.419.refs_4_.refs_5_), channel_id=1, source_target_pairs={{0,1},{1,0},{2,3},{3,2},{4,5},{5,4},{6,7},{7,6},{8,9},{9,8},{10,11... | collective-permute-start | bytes 2764808 | tf_op jit(solution)/shard_map/ppermute | solution.py:837
  49.8 56.4 %collective-permute-start.18 = (bf16[80,5760]{1,0:T(8,128)(2,1)S(1)}, bf16[80,5760]{1,0:T(8,128)(2,1)}, u32[]{:S(2)}, u32[]{:S(2)}) collective-permute-start(bf16[80,5760]{1,0:T(8,128)(2,1)S(1)} %shard_map.421.refs_5_.refs_10_), channel_id=1, source_target_pairs={{0,8},{8,0},{16,24},{24,16},{1,9},{9,1},{17,25},{25,17},{2,10},{10... | collective-permute-start | bytes 2764808 | tf_op jit(solution)/shard_map/ppermute | solution.py:834
  66.6 66.9 %collective-permute-start.20 = (bf16[80,5760]{1,0:T(8,128)(2,1)S(1)}, bf16[80,5760]{1,0:T(8,128)(2,1)}, u32[]{:S(2)}, u32[]{:S(2)}) collective-permute-start(bf16[80,5760]{1,0:T(8,128)(2,1)S(1)} %shard_map.421.refs_5_.refs_10_), channel_id=1, source_target_pairs={{0,16},{8,24},{16,0},{24,8},{1,17},{9,25},{17,1},{25,9},{2,18},{10... | collective-permute-start | bytes 2764808 | tf_op jit(solution)/shard_map/ppermute | solution.py:834
  87.0 47.0 %collective-permute-start.22 = (bf16[80,5760]{1,0:T(8,128)(2,1)S(1)}, bf16[80,5760]{1,0:T(8,128)(2,1)}, u32[]{:S(2)}, u32[]{:S(2)}) collective-permute-start(bf16[80,5760]{1,0:T(8,128)(2,1)S(1)} %shard_map.421.refs_5_.refs_10_), channel_id=1, source_target_pairs={{0,24},{8,16},{16,8},{24,0},{1,25},{9,17},{17,9},{25,1},{2,26},{10... | collective-permute-start | bytes 2764808 | tf_op jit(solution)/shard_map/ppermute | solution.py:834
  89.0 45.1 %collective-permute-start.12 = (bf16[80,5760]{1,0:T(8,128)(2,1)}, bf16[80,5760]{1,0:T(8,128)(2,1)}, u32[]{:S(2)}, u32[]{:S(2)}) collective-permute-start(bf16[80,5760]{1,0:T(8,128)(2,1)} %collective-permute-done.11.refs_6_.refs_7_), channel_id=1, source_target_pairs={{0,1},{1,0},{2,3},{3,2},{4,5},{5,4},{6,7},{7,6},{8,9},{9,8},{10,11... | collective-permute-start | bytes 2764808 | tf_op jit(solution)/shard_map/ppermute | solution.py:837
  90.0 44.5 %collective-permute-start.14 = (bf16[80,5760]{1,0:T(8,128)(2,1)}, bf16[80,5760]{1,0:T(8,128)(2,1)}, u32[]{:S(2)}, u32[]{:S(2)}) collective-permute-start(bf16[80,5760]{1,0:T(8,128)(2,1)} %collective-permute-done.13.refs_8_.refs_9_), channel_id=1, source_target_pairs={{0,1},{1,0},{2,3},{3,2},{4,5},{5,4},{6,7},{7,6},{8,9},{9,8},{10,11... | collective-permute-start | bytes 2764808 | tf_op jit(solution)/shard_map/ppermute | solution.py:837
  106.2 35.8 %collective-permute-start.16 = (bf16[80,5760]{1,0:T(8,128)(2,1)}, bf16[80,5760]{1,0:T(8,128)(2,1)}, u32[]{:S(2)}, u32[]{:S(2)}) collective-permute-start(bf16[80,5760]{1,0:T(8,128)(2,1)} %collective-permute-done.15.refs_10_.refs_11_), channel_id=1, source_target_pairs={{0,1},{1,0},{2,3},{3,2},{4,5},{5,4},{6,7},{7,6},{8,9},{9,8},{10,11... | collective-permute-start | bytes 2764808 | tf_op jit(solution)/shard_map/ppermute | solution.py:837
  125.6 16.4 %all-to-all-start = ((f32[32,1,1280]{2,1,0:T(1,128)}), f32[32,1,1280]{2,1,0:T(1,128)S(1)}, u32[]{:S(2)}, u32[]{:S(2)}) async-start(f32[32,1,1280]{2,1,0:T(1,128)} %get-tuple-element.81), calls=%async_computation | async-start | bytes 327680 | tf_op jit(solution)/shard_map/all_to_all | solution.py:840
  133.6 30.0 %collective-permute-start.17 = (bf16[80,5760]{1,0:T(8,128)(2,1)S(1)}, bf16[80,5760]{1,0:T(8,128)(2,1)}, u32[]{:S(2)}, u32[]{:S(2)}) collective-permute-start(bf16[80,5760]{1,0:T(8,128)(2,1)S(1)} %shard_map.421.refs_5_.refs_10_), channel_id=1, source_target_pairs={{0,1},{1,0},{2,3},{3,2},{4,5},{5,4},{6,7},{7,6},{8,9},{9,8},{10,11... | collective-permute-start | bytes 2764808 | tf_op jit(solution)/shard_map/ppermute | solution.py:837
  134.0 29.6 %collective-permute-start.19 = (bf16[80,5760]{1,0:T(8,128)(2,1)}, bf16[80,5760]{1,0:T(8,128)(2,1)}, u32[]{:S(2)}, u32[]{:S(2)}) collective-permute-start(bf16[80,5760]{1,0:T(8,128)(2,1)} %collective-permute-done.18.refs_7_.refs_12_), channel_id=1, source_target_pairs={{0,1},{1,0},{2,3},{3,2},{4,5},{5,4},{6,7},{7,6},{8,9},{9,8},{10,11... | collective-permute-start | bytes 2764808 | tf_op jit(solution)/shard_map/ppermute | solution.py:837
  134.1 29.4 %collective-permute-start.21 = (bf16[80,5760]{1,0:T(8,128)(2,1)}, bf16[80,5760]{1,0:T(8,128)(2,1)}, u32[]{:S(2)}, u32[]{:S(2)}) collective-permute-start(bf16[80,5760]{1,0:T(8,128)(2,1)} %collective-permute-done.20.refs_9_.refs_14_), channel_id=1, source_target_pairs={{0,1},{1,0},{2,3},{3,2},{4,5},{5,4},{6,7},{7,6},{8,9},{9,8},{10,11... | collective-permute-start | bytes 2764808 | tf_op jit(solution)/shard_map/ppermute | solution.py:837
  134.5 29.1 %collective-permute-start.23 = (bf16[80,5760]{1,0:T(8,128)(2,1)}, bf16[80,5760]{1,0:T(8,128)(2,1)}, u32[]{:S(2)}, u32[]{:S(2)}) collective-permute-start(bf16[80,5760]{1,0:T(8,128)(2,1)} %collective-permute-done.22.refs_11_.refs_16_), channel_id=1, source_target_pairs={{0,1},{1,0},{2,3},{3,2},{4,5},{5,4},{6,7},{7,6},{8,9},{9,8},{10,11... | collective-permute-start | bytes 2764808 | tf_op jit(solution)/shard_map/ppermute | solution.py:837
  160.6 11.4 %all-to-all-start.1 = ((f32[32,1,1280]{2,1,0:T(1,128)}), f32[32,1,1280]{2,1,0:T(1,128)S(1)}, u32[]{:S(2)}, u32[]{:S(2)}) async-start(f32[32,1,1280]{2,1,0:T(1,128)} %get-tuple-element.84), calls=%async_computation.1 | async-start | bytes 327680 | tf_op jit(solution)/shard_map/all_to_all | solution.py:840
  242.4 20.4 %all-to-all-start.4 = ((f32[32,1,1280]{2,1,0:T(1,128)}), f32[32,1,1280]{2,1,0:T(1,128)S(1)}, u32[]{:S(2)}, u32[]{:S(2)}) async-start(f32[32,1,1280]{2,1,0:T(1,128)} %get-tuple-element.94), calls=%async_computation.4 | async-start | bytes 327680 | tf_op jit(solution)/shard_map/all_to_all | solution.py:840
  262.4 69.0 %collective-permute-start.31 = (bf16[4,48,80,128]{3,2,1,0:T(8,128)(2,1)}, bf16[4,48,80,128]{3,2,1,0:T(8,128)(2,1)}, u32[]{:S(2)}, u32[]{:S(2)}) collective-permute-start(bf16[4,48,80,128]{3,2,1,0:T(8,128)(2,1)} %get-tuple-element.101), channel_id=1, source_target_pairs={{0,1},{1,0},{2,3},{3,2},{4,5},{5,4},{6,7},{7,6},{8,9},{9,8},{10,11... | collective-permute-start | bytes 11796488 | tf_op jit(solution)/shard_map/ppermute | solution.py:837
  283.5 57.4 %collective-permute-start.24 = (bf16[4,48,80,128]{3,2,1,0:T(8,128)(2,1)}, bf16[4,48,80,128]{3,2,1,0:T(8,128)(2,1)}, u32[]{:S(2)}, u32[]{:S(2)}) collective-permute-start(bf16[4,48,80,128]{3,2,1,0:T(8,128)(2,1)} %get-tuple-element.97), channel_id=1, source_target_pairs={{0,1},{1,0},{2,3},{3,2},{4,5},{5,4},{6,7},{7,6},{8,9},{9,8},{10,11... | collective-permute-start | bytes 11796488 | tf_op jit(solution)/shard_map/ppermute | solution.py:837
  330.8 8.8 %collective-permute-start.38 = (bf16[4,160,384]{2,1,0:T(8,128)(2,1)}, bf16[4,160,384]{2,1,0:T(8,128)(2,1)S(1)}, u32[]{:S(2)}, u32[]{:S(2)}) collective-permute-start(bf16[4,160,384]{2,1,0:T(8,128)(2,1)} %get-tuple-element.114), channel_id=1, source_target_pairs={{0,1},{1,0},{2,3},{3,2},{4,5},{5,4},{6,7},{7,6},{8,9},{9,8},{10,11... | collective-permute-start | bytes 1474568 | tf_op jit(solution)/shard_map/ppermute | solution.py:837
  336.1 24.9 %collective-permute-start.32 = (bf16[48,80,128]{2,1,0:T(8,128)(2,1)}, bf16[48,80,128]{2,1,0:T(8,128)(2,1)}, u32[]{:S(2)}, u32[]{:S(2)}) collective-permute-start(bf16[48,80,128]{2,1,0:T(8,128)(2,1)} %get-tuple-element.192), channel_id=1, source_target_pairs={{0,8},{8,0},{16,24},{24,16},{1,9},{9,1},{17,25},{25,17},{2,10},{10... | collective-permute-start | bytes 2949128 | tf_op jit(solution)/shard_map/ppermute | solution.py:834
  336.6 45.9 %collective-permute-start.33 = (bf16[48,80,128]{2,1,0:T(8,128)(2,1)}, bf16[48,80,128]{2,1,0:T(8,128)(2,1)S(1)}, u32[]{:S(2)}, u32[]{:S(2)}) collective-permute-start(bf16[48,80,128]{2,1,0:T(8,128)(2,1)} %get-tuple-element.191), channel_id=1, source_target_pairs={{0,16},{8,24},{16,0},{24,8},{1,17},{9,25},{17,1},{25,9},{2,18},{10... | collective-permute-start | bytes 2949128 | tf_op jit(solution)/shard_map/ppermute | solution.py:834
  337.4 45.6 %collective-permute-start.34 = (bf16[48,80,128]{2,1,0:T(8,128)(2,1)}, bf16[48,80,128]{2,1,0:T(8,128)(2,1)}, u32[]{:S(2)}, u32[]{:S(2)}) collective-permute-start(bf16[48,80,128]{2,1,0:T(8,128)(2,1)} %get-tuple-element.190), channel_id=1, source_target_pairs={{0,24},{8,16},{16,8},{24,0},{1,25},{9,17},{17,9},{25,1},{2,26},{10... | collective-permute-start | bytes 2949128 | tf_op jit(solution)/shard_map/ppermute | solution.py:834
  340.4 48.2 %collective-permute-start.39 = (bf16[160,384]{1,0:T(8,128)(2,1)S(1)}, bf16[160,384]{1,0:T(8,128)(2,1)S(1)}, u32[]{:S(2)}, u32[]{:S(2)}) collective-permute-start(bf16[160,384]{1,0:T(8,128)(2,1)S(1)} %get-tuple-element.203), channel_id=1, source_target_pairs={{0,8},{8,0},{16,24},{24,16},{1,9},{9,1},{17,25},{25,17},{2,10},{10... | collective-permute-start | bytes 368648 | tf_op jit(solution)/shard_map/ppermute | solution.py:834
  340.9 49.8 %collective-permute-start.40 = (bf16[160,384]{1,0:T(8,128)(2,1)}, bf16[160,384]{1,0:T(8,128)(2,1)}, u32[]{:S(2)}, u32[]{:S(2)}) collective-permute-start(bf16[160,384]{1,0:T(8,128)(2,1)} %get-tuple-element.205), channel_id=1, source_target_pairs={{0,16},{8,24},{16,0},{24,8},{1,17},{9,25},{17,1},{25,9},{2,18},{10... | collective-permute-start | bytes 368648 | tf_op jit(solution)/shard_map/ppermute | solution.py:834
  361.1 95.3 %collective-permute-start.25 = (bf16[48,80,128]{2,1,0:T(8,128)(2,1)}, bf16[48,80,128]{2,1,0:T(8,128)(2,1)}, u32[]{:S(2)}, u32[]{:S(2)}) collective-permute-start(bf16[48,80,128]{2,1,0:T(8,128)(2,1)} %get-tuple-element.196), channel_id=1, source_target_pairs={{0,8},{8,0},{16,24},{24,16},{1,9},{9,1},{17,25},{25,17},{2,10},{10... | collective-permute-start | bytes 2949128 | tf_op jit(solution)/shard_map/ppermute | solution.py:834
  382.5 76.4 %collective-permute-start.26 = (bf16[48,80,128]{2,1,0:T(8,128)(2,1)}, bf16[48,80,128]{2,1,0:T(8,128)(2,1)}, u32[]{:S(2)}, u32[]{:S(2)}) collective-permute-start(bf16[48,80,128]{2,1,0:T(8,128)(2,1)} %get-tuple-element.195), channel_id=1, source_target_pairs={{0,16},{8,24},{16,0},{24,8},{1,17},{9,25},{17,1},{25,9},{2,18},{10... | collective-permute-start | bytes 2949128 | tf_op jit(solution)/shard_map/ppermute | solution.py:834
  382.9 76.0 %collective-permute-start.27 = (bf16[48,80,128]{2,1,0:T(8,128)(2,1)}, bf16[48,80,128]{2,1,0:T(8,128)(2,1)}, u32[]{:S(2)}, u32[]{:S(2)}) collective-permute-start(bf16[48,80,128]{2,1,0:T(8,128)(2,1)} %get-tuple-element.194), channel_id=1, source_target_pairs={{0,24},{8,16},{16,8},{24,0},{1,25},{9,17},{17,9},{25,1},{2,26},{10... | collective-permute-start | bytes 2949128 | tf_op jit(solution)/shard_map/ppermute | solution.py:834
  388.6 41.7 %collective-permute-start.35 = (bf16[12,80,128]{2,1,0:T(8,128)(2,1)}, bf16[12,80,128]{2,1,0:T(8,128)(2,1)}, u32[]{:S(2)}, u32[]{:S(2)}) collective-permute-start(bf16[12,80,128]{2,1,0:T(8,128)(2,1)} %get-tuple-element.197), channel_id=1, source_target_pairs={{0,2},{1,3},{2,0},{3,1},{4,6},{5,7},{6,4},{7,5},{8,10},{9,11},{10,... | collective-permute-start | bytes 737288 | tf_op jit(solution)/shard_map/ppermute | solution.py:837
  390.7 38.3 %collective-permute-start.41 = (bf16[160,384]{1,0:T(8,128)(2,1)}, bf16[160,384]{1,0:T(8,128)(2,1)S(1)}, u32[]{:S(2)}, u32[]{:S(2)}) collective-permute-start(bf16[160,384]{1,0:T(8,128)(2,1)} %get-tuple-element.204), channel_id=1, source_target_pairs={{0,24},{8,16},{16,8},{24,0},{1,25},{9,17},{17,9},{25,1},{2,26},{10... | collective-permute-start | bytes 368648 | tf_op jit(solution)/shard_map/ppermute | solution.py:834
  429.7 18.7 %collective-permute-start.36 = (bf16[12,80,128]{2,1,0:T(8,128)(2,1)}, bf16[12,80,128]{2,1,0:T(8,128)(2,1)S(1)}, u32[]{:S(2)}, u32[]{:S(2)}) collective-permute-start(bf16[12,80,128]{2,1,0:T(8,128)(2,1)} %get-tuple-element.199), channel_id=1, source_target_pairs={{0,4},{1,5},{2,6},{3,7},{4,0},{5,1},{6,2},{7,3},{8,12},{9,13},{10,... | collective-permute-start | bytes 737288 | tf_op jit(solution)/shard_map/ppermute | solution.py:837
  430.3 18.1 %collective-permute-start.37 = (bf16[12,80,128]{2,1,0:T(8,128)(2,1)}, bf16[12,80,128]{2,1,0:T(8,128)(2,1)}, u32[]{:S(2)}, u32[]{:S(2)}) collective-permute-start(bf16[12,80,128]{2,1,0:T(8,128)(2,1)} %get-tuple-element.198), channel_id=1, source_target_pairs={{0,6},{1,7},{2,4},{3,5},{4,2},{5,3},{6,0},{7,1},{8,14},{9,15},{10,... | collective-permute-start | bytes 737288 | tf_op jit(solution)/shard_map/ppermute | solution.py:837
  448.4 15.4 %collective-permute-start.42 = (bf16[160,384]{1,0:T(8,128)(2,1)S(1)}, bf16[160,384]{1,0:T(8,128)(2,1)S(1)}, u32[]{:S(2)}, u32[]{:S(2)}) collective-permute-start(bf16[160,384]{1,0:T(8,128)(2,1)S(1)} %fusion.32), channel_id=1, source_target_pairs={{0,2},{1,3},{2,0},{3,1},{4,6},{5,7},{6,4},{7,5},{8,10},{9,11},{10,... | collective-permute-start | bytes 368648 | tf_op jit(solution)/shard_map/ppermute | solution.py:837
  448.4 15.7 %collective-permute-start.43 = (bf16[160,384]{1,0:T(8,128)(2,1)S(1)}, bf16[160,384]{1,0:T(8,128)(2,1)S(1)}, u32[]{:S(2)}, u32[]{:S(2)}) collective-permute-start(bf16[160,384]{1,0:T(8,128)(2,1)S(1)} %fusion.32), channel_id=1, source_target_pairs={{0,4},{1,5},{2,6},{3,7},{4,0},{5,1},{6,2},{7,3},{8,12},{9,13},{10,... | collective-permute-start | bytes 368648 | tf_op jit(solution)/shard_map/ppermute | solution.py:837
  456.3 10.6 %collective-permute-start.44 = (bf16[160,384]{1,0:T(8,128)(2,1)S(1)}, bf16[160,384]{1,0:T(8,128)(2,1)S(1)}, u32[]{:S(2)}, u32[]{:S(2)}) collective-permute-start(bf16[160,384]{1,0:T(8,128)(2,1)S(1)} %fusion.32), channel_id=1, source_target_pairs={{0,6},{1,7},{2,4},{3,5},{4,2},{5,3},{6,0},{7,1},{8,14},{9,15},{10,... | collective-permute-start | bytes 368648 | tf_op jit(solution)/shard_map/ppermute | solution.py:837
  458.9 12.9 %collective-permute-start.54 = (bf16[12,80,128]{2,1,0:T(8,128)(2,1)S(1)}, bf16[12,80,128]{2,1,0:T(8,128)(2,1)S(1)}, u32[]{:S(2)}, u32[]{:S(2)}) collective-permute-start(bf16[12,80,128]{2,1,0:T(8,128)(2,1)S(1)} %get-tuple-element.186.refs_13_), channel_id=1, source_target_pairs={{0,2},{1,3},{2,0},{3,1},{4,6},{5,7},{6,4},{7,5},{8,10},{9,11},{10,... | collective-permute-start | bytes 737288 | tf_op jit(solution)/shard_map/ppermute | solution.py:837
  458.9 16.9 %collective-permute-start.56 = (bf16[12,80,128]{2,1,0:T(8,128)(2,1)S(1)}, bf16[12,80,128]{2,1,0:T(8,128)(2,1)S(1)}, u32[]{:S(2)}, u32[]{:S(2)}) collective-permute-start(bf16[12,80,128]{2,1,0:T(8,128)(2,1)S(1)} %get-tuple-element.186.refs_13_), channel_id=1, source_target_pairs={{0,4},{1,5},{2,6},{3,7},{4,0},{5,1},{6,2},{7,3},{8,12},{9,13},{10,... | collective-permute-start | bytes 737288 | tf_op jit(solution)/shard_map/ppermute | solution.py:837
  463.7 17.3 %collective-permute-start.28 = (bf16[12,80,128]{2,1,0:T(8,128)(2,1)S(1)}, bf16[12,80,128]{2,1,0:T(8,128)(2,1)S(1)}, u32[]{:S(2)}, u32[]{:S(2)}) collective-permute-start(bf16[12,80,128]{2,1,0:T(8,128)(2,1)S(1)} %get-tuple-element.200), channel_id=1, source_target_pairs={{0,2},{1,3},{2,0},{3,1},{4,6},{5,7},{6,4},{7,5},{8,10},{9,11},{10,... | collective-permute-start | bytes 737288 | tf_op jit(solution)/shard_map/ppermute | solution.py:837
  464.0 32.8 %collective-permute-start.29 = (bf16[12,80,128]{2,1,0:T(8,128)(2,1)S(1)}, bf16[12,80,128]{2,1,0:T(8,128)(2,1)}, u32[]{:S(2)}, u32[]{:S(2)}) collective-permute-start(bf16[12,80,128]{2,1,0:T(8,128)(2,1)S(1)} %get-tuple-element.202), channel_id=1, source_target_pairs={{0,4},{1,5},{2,6},{3,7},{4,0},{5,1},{6,2},{7,3},{8,12},{9,13},{10,... | collective-permute-start | bytes 737288 | tf_op jit(solution)/shard_map/ppermute | solution.py:837
  467.6 29.3 %collective-permute-start.30 = (bf16[12,80,128]{2,1,0:T(8,128)(2,1)}, bf16[12,80,128]{2,1,0:T(8,128)(2,1)}, u32[]{:S(2)}, u32[]{:S(2)}) collective-permute-start(bf16[12,80,128]{2,1,0:T(8,128)(2,1)} %get-tuple-element.201), channel_id=1, source_target_pairs={{0,6},{1,7},{2,4},{3,5},{4,2},{5,3},{6,0},{7,1},{8,14},{9,15},{10,... | collective-permute-start | bytes 737288 | tf_op jit(solution)/shard_map/ppermute | solution.py:837
  471.8 28.0 %collective-permute-start.45 = (bf16[160,384]{1,0:T(8,128)(2,1)S(1)}, bf16[160,384]{1,0:T(8,128)(2,1)S(1)}, u32[]{:S(2)}, u32[]{:S(2)}) collective-permute-start(bf16[160,384]{1,0:T(8,128)(2,1)S(1)} %add_convert_fusion.10.refs_2_), channel_id=1, source_target_pairs={{0,1},{1,0},{2,3},{3,2},{4,5},{5,4},{6,7},{7,6},{8,9},{9,8},{10,11... | collective-permute-start | bytes 368648 | tf_op jit(solution)/shard_map/ppermute | solution.py:837
  475.8 29.4 %collective-permute-start.58 = (bf16[12,80,128]{2,1,0:T(8,128)(2,1)S(1)}, bf16[12,80,128]{2,1,0:T(8,128)(2,1)}, u32[]{:S(2)}, u32[]{:S(2)}) collective-permute-start(bf16[12,80,128]{2,1,0:T(8,128)(2,1)S(1)} %get-tuple-element.186.refs_13_), channel_id=1, source_target_pairs={{0,6},{1,7},{2,4},{3,5},{4,2},{5,3},{6,0},{7,1},{8,14},{9,15},{10,... | collective-permute-start | bytes 737288 | tf_op jit(solution)/shard_map/ppermute | solution.py:837
  481.1 28.3 %collective-permute-start.53 = (bf16[12,80,128]{2,1,0:T(8,128)(2,1)S(1)}, bf16[12,80,128]{2,1,0:T(8,128)(2,1)S(1)}, u32[]{:S(2)}, u32[]{:S(2)}) collective-permute-start(bf16[12,80,128]{2,1,0:T(8,128)(2,1)S(1)} %get-tuple-element.186.refs_13_), channel_id=1, source_target_pairs={{0,1},{1,0},{2,3},{3,2},{4,5},{5,4},{6,7},{7,6},{8,9},{9,8},{10,11... | collective-permute-start | bytes 737288 | tf_op jit(solution)/shard_map/ppermute | solution.py:837
  496.9 14.7 %collective-permute-start.55 = (bf16[12,80,128]{2,1,0:T(8,128)(2,1)S(1)}, bf16[12,80,128]{2,1,0:T(8,128)(2,1)S(1)}, u32[]{:S(2)}, u32[]{:S(2)}) collective-permute-start(bf16[12,80,128]{2,1,0:T(8,128)(2,1)S(1)} %collective-permute-done.54.refs_15_), channel_id=1, source_target_pairs={{0,1},{1,0},{2,3},{3,2},{4,5},{5,4},{6,7},{7,6},{8,9},{9,8},{10,11... | collective-permute-start | bytes 737288 | tf_op jit(solution)/shard_map/ppermute | solution.py:837
  496.9 15.4 %collective-permute-start.57 = (bf16[12,80,128]{2,1,0:T(8,128)(2,1)S(1)}, bf16[12,80,128]{2,1,0:T(8,128)(2,1)}, u32[]{:S(2)}, u32[]{:S(2)}) collective-permute-start(bf16[12,80,128]{2,1,0:T(8,128)(2,1)S(1)} %collective-permute-done.56.refs_17_), channel_id=1, source_target_pairs={{0,1},{1,0},{2,3},{3,2},{4,5},{5,4},{6,7},{7,6},{8,9},{9,8},{10,11... | collective-permute-start | bytes 737288 | tf_op jit(solution)/shard_map/ppermute | solution.py:837
  499.8 16.6 %collective-permute-start.47 = (bf16[12,80,128]{2,1,0:T(8,128)(2,1)S(1)}, bf16[12,80,128]{2,1,0:T(8,128)(2,1)}, u32[]{:S(2)}, u32[]{:S(2)}) collective-permute-start(bf16[12,80,128]{2,1,0:T(8,128)(2,1)S(1)} %get-tuple-element.188.refs_5_), channel_id=1, source_target_pairs={{0,2},{1,3},{2,0},{3,1},{4,6},{5,7},{6,4},{7,5},{8,10},{9,11},{10,... | collective-permute-start | bytes 737288 | tf_op jit(solution)/shard_map/ppermute | solution.py:837
  505.1 21.7 %collective-permute-start.49 = (bf16[12,80,128]{2,1,0:T(8,128)(2,1)S(1)}, bf16[12,80,128]{2,1,0:T(8,128)(2,1)}, u32[]{:S(2)}, u32[]{:S(2)}) collective-permute-start(bf16[12,80,128]{2,1,0:T(8,128)(2,1)S(1)} %get-tuple-element.188.refs_5_), channel_id=1, source_target_pairs={{0,4},{1,5},{2,6},{3,7},{4,0},{5,1},{6,2},{7,3},{8,12},{9,13},{10,... | collective-permute-start | bytes 737288 | tf_op jit(solution)/shard_map/ppermute | solution.py:837
  509.4 17.5 %collective-permute-start.51 = (bf16[12,80,128]{2,1,0:T(8,128)(2,1)S(1)}, bf16[12,80,128]{2,1,0:T(8,128)(2,1)}, u32[]{:S(2)}, u32[]{:S(2)}) collective-permute-start(bf16[12,80,128]{2,1,0:T(8,128)(2,1)S(1)} %get-tuple-element.188.refs_5_), channel_id=1, source_target_pairs={{0,6},{1,7},{2,4},{3,5},{4,2},{5,3},{6,0},{7,1},{8,14},{9,15},{10,... | collective-permute-start | bytes 737288 | tf_op jit(solution)/shard_map/ppermute | solution.py:837
  512.3 49.6 %collective-permute-start.59 = (bf16[12,80,128]{2,1,0:T(8,128)(2,1)}, bf16[12,80,128]{2,1,0:T(8,128)(2,1)}, u32[]{:S(2)}, u32[]{:S(2)}) collective-permute-start(bf16[12,80,128]{2,1,0:T(8,128)(2,1)} %collective-permute-done.58.refs_19_), channel_id=1, source_target_pairs={{0,1},{1,0},{2,3},{3,2},{4,5},{5,4},{6,7},{7,6},{8,9},{9,8},{10,11... | collective-permute-start | bytes 737288 | tf_op jit(solution)/shard_map/ppermute | solution.py:837
  512.3 49.6 %collective-permute-start.46 = (bf16[12,80,128]{2,1,0:T(8,128)(2,1)S(1)}, bf16[12,80,128]{2,1,0:T(8,128)(2,1)}, u32[]{:S(2)}, u32[]{:S(2)}) collective-permute-start(bf16[12,80,128]{2,1,0:T(8,128)(2,1)S(1)} %get-tuple-element.188.refs_5_), channel_id=1, source_target_pairs={{0,1},{1,0},{2,3},{3,2},{4,5},{5,4},{6,7},{7,6},{8,9},{9,8},{10,11... | collective-permute-start | bytes 737288 | tf_op jit(solution)/shard_map/ppermute | solution.py:837
  516.3 45.5 %collective-permute-start.48 = (bf16[12,80,128]{2,1,0:T(8,128)(2,1)}, bf16[12,80,128]{2,1,0:T(8,128)(2,1)}, u32[]{:S(2)}, u32[]{:S(2)}) collective-permute-start(bf16[12,80,128]{2,1,0:T(8,128)(2,1)} %collective-permute-done.47.refs_7_), channel_id=1, source_target_pairs={{0,1},{1,0},{2,3},{3,2},{4,5},{5,4},{6,7},{7,6},{8,9},{9,8},{10,11... | collective-permute-start | bytes 737288 | tf_op jit(solution)/shard_map/ppermute | solution.py:837
  526.8 35.1 %collective-permute-start.50 = (bf16[12,80,128]{2,1,0:T(8,128)(2,1)}, bf16[12,80,128]{2,1,0:T(8,128)(2,1)}, u32[]{:S(2)}, u32[]{:S(2)}) collective-permute-start(bf16[12,80,128]{2,1,0:T(8,128)(2,1)} %collective-permute-done.49.refs_9_), channel_id=1, source_target_pairs={{0,1},{1,0},{2,3},{3,2},{4,5},{5,4},{6,7},{7,6},{8,9},{9,8},{10,11... | collective-permute-start | bytes 737288 | tf_op jit(solution)/shard_map/ppermute | solution.py:837
  526.9 35.1 %collective-permute-start.52 = (bf16[12,80,128]{2,1,0:T(8,128)(2,1)}, bf16[12,80,128]{2,1,0:T(8,128)(2,1)}, u32[]{:S(2)}, u32[]{:S(2)}) collective-permute-start(bf16[12,80,128]{2,1,0:T(8,128)(2,1)} %collective-permute-done.51.refs_11_), channel_id=1, source_target_pairs={{0,1},{1,0},{2,3},{3,2},{4,5},{5,4},{6,7},{7,6},{8,9},{9,8},{10,11... | collective-permute-start | bytes 737288 | tf_op jit(solution)/shard_map/ppermute | solution.py:837
  532.5 13.2 %all-to-all-start.6 = ((f32[32,1,128]{2,1,0:T(1,128)}), f32[32,1,128]{2,1,0:T(1,128)S(1)}, u32[]{:S(2)}, u32[]{:S(2)}) async-start(f32[32,1,128]{2,1,0:T(1,128)} %broadcast_in_dim.3), calls=%async_computation.6 | async-start | bytes 32768 | tf_op jit(solution)/shard_map/all_to_all | solution.py:840
  (94 other events, 1672.0 us)

commit v2 on v1

v2 whole, which is shorter than its diff:
```python
import functools
import math

import jax
import jax.numpy as jnp
from jax import lax
from jax.experimental import pallas as pl
from jax.experimental.pallas import tpu as pltpu
from jax.sharding import PartitionSpec as P

C0 = 16
C1 = 160
C2 = 320
C3 = 640
WIDE = 384
TRIPLE = 3 * C3
SIDE = 32
CUT = 16
STEP = 10
PLANE = 640
META = 576
CHUNK = 48
QUARTERS = 4

beta_one = 0.9
beta_two = 0.999
adam_eps = 1e-08
weight_decay = 0.0005
clip_limit = 0.05
norm_eps = 1e-05
gelu_one = math.sqrt(2.0 / math.pi)
gelu_three = 0.044715 * gelu_one

half = jnp.bfloat16
full = jnp.float32
NT = (((1,), (1,)), ((), ()))
NN = (((1,), (0,)), ((), ()))
TN = (((0,), (0,)), ((), ()))
VMEM = pl.BlockSpec(memory_space=pltpu.VMEM)
SMEM = pl.BlockSpec(memory_space=pltpu.SMEM)
ANY = pl.BlockSpec(memory_space=pl.ANY)
MIB = 2**20


def shape(dims, kind=full):
    return jax.ShapeDtypeStruct(dims, kind)


def dot(left, right, dims=NN):
    return lax.dot_general(left, right, dims, preferred_element_type=full)


def iota(dims, axis):
    return lax.broadcasted_iota(jnp.int32, dims, axis)


def hot(condition):
    return condition.astype(full).astype(half)


def call(kernel, ins, outs, scratch, micros, after=0):
    used = len(ins)

    def body(*refs):
        kernel(*refs[:used], *refs[used + after :])

    return pl.pallas_call(
        body,
        out_shape=[item[0] for item in outs],
        in_specs=ins + [ANY] * after,
        out_specs=[item[1] for item in outs],
        scratch_shapes=scratch,
        cost_estimate=pl.CostEstimate(
            flops=int(micros * 35 * 10**7), bytes_accessed=1, transcendentals=0
        ),
        compiler_params=pltpu.CompilerParams(vmem_limit_bytes=60 * MIB),
    )


def gelu_pair(values):
    square = values * values
    bent = jnp.tanh(values * (gelu_one + gelu_three * square))
    gate = 0.5 + 0.5 * bent
    slope = gate + (0.5 * values) * (1.0 - bent * bent) * (gelu_one + (3.0 * gelu_three) * square)
    return (values * gate, slope)


def adamw(weight, gradient, first, second, step_rate):
    first_new = beta_one * first + (1.0 - beta_one) * gradient
    second_new = beta_two * second + (1.0 - beta_two) * (gradient * gradient)
    second_hat = second_new * (1.0 / (1.0 - beta_two**STEP))
    root = second_hat * lax.rsqrt(second_hat) + adam_eps
    weight_new = weight * (1.0 - step_rate * weight_decay) - (
        step_rate / (1.0 - beta_one**STEP)
    ) * (first_new / root)
    return (first_new, second_new, weight_new)


def fetch(source, target, sem):
    copy = pltpu.make_async_copy(source, target, sem)
    copy.start()
    return copy


def lane_pixel(lanes):
    tap = lanes // 64
    cell = lanes % 64
    row = 4 * (cell // 8) + tap // 3 - 1
    col = 4 * (cell % 8) + tap % 3 - 1
    return (tap, row, col)


def image_kernel(planes, labels, corners, partners, out, numbers):
    count = planes.shape[1]
    tap, row, col = lane_pixel(iota((1, PLANE), 1))
    pixel = jnp.where((row >= 0) & (col >= 0) & (tap < 9), row * SIDE + col, -1)
    pick = hot(iota((SIDE * SIDE, PLANE), 0) == pixel)
    numbers[...] = jnp.zeros(numbers.shape, full)
    numbers[0:1] = labels[...].astype(full)
    numbers[1:3] = corners[...].astype(full)
    numbers[3:4] = (partners[...] // count).astype(full)
    numbers[4:5] = (partners[...] % count).astype(full)
    place = hot(iota((8, PLANE), 0) + META == iota((8, PLANE), 1))
    for colour in range(3):
        taken = dot(planes[colour], pick)
        if colour == 0:
            taken = taken + dot(numbers[...].astype(half), place, TN)
        out[:, colour * PLANE : (colour + 1) * PLANE] = taken.astype(half)


def pack_kernel(proj_c, head, norm, out):
    place = hot(iota((C2, WIDE), 0) == iota((C2, WIDE), 1))
    total = dot(proj_c[...].astype(half), place)
    classes = head.shape[0]
    place = hot(iota((classes, WIDE), 0) + C2 == iota((classes, WIDE), 1))
    total = total + dot(head[...].astype(half), place, TN)
    rest = norm[...]
    for part in range(3):
        piece = rest.astype(half)
        rest = rest - piece.astype(full)
        place = hot(iota((6, WIDE), 0) + (C2 + 16 + 8 * part) == iota((6, WIDE), 1))
        total = total + dot(piece, place, TN)
    out[...] = total.astype(half)


def cast_kernel(layer, ids, weights, out, wide, narrow, in_sems, out_sems):
    rows = out.shape[0]
    parts = rows // 16
    inputs = []
    for part in range(parts):
        spot = pl.multiple_of(ids[2] * rows + part * 16, 16)
        inputs.append(
            fetch(
                weights.at[layer, pl.ds(spot, 16)],
                wide.at[part * 16 : part * 16 + 16],
                in_sems.at[part],
            )
        )
    outputs = []
    for part in range(parts):
        here = slice(part * 16, part * 16 + 16)
        inputs[part].wait()
        narrow[here] = wide[here].astype(half)
        outputs.append(fetch(narrow.at[here], out.at[here], out_sems.at[part]))
    for copy in outputs:
        copy.wait()


def cast_half(ids, conv_w, layer, after):
    rows = conv_w.shape[1] // 2
    cols = conv_w.shape[2]
    (result,) = call(
        functools.partial(cast_kernel, layer),
        [SMEM, ANY],
        [(shape((rows, cols), half), ANY)],
        [
            pltpu.VMEM((rows, cols), full),
            pltpu.VMEM((rows, cols), half),
            pltpu.SemaphoreType.DMA((rows // 16,)),
            pltpu.SemaphoreType.DMA((rows // 16,)),
        ],
        3,
        len(after),
    )(ids, conv_w, *after)
    return result


def merge_spans(plan):
    spans = []
    for out, (size, terms) in enumerate(plan):
        edges = {0, size}
        for _, _, start, length in terms:
            edges |= {start, start + length}
        edges = sorted(edges)
        for low, high in zip(edges[:-1], edges[1:]):
            used = [
                (source, first - start)
                for source, first, start, length in terms
                if start <= low and high <= start + length
            ]
            for begin in range(low, high, 8):
                spans.append((out, begin, min(8, high - begin), used))
    return spans


def merge_kernel(plan, count, *refs):
    values = refs[:count]
    results = refs[count : count + len(plan)]
    held = refs[count + len(plan) : 2 * count + len(plan)]
    kept = refs[2 * count + len(plan) : 2 * (count + len(plan))]
    in_sems, out_sems = refs[2 * (count + len(plan)) :]
    arrivals = []
    number = 0
    for _, begin, size, used in merge_spans(plan):
        copies = []
        for source, shift in used:
            here = slice(begin + shift, begin + shift + size)
            copies.append(
                fetch(values[source].at[here], held[source].at[here], in_sems.at[number])
            )
            number += 1
        arrivals.append(copies)
    departures = []
    for (out, begin, size, used), copies in zip(merge_spans(plan), arrivals):
        for copy in copies:
            copy.wait()
        total = None
        for source, shift in used:
            value = held[source][begin + shift : begin + shift + size].astype(full)
            total = value if total is None else total + value
        here = slice(begin, begin + size)
        kept[out][here] = total.astype(half)
        departures.append(
            fetch(kept[out].at[here], results[out].at[here], out_sems.at[len(departures)])
        )
    for copy in departures:
        copy.wait()


def merge(values, plan, after, micros):
    dims = values[0].shape[1:]
    spans = merge_spans(plan)
    return call(
        functools.partial(merge_kernel, plan, len(values)),
        [ANY] * len(values),
        [(shape((size,) + dims, half), ANY) for size, _ in plan],
        [pltpu.VMEM(value.shape, half) for value in values]
        + [pltpu.VMEM((size,) + dims, half) for size, _ in plan]
        + [
            pltpu.SemaphoreType.DMA((sum(len(used) for _, _, _, used in spans),)),
            pltpu.SemaphoreType.DMA((len(spans),)),
        ],
        micros,
        len(after),
    )(*values, *after)


def cut_kernel(places, *refs):
    count = len(places)
    outs = refs[count : 2 * count]
    sems = refs[2 * count]
    copies = []
    for index, (start, size) in enumerate(places):
        copies.append(
            fetch(refs[index].at[start : start + size], outs[index], sems.at[index])
        )
    for copy in copies:
        copy.wait()


def cut_rows(values, places, after):
    cols = values[0].shape[1]
    return call(
        functools.partial(cut_kernel, places),
        [ANY] * len(values),
        [(shape((size, cols), half), VMEM) for _, size in places],
        [pltpu.SemaphoreType.DMA((len(values),))],
        1,
        len(after),
    )(*values, *after)


def stack_kernel(places, *refs):
    count = len(places)
    out, sems = refs[count:]
    copies = []
    for index, (slot, start, size) in enumerate(places):
        copy = pltpu.make_async_copy(
            refs[index], out.at[slot, start : start + size], sems.at[index]
        )
        copy.start()
        copies.append(copy)
    for copy in copies:
        copy.wait()


def stack(pieces, places, dims, after):
    (result,) = call(
        functools.partial(stack_kernel, places),
        [ANY] * len(pieces),
        [(shape(dims, half), VMEM)],
        [pltpu.SemaphoreType.DMA((len(pieces),))],
        3,
        len(after),
    )(*pieces, *after)
    return result


def front_kernel(sizes, *refs):
    per, count, groups, devices, split = sizes
    rows = per * 64
    band = per * 8
    ids = refs[0]
    images, far_images = refs[1:3]
    packs = refs[3 : 3 + split]
    stem_w, proj_a, proj_b = refs[3 + split : 6 + split]
    (
        patches,
        stem_out,
        mid_one,
        mid_two,
        act_three,
        base,
        stats,
        norm_rows,
        head_all,
        proj_t,
        facts,
        gathered,
        tiles,
        loose,
        stem_pad,
        proj_b_pad,
        totals,
        sems,
    ) = refs[6 + split :]
    quarter = gathered.shape[0] // split
    copies = []
    for turn in range(split):
        spot = pl.multiple_of((ids[0] ^ turn) * quarter, 16)
        copies.append(fetch(packs[turn], gathered.at[pl.ds(spot, quarter)], sems.at[turn]))
    slot = iota((per, count), 0)
    column = iota((per, count), 1)
    own = dot(hot(column == slot + ids[0] * per), images[0])
    group_of = own[:, META + 3 : META + 4].astype(jnp.int32)
    local_of = own[:, META + 4 : META + 5].astype(jnp.int32)
    turn_of = group_of ^ ids[1]
    other = jnp.zeros((per, 3 * PLANE), full)
    for turn in range(groups):
        source = far_images[turn // 2] if turn % 2 else images[turn // 2]
        other = other + dot(hot((turn_of == turn) & (column == local_of)), source)
    top = own[:, META + 1 : META + 2]
    left = own[:, META + 2 : META + 3]
    tap, row, col = lane_pixel(iota((1, 3 * PLANE), 1) % PLANE)
    row = row.astype(full)
    col = col.astype(full)
    inside = (row >= top) & (row < top + CUT) & (col >= left) & (col < left + CUT) & (tap < 9)
    blended = jnp.where(inside, other, own)
    tall = jnp.maximum(jnp.minimum(top + CUT, float(SIDE)) - jnp.maximum(top, 0.0), 0.0)
    broad = jnp.maximum(jnp.minimum(left + CUT, float(SIDE)) - jnp.maximum(left, 0.0), 0.0)
    share = 1.0 - tall * broad / float(SIDE * SIDE)
    lanes = iota((per, 128), 1)
    facts[...] = jnp.where(
        lanes == 0,
        own[:, META : META + 1],
        jnp.where(lanes == 1, other[:, META : META + 1], share),
    )
    tiles[...] = jnp.zeros(tiles.shape, full)
    for piece in range(15):
        tiles[:, piece, :] = blended[:, piece * 128 : (piece + 1) * 128]
    tiles[:, 16:32, :] = pltpu.roll(tiles[:, 0:16, :], 64, 2)
    spot = iota((32, 32), 0)
    tap_at = ((spot % 16) % 5) * 2 + spot // 16
    colour_at = (spot % 16) // 5
    order = hot(
        (iota((32, 32), 1) == tap_at * 3 + colour_at) & (tap_at < 9) & (spot % 16 < 15)
    )
    for image in range(per):
        cells = dot(tiles[image].astype(half), order, TN)
        for line in range(8):
            loose[line * band + image * 8 : line * band + image * 8 + 8, :] = cells[
                line * 8 : line * 8 + 8
            ]
    patches[...] = loose[...].astype(half)
    stem_pad[...] = jnp.zeros(stem_pad.shape, full)
    stem_pad[:, 0:27] = stem_w[...]
    proj_b_pad[...] = jnp.zeros(proj_b_pad.shape, half)
    proj_b_pad[:, 0:C2] = proj_b[...].astype(half)
    for copy in copies:
        copy.wait()
    lanes = iota((1, WIDE), 1)
    packed = gathered[...]
    proj_t[...] = jnp.where(lanes < C2, packed.astype(full), 0.0).astype(half)
    place = hot(iota((WIDE, 16), 0) == iota((WIDE, 16), 1) + C2)
    head_all[...] = dot(packed, place).astype(half)
    column = iota((8, WIDE), 1)
    name = iota((8, WIDE), 0)
    pieces = [
        dot(hot((column == name + (C2 + 16 + 8 * part)) & (name < 6)), packed, NT)
        for part in range(3)
    ]
    norm_rows[...] = pieces[0] + (pieces[1] + pieces[2])
    stem_half = stem_pad[...].astype(half)
    proj_a_half = proj_a[...].astype(half)
    totals[...] = jnp.zeros(totals.shape, full)
    tall_chunk = 2 * band

    def step(index, carry):
        at = pl.ds(pl.multiple_of(index * tall_chunk, 16), tall_chunk)
        stem = dot(patches[at], stem_half, NT)
        stem_out[at] = stem
        one = dot(gelu_pair(stem)[0].astype(half), proj_a_half)
        mid_one[at] = one
        two = dot(gelu_pair(one)[0].astype(half), proj_b_pad[...])
        mid_two[at] = two
        three = gelu_pair(two)[0].astype(half)
        act_three[at] = three
        result = dot(three, proj_t[...], NT)
        base[at] = result
        totals[0:1] += jnp.sum(result, axis=0, keepdims=True)
        totals[1:2] += jnp.sum(result * result, axis=0, keepdims=True)
        return carry

    lax.fori_loop(0, rows // tall_chunk, step, 0)
    spread_stats(stats, [totals[0:1], totals[1:2]])


def spread_stats(out, parts):
    line = jnp.concatenate(parts, axis=1)
    out[...] = jnp.broadcast_to(line[None], out.shape)


def moments(stats, row_total):
    line = jnp.sum(stats[...], axis=0)
    mean = line[:, 0:C3] / row_total
    rstd = lax.rsqrt(line[:, C3 : 2 * C3] / row_total - mean * mean + norm_eps)
    return (mean, rstd)


def quarter_rows(rows, part):
    step = rows // QUARTERS
    return pl.ds(part * step, step)


def fetch_quarter(source, target, sem, part):
    here = quarter_rows(source.shape[0], part)
    return fetch(source.at[here], target.at[here], sem)


def walk_quarter(rows, part, body, carry):
    step = rows // QUARTERS // CHUNK
    return lax.fori_loop(part * step, (part + 1) * step, body, carry)


def start_weights(ids, pieces, weights, sems):
    rows = pieces[0].shape[0]
    low = pieces[3].shape[0]
    copies = []
    for side in range(2):
        for place in range(5):
            piece = pieces[5 * side + place]
            turn = min(place, 3)
            spot = (ids[0] ^ turn) * (2 * rows) + (ids[2] ^ side) * rows
            if place == 4:
                spot = spot + low
            spot = pl.multiple_of(spot, 16)
            copies.append(
                fetch(piece, weights.at[pl.ds(spot, piece.shape[0])], sems.at[5 * side + place])
            )
    return copies


def shifted(values, by):
    block = values.reshape(CHUNK // 8, 8, C3)
    place = iota((1, 8, 1), 1)
    if by == 1:
        moved = jnp.where(place == 0, 0.0, pltpu.roll(block, 1, 1))
    else:
        moved = jnp.where(place == 7, 0.0, pltpu.roll(block, 7, 1))
    return moved.reshape(CHUNK, C3)


def conv_kernel(sizes, layer, *refs):
    per, row_total, split = sizes
    rows = per * 64
    band = per * 8
    ids, source, stats_in, norm_rows = refs[0:4]
    offset = 4
    if layer == 1:
        base = refs[4]
        offset = 5
    pieces = refs[offset : offset + 10]
    offset += 10
    (result, field_out, slope_out, stats, held, weights, field, slope, total) = refs[
        offset : offset + 9
    ]
    weight_sems, in_sems, out_sems = refs[offset + 9 : offset + 12]
    inputs = [fetch_quarter(source, held, in_sems.at[part], part) for part in range(QUARTERS)]
    copies = start_weights(ids, pieces, weights, weight_sems)
    mean, rstd = moments(stats_in, row_total)
    factor = rstd * norm_rows[2 * layer : 2 * layer + 1]
    shift = norm_rows[2 * layer + 1 : 2 * layer + 2] - mean * factor

    def prepare(index, carry):
        at = pl.ds(pl.multiple_of(index * CHUNK, 16), CHUNK)
        value, gradient = gelu_pair(held[at] * factor + shift)
        slope[at] = gradient
        field[at, 0:C3] = shifted(value, 1).astype(half)
        field[at, C3 : 2 * C3] = value.astype(half)
        field[at, 2 * C3 : TRIPLE] = shifted(value, -1).astype(half)
        return carry

    for part in range(QUARTERS):
        inputs[part].wait()
        walk_quarter(rows, part, prepare, 0)
    outputs = [
        fetch(field.at[:, C3 : 2 * C3], field_out, out_sems.at[QUARTERS]),
        fetch(slope, slope_out, out_sems.at[QUARTERS + 1]),
    ]
    if layer == 1:
        inputs = [fetch_quarter(base, held, in_sems.at[part], part) for part in range(QUARTERS)]
    for copy in copies:
        copy.wait()
    inner = rows - band
    total[...] = dot(field[...], weights[:, TRIPLE : 2 * TRIPLE], NT)
    total[band:rows] += dot(field[0:inner], weights[:, 0:TRIPLE], NT)
    total[0:inner] += dot(field[band:rows], weights[:, 2 * TRIPLE : 3 * TRIPLE], NT)

    def count(index, carry):
        at = pl.ds(pl.multiple_of(index * CHUNK, 16), CHUNK)
        value = total[at]
        if layer == 1:
            value = value + held[at]
            total[at] = value
        return (
            carry[0] + jnp.sum(value.reshape(CHUNK // 8, 8, C3), axis=0),
            carry[1] + jnp.sum((value * value).reshape(CHUNK // 8, 8, C3), axis=0),
        )

    zero = jnp.zeros((8, C3), full)
    sums = (zero, zero)
    for part in range(QUARTERS):
        if layer == 1:
            inputs[part].wait()
        else:
            outputs.append(fetch_quarter(total, result, out_sems.at[part], part))
        sums = walk_quarter(rows, part, count, sums)
        if layer == 1:
            outputs.append(fetch_quarter(total, result, out_sems.at[part], part))
    spread_stats(stats, [jnp.sum(item, axis=0, keepdims=True) for item in sums])
    for copy in outputs:
        copy.wait()


def head_kernel(sizes, *refs):
    per, row_total, image_total, classes = sizes
    rows = per * 64
    band = per * 8
    (
        summed,
        stats_in,
        norm_rows,
        head_all,
        facts,
        slope,
        spread,
        stats,
        grad_head,
        sum_value,
        sum_slope,
        sum_cross,
    ) = refs
    mean, rstd = moments(stats_in, row_total)
    gain = norm_rows[4:5]
    bias = norm_rows[5:6]
    sum_value[...] = jnp.zeros((band, C3), full)
    sum_slope[...] = jnp.zeros((band, C3), full)
    sum_cross[...] = jnp.zeros((band, C3), full)

    def walk(index, carry):
        for part in range(band // CHUNK):
            at = pl.ds(pl.multiple_of(index * band + part * CHUNK, 16), CHUNK)
            here = slice(part * CHUNK, part * CHUNK + CHUNK)
            unit = (summed[at] - mean) * rstd
            value, gradient = gelu_pair(unit * gain + bias)
            slope[at] = gradient
            sum_value[here] += value
            sum_slope[here] += gradient
            sum_cross[here] += gradient * unit
        return carry

    lax.fori_loop(0, 8, walk, 0)

    def by_image(ref):
        return jnp.sum(ref[...].reshape(per, 8, C3), axis=1)

    pooled = (by_image(sum_value) / 64.0).astype(half)
    logits = dot(pooled, head_all[...])
    lanes = iota((per, 16), 1)
    inside = lanes < classes
    own = facts[:, 0:1].astype(jnp.int32)
    other = facts[:, 1:2].astype(jnp.int32)
    share = facts[:, 2:3]
    target = jnp.where(lanes == own, share, 0.0) + jnp.where(lanes == other, 1.0 - share, 0.0)
    top = jnp.max(jnp.where(inside, logits, -3e38), axis=1, keepdims=True)
    powers = jnp.where(inside, jnp.exp(jnp.where(inside, logits - top, 0.0)), 0.0)
    lse = top + jnp.log(jnp.sum(powers, axis=1, keepdims=True))
    losses = lse - jnp.sum(target * logits, axis=1, keepdims=True)
    loss = jnp.sum(losses, axis=0, keepdims=True)
    soft = jnp.where(inside, jnp.exp(jnp.where(inside, logits - lse, 0.0)), 0.0)
    grad_logits = ((soft - target) / image_total).astype(half)
    grad_head[...] = dot(pooled, grad_logits, TN)
    pull = dot(grad_logits, head_all[...], NT) / 64.0
    spread[...] = jnp.broadcast_to(pull[:, None, :], (per, 8, C3)).reshape(band, C3)
    bias_sum = jnp.sum(pull * by_image(sum_slope), axis=0, keepdims=True)
    gain_sum = jnp.sum(pull * by_image(sum_cross), axis=0, keepdims=True)
    spread_stats(stats, [bias_sum, gain_sum, jnp.broadcast_to(loss, (1, 128))])


def grad_moments(stats, row_total):
    line = jnp.sum(stats[...], axis=0)
    return (line[:, 0:C3] / row_total, line[:, C3 : 2 * C3] / row_total)


def input_grad(gradient, weights, out, band):
    rows = gradient.shape[0]
    inner = rows - band
    spans = (
        (1, slice(0, rows), slice(0, rows)),
        (0, slice(0, inner), slice(band, rows)),
        (2, slice(band, rows), slice(0, inner)),
    )
    for line, to, of in spans:
        for col in range(3):
            tap = 3 * line + col
            part = dot(
                gradient[of, col * C3 : (col + 1) * C3], weights[:, tap * C3 : (tap + 1) * C3]
            )
            if line == 1 and col == 0:
                out[to] = part
            else:
                out[to] += part


def half_filters(ids, split):
    tall = C3 // (2 * split)
    place = iota((1, 2 * WIDE), 1)
    side = jnp.where(place < WIDE, 0, 1)
    place = place - side * WIDE
    target = (ids[0] ^ (place // tall)) * (2 * tall) + (ids[2] ^ side) * tall + place % tall
    target = jnp.where(place < C3 // 2, target, -1)
    return hot(iota((C3, 2 * WIDE), 0) == target)


def norm_back(arriving, unit, factor, low, high):
    return factor * (arriving - low - unit * high)


def send_halves(middle, pick, helds, halves, sems, part):
    here = quarter_rows(helds[0].shape[0], part)
    both = dot(middle, pick).astype(half)
    copies = []
    for side in range(2):
        helds[side][here] = both[:, side * WIDE : (side + 1) * WIDE]
        copies.append(
            fetch(helds[side].at[here], halves[side].at[here], sems.at[2 * part + side])
        )
    return copies


def back_kernel(sizes, layer, *refs):
    per, row_total, split = sizes
    rows = per * 64
    band = per * 8
    last = layer == 1
    ids = refs[0]
    if last:
        incoming, source, stats_here, stats_grad, norm_rows, spread = refs[1:7]
        offset = 7
    else:
        incoming = refs[1]
        offset = 2
    before, slope_before, stats_before = refs[offset : offset + 3]
    pieces = refs[offset + 3 : offset + 13]
    result, stats = refs[offset + 13 : offset + 15]
    offset += 15
    if last:
        own_half, far_half, grad_out, kept, own_held, far_held, pick, half_sems = refs[
            offset : offset + 8
        ]
        offset += 8
    else:
        arrived = refs[offset]
        offset += 1
    held, origin, weights, gradient, total = refs[offset : offset + 5]
    weight_sems, in_sems, out_sems = refs[offset + 5 : offset + 8]
    inputs = []
    for part in range(QUARTERS):
        if last:
            inputs.append(
                (
                    fetch_quarter(incoming, held, in_sems.at[2 * part], part),
                    fetch_quarter(source, origin, in_sems.at[2 * part + 1], part),
                )
            )
        else:
            inputs.append((fetch_quarter(incoming, arrived, in_sems.at[2 * part], part),))
    copies = start_weights(ids, pieces, weights, weight_sems)
    if last:
        mean, rstd = moments(stats_here, row_total)
        low, high = grad_moments(stats_grad, row_total)
        factor = rstd * norm_rows[4:5]
        parts = band // CHUNK
        pick[...] = half_filters(ids, split)

    def prepare(index, carry):
        at = pl.ds(pl.multiple_of(index * CHUNK, 16), CHUNK)
        if last:
            here = pl.ds(pl.multiple_of(lax.rem(index, parts) * CHUNK, 16), CHUNK)
            unit = (origin[at] - mean) * rstd
            value = norm_back(held[at] * spread[here], unit, factor, low, high)
            kept[at] = value
            gradient[at, C3 : 2 * C3] = value.astype(half)
        else:
            gradient[at, C3 : 2 * C3] = arrived[at]
            value = arrived[at].astype(full)
        gradient[at, 0:C3] = shifted(value, -1).astype(half)
        gradient[at, 2 * C3 : TRIPLE] = shifted(value, 1).astype(half)
        return carry

    for part in range(QUARTERS):
        for copy in inputs[part]:
            copy.wait()
        walk_quarter(rows, part, prepare, 0)
    outputs = []
    if last:
        outputs.append(fetch(kept, grad_out, half_sems.at[2 * QUARTERS]))
        for part in range(QUARTERS):
            outputs += send_halves(
                gradient[quarter_rows(rows, part), C3 : 2 * C3],
                pick[...],
                (own_held, far_held),
                (own_half, far_half),
                half_sems,
                part,
            )
    inputs = []
    for part in range(QUARTERS):
        inputs.append(
            (
                fetch_quarter(before, origin, in_sems.at[2 * part], part),
                fetch_quarter(slope_before, held, in_sems.at[2 * part + 1], part),
            )
        )
    for copy in copies:
        copy.wait()
    input_grad(gradient, weights, total, band)
    mean, rstd = moments(stats_before, row_total)

    def finish(index, carry):
        at = pl.ds(pl.multiple_of(index * CHUNK, 16), CHUNK)
        value = total[at] * held[at]
        total[at] = value
        unit = (origin[at] - mean) * rstd
        return (
            carry[0] + jnp.sum(value.reshape(CHUNK // 8, 8, C3), axis=0),
            carry[1] + jnp.sum((value * unit).reshape(CHUNK // 8, 8, C3), axis=0),
        )

    zero = jnp.zeros((8, C3), full)
    sums = (zero, zero)
    for part in range(QUARTERS):
        for copy in inputs[part]:
            copy.wait()
        sums = walk_quarter(rows, part, finish, sums)
        outputs.append(fetch_quarter(total, result, out_sems.at[part], part))
    spread_stats(stats, [jnp.sum(item, axis=0, keepdims=True) for item in sums])
    for copy in outputs:
        copy.wait()


def norm_back_kernel(sizes, *refs):
    row_total, split = sizes
    ids, incoming, source, stats_here, stats_grad, norm_rows = refs[0:6]
    grad_half, own_half, far_half = refs[6:9]
    held, origin, middle, own_held, far_held, pick, in_sems, out_sems = refs[9:]
    rows = held.shape[0]
    inputs = []
    for part in range(QUARTERS):
        inputs.append(
            (
                fetch_quarter(incoming, held, in_sems.at[2 * part], part),
                fetch_quarter(source, origin, in_sems.at[2 * part + 1], part),
            )
        )
    mean, rstd = moments(stats_here, row_total)
    low, high = grad_moments(stats_grad, row_total)
    factor = rstd * norm_rows[2:3]
    pick[...] = half_filters(ids, split)

    def prepare(index, carry):
        at = pl.ds(pl.multiple_of(index * CHUNK, 16), CHUNK)
        unit = (origin[at] - mean) * rstd
        middle[at] = norm_back(held[at], unit, factor, low, high).astype(half)
        return carry

    outputs = []
    for part in range(QUARTERS):
        for copy in inputs[part]:
            copy.wait()
        walk_quarter(rows, part, prepare, 0)
        here = quarter_rows(rows, part)
        outputs.append(fetch(middle.at[here], grad_half.at[here], out_sems.at[8 + part]))
        outputs += send_halves(
            middle[here], pick[...], (own_held, far_held), (own_half, far_half), out_sems, part
        )
    for copy in outputs:
        copy.wait()


def weight_grad_kernel(sizes, *refs):
    chunks, split, band = sizes
    gradients = refs[0:2]
    fields = refs[2:4]
    count = sum(len(part_sizes(split, lines)) for lines in chunks)
    outs = refs[4 : 4 + count]
    (gradient, field, plain, held, in_sems, grad_sems, sems) = refs[4 + count :]
    inputs = []
    for line in range(8):
        for side in range(2):
            of = pl.ds(line * band, band)
            inputs.append(
                fetch(fields[side].at[of], plain.at[side, of], in_sems.at[2 * line + side])
            )
    arriving = []
    for line in range(8):
        for side in range(2):
            of = pl.ds(line * band, band)
            to = pl.ds((2 * line + side) * band, band)
            arriving.append(
                fetch(gradients[side].at[of], gradient.at[to], grad_sems.at[2 * line + side])
            )

    def prepare(index, carry):
        for side in range(2):
            for part in range(band // CHUNK):
                to = pl.ds(
                    pl.multiple_of((2 * index + side) * band + part * CHUNK, 16), CHUNK
                )
                of = pl.ds(pl.multiple_of(index * band + part * CHUNK, 16), CHUNK)
                value = plain[side, of]
                wide = value.astype(full)
                field[to, 0:C3] = shifted(wide, 1).astype(half)
                field[to, C3 : 2 * C3] = value
                field[to, 2 * C3 : TRIPLE] = shifted(wide, -1).astype(half)
        return carry

    for part in range(QUARTERS):
        for copy in inputs[4 * part : 4 * part + 4]:
            copy.wait()
        lax.fori_loop(2 * part, 2 * part + 2, prepare, 0)
    for copy in arriving:
        copy.wait()
    rows = field.shape[0]
    inner = rows - 2 * band
    spans = {
        0: (slice(2 * band, rows), slice(0, inner)),
        1: (slice(0, rows), slice(0, rows)),
        2: (slice(0, inner), slice(2 * band, rows)),
    }
    tall = held.shape[2]
    copies = []
    start = 0
    number = 0
    for lines in chunks:
        for place, line in enumerate(lines):
            left, right = spans[line]
            part = dot(gradient[left, 0 : C3 // 2], field[right], TN).astype(half)
            for turn in range(split):
                for block in range(15):
                    held[turn, start + place * 15 + block] = part[
                        turn * tall : (turn + 1) * tall, block * 128 : (block + 1) * 128
                    ]
        for turn, first, size in part_sizes(split, lines):
            copies.append(
                fetch(
                    held.at[turn, start + first : start + first + size],
                    outs[number],
                    sems.at[number],
                )
            )
            number += 1
        start += 15 * len(lines)
    for copy in copies:
        copy.wait()


def part_sizes(split, lines):
    blocks = 15 * len(lines)
    sizes = [(turn, 0, blocks) for turn in range(split - 1)]
    return sizes + [(split - 1, 0, blocks // 2), (split - 1, blocks // 2, blocks - blocks // 2)]


def trunk_kernel(sizes, *refs):
    per, row_total, split = sizes
    rows = per * 64
    band = per * 8
    (
        ids,
        incoming,
        grad_summed,
        base,
        stats_one,
        stats_six,
        norm_rows,
        proj_t,
        act_three,
        mid_two,
        mid_one,
        stem_out,
        patches,
        proj_a,
        proj_b,
        grad_head,
        mine,
        other,
        trunk,
        grad_two,
        act_two,
        grad_one,
        act_one,
        grad_stem,
        proj_b_pad,
        split_part,
        shared_part,
        sems,
    ) = refs
    mean, rstd = moments(stats_one, row_total)
    low, high = grad_moments(stats_six, row_total)
    factor = rstd * norm_rows[0:1]
    proj_b_pad[...] = jnp.zeros(proj_b_pad.shape, half)
    proj_b_pad[:, 0:C2] = proj_b[...].astype(half)
    proj_a_half = proj_a[...].astype(half)

    def prepare(index, carry):
        at = pl.ds(pl.multiple_of(index * CHUNK, 16), CHUNK)
        unit = (base[at] - mean) * rstd
        value = grad_summed[at] + factor * (incoming[at] - low - unit * high)
        trunk[at] = value.astype(half)
        return carry

    lax.fori_loop(0, rows // CHUNK, prepare, 0)
    tall_chunk = 2 * band

    def step(index, carry):
        at = pl.ds(pl.multiple_of(index * tall_chunk, 16), tall_chunk)
        three = dot(trunk[at], proj_t[...])
        two = (three * gelu_pair(mid_two[at])[1]).astype(half)
        grad_two[at] = two
        value, slope = gelu_pair(mid_one[at])
        act_two[at] = value.astype(half)
        one = (dot(two, proj_b_pad[...], NT) * slope).astype(half)
        grad_one[at] = one
        value, slope = gelu_pair(stem_out[at])
        act_one[at] = value.astype(half)
        grad_stem[at] = (dot(one, proj_a_half, NT) * slope).astype(half)
        return carry

    lax.fori_loop(0, rows // tall_chunk, step, 0)
    place = hot(iota((16, WIDE), 0) + C2 == iota((16, WIDE), 1))
    split_part[...] = (
        dot(trunk[...], act_three[...], TN) + dot(grad_head[...].astype(half), place)
    ).astype(half)
    shared = dot(act_two[...], grad_two[...], TN)
    shared = shared + dot(dot(grad_one[...], act_one[...], TN).astype(half), place)
    stem = dot(patches[...], grad_stem[...], TN).astype(half)
    tall = split_part.shape[0] // (2 * split)
    spot = iota((C1, 32), 0)
    twice = hot((spot % tall == iota((C1, 32), 1)) & (spot % tall < 27))
    place = hot(iota((16, WIDE), 0) + (C2 + 16) == iota((16, WIDE), 1))
    shared = shared + dot(dot(twice, stem).astype(half), place)
    shared_part[...] = shared.astype(half)
    copies = []
    for turn in range(split):
        for side, target in ((0, mine), (1, other)):
            place = pl.multiple_of((ids[2] ^ side) * tall, 16)
            spot = pl.multiple_of((ids[0] ^ turn) * (2 * tall) + (ids[2] ^ side) * tall, 16)
            number = 2 * (2 * turn + side)
            copy = pltpu.make_async_copy(
                split_part.at[pl.ds(spot, tall)], target.at[turn, 0:tall], sems.at[number]
            )
            copy.start()
            copies.append(copy)
            copy = pltpu.make_async_copy(
                shared_part.at[pl.ds(place, tall)],
                target.at[turn, tall : 2 * tall],
                sems.at[number + 1],
            )
            copy.start()
            copies.append(copy)
    for copy in copies:
        copy.wait()


def clip_scale(squares):
    total = jnp.sum(jnp.sum(squares[...], axis=0), axis=1, keepdims=True)
    size = jnp.sqrt(total[:, 0:1] / 128.0)
    return (size, jnp.minimum(1.0, clip_limit / size))


def conv_update_kernel(sizes, *refs):
    pieces_count, places, step_rate = sizes
    ids = refs[0]
    squares, weight, first, second = refs[1:5]
    pieces = refs[5 : 5 + pieces_count]
    (first_new, second_new, weight_new, held, sems) = refs[5 + pieces_count :]
    layer = pl.program_id(0)
    line = pl.program_id(1)

    def copies(wanted):
        made = []
        for number, (owner, start, size, side) in enumerate(places):
            if owner not in wanted:
                continue
            tall = pieces[number].shape[1]
            row = pl.multiple_of((ids[2] ^ side) * tall, 16)
            made.append(
                pltpu.make_async_copy(
                    pieces[number],
                    held.at[owner, start : start + size, pl.ds(row, tall), :],
                    sems.at[number],
                )
            )
        return made

    @pl.when((layer == 0) & (line == 0))
    def _():
        for copy in copies((0, 1)):
            copy.start()

    for owner in range(2):

        @pl.when((layer == owner) & (line == 0))
        def _():
            for copy in copies((owner,)):
                copy.wait()

    size, scale = clip_scale(squares)
    for part in range(9):
        lanes = slice(part * 128, part * 128 + 128)
        block = line * 9 + part
        gradient = held[layer, block].astype(full) * scale
        results = adamw(
            weight[0, :, lanes], gradient, first[0, :, lanes], second[0, :, lanes], step_rate
        )
        first_new[0, :, lanes] = results[0]
        second_new[0, :, lanes] = results[1]
        weight_new[0, :, lanes] = results[2]


def small_update_kernel(rates, *refs):
    ids, squares, mine, other, grad_norm_p = refs[0:5]
    states = refs[5:23]
    outs = refs[23:41]
    size_out = refs[41]
    size, scale = clip_scale(squares)
    size_out[...] = jnp.broadcast_to(size, size_out.shape)
    first_core = ids[2] == 0
    tall = mine.shape[0] // 2
    here = mine[...].astype(full)
    there = other[...].astype(full)
    even = jnp.where(first_core, here, there)
    odd = jnp.where(first_core, there, here)
    split_part = jnp.concatenate([even[0:tall], odd[0:tall]], axis=0).astype(half)
    shared = jnp.concatenate([even[tall:], odd[tall:]], axis=0).astype(half)
    grad_c = split_part[:, 0:C2].astype(full)
    classes = states[12].shape[0]
    pick = hot(iota((classes, WIDE), 0) + C2 == iota((classes, WIDE), 1))
    grad_head = dot(pick, split_part, NT)
    grad_b = shared[:, 0:C2].astype(full)
    pick = hot(iota((C0, WIDE), 0) + C2 == iota((C0, WIDE), 1))
    grad_a = dot(pick, shared, NT)
    pick = hot(iota((C0, WIDE), 0) + (C2 + 16) == iota((C0, WIDE), 1))
    grad_stem = dot(pick, shared[0:32], NT)[:, 0:27]
    gradients = (grad_stem, grad_a, grad_b, grad_c, grad_head, grad_norm_p[...])
    for index in range(6):
        weight, first, second = states[3 * index : 3 * index + 3]
        results = adamw(
            weight[...], gradients[index] * scale, first[...], second[...], rates[index]
        )
        for item in range(3):
            outs[3 * index + item][...] = results[item]


def xor_pairs(size, turn):
    return [(index, index ^ turn) for index in range(size)]


def shards(
    images,
    labels,
    corners,
    partners,
    stem_w,
    stem_w_m,
    stem_w_v,
    proj_a,
    proj_a_m,
    proj_a_v,
    proj_b,
    proj_b_m,
    proj_b_v,
    proj_c,
    proj_c_m,
    proj_c_v,
    conv_w,
    conv_w_m,
    conv_w_v,
    head_w,
    head_w_m,
    head_w_v,
    norm_p,
    norm_p_m,
    norm_p_v,
):
    split = lax.axis_size("dp")
    groups = lax.axis_size("filt")
    chips = groups // 2
    devices = split * groups
    count = images.shape[0]
    per = count // split
    rows = per * 64
    band = per * 8
    image_total = float(count * groups)
    row_total = image_total * 64.0
    tall = conv_w.shape[1] // 2
    spot_d = lax.axis_index("dp")
    spot_f = lax.axis_index("filt")
    ids = jnp.stack([spot_d, spot_f, spot_f % 2, spot_f // 2]).astype(jnp.int32)

    def over_dp(value, turn):
        return lax.ppermute(value, "dp", xor_pairs(split, turn))

    def over_filt(value, turn):
        return lax.ppermute(value, "filt", xor_pairs(groups, turn))

    def exchange(stats):
        return lax.all_to_all(stats, ("dp", "filt"), 0, 0)

    (own_images,) = call(
        image_kernel,
        [VMEM] * 4,
        [(shape((count, 3 * PLANE), half), VMEM)],
        [pltpu.VMEM((8, count), full)],
        3,
    )(
        images.transpose(1, 0, 2),
        labels.reshape(1, count),
        corners.T,
        partners.reshape(1, count),
    )
    (own_pack,) = call(
        pack_kernel,
        [VMEM] * 3,
        [(shape((2 * tall, WIDE), half), VMEM)],
        [],
        2,
        1,
    )(proj_c.T, head_w.T, norm_p, own_images)
    packs = [own_pack] + [over_dp(own_pack, turn) for turn in range(1, split)]
    far_images = [own_images] + [over_filt(own_images, 2 * turn) for turn in range(1, chips)]
    def start_gather(layer, after):
        own = cast_half(ids, conv_w, layer, after)
        return [own, over_dp(own, 1), over_dp(own, 2)]

    def middle_gather(pieces, after):
        rows = pieces[0].shape[0]
        return cut_rows(pieces[:0:-1], [(0, 48), (48, rows - 48)], after)

    def end_gather(pieces, far):
        pieces = [*pieces, over_dp(far[0], 1), over_dp(far[1], 2)]
        return pieces + [over_filt(piece, 1) for piece in pieces]

    pieces = start_gather(0, packs)
    far = middle_gather(pieces, [])
    all_images = stack(
        far_images,
        [(turn, 0, count) for turn in range(chips)],
        (chips, count, 3 * PLANE),
        pieces[:1],
    )

    line = shape((devices, 1, 2 * C3))
    (
        patches,
        stem_out,
        mid_one,
        mid_two,
        act_three,
        base,
        stats,
        norm_rows,
        head_all,
        proj_t,
        facts,
    ) = call(
        functools.partial(front_kernel, (per, count, groups, devices, split)),
        [SMEM] + [VMEM] * 2 + [ANY] * split + [VMEM] * 3,
        [
            (shape((rows, 32), half), VMEM),
            (shape((rows, C0)), VMEM),
            (shape((rows, C1)), VMEM),
            (shape((rows, WIDE)), VMEM),
            (shape((rows, WIDE), half), VMEM),
            (shape((rows, C3)), VMEM),
            (line, VMEM),
            (shape((8, C3)), VMEM),
            (shape((C3, 16), half), VMEM),
            (shape((C3, WIDE), half), VMEM),
            (shape((per, 128)), VMEM),
        ],
        [
            pltpu.VMEM((C3, WIDE), half),
            pltpu.VMEM((per, 32, 128), full),
            pltpu.VMEM((rows, 32), full),
            pltpu.VMEM((C0, 32), full),
            pltpu.VMEM((C1, WIDE), half),
            pltpu.VMEM((8, C3), full),
            pltpu.SemaphoreType.DMA((split,)),
        ],
        10,
        1,
    )(ids, all_images, over_filt(all_images, 1), *packs, stem_w.T, proj_a, proj_b, far[0])
    kernels = [end_gather(pieces, far)]
    stats_one = exchange(stats)
    pieces = start_gather(1, [stats_one])

    table = pltpu.VMEM((rows, C3), full)
    conv_outs = [
        (shape((rows, C3)), ANY),
        (shape((rows, C3), half), ANY),
        (shape((rows, C3)), ANY),
        (line, VMEM),
    ]
    conv_scratch = [
        table,
        pltpu.VMEM((C3, 9 * C3), half),
        pltpu.VMEM((rows, TRIPLE), half),
        table,
        table,
        pltpu.SemaphoreType.DMA((10,)),
        pltpu.SemaphoreType.DMA((QUARTERS,)),
        pltpu.SemaphoreType.DMA((QUARTERS + 2,)),
    ]
    conv_one, field_one, slope_one, stats = call(
        functools.partial(conv_kernel, (per, row_total, split), 0),
        [SMEM, ANY, VMEM, VMEM] + [ANY] * 10,
        conv_outs,
        conv_scratch,
        18,
    )(ids, base, stats_one, norm_rows, *kernels[0])
    kernels.append(end_gather(pieces, middle_gather(pieces, [stats])))
    stats_two = exchange(stats)
    far_field_one = over_filt(field_one, 1)
    summed, field_two, slope_two, stats = call(
        functools.partial(conv_kernel, (per, row_total, split), 1),
        [SMEM, ANY, VMEM, VMEM, ANY] + [ANY] * 10,
        conv_outs,
        conv_scratch,
        18,
    )(ids, conv_one, stats_two, norm_rows, base, *kernels[1])
    stats_three = exchange(stats)
    far_field_two = over_filt(field_two, 1)
    slope_three, spread, stats, grad_head = call(
        functools.partial(head_kernel, (per, row_total, image_total, head_w.shape[1])),
        [VMEM] * 5,
        [
            (shape((rows, C3)), VMEM),
            (shape((band, C3)), VMEM),
            (shape((devices, 1, 2 * C3 + 128)), VMEM),
            (shape((C3, 16)), VMEM),
        ],
        [pltpu.VMEM((band, C3), full)] * 3,
        7,
    )(summed, stats_three, norm_rows, head_all, facts)
    stats_four = exchange(stats)
    loss = jnp.sum(stats_four[:, 0, 2 * C3])

    wide_half = pltpu.VMEM((rows, WIDE), half)
    picks = pltpu.VMEM((C3, 2 * WIDE), half)
    half_outs = [(shape((rows, WIDE), half), ANY)] * 2

    def back(layer, heads, tails, after):
        last = layer == 1
        return call(
            functools.partial(back_kernel, (per, row_total, split), layer),
            ([SMEM, ANY, ANY] + [VMEM] * 4 if last else [SMEM, ANY])
            + [ANY, ANY, VMEM]
            + [ANY] * 10,
            [(shape((rows, C3)), ANY), (line, VMEM)]
            + (half_outs + [(shape((rows, C3)), ANY)] if last else []),
            (
                [table, wide_half, wide_half, picks, pltpu.SemaphoreType.DMA((2 * QUARTERS + 1,))]
                if last
                else [pltpu.VMEM((rows, C3), half)]
            )
            + [
                table,
                table,
                pltpu.VMEM((C3, 9 * C3), half),
                pltpu.VMEM((rows, TRIPLE), half),
                table,
                pltpu.SemaphoreType.DMA((10,)),
                pltpu.SemaphoreType.DMA((2 * QUARTERS,)),
                pltpu.SemaphoreType.DMA((QUARTERS,)),
            ],
            22,
            len(after),
        )(ids, *heads, *tails, *kernels[layer], *after)

    grad_conv_one, stats, own_half, far_half, grad_summed = back(
        1,
        [slope_three, summed, stats_three, stats_four, norm_rows, spread],
        [conv_one, slope_two, stats_two],
        [],
    )
    stats_five = exchange(stats)

    def weight_grad(own_half, far_half, field, far_field, chunks, after):
        sizes = [part_sizes(split, lines) for lines in chunks]
        outs = [
            (shape((size, tall, 128), half), ANY) for parts in sizes for _, _, size in parts
        ]
        flat = call(
            functools.partial(weight_grad_kernel, (chunks, split, band)),
            [ANY] * 4,
            outs,
            [
                pltpu.VMEM((2 * rows, WIDE), half),
                pltpu.VMEM((2 * rows, TRIPLE), half),
                pltpu.VMEM((2, rows, C3), half),
                pltpu.VMEM((split, 45, tall, 128), half),
                pltpu.SemaphoreType.DMA((16,)),
                pltpu.SemaphoreType.DMA((16,)),
                pltpu.SemaphoreType.DMA((len(outs),)),
            ],
            13,
            len(after),
        )(own_half, over_filt(far_half, 1), field, far_field, *after)
        result = []
        for parts in sizes:
            result.append(flat[: len(parts)])
            flat = flat[len(parts) :]
        return result

    def square_sum(value):
        wide = value.astype(full)
        return jnp.sum(wide * wide)

    def add(values):
        return sum(value.astype(full) for value in values).astype(half)

    def start_dp(parts, after):
        own, near, next_near, far_low, far_high = parts
        blocks = near.shape[0]
        cut = far_low.shape[0]
        from_near = over_dp(far_low, 1)
        from_next = over_dp(far_high, 2)
        near, next_near = merge(
            [near, next_near, from_near, from_next],
            [
                (blocks, [(0, 0, 0, blocks), (3, 0, cut, blocks - cut)]),
                (blocks, [(1, 0, 0, blocks), (2, 0, 0, cut)]),
            ],
            after,
            3,
        )
        return [own, near, next_near]

    def end_dp(parts, sizes, after):
        own, near, next_near = parts
        plan = []
        start = 0
        for size in sizes:
            plan.append((size, [(source, start, 0, size) for source in range(3)]))
            start += size
        return merge([own, over_dp(near, 1), over_dp(next_near, 2)], plan, after, 2)

    def over_all_chips(value, after=()):
        result = value
        reach = 1
        while reach < chips:
            digit = ids[3] // reach % 4
            outer = (digit == 0) | (digit == 3)
            moves = ({0: 1, 3: 2}, {1: 2, 2: 1}, {1: 0, 2: 3})
            routes = []
            for move in moves:
                pairs = []
                for index in range(groups):
                    here = index // 2 // reach % 4
                    if here in move:
                        pairs.append((index, index + (move[here] - here) * 2 * reach))
                routes.append(pairs)
            arrived = lax.ppermute(result, "filt", routes[0])
            if after:
                size = result.shape[0]
                plan = [(size, [(0, 0, 0, size), (1, 0, 0, size)])]
                (result,) = merge([result, arrived], plan, after, 2)
            else:
                result = add([result, arrived])
            result = add([result, lax.ppermute(result, "filt", routes[1])])
            squares = jnp.where(outer, 0.0, square_sum(result))
            arrived = lax.ppermute(result, "filt", routes[2])
            result = jnp.where(outer, arrived, result)
            reach *= 4
        return (result, squares)

    chunks_two = ((0, 1, 2),)
    chunks_one = ((0, 1, 2),)
    grad_one_half, own_half_one, far_half_one = call(
        functools.partial(norm_back_kernel, (row_total, split)),
        [SMEM, ANY, ANY, VMEM, VMEM, VMEM],
        [(shape((rows, C3), half), ANY)] + half_outs,
        [
            table,
            table,
            pltpu.VMEM((rows, C3), half),
            wide_half,
            wide_half,
            picks,
            pltpu.SemaphoreType.DMA((2 * QUARTERS,)),
            pltpu.SemaphoreType.DMA((3 * QUARTERS,)),
        ],
        6,
    )(ids, grad_conv_one, conv_one, stats_two, stats_five, norm_rows)
    pairs_two = weight_grad(
        own_half, far_half, field_two, far_field_two, chunks_two, [grad_one_half]
    )
    pairs_one = weight_grad(
        own_half_one, far_half_one, field_one, far_field_one, chunks_one, [pairs_two[0][0]]
    )
    begun_two = start_dp(pairs_two[0], [pairs_one[0][0]])
    grad_base, stats = back(
        0,
        [grad_one_half],
        [base, slope_one, stats_one],
        [pairs_one[0][0], begun_two[1]],
    )
    stats_six = exchange(stats)
    (part_two,) = end_dp(begun_two, [begun_two[0].shape[0]], [stats_six])
    begun_one = start_dp(pairs_one[0], [stats_six])
    small = shape((split, 2 * tall, WIDE), half)
    small_mine, small_other = call(
        functools.partial(trunk_kernel, (per, row_total, split)),
        [SMEM] + [VMEM] * 15,
        [(small, ANY), (small, ANY)],
        [
            pltpu.VMEM((rows, C3), half),
            pltpu.VMEM((rows, WIDE), half),
            pltpu.VMEM((rows, C1), half),
            pltpu.VMEM((rows, C1), half),
            pltpu.VMEM((rows, C0), half),
            pltpu.VMEM((rows, C0), half),
            pltpu.VMEM((C1, WIDE), half),
            pltpu.VMEM((C3, WIDE), half),
            pltpu.VMEM((C1, WIDE), half),
            pltpu.SemaphoreType.DMA((4 * split,)),
        ],
        13,
    )(
        ids,
        grad_base,
        grad_summed,
        base,
        stats_one,
        stats_six,
        norm_rows,
        proj_t,
        act_three,
        mid_two,
        mid_one,
        stem_out,
        patches,
        proj_a,
        proj_b,
        grad_head,
    )
    blocks = begun_one[0].shape[0]
    parts_one = end_dp(begun_one, [blocks // 2, blocks - blocks // 2], [small_mine])
    reduced_two, squares_two = zip(over_all_chips(part_two, [small_mine]))
    reduced_one, squares_one = zip(*[over_all_chips(part) for part in parts_one])
    crossed = over_filt(small_other, 1)
    pair = [add([small_mine[turn], crossed[turn]]) for turn in range(split)]
    small_sum = add([pair[0]] + [over_dp(pair[turn], turn) for turn in range(1, split)])
    small_sum = add(
        [small_sum] + [over_filt(small_sum, 2 * turn) for turn in range(1, chips)]
    )
    small_far = over_filt(small_sum, 1)

    norm_sums = []
    for stats in (stats_six, stats_five, stats_four):
        sums = jnp.sum(stats[:, 0, :], axis=0)
        norm_sums += [sums[C3 : 2 * C3], sums[0:C3]]
    grad_norm_all = jnp.stack(norm_sums)
    grad_norm_p = lax.dynamic_slice_in_dim(grad_norm_all, spot_d * 2 * tall, 2 * tall, axis=1)
    squares = (
        sum(squares_one + squares_two) / (chips // 2)
        + square_sum(small_sum[0:tall, 0 : C2 + 16]) / chips
        + square_sum(small_sum[tall:, 0 : C2 + 16]) / (chips * split)
        + square_sum(small_sum[tall:, C2 + 16 :]) / (2 * chips * split)
        + jnp.sum(grad_norm_all * grad_norm_all) / devices
    )
    squares = exchange(jnp.broadcast_to(squares, (devices, 1, 128)))

    pieces = []
    places = []
    for owner, reduced in ((0, reduced_one), (1, reduced_two)):
        start = 0
        for part in reduced:
            size = part.shape[0]
            pieces += [part, over_filt(part, 1)]
            places += [(owner, start, size, side) for side in range(2)]
            start += size
    whole_spec = pl.BlockSpec((1, 2 * tall, 1152), lambda layer, line: (layer, 0, line))
    conv_shape = shape(conv_w.shape)
    conv_new = pl.pallas_call(
        functools.partial(
            conv_update_kernel, (len(pieces), places, 0.7 / math.sqrt(9.0 * C3))
        ),
        grid=(2, 5),
        in_specs=[SMEM, VMEM, whole_spec, whole_spec, whole_spec] + [ANY] * len(pieces),
        out_specs=[whole_spec] * 3,
        out_shape=[conv_shape] * 3,
        scratch_shapes=[
            pltpu.VMEM((2, 45, 2 * tall, 128), half),
            pltpu.SemaphoreType.DMA((len(pieces),)),
        ],
        compiler_params=pltpu.CompilerParams(vmem_limit_bytes=60 * MIB),
        cost_estimate=pl.CostEstimate(
            flops=20 * conv_w.size, bytes_accessed=26 * conv_w.size, transcendentals=0
        ),
    )(ids, squares, conv_w, conv_w_m, conv_w_v, *pieces)
    states = (
        (stem_w.T, stem_w_m.T, stem_w_v.T),
        (proj_a, proj_a_m, proj_a_v),
        (proj_b, proj_b_m, proj_b_v),
        (proj_c.T, proj_c_m.T, proj_c_v.T),
        (head_w.T, head_w_m.T, head_w_v.T),
        (norm_p, norm_p_m, norm_p_v),
    )
    rates = (
        0.7 / math.sqrt(27.0),
        0.7 / math.sqrt(C0),
        0.7 / math.sqrt(C1),
        0.7 / math.sqrt(C2),
        0.7 / math.sqrt(C3 / 8.0),
        0.8,
    )
    flat = [item for group in states for item in group]
    small_new = call(
        functools.partial(small_update_kernel, rates),
        [SMEM] + [VMEM] * 22,
        [(shape(item.shape), VMEM) for item in flat] + [(shape((1, 128)), VMEM)],
        [],
        3,
    )(ids, squares, small_sum, small_far, grad_norm_p, *flat)
    size = small_new[18][0, 0]
    turned = [
        item.T if index // 3 in (0, 3, 4) else item for index, item in enumerate(small_new[:18])
    ]
    return (
        *turned[0:12],
        *conv_new,
        *turned[12:18],
        loss,
        size,
    )


def solution(mesh):
    placed = (
        P("filt", None, None),
        P("filt"),
        P("filt", None),
        P("filt"),
        *([P()] * 9),
        *([P(None, "dp")] * 3),
        *([P(None, "dp", None)] * 3),
        *([P("dp", None)] * 3),
        *([P(None, "dp")] * 3),
    )
    return jax.shard_map(
        shards,
        mesh=mesh,
        in_specs=placed,
        out_specs=(
            *([P()] * 9),
            *([P(None, "dp")] * 3),
            *([P(None, "dp", None)] * 3),
            *([P("dp", None)] * 3),
            *([P(None, "dp")] * 3),
            P(),
            P(),
        ),
        check_vma=False,
    )
```

time: 595 us -> 476 us (0.80)
  waiting for transfers between devices: 217 us -> 130 us
  local copies, waits for them, and re-layouts: 61.1 us -> 20 us
  Pallas kernels: 157 us -> 195 us
  other arithmetic: 28.5 us -> 11.1 us
  blocking collectives: 36.4 us -> 23.7 us
    ppermute x18 -> x22, waiting for transfers between devices: 128 us -> 42.5 us  [over_dp(): return lax.ppermute(value, 'dp', xor_pairs(split, turn))]
    ppermute x42 -> x26, waiting for transfers between devices: 67.1 us -> 7.89 us  [over_filt(): return lax.ppermute(value, 'filt', xor_pairs(groups, turn))]
    unnamed x206 -> x98, local copies, waits for them, and re-layouts: 60.2 us -> 18.7 us
    ppermute x0 -> x9, waiting for transfers between devices: none -> 41.4 us  [the longest x3 37 us: over_all_chips(): arrived = lax.ppermute(result, 'filt', routes[2])]
    pallas_call x10 -> x18, Pallas kernels: 106 us -> 139 us  [the longest x2 40.2 us: back(): call(functools.partial(back_kernel, (per, row_total, split), layer), ([SM...]
    all_to_all x4 -> x5, waiting for transfers between devices: 22.8 us -> 38.5 us  [exchange(): return lax.all_to_all(stats, ('dp', 'filt'), 0, 0)]
    ppermute x42 -> x26, starting transfers between devices: 41.4 us -> 26.4 us  [over_filt(): return lax.ppermute(value, 'filt', xor_pairs(groups, turn))]
    convert_element_type x7 -> x5, other arithmetic: 19.5 us -> 4.59 us  [add(): return sum((value.astype(full) for value in values)).astype(half)]
  transfers between devices with their start and end apart: 64 -> 62, of which waited for: 19 -> 17; matrix products, arithmetic and copies ran while one was open for 7% -> 3% of each run, Pallas kernels for 15% -> 30%
where the time goes in v2:
time: 476 us; the launch traced here: 470 us
  Pallas kernels  195 us (41%)
  waiting for transfers between devices  130 us (27%)
  starting transfers between devices  84 us (18%)
  blocking collectives  23.7 us (5%)
  local copies, waits for them, and re-layouts  20 us (4%)
  other arithmetic  11.1 us (2%)
  between operations  6.34 us (1%)
    ppermute x22, waiting for transfers between devices, over_dp(): return lax.ppermute(value, 'dp', xor_pairs(split, turn))  42.5 us
    pallas_call x2, Pallas kernels, back(): call(functools.partial(back_kernel, (per, row_total, split), layer), ([SM...  40.2 us
    all_to_all x5, waiting for transfers between devices, exchange(): return lax.all_to_all(stats, ('dp', 'filt'), 0, 0)  38.5 us
    ppermute x3, waiting for transfers between devices, over_all_chips(): arrived = lax.ppermute(result, 'filt', routes[2])  37 us
    pallas_call x2, Pallas kernels, weight_grad(): call(functools.partial(weight_grad_kernel, (chunks, split, band)), [ANY]...  27.1 us
    ppermute x26, starting transfers between devices, over_filt(): return lax.ppermute(value, 'filt', xor_pairs(groups, turn))  26.4 us
    all_to_all x2, blocking collectives, exchange(): return lax.all_to_all(stats, ('dp', 'filt'), 0, 0)  23.7 us
    ppermute x22, starting transfers between devices, over_dp(): return lax.ppermute(value, 'dp', xor_pairs(split, turn))  23.4 us
  transfers between devices with their start and end apart: 62, of which 17 were waited for; matrix products, arithmetic and copies ran while one was open for 3% of the time, Pallas kernels for 30%

profile of v2, /device:TPU:0, one launch (start us, length us, event | category | flops | bytes accessed | tf_op | source)
XLA Modules:
  0.0 470.3 jit_solution(5434390209132200041)
XLA Ops:
  0.7 2.7 shard_map.416.refs_3_.refs_0_
  3.4 2.0 shard_map.417.refs_2_.refs_3_
  5.3 2.9 collective-permute-start.3
  8.3 1.6 collective-permute-start
  9.9 2.6 collective-permute-start.1
  12.7 1.5 collective-permute-start.4
  15.2 5.2 %collective-permute-done.4.refs_4_.refs_5_ = bf16[160,384]{1,0:T(8,128)(2,1)S(1)} collective-permute-done((bf16[160,384]{1,0:T(8,128)(2,1)}, bf16[160,384]{1,0:T(8,128)(2,1)S(1)}, u32[]{:S(2)}, u32[]{:S(2)}) %collective-permute-start.4) | collective-permute-done | bytes 122912 | tf_op jit(solution)/shard_map/ppermute | solution.py:1142
  21.6 2.9 shard_map.418.refs_4_.refs_5_
  24.6 7.8 %collective-permute-done.1.refs_2_ = bf16[72,1920]{1,0:T(8,128)(2,1)S(1)} collective-permute-done((bf16[72,1920]{1,0:T(8,128)(2,1)}, bf16[72,1920]{1,0:T(8,128)(2,1)S(1)}, u32[]{:S(2)}, u32[]{:S(2)}) %collective-permute-start.1) | collective-permute-done | bytes 276512 | tf_op jit(solution)/shard_map/ppermute | solution.py:1145
  33.8 2.2 shard_map.419.refs_1_
  36.1 1.6 collective-permute-start.7
  38.2 20.7 %collective-permute-done.7.refs_0_.refs_6_.refs_7_ = bf16[80,5760]{1,0:T(8,128)(2,1)S(1)} collective-permute-done((bf16[80,5760]{1,0:T(8,128)(2,1)S(1)}, bf16[80,5760]{1,0:T(8,128)(2,1)S(1)}, u32[]{:S(2)}, u32[]{:S(2)}) %collective-permute-start.7) | collective-permute-done | bytes 921632 | tf_op jit(solution)/shard_map/ppermute | solution.py:1142
  61.2 2.1 shard_map.420
  65.6 10.5 %shard_map.421 = (bf16[1152,32]{1,0:T(8,128)(2,1)}, f32[1152,16]{1,0:T(8,128)}, f32[1152,160]{1,0:T(8,128)}, f32[1152,384]{1,0:T(8,128)}, bf16[1152,384]{1,0:T(8...) custom-call(s32[4]{0:T(128)} %pad_add_fusion.refs_0_, ...), custom_call_target="tpu_custom_call" | custom-call | flops 3500000000 | bytes 1 | tf_op jit(solution)/shard_map/pallas_call | solution.py:1206
  76.1 7.2 %all-to-all-start = ((f32[32,1,1280]{2,1,0:T(1,128)}), f32[32,1,1280]{2,1,0:T(1,128)S(1)}, u32[]{:S(2)}, u32[]{:S(2)}) async-start(f32[32,1,1280]{2,1,0:T(1,128)} %get-tuple-element.102), calls=%async_computation | async-start | bytes 327680 | tf_op jit(solution)/shard_map/all_to_all | solution.py:1148
  83.8 7.9 %all-to-all-done.refs_2_.refs_4_ = f32[32,1,1280]{2,1,0:T(1,128)S(1)} async-done(((f32[32,1,1280]{2,1,0:T(1,128)}), f32[32,1,1280]{2,1,0:T(1,128)S(1)}, u32[]{:S(2)}, u32[]{:S(2)}) %all-to-all-start) | async-done | bytes 163872 | tf_op jit(solution)/shard_map/all_to_all | solution.py:1148
  92.4 2.9 shard_map.423.refs_5_.refs_10_
  98.4 18.5 %shard_map.422 = (f32[1152,640]{1,0:T(8,128)}, bf16[1152,640]{1,0:T(8,128)(2,1)}, f32[1152,640]{1,0:T(8,128)}, f32[32,1,1280]{2,1,0:T(1,128)}) custom-call(s32[4]{0:T(128)} %pad_add_fusion.refs_0_, f32[1152,640]{1,0:T(8,128)} %get-tuple-element.101.refs_1_.refs_4_.refs_2_.refs_3_, f32[32,1,1280]{2,1,0:T(1,128)} %copy-done.22, ...), custom_call_target="tpu_custom_call" | custom-call | flops 6300000256 | bytes 1 | tf_op jit(solution)/shard_map/pallas_call | solution.py:1255
  116.9 1.6 collective-permute-done.16.refs_1_.refs_6_.refs_11_
  119.6 2.1 shard_map.424
  121.8 1.5 collective-permute-start.18
  124.3 11.9 %collective-permute-done.18.refs_8_.refs_13_ = bf16[48,5760]{1,0:T(8,128)(2,1)S(1)} collective-permute-done((bf16[48,5760]{1,0:T(8,128)(2,1)}, bf16[48,5760]{1,0:T(8,128)(2,1)S(1)}, u32[]{:S(2)}, u32[]{:S(2)}) %collective-permute-start.18) | collective-permute-done | bytes 552992 | tf_op jit(solution)/shard_map/ppermute | solution.py:1142
  136.8 11.9 %all_to_all.35.refs_2_.refs_9_.refs_3_ = f32[32,1,1280]{2,1,0:T(1,128)} all-to-all(f32[32,1,1280]{2,1,0:T(1,128)} %get-tuple-element.106.refs_2_), channel_id=1, replica_groups=mesh['dp'=4,'filt'=8] {'dp','filt'}, dimensions={0} | all-to-all | bytes 327680 | tf_op jit(solution)/shard_map/all_to_all | solution.py:1148
  150.5 18.6 %shard_map.425 = (f32[1152,640]{1,0:T(8,128)}, bf16[1152,640]{1,0:T(8,128)(2,1)}, f32[1152,640]{1,0:T(8,128)}, f32[32,1,1280]{2,1,0:T(1,128)}) custom-call(s32[4]{0:T(128)} %pad_add_fusion.refs_0_, f32[1152,640]{1,0:T(8,128)} %get-tuple-element.105.refs_1_.refs_7_.refs_2_, f32[32,1,1280]{2,1,0:T(1,128)} %all_to_all.35.refs_2_.refs_9_.refs_3_, ...), custom_call_target="tpu_custom_call" | custom-call | flops 6300000256 | bytes 1 | tf_op jit(solution)/shard_map/pallas_call | solution.py:1265
  169.1 11.8 %all_to_all.36.refs_1_.refs_3_ = f32[32,1,1280]{2,1,0:T(1,128)} all-to-all(f32[32,1,1280]{2,1,0:T(1,128)} %get-tuple-element.110), channel_id=1, replica_groups=mesh['dp'=4,'filt'=8] {'dp','filt'}, dimensions={0} | all-to-all | bytes 327680 | tf_op jit(solution)/shard_map/all_to_all | solution.py:1148
  180.9 7.0 %shard_map.426 = (f32[1152,640]{1,0:T(8,128)}, f32[144,640]{1,0:T(8,128)}, f32[32,1,1408]{2,1,0:T(1,128)}, f32[640,16]{1,0:T(8,128)}) custom-call(f32[1152,640]{1,0:T(8,128)} %get-tuple-element.109.refs_0_.refs_2_, f32[32,1,1280]{2,1,0:T(1,128)} %all_to_all.36.refs_1_.refs_3_, f32[8,640]{1,0:T(8,128)} %get-tuple-element.103.refs_3_.refs_2_.refs_5_.refs_6_, ...), custom_call_target="tpu_custom_call" | custom-call | flops 2449999872 | bytes 1 | tf_op jit(solution)/shard_map/pallas_call | solution.py:1274
  187.9 2.8 all-to-all-start.3
  191.3 8.0 %all-to-all-done.3.refs_4_ = f32[32,1,1408]{2,1,0:T(1,128)S(1)} async-done(((f32[32,1,1408]{2,1,0:T(1,128)}), f32[32,1,1408]{2,1,0:T(1,128)S(1)}, u32[]{:S(2)}, u32[]{:S(2)}) %all-to-all-start.3) | async-done | bytes 180256 | tf_op jit(solution)/shard_map/all_to_all | solution.py:1148
  200.0 21.6 %shard_map.427 = (f32[1152,640]{1,0:T(8,128)}, f32[32,1,1280]{2,1,0:T(1,128)}, bf16[1152,384]{1,0:T(8,128)(2,1)}, bf16[1152,384]{1,0:T(8,128)(2,1)}, f32[1152,640]{1,0:T(8,128)}) custom-call(s32[4]{0:T(128)} %pad_add_fusion.refs_0_, f32[1152,640]{1,0:T(8,128)} %get-tuple-element.113.refs_1_, f32[1152,640]{1,0:T(8,128)} %get-tuple-element.109.refs_0_.refs_2_, ...), custom_call_target="tpu_custom_call" | custom-call | flops 7699999744 | bytes 1 | tf_op jit(solution)/shard_map/pallas_call | solution.py:1295
  221.5 3.1 all-to-all-start.4
  225.1 8.0 %all-to-all-done.4.refs_4_ = f32[32,1,1280]{2,1,0:T(1,128)S(1)} async-done(((f32[32,1,1280]{2,1,0:T(1,128)}), f32[32,1,1280]{2,1,0:T(1,128)S(1)}, u32[]{:S(2)}, u32[]{:S(2)}) %all-to-all-start.4) | async-done | bytes 163872 | tf_op jit(solution)/shard_map/all_to_all | solution.py:1148
  233.7 6.5 %shard_map.428 = (bf16[1152,640]{1,0:T(8,128)(2,1)}, bf16[1152,384]{1,0:T(8,128)(2,1)}, bf16[1152,384]{1,0:T(8,128)(2,1)}) custom-call(s32[4]{0:T(128)} %pad_add_fusion.refs_0_, f32[1152,640]{1,0:T(8,128)} %get-tuple-element.117.refs_1_, f32[1152,640]{1,0:T(8,128)} %get-tuple-element.105.refs_1_.refs_7_.refs_2_, ...), custom_call_target="tpu_custom_call" | custom-call | flops 2100000000 | bytes 1 | tf_op jit(solution)/shard_map/pallas_call | solution.py:1420
  241.8 13.5 %shard_map.429 = (bf16[45,80,128]{2,1,0:T(8,128)(2,1)}, bf16[45,80,128]{2,1,0:T(8,128)(2,1)}, bf16[45,80,128]{2,1,0:T(8,128)(2,1)}, bf16[22,80,128]{2,1,0:T(8,128)(2,1)}, bf16[23,80,128]{2,1,0:T(8,128)(2,1)}) custom-call(bf16[1152,384]{1,0:T(8,128)(2,1)} %get-tuple-element.122.refs_0_, bf16[1152,384]{1,0:T(8,128)(2,1)} %copy-done.36, ...), custom_call_target="tpu_custom_call" | custom-call | flops 4550000128 | bytes 1 | tf_op jit(solution)/shard_map/pallas_call | solution.py:1334
  257.6 13.6 %shard_map.430 = (bf16[45,80,128]{2,1,0:T(8,128)(2,1)}, bf16[45,80,128]{2,1,0:T(8,128)(2,1)}, bf16[45,80,128]{2,1,0:T(8,128)(2,1)}, bf16[22,80,128]{2,1,0:T(8,128)(2,1)}, bf16[23,80,128]{2,1,0:T(8,128)(2,1)}) custom-call(bf16[1152,384]{1,0:T(8,128)(2,1)} %get-tuple-element.119.refs_0_, bf16[1152,384]{1,0:T(8,128)(2,1)} %copy-done.35, ...), custom_call_target="tpu_custom_call" | custom-call | flops 4550000128 | bytes 1 | tf_op jit(solution)/shard_map/pallas_call | solution.py:1334
  271.1 1.3 collective-permute-start.30
  272.5 1.5 collective-permute-start.29
  274.9 2.8 shard_map.431
  279.1 18.6 %shard_map.432 = (f32[1152,640]{1,0:T(8,128)}, f32[32,1,1280]{2,1,0:T(1,128)}) custom-call(s32[4]{0:T(128)} %pad_add_fusion.refs_0_, bf16[1152,640]{1,0:T(8,128)(2,1)} %get-tuple-element.125.refs_4_.refs_1_, f32[1152,640]{1,0:T(8,128)} %get-tuple-element.101.refs_1_.refs_4_.refs_2_.refs_3_, f32[1152,640]{1,0:T(8,128)} %get-tuple-element.132.refs_3_, ...), custom_call_target="tpu_custom_call" | custom-call | flops 7699999744 | bytes 1 | tf_op jit(solution)/shard_map/pallas_call | solution.py:1295
  297.7 3.1 all-to-all-start.5
  300.9 8.3 %all-to-all-done.5.refs_4_.refs_5_.refs_3_ = f32[32,1,1280]{2,1,0:T(1,128)S(1)} async-done(((f32[32,1,1280]{2,1,0:T(1,128)}), f32[32,1,1280]{2,1,0:T(1,128)S(1)}, u32[]{:S(2)}, u32[]{:S(2)}) %all-to-all-start.5) | async-done | bytes 163872 | tf_op jit(solution)/shard_map/all_to_all | solution.py:1148
  310.1 2.8 shard_map.433
  315.7 2.7 shard_map.436.refs_0_
  318.4 2.1 collective-permute-start.41
  321.3 12.9 %shard_map.434 = (bf16[4,160,384]{2,1,0:T(8,128)(2,1)}, bf16[4,160,384]{2,1,0:T(8,128)(2,1)}) custom-call(s32[4]{0:T(128)} %pad_add_fusion.refs_0_, f32[1152,640]{1,0:T(8,128)} %get-tuple-element.141.refs_1_, f32[1152,640]{1,0:T(8,128)} %get-tuple-element.142.refs_2_, f32[1152,640]{1,0:T(8,128)} %get-tuple-element.101.refs_1_.refs_4_.refs_2_.refs_3_, ...), custom_call_target="tpu_custom_call" | custom-call | flops 4550000128 | bytes 1 | tf_op jit(solution)/shard_map/pallas_call | solution.py:1453
  334.5 1.6 collective-permute-done.33.refs_1_
  337.3 2.8 shard_map.435
  340.1 3.1 collective-permute-start.35
  344.2 2.4 shard_map.437
  348.8 3.1 collective-permute-start.37
  353.0 1.4 collective-permute-start.44
  354.3 1.4 collective-permute-start.45
  356.5 1.3 add_convert_fusion.4
  357.8 4.4 collective-permute-done.37
  365.8 1.3 collective-permute-start.55
  367.9 1.3 collective-permute-start.51
  370.2 14.9 %collective-permute-start.47 = (bf16[160,384]{1,0:T(8,128)(2,1)S(1)}, bf16[160,384]{1,0:T(8,128)(2,1)S(1)}, u32[]{:S(2)}, u32[]{:S(2)}) collective-permute-start(bf16[160,384]{1,0:T(8,128)(2,1)S(1)} %fusion.2), channel_id=1, source_target_pairs={{0,2},{1,3},{2,0},{3,1},{4,6},{5,7},{6,4},{7,5},{8,10},{9,11},{10,... | collective-permute-start | bytes 368648 | tf_op jit(solution)/shard_map/ppermute | solution.py:1145
  385.1 2.4 collective-permute-start.49
  388.4 27.7 %collective-permute-done.51 = bf16[22,80,128]{2,1,0:T(8,128)(2,1)S(1)} collective-permute-done((bf16[22,80,128]{2,1,0:T(8,128)(2,1)S(1)}, bf16[22,80,128]{2,1,0:T(8,128)(2,1)S(1)}, u32[]{:S(2)}, u32[]{:S(2)}) %collective-permute-start.51) | collective-permute-done | bytes 450592 | tf_op jit(solution)/shard_map/ppermute | solution.py:1413
  416.1 1.3 collective-permute-start.53
  417.7 9.3 %collective-permute-done.53 = bf16[23,80,128]{2,1,0:T(8,128)(2,1)S(1)} collective-permute-done((bf16[23,80,128]{2,1,0:T(8,128)(2,1)S(1)}, bf16[23,80,128]{2,1,0:T(8,128)(2,1)S(1)}, u32[]{:S(2)}, u32[]{:S(2)}) %collective-permute-start.53) | collective-permute-done | bytes 471072 | tf_op jit(solution)/shard_map/ppermute | solution.py:1413
  433.6 3.7 all-to-all-start.6
  438.0 6.4 %all-to-all-done.6.refs_1_ = f32[32,1,128]{2,1,0:T(1,128)S(1)} async-done(((f32[32,1,128]{2,1,0:T(1,128)}), f32[32,1,128]{2,1,0:T(1,128)S(1)}, u32[]{:S(2)}, u32[]{:S(2)}) %all-to-all-start.6) | async-done | bytes 16416 | tf_op jit(solution)/shard_map/all_to_all | solution.py:1148
  445.0 3.1 shard_map.438
  449.9 20.1 %shard_map.439 = (f32[2,160,5760]{2,1,0:T(8,128)}, f32[2,160,5760]{2,1,0:T(8,128)}, f32[2,160,5760]{2,1,0:T(8,128)}) custom-call(s32[4]{0:T(128)} %pad_add_fusion.refs_0_, f32[32,1,128]{2,1,0:T(1,128)} %copy-done.28, f32[2,160,5760]{2,1,0:T(8,128)} %refs_2_.3, f32[2,160,5760]{2,1,0:T(8,128)} %refs_3_.1, f32[2,160,5760]{2,1,0:T(8,128)} %refs_4_.1, ...), custom_call_target="tpu_custom_call" | custom-call | flops 36864000 | bytes 47923200 | tf_op jit(solution)/shard_map/pallas_call | solution.py:1526
  (215 shorter events, 48.8 us)
Async XLA Ops:
  5.3 8.8 %collective-permute-start.3 = (bf16[160,384]{1,0:T(8,128)(2,1)}, bf16[160,384]{1,0:T(8,128)(2,1)S(1)}, u32[]{:S(2)}, u32[]{:S(2)}) collective-permute-start(bf16[160,384]{1,0:T(8,128)(2,1)} %shard_map.417.refs_2_.refs_3_), channel_id=1, source_target_pairs={{0,8},{8,0},{16,24},{24,16},{1,9},{9,1},{17,25},{25,17},{2,10},{10... | collective-permute-start | bytes 368648 | tf_op jit(solution)/shard_map/ppermute | solution.py:1142
  8.3 16.2 %collective-permute-start = (bf16[72,1920]{1,0:T(8,128)(2,1)}, bf16[72,1920]{1,0:T(8,128)(2,1)S(1)}, u32[]{:S(2)}, u32[]{:S(2)}) collective-permute-start(bf16[72,1920]{1,0:T(8,128)(2,1)} %shard_map.416.refs_3_.refs_0_), channel_id=1, source_target_pairs={{0,2},{1,3},{2,0},{3,1},{4,6},{5,7},{6,4},{7,5},{8,10},{9,11},{10,... | collective-permute-start | bytes 829448 | tf_op jit(solution)/shard_map/ppermute | solution.py:1145
  9.9 22.5 %collective-permute-start.1 = (bf16[72,1920]{1,0:T(8,128)(2,1)}, bf16[72,1920]{1,0:T(8,128)(2,1)S(1)}, u32[]{:S(2)}, u32[]{:S(2)}) collective-permute-start(bf16[72,1920]{1,0:T(8,128)(2,1)} %shard_map.416.refs_3_.refs_0_), channel_id=1, source_target_pairs={{0,4},{1,5},{2,6},{3,7},{4,0},{5,1},{6,2},{7,3},{8,12},{9,13},{10,... | collective-permute-start | bytes 829448 | tf_op jit(solution)/shard_map/ppermute | solution.py:1145
  12.4 19.9 %collective-permute-start.2 = (bf16[72,1920]{1,0:T(8,128)(2,1)}, bf16[72,1920]{1,0:T(8,128)(2,1)S(1)}, u32[]{:S(2)}, u32[]{:S(2)}) collective-permute-start(bf16[72,1920]{1,0:T(8,128)(2,1)} %shard_map.416.refs_3_.refs_0_), channel_id=1, source_target_pairs={{0,6},{1,7},{2,4},{3,5},{4,2},{5,3},{6,0},{7,1},{8,14},{9,15},{10,... | collective-permute-start | bytes 829448 | tf_op jit(solution)/shard_map/ppermute | solution.py:1145
  12.7 7.7 %collective-permute-start.4 = (bf16[160,384]{1,0:T(8,128)(2,1)}, bf16[160,384]{1,0:T(8,128)(2,1)S(1)}, u32[]{:S(2)}, u32[]{:S(2)}) collective-permute-start(bf16[160,384]{1,0:T(8,128)(2,1)} %shard_map.417.refs_2_.refs_3_), channel_id=1, source_target_pairs={{0,16},{8,24},{16,0},{24,8},{1,17},{9,25},{17,1},{25,9},{2,18},{10... | collective-permute-start | bytes 368648 | tf_op jit(solution)/shard_map/ppermute | solution.py:1142
  14.2 6.2 %collective-permute-start.5 = (bf16[160,384]{1,0:T(8,128)(2,1)}, bf16[160,384]{1,0:T(8,128)(2,1)S(1)}, u32[]{:S(2)}, u32[]{:S(2)}) collective-permute-start(bf16[160,384]{1,0:T(8,128)(2,1)} %shard_map.417.refs_2_.refs_3_), channel_id=1, source_target_pairs={{0,24},{8,16},{16,8},{24,0},{1,25},{9,17},{17,9},{25,1},{2,26},{10... | collective-permute-start | bytes 368648 | tf_op jit(solution)/shard_map/ppermute | solution.py:1142
  36.0 29.0 %collective-permute-start.6 = (bf16[4,72,1920]{2,1,0:T(8,128)(2,1)}, bf16[4,72,1920]{2,1,0:T(8,128)(2,1)}, u32[]{:S(2)}, u32[]{:S(2)}) collective-permute-start(bf16[4,72,1920]{2,1,0:T(8,128)(2,1)} %shard_map.419.refs_1_), channel_id=1, source_target_pairs={{0,1},{1,0},{2,3},{3,2},{4,5},{5,4},{6,7},{7,6},{8,9},{9,8},{10,11... | collective-permute-start | bytes 3317768 | tf_op jit(solution)/shard_map/ppermute | solution.py:1145
  36.1 22.8 %collective-permute-start.7 = (bf16[80,5760]{1,0:T(8,128)(2,1)S(1)}, bf16[80,5760]{1,0:T(8,128)(2,1)S(1)}, u32[]{:S(2)}, u32[]{:S(2)}) collective-permute-start(bf16[80,5760]{1,0:T(8,128)(2,1)S(1)} %copy-done.14), channel_id=1, source_target_pairs={{0,16},{8,24},{16,0},{24,8},{1,17},{9,25},{17,1},{25,9},{2,18},{10... | collective-permute-start | bytes 2764808 | tf_op jit(solution)/shard_map/ppermute | solution.py:1142
  37.7 22.5 %collective-permute-start.8 = (bf16[80,5760]{1,0:T(8,128)(2,1)S(1)}, bf16[80,5760]{1,0:T(8,128)(2,1)S(1)}, u32[]{:S(2)}, u32[]{:S(2)}) collective-permute-start(bf16[80,5760]{1,0:T(8,128)(2,1)S(1)} %copy-done.14), channel_id=1, source_target_pairs={{0,8},{8,0},{16,24},{24,16},{1,9},{9,1},{17,25},{25,17},{2,10},{10... | collective-permute-start | bytes 2764808 | tf_op jit(solution)/shard_map/ppermute | solution.py:1142
  38.2 57.0 %collective-permute-start.11 = (bf16[80,5760]{1,0:T(8,128)(2,1)S(1)}, bf16[80,5760]{1,0:T(8,128)(2,1)}, u32[]{:S(2)}, u32[]{:S(2)}) collective-permute-start(bf16[80,5760]{1,0:T(8,128)(2,1)S(1)} %copy-done.14), channel_id=1, source_target_pairs={{0,1},{1,0},{2,3},{3,2},{4,5},{5,4},{6,7},{7,6},{8,9},{9,8},{10,11... | collective-permute-start | bytes 2764808 | tf_op jit(solution)/shard_map/ppermute | solution.py:1145
  63.3 20.4 %collective-permute-start.9 = (bf16[48,5760]{1,0:T(8,128)(2,1)}, bf16[48,5760]{1,0:T(8,128)(2,1)}, u32[]{:S(2)}, u32[]{:S(2)}) collective-permute-start(bf16[48,5760]{1,0:T(8,128)(2,1)} %get-tuple-element.100.refs_10_), channel_id=1, source_target_pairs={{0,8},{8,0},{16,24},{24,16},{1,9},{9,1},{17,25},{25,17},{2,10},{10... | collective-permute-start | bytes 1658888 | tf_op jit(solution)/shard_map/ppermute | solution.py:1142
  63.8 19.4 %collective-permute-start.10 = (bf16[32,5760]{1,0:T(8,128)(2,1)}, bf16[32,5760]{1,0:T(8,128)(2,1)}, u32[]{:S(2)}, u32[]{:S(2)}) collective-permute-start(bf16[32,5760]{1,0:T(8,128)(2,1)} %get-tuple-element.104), channel_id=1, source_target_pairs={{0,16},{8,24},{16,0},{24,8},{1,17},{9,25},{17,1},{25,9},{2,18},{10... | collective-permute-start | bytes 1105928 | tf_op jit(solution)/shard_map/ppermute | solution.py:1142
  65.1 32.0 %collective-permute-start.12 = (bf16[80,5760]{1,0:T(8,128)(2,1)}, bf16[80,5760]{1,0:T(8,128)(2,1)S(1)}, u32[]{:S(2)}, u32[]{:S(2)}) collective-permute-start(bf16[80,5760]{1,0:T(8,128)(2,1)} %copy-done.8), channel_id=1, source_target_pairs={{0,1},{1,0},{2,3},{3,2},{4,5},{5,4},{6,7},{7,6},{8,9},{9,8},{10,11... | collective-permute-start | bytes 2764808 | tf_op jit(solution)/shard_map/ppermute | solution.py:1145
  65.1 32.0 %collective-permute-start.13 = (bf16[80,5760]{1,0:T(8,128)(2,1)}, bf16[80,5760]{1,0:T(8,128)(2,1)S(1)}, u32[]{:S(2)}, u32[]{:S(2)}) collective-permute-start(bf16[80,5760]{1,0:T(8,128)(2,1)} %copy-done.7), channel_id=1, source_target_pairs={{0,1},{1,0},{2,3},{3,2},{4,5},{5,4},{6,7},{7,6},{8,9},{9,8},{10,11... | collective-permute-start | bytes 2764808 | tf_op jit(solution)/shard_map/ppermute | solution.py:1145
  76.1 15.6 %all-to-all-start = ((f32[32,1,1280]{2,1,0:T(1,128)}), f32[32,1,1280]{2,1,0:T(1,128)S(1)}, u32[]{:S(2)}, u32[]{:S(2)}) async-start(f32[32,1,1280]{2,1,0:T(1,128)} %get-tuple-element.102), calls=%async_computation | async-start | bytes 327680 | tf_op jit(solution)/shard_map/all_to_all | solution.py:1148
  83.3 13.1 %collective-permute-start.15 = (bf16[32,5760]{1,0:T(8,128)(2,1)}, bf16[32,5760]{1,0:T(8,128)(2,1)}, u32[]{:S(2)}, u32[]{:S(2)}) collective-permute-start(bf16[32,5760]{1,0:T(8,128)(2,1)} %collective-permute-done.10.refs_8_.refs_9_), channel_id=1, source_target_pairs={{0,1},{1,0},{2,3},{3,2},{4,5},{5,4},{6,7},{7,6},{8,9},{9,8},{10,11... | collective-permute-start | bytes 1105928 | tf_op jit(solution)/shard_map/ppermute | solution.py:1145
  83.7 13.4 %collective-permute-start.14 = (bf16[48,5760]{1,0:T(8,128)(2,1)}, bf16[48,5760]{1,0:T(8,128)(2,1)}, u32[]{:S(2)}, u32[]{:S(2)}) collective-permute-start(bf16[48,5760]{1,0:T(8,128)(2,1)} %collective-permute-done.9.refs_7_.refs_8_), channel_id=1, source_target_pairs={{0,1},{1,0},{2,3},{3,2},{4,5},{5,4},{6,7},{7,6},{8,9},{9,8},{10,11... | collective-permute-start | bytes 1658888 | tf_op jit(solution)/shard_map/ppermute | solution.py:1145
  95.3 23.2 %collective-permute-start.16 = (bf16[80,5760]{1,0:T(8,128)(2,1)}, bf16[80,5760]{1,0:T(8,128)(2,1)S(1)}, u32[]{:S(2)}, u32[]{:S(2)}) collective-permute-start(bf16[80,5760]{1,0:T(8,128)(2,1)} %shard_map.423.refs_5_.refs_10_), channel_id=1, source_target_pairs={{0,8},{8,0},{16,24},{24,16},{1,9},{9,1},{17,25},{25,17},{2,10},{10... | collective-permute-start | bytes 2764808 | tf_op jit(solution)/shard_map/ppermute | solution.py:1142
  96.3 22.2 %collective-permute-start.17 = (bf16[80,5760]{1,0:T(8,128)(2,1)}, bf16[80,5760]{1,0:T(8,128)(2,1)S(1)}, u32[]{:S(2)}, u32[]{:S(2)}) collective-permute-start(bf16[80,5760]{1,0:T(8,128)(2,1)} %shard_map.423.refs_5_.refs_10_), channel_id=1, source_target_pairs={{0,16},{8,24},{16,0},{24,8},{1,17},{9,25},{17,1},{25,9},{2,18},{10... | collective-permute-start | bytes 2764808 | tf_op jit(solution)/shard_map/ppermute | solution.py:1142
  121.8 14.5 %collective-permute-start.18 = (bf16[48,5760]{1,0:T(8,128)(2,1)}, bf16[48,5760]{1,0:T(8,128)(2,1)S(1)}, u32[]{:S(2)}, u32[]{:S(2)}) collective-permute-start(bf16[48,5760]{1,0:T(8,128)(2,1)} %get-tuple-element.107), channel_id=1, source_target_pairs={{0,8},{8,0},{16,24},{24,16},{1,9},{9,1},{17,25},{25,17},{2,10},{10... | collective-permute-start | bytes 1658888 | tf_op jit(solution)/shard_map/ppermute | solution.py:1142
  123.3 25.4 %collective-permute-start.20 = (bf16[80,5760]{1,0:T(8,128)(2,1)S(1)}, bf16[80,5760]{1,0:T(8,128)(2,1)S(1)}, u32[]{:S(2)}, u32[]{:S(2)}) collective-permute-start(bf16[80,5760]{1,0:T(8,128)(2,1)S(1)} %copy-done.15), channel_id=1, source_target_pairs={{0,1},{1,0},{2,3},{3,2},{4,5},{5,4},{6,7},{7,6},{8,9},{9,8},{10,11... | collective-permute-start | bytes 2764808 | tf_op jit(solution)/shard_map/ppermute | solution.py:1145
  123.3 25.4 %collective-permute-start.21 = (bf16[80,5760]{1,0:T(8,128)(2,1)}, bf16[80,5760]{1,0:T(8,128)(2,1)S(1)}, u32[]{:S(2)}, u32[]{:S(2)}) collective-permute-start(bf16[80,5760]{1,0:T(8,128)(2,1)} %copy-done.9), channel_id=1, source_target_pairs={{0,1},{1,0},{2,3},{3,2},{4,5},{5,4},{6,7},{7,6},{8,9},{9,8},{10,11... | collective-permute-start | bytes 2764808 | tf_op jit(solution)/shard_map/ppermute | solution.py:1145
  123.8 24.9 %collective-permute-start.22 = (bf16[80,5760]{1,0:T(8,128)(2,1)}, bf16[80,5760]{1,0:T(8,128)(2,1)S(1)}, u32[]{:S(2)}, u32[]{:S(2)}) collective-permute-start(bf16[80,5760]{1,0:T(8,128)(2,1)} %copy-done.10), channel_id=1, source_target_pairs={{0,1},{1,0},{2,3},{3,2},{4,5},{5,4},{6,7},{7,6},{8,9},{9,8},{10,11... | collective-permute-start | bytes 2764808 | tf_op jit(solution)/shard_map/ppermute | solution.py:1145
  123.8 12.4 %collective-permute-start.19 = (bf16[32,5760]{1,0:T(8,128)(2,1)}, bf16[32,5760]{1,0:T(8,128)(2,1)S(1)}, u32[]{:S(2)}, u32[]{:S(2)}) collective-permute-start(bf16[32,5760]{1,0:T(8,128)(2,1)} %get-tuple-element.108), channel_id=1, source_target_pairs={{0,16},{8,24},{16,0},{24,8},{1,17},{9,25},{17,1},{25,9},{2,18},{10... | collective-permute-start | bytes 1105928 | tf_op jit(solution)/shard_map/ppermute | solution.py:1142
  136.2 12.5 %collective-permute-start.23 = (bf16[48,5760]{1,0:T(8,128)(2,1)S(1)}, bf16[48,5760]{1,0:T(8,128)(2,1)S(1)}, u32[]{:S(2)}, u32[]{:S(2)}) collective-permute-start(bf16[48,5760]{1,0:T(8,128)(2,1)S(1)} %collective-permute-done.18.refs_8_.refs_13_), channel_id=1, source_target_pairs={{0,1},{1,0},{2,3},{3,2},{4,5},{5,4},{6,7},{7,6},{8,9},{9,8},{10,11... | collective-permute-start | bytes 1658888 | tf_op jit(solution)/shard_map/ppermute | solution.py:1145
  136.3 12.4 %collective-permute-start.24 = (bf16[32,5760]{1,0:T(8,128)(2,1)S(1)}, bf16[32,5760]{1,0:T(8,128)(2,1)S(1)}, u32[]{:S(2)}, u32[]{:S(2)}) collective-permute-start(bf16[32,5760]{1,0:T(8,128)(2,1)S(1)} %collective-permute-done.19.refs_9_.refs_14_), channel_id=1, source_target_pairs={{0,1},{1,0},{2,3},{3,2},{4,5},{5,4},{6,7},{7,6},{8,9},{9,8},{10,11... | collective-permute-start | bytes 1105928 | tf_op jit(solution)/shard_map/ppermute | solution.py:1145
  187.9 11.4 %all-to-all-start.3 = ((f32[32,1,1408]{2,1,0:T(1,128)}), f32[32,1,1408]{2,1,0:T(1,128)S(1)}, u32[]{:S(2)}, u32[]{:S(2)}) async-start(f32[32,1,1408]{2,1,0:T(1,128)} %get-tuple-element.114), calls=%async_computation.3 | async-start | bytes 360448 | tf_op jit(solution)/shard_map/all_to_all | solution.py:1148
  190.7 65.9 %collective-permute-start.26 = (bf16[1152,640]{1,0:T(8,128)(2,1)S(1)}, bf16[1152,640]{1,0:T(8,128)(2,1)}, u32[]{:S(2)}, u32[]{:S(2)}) collective-permute-start(bf16[1152,640]{1,0:T(8,128)(2,1)S(1)} %copy-done.29), channel_id=1, source_target_pairs={{0,1},{1,0},{2,3},{3,2},{4,5},{5,4},{6,7},{7,6},{8,9},{9,8},{10,11... | collective-permute-start | bytes 4423688 | tf_op jit(solution)/shard_map/ppermute | solution.py:1145
  191.1 49.8 %collective-permute-start.28 = (bf16[1152,640]{1,0:T(8,128)(2,1)}, bf16[1152,640]{1,0:T(8,128)(2,1)}, u32[]{:S(2)}, u32[]{:S(2)}) collective-permute-start(bf16[1152,640]{1,0:T(8,128)(2,1)} %get-tuple-element.124.refs_2_), channel_id=1, source_target_pairs={{0,1},{1,0},{2,3},{3,2},{4,5},{5,4},{6,7},{7,6},{8,9},{9,8},{10,11... | collective-permute-start | bytes 4423688 | tf_op jit(solution)/shard_map/ppermute | solution.py:1145
  221.5 11.5 %all-to-all-start.4 = ((f32[32,1,1280]{2,1,0:T(1,128)}), f32[32,1,1280]{2,1,0:T(1,128)S(1)}, u32[]{:S(2)}, u32[]{:S(2)}) async-start(f32[32,1,1280]{2,1,0:T(1,128)} %get-tuple-element.118), calls=%async_computation.4 | async-start | bytes 327680 | tf_op jit(solution)/shard_map/all_to_all | solution.py:1148
  224.6 16.3 %collective-permute-start.27 = (bf16[1152,384]{1,0:T(8,128)(2,1)}, bf16[1152,384]{1,0:T(8,128)(2,1)S(1)}, u32[]{:S(2)}, u32[]{:S(2)}) collective-permute-start(bf16[1152,384]{1,0:T(8,128)(2,1)} %get-tuple-element.123), channel_id=1, source_target_pairs={{0,1},{1,0},{2,3},{3,2},{4,5},{5,4},{6,7},{7,6},{8,9},{9,8},{10,11... | collective-permute-start | bytes 2654216 | tf_op jit(solution)/shard_map/ppermute | solution.py:1145
  240.3 16.4 %collective-permute-start.25 = (bf16[1152,384]{1,0:T(8,128)(2,1)}, bf16[1152,384]{1,0:T(8,128)(2,1)S(1)}, u32[]{:S(2)}, u32[]{:S(2)}) collective-permute-start(bf16[1152,384]{1,0:T(8,128)(2,1)} %get-tuple-element.120), channel_id=1, source_target_pairs={{0,1},{1,0},{2,3},{3,2},{4,5},{5,4},{6,7},{7,6},{8,9},{9,8},{10,11... | collective-permute-start | bytes 2654216 | tf_op jit(solution)/shard_map/ppermute | solution.py:1145
  255.3 18.7 %collective-permute-start.32 = (bf16[23,80,128]{2,1,0:T(8,128)(2,1)}, bf16[23,80,128]{2,1,0:T(8,128)(2,1)S(1)}, u32[]{:S(2)}, u32[]{:S(2)}) collective-permute-start(bf16[23,80,128]{2,1,0:T(8,128)(2,1)} %get-tuple-element.136), channel_id=1, source_target_pairs={{0,16},{8,24},{16,0},{24,8},{1,17},{9,25},{17,1},{25,9},{2,18},{10... | collective-permute-start | bytes 1413128 | tf_op jit(solution)/shard_map/ppermute | solution.py:1142
  255.9 18.1 %collective-permute-start.31 = (bf16[22,80,128]{2,1,0:T(8,128)(2,1)}, bf16[22,80,128]{2,1,0:T(8,128)(2,1)S(1)}, u32[]{:S(2)}, u32[]{:S(2)}) collective-permute-start(bf16[22,80,128]{2,1,0:T(8,128)(2,1)} %get-tuple-element.135), channel_id=1, source_target_pairs={{0,8},{8,0},{16,24},{24,16},{1,9},{9,1},{17,25},{25,17},{2,10},{10... | collective-permute-start | bytes 1351688 | tf_op jit(solution)/shard_map/ppermute | solution.py:1142
  271.1 38.1 %collective-permute-start.30 = (bf16[23,80,128]{2,1,0:T(8,128)(2,1)}, bf16[23,80,128]{2,1,0:T(8,128)(2,1)S(1)}, u32[]{:S(2)}, u32[]{:S(2)}) collective-permute-start(bf16[23,80,128]{2,1,0:T(8,128)(2,1)} %get-tuple-element.131), channel_id=1, source_target_pairs={{0,16},{8,24},{16,0},{24,8},{1,17},{9,25},{17,1},{25,9},{2,18},{10... | collective-permute-start | bytes 1413128 | tf_op jit(solution)/shard_map/ppermute | solution.py:1142
  272.5 28.4 %collective-permute-start.29 = (bf16[22,80,128]{2,1,0:T(8,128)(2,1)}, bf16[22,80,128]{2,1,0:T(8,128)(2,1)S(1)}, u32[]{:S(2)}, u32[]{:S(2)}) collective-permute-start(bf16[22,80,128]{2,1,0:T(8,128)(2,1)} %get-tuple-element.130), channel_id=1, source_target_pairs={{0,8},{8,0},{16,24},{24,16},{1,9},{9,1},{17,25},{25,17},{2,10},{10... | collective-permute-start | bytes 1351688 | tf_op jit(solution)/shard_map/ppermute | solution.py:1142
  277.7 37.0 %collective-permute-start.39 = (bf16[45,80,128]{2,1,0:T(8,128)(2,1)}, bf16[45,80,128]{2,1,0:T(8,128)(2,1)S(1)}, u32[]{:S(2)}, u32[]{:S(2)}) collective-permute-start(bf16[45,80,128]{2,1,0:T(8,128)(2,1)} %get-tuple-element.137.refs_16_), channel_id=1, source_target_pairs={{0,8},{8,0},{16,24},{24,16},{1,9},{9,1},{17,25},{25,17},{2,10},{10... | collective-permute-start | bytes 2764808 | tf_op jit(solution)/shard_map/ppermute | solution.py:1142
  278.3 36.4 %collective-permute-start.40 = (bf16[45,80,128]{2,1,0:T(8,128)(2,1)}, bf16[45,80,128]{2,1,0:T(8,128)(2,1)}, u32[]{:S(2)}, u32[]{:S(2)}) collective-permute-start(bf16[45,80,128]{2,1,0:T(8,128)(2,1)} %get-tuple-element.153), channel_id=1, source_target_pairs={{0,16},{8,24},{16,0},{24,8},{1,17},{9,25},{17,1},{25,9},{2,18},{10... | collective-permute-start | bytes 2764808 | tf_op jit(solution)/shard_map/ppermute | solution.py:1142
  297.7 11.6 %all-to-all-start.5 = ((f32[32,1,1280]{2,1,0:T(1,128)}), f32[32,1,1280]{2,1,0:T(1,128)S(1)}, u32[]{:S(2)}, u32[]{:S(2)}) async-start(f32[32,1,1280]{2,1,0:T(1,128)} %get-tuple-element.138), calls=%async_computation.5 | async-start | bytes 327680 | tf_op jit(solution)/shard_map/all_to_all | solution.py:1148
  312.9 23.2 %collective-permute-start.33 = (bf16[45,80,128]{2,1,0:T(8,128)(2,1)}, bf16[45,80,128]{2,1,0:T(8,128)(2,1)S(1)}, u32[]{:S(2)}, u32[]{:S(2)}) collective-permute-start(bf16[45,80,128]{2,1,0:T(8,128)(2,1)} %get-tuple-element.139), channel_id=1, source_target_pairs={{0,8},{8,0},{16,24},{24,16},{1,9},{9,1},{17,25},{25,17},{2,10},{10... | collective-permute-start | bytes 2764808 | tf_op jit(solution)/shard_map/ppermute | solution.py:1142
  314.0 22.2 %collective-permute-start.34 = (bf16[45,80,128]{2,1,0:T(8,128)(2,1)}, bf16[45,80,128]{2,1,0:T(8,128)(2,1)S(1)}, u32[]{:S(2)}, u32[]{:S(2)}) collective-permute-start(bf16[45,80,128]{2,1,0:T(8,128)(2,1)} %get-tuple-element.140), channel_id=1, source_target_pairs={{0,16},{8,24},{16,0},{24,8},{1,17},{9,25},{17,1},{25,9},{2,18},{10... | collective-permute-start | bytes 2764808 | tf_op jit(solution)/shard_map/ppermute | solution.py:1142
  318.4 24.9 %collective-permute-start.41 = (bf16[45,80,128]{2,1,0:T(8,128)(2,1)}, bf16[45,80,128]{2,1,0:T(8,128)(2,1)S(1)}, u32[]{:S(2)}, u32[]{:S(2)}) collective-permute-start(bf16[45,80,128]{2,1,0:T(8,128)(2,1)} %shard_map.436.refs_0_), channel_id=1, source_target_pairs={{0,2},{1,3},{6,4},{7,5},{8,10},{9,11},{14,12},{15,13},{16,18},{17,... | collective-permute-start | bytes 2764808 | tf_op jit(solution)/shard_map/ppermute | solution.py:1404
  334.2 17.6 %collective-permute-start.43 = (bf16[4,160,384]{2,1,0:T(8,128)(2,1)}, bf16[4,160,384]{2,1,0:T(8,128)(2,1)}, u32[]{:S(2)}, u32[]{:S(2)}) collective-permute-start(bf16[4,160,384]{2,1,0:T(8,128)(2,1)} %get-tuple-element.154), channel_id=1, source_target_pairs={{0,1},{1,0},{2,3},{3,2},{4,5},{5,4},{6,7},{7,6},{8,9},{9,8},{10,11... | collective-permute-start | bytes 1474568 | tf_op jit(solution)/shard_map/ppermute | solution.py:1145
  340.1 15.6 %collective-permute-start.35 = (bf16[22,80,128]{2,1,0:T(8,128)(2,1)}, bf16[22,80,128]{2,1,0:T(8,128)(2,1)}, u32[]{:S(2)}, u32[]{:S(2)}) collective-permute-start(bf16[22,80,128]{2,1,0:T(8,128)(2,1)} %get-tuple-element.151), channel_id=1, source_target_pairs={{0,2},{1,3},{6,4},{7,5},{8,10},{9,11},{14,12},{15,13},{16,18},{17,... | collective-permute-start | bytes 1351688 | tf_op jit(solution)/shard_map/ppermute | solution.py:1404
  346.6 17.4 %collective-permute-start.42 = (bf16[45,80,128]{2,1,0:T(8,128)(2,1)}, bf16[45,80,128]{2,1,0:T(8,128)(2,1)S(1)}, u32[]{:S(2)}, u32[]{:S(2)}) collective-permute-start(bf16[45,80,128]{2,1,0:T(8,128)(2,1)} %shard_map.437), channel_id=1, source_target_pairs={{2,4},{3,5},{4,2},{5,3},{10,12},{11,13},{12,10},{13,11},{18,20},{1... | collective-permute-start | bytes 2764808 | tf_op jit(solution)/shard_map/ppermute | solution.py:1411
  348.8 13.4 %collective-permute-start.37 = (bf16[23,80,128]{2,1,0:T(8,128)(2,1)}, bf16[23,80,128]{2,1,0:T(8,128)(2,1)S(1)}, u32[]{:S(2)}, u32[]{:S(2)}) collective-permute-start(bf16[23,80,128]{2,1,0:T(8,128)(2,1)} %get-tuple-element.152), channel_id=1, source_target_pairs={{0,2},{1,3},{6,4},{7,5},{8,10},{9,11},{14,12},{15,13},{16,18},{17,... | collective-permute-start | bytes 1413128 | tf_op jit(solution)/shard_map/ppermute | solution.py:1404
  353.0 15.0 %collective-permute-start.44 = (bf16[160,384]{1,0:T(8,128)(2,1)S(1)}, bf16[160,384]{1,0:T(8,128)(2,1)S(1)}, u32[]{:S(2)}, u32[]{:S(2)}) collective-permute-start(bf16[160,384]{1,0:T(8,128)(2,1)S(1)} %get-tuple-element.185), channel_id=1, source_target_pairs={{0,8},{8,0},{16,24},{24,16},{1,9},{9,1},{17,25},{25,17},{2,10},{10... | collective-permute-start | bytes 368648 | tf_op jit(solution)/shard_map/ppermute | solution.py:1142
  354.3 14.9 %collective-permute-start.45 = (bf16[160,384]{1,0:T(8,128)(2,1)S(1)}, bf16[160,384]{1,0:T(8,128)(2,1)S(1)}, u32[]{:S(2)}, u32[]{:S(2)}) collective-permute-start(bf16[160,384]{1,0:T(8,128)(2,1)S(1)} %get-tuple-element.187), channel_id=1, source_target_pairs={{0,16},{8,24},{16,0},{24,8},{1,17},{9,25},{17,1},{25,9},{2,18},{10... | collective-permute-start | bytes 368648 | tf_op jit(solution)/shard_map/ppermute | solution.py:1142
  355.7 13.5 %collective-permute-start.46 = (bf16[160,384]{1,0:T(8,128)(2,1)S(1)}, bf16[160,384]{1,0:T(8,128)(2,1)S(1)}, u32[]{:S(2)}, u32[]{:S(2)}) collective-permute-start(bf16[160,384]{1,0:T(8,128)(2,1)S(1)} %get-tuple-element.186), channel_id=1, source_target_pairs={{0,24},{8,16},{16,8},{24,0},{1,25},{9,17},{17,9},{25,1},{2,26},{10... | collective-permute-start | bytes 368648 | tf_op jit(solution)/shard_map/ppermute | solution.py:1142
  362.2 3.6 collective-permute-start.36
  364.0 21.1 %collective-permute-start.38 = (bf16[23,80,128]{2,1,0:T(8,128)(2,1)S(1)}, bf16[23,80,128]{2,1,0:T(8,128)(2,1)S(1)}, u32[]{:S(2)}, u32[]{:S(2)}) collective-permute-start(bf16[23,80,128]{2,1,0:T(8,128)(2,1)S(1)} %add_convert_fusion.2), channel_id=1, source_target_pairs={{2,4},{3,5},{4,2},{5,3},{10,12},{11,13},{12,10},{13,11},{18,20},{1... | collective-permute-start | bytes 1413128 | tf_op jit(solution)/shard_map/ppermute | solution.py:1411
  365.8 51.6 %collective-permute-start.55 = (bf16[45,80,128]{2,1,0:T(8,128)(2,1)S(1)}, bf16[45,80,128]{2,1,0:T(8,128)(2,1)S(1)}, u32[]{:S(2)}, u32[]{:S(2)}) collective-permute-start(bf16[45,80,128]{2,1,0:T(8,128)(2,1)S(1)} %get-tuple-element.180), channel_id=1, source_target_pairs={{2,0},{3,1},{4,6},{5,7},{10,8},{11,9},{12,14},{13,15},{18,16},{19,... | collective-permute-start | bytes 2764808 | tf_op jit(solution)/shard_map/ppermute | solution.py:1413
  367.9 48.2 %collective-permute-start.51 = (bf16[22,80,128]{2,1,0:T(8,128)(2,1)S(1)}, bf16[22,80,128]{2,1,0:T(8,128)(2,1)S(1)}, u32[]{:S(2)}, u32[]{:S(2)}) collective-permute-start(bf16[22,80,128]{2,1,0:T(8,128)(2,1)S(1)} %get-tuple-element.184), channel_id=1, source_target_pairs={{2,0},{3,1},{4,6},{5,7},{10,8},{11,9},{12,14},{13,15},{18,16},{19,... | collective-permute-start | bytes 1351688 | tf_op jit(solution)/shard_map/ppermute | solution.py:1413
  370.2 56.8 %collective-permute-start.47 = (bf16[160,384]{1,0:T(8,128)(2,1)S(1)}, bf16[160,384]{1,0:T(8,128)(2,1)S(1)}, u32[]{:S(2)}, u32[]{:S(2)}) collective-permute-start(bf16[160,384]{1,0:T(8,128)(2,1)S(1)} %fusion.2), channel_id=1, source_target_pairs={{0,2},{1,3},{2,0},{3,1},{4,6},{5,7},{6,4},{7,5},{8,10},{9,11},{10,... | collective-permute-start | bytes 368648 | tf_op jit(solution)/shard_map/ppermute | solution.py:1145
  385.1 42.5 %collective-permute-start.48 = (bf16[160,384]{1,0:T(8,128)(2,1)S(1)}, bf16[160,384]{1,0:T(8,128)(2,1)S(1)}, u32[]{:S(2)}, u32[]{:S(2)}) collective-permute-start(bf16[160,384]{1,0:T(8,128)(2,1)S(1)} %fusion.2), channel_id=1, source_target_pairs={{0,4},{1,5},{2,6},{3,7},{4,0},{5,1},{6,2},{7,3},{8,12},{9,13},{10,... | collective-permute-start | bytes 368648 | tf_op jit(solution)/shard_map/ppermute | solution.py:1145
  385.1 42.5 %collective-permute-start.49 = (bf16[160,384]{1,0:T(8,128)(2,1)S(1)}, bf16[160,384]{1,0:T(8,128)(2,1)S(1)}, u32[]{:S(2)}, u32[]{:S(2)}) collective-permute-start(bf16[160,384]{1,0:T(8,128)(2,1)S(1)} %fusion.2), channel_id=1, source_target_pairs={{0,6},{1,7},{2,4},{3,5},{4,2},{5,3},{6,0},{7,1},{8,14},{9,15},{10,... | collective-permute-start | bytes 368648 | tf_op jit(solution)/shard_map/ppermute | solution.py:1145
  416.1 10.9 %collective-permute-start.53 = (bf16[23,80,128]{2,1,0:T(8,128)(2,1)S(1)}, bf16[23,80,128]{2,1,0:T(8,128)(2,1)S(1)}, u32[]{:S(2)}, u32[]{:S(2)}) collective-permute-start(bf16[23,80,128]{2,1,0:T(8,128)(2,1)S(1)} %get-tuple-element.182), channel_id=1, source_target_pairs={{2,0},{3,1},{4,6},{5,7},{10,8},{11,9},{12,14},{13,15},{18,16},{19,... | collective-permute-start | bytes 1413128 | tf_op jit(solution)/shard_map/ppermute | solution.py:1413
  417.4 30.7 %copy-start.4 = (bf16[22,80,128]{2,1,0:T(8,128)(2,1)}, bf16[22,80,128]{2,1,0:T(8,128)(2,1)S(1)}, u32[]{:S(2)}) copy-start(bf16[22,80,128]{2,1,0:T(8,128)(2,1)S(1)} %broadcast_select_fusion.2.refs_5_) | copy-start | bytes 1351684
  417.5 30.7 %collective-permute-start.52 = (bf16[22,80,128]{2,1,0:T(8,128)(2,1)S(1)}, bf16[22,80,128]{2,1,0:T(8,128)(2,1)}, u32[]{:S(2)}, u32[]{:S(2)}) collective-permute-start(bf16[22,80,128]{2,1,0:T(8,128)(2,1)S(1)} %broadcast_select_fusion.2.refs_5_), channel_id=1, source_target_pairs={{0,1},{1,0},{2,3},{3,2},{4,5},{5,4},{6,7},{7,6},{8,9},{9,8},{10,11... | collective-permute-start | bytes 1351688 | tf_op jit(solution)/shard_map/ppermute | solution.py:1145
  417.6 30.6 %copy-start.2 = (bf16[45,80,128]{2,1,0:T(8,128)(2,1)}, bf16[45,80,128]{2,1,0:T(8,128)(2,1)S(1)}, u32[]{:S(2)}) copy-start(bf16[45,80,128]{2,1,0:T(8,128)(2,1)S(1)} %broadcast_select_fusion.refs_9_) | copy-start | bytes 2764804
  427.0 21.3 %collective-permute-start.56 = (bf16[45,80,128]{2,1,0:T(8,128)(2,1)S(1)}, bf16[45,80,128]{2,1,0:T(8,128)(2,1)S(1)}, u32[]{:S(2)}, u32[]{:S(2)}) collective-permute-start(bf16[45,80,128]{2,1,0:T(8,128)(2,1)S(1)} %broadcast_select_fusion.refs_9_), channel_id=1, source_target_pairs={{0,1},{1,0},{2,3},{3,2},{4,5},{5,4},{6,7},{7,6},{8,9},{9,8},{10,11... | collective-permute-start | bytes 2764808 | tf_op jit(solution)/shard_map/ppermute | solution.py:1145
  427.1 21.2 %collective-permute-start.54 = (bf16[23,80,128]{2,1,0:T(8,128)(2,1)S(1)}, bf16[23,80,128]{2,1,0:T(8,128)(2,1)S(1)}, u32[]{:S(2)}, u32[]{:S(2)}) collective-permute-start(bf16[23,80,128]{2,1,0:T(8,128)(2,1)S(1)} %broadcast_select_fusion.1.refs_7_), channel_id=1, source_target_pairs={{0,1},{1,0},{2,3},{3,2},{4,5},{5,4},{6,7},{7,6},{8,9},{9,8},{10,11... | collective-permute-start | bytes 1413128 | tf_op jit(solution)/shard_map/ppermute | solution.py:1145
  427.7 10.3 %collective-permute-start.50 = (bf16[160,384]{1,0:T(8,128)(2,1)S(1)}, bf16[160,384]{1,0:T(8,128)(2,1)S(1)}, u32[]{:S(2)}, u32[]{:S(2)}) collective-permute-start(bf16[160,384]{1,0:T(8,128)(2,1)S(1)} %add_convert_fusion.5.refs_2_), channel_id=1, source_target_pairs={{0,1},{1,0},{2,3},{3,2},{4,5},{5,4},{6,7},{7,6},{8,9},{9,8},{10,11... | collective-permute-start | bytes 368648 | tf_op jit(solution)/shard_map/ppermute | solution.py:1145
  433.6 10.8 %all-to-all-start.6 = ((f32[32,1,128]{2,1,0:T(1,128)}), f32[32,1,128]{2,1,0:T(1,128)S(1)}, u32[]{:S(2)}, u32[]{:S(2)}) async-start(f32[32,1,128]{2,1,0:T(1,128)} %broadcast_in_dim.3), calls=%async_computation.6 | async-start | bytes 32768 | tf_op jit(solution)/shard_map/all_to_all | solution.py:1148
  (47 other events, 247.9 us)

commit v3 on v2

--- a/solution.py
+++ b/solution.py
@@ -73,7 +73,7 @@
         cost_estimate=pl.CostEstimate(
             flops=int(micros * 35 * 10**7), bytes_accessed=1, transcendentals=0
         ),
-        compiler_params=pltpu.CompilerParams(vmem_limit_bytes=60 * MIB),
+        compiler_params=pltpu.CompilerParams(vmem_limit_bytes=63 * MIB),
     )
 
 
@@ -128,7 +128,7 @@
         out[:, colour * PLANE : (colour + 1) * PLANE] = taken.astype(half)
 
 
-def pack_kernel(proj_c, head, norm, out):
+def pack_lanes(proj_c, head, norm):
     place = hot(iota((C2, WIDE), 0) == iota((C2, WIDE), 1))
     total = dot(proj_c[...].astype(half), place)
     classes = head.shape[0]
@@ -140,11 +140,14 @@
         rest = rest - piece.astype(full)
         place = hot(iota((6, WIDE), 0) + (C2 + 16 + 8 * part) == iota((6, WIDE), 1))
         total = total + dot(piece, place, TN)
-    out[...] = total.astype(half)
-
-
-def cast_kernel(layer, ids, weights, out, wide, narrow, in_sems, out_sems):
+    return total
+
+
+def cast_kernel(layer, *refs):
+    ids, weights = refs[0:2]
+    out, wide, narrow, in_sems, out_sems = refs[-5:]
     rows = out.shape[0]
+    cols = wide.shape[1]
     parts = rows // 16
     inputs = []
     for part in range(parts):
@@ -156,33 +159,54 @@
                 in_sems.at[part],
             )
         )
+    if layer == 0:
+        total = pack_lanes(*refs[2:5])
+        mine = jnp.where(ids[2] == 0, total[0:rows], total[rows : 2 * rows])
+        narrow[:, cols : cols + WIDE] = mine.astype(half)
     outputs = []
     for part in range(parts):
         here = slice(part * 16, part * 16 + 16)
         inputs[part].wait()
-        narrow[here] = wide[here].astype(half)
+        narrow[here, 0:cols] = wide[here].astype(half)
         outputs.append(fetch(narrow.at[here], out.at[here], out_sems.at[part]))
     for copy in outputs:
         copy.wait()
 
 
-def cast_half(ids, conv_w, layer, after):
+def cast_half(ids, conv_w, layer, packed, after):
     rows = conv_w.shape[1] // 2
     cols = conv_w.shape[2]
+    total = cols + WIDE if layer == 0 else cols
     (result,) = call(
         functools.partial(cast_kernel, layer),
-        [SMEM, ANY],
-        [(shape((rows, cols), half), ANY)],
+        [SMEM, ANY] + [VMEM] * len(packed),
+        [(shape((rows, total), half), ANY)],
         [
             pltpu.VMEM((rows, cols), full),
-            pltpu.VMEM((rows, cols), half),
+            pltpu.VMEM((rows, total), half),
             pltpu.SemaphoreType.DMA((rows // 16,)),
             pltpu.SemaphoreType.DMA((rows // 16,)),
         ],
         3,
         len(after),
-    )(ids, conv_w, *after)
+    )(ids, conv_w, *packed, *after)
     return result
+
+
+def hold_kernel(*refs):
+    pass
+
+
+def hold(value, after):
+    return pl.pallas_call(
+        hold_kernel,
+        out_shape=shape(value.shape, value.dtype),
+        in_specs=[ANY] * 2,
+        out_specs=ANY,
+        input_output_aliases={0: 0},
+        compiler_params=pltpu.CompilerParams(has_side_effects=True),
+        cost_estimate=pl.CostEstimate(flops=1, bytes_accessed=1, transcendentals=0),
+    )(value, after)
 
 
 def merge_spans(plan):
@@ -255,6 +279,19 @@
     )(*values, *after)
 
 
+def pick_kernel(reach, ids, value, arrived, out, sem):
+    digit = ids[3] // reach % 4
+    outer = (digit == 0) | (digit == 3)
+
+    @pl.when(outer)
+    def _():
+        fetch(arrived, out, sem).wait()
+
+    @pl.when(jnp.logical_not(outer))
+    def _():
+        fetch(value, out, sem).wait()
+
+
 def cut_kernel(places, *refs):
     count = len(places)
     outs = refs[count : 2 * count]
@@ -311,34 +348,19 @@
     rows = per * 64
     band = per * 8
     ids = refs[0]
-    images, far_images = refs[1:3]
-    packs = refs[3 : 3 + split]
-    stem_w, proj_a, proj_b = refs[3 + split : 6 + split]
+    images, far_images, stem_w, proj_a, proj_b = refs[1:6]
     (
         patches,
         stem_out,
         mid_one,
         mid_two,
         act_three,
-        base,
-        stats,
-        norm_rows,
-        head_all,
-        proj_t,
         facts,
-        gathered,
         tiles,
         loose,
         stem_pad,
         proj_b_pad,
-        totals,
-        sems,
-    ) = refs[6 + split :]
-    quarter = gathered.shape[0] // split
-    copies = []
-    for turn in range(split):
-        spot = pl.multiple_of((ids[0] ^ turn) * quarter, 16)
-        copies.append(fetch(packs[turn], gathered.at[pl.ds(spot, quarter)], sems.at[turn]))
+    ) = refs[6:]
     slot = iota((per, count), 0)
     column = iota((per, count), 1)
     own = dot(hot(column == slot + ids[0] * per), images[0])
@@ -386,11 +408,35 @@
     stem_pad[:, 0:27] = stem_w[...]
     proj_b_pad[...] = jnp.zeros(proj_b_pad.shape, half)
     proj_b_pad[:, 0:C2] = proj_b[...].astype(half)
-    for copy in copies:
+    stem_half = stem_pad[...].astype(half)
+    proj_a_half = proj_a[...].astype(half)
+    tall_chunk = 2 * band
+
+    def step(index, carry):
+        at = pl.ds(pl.multiple_of(index * tall_chunk, 16), tall_chunk)
+        stem = dot(patches[at], stem_half, NT)
+        stem_out[at] = stem
+        one = dot(gelu_pair(stem)[0].astype(half), proj_a_half)
+        mid_one[at] = one
+        two = dot(gelu_pair(one)[0].astype(half), proj_b_pad[...])
+        mid_two[at] = two
+        act_three[at] = gelu_pair(two)[0].astype(half)
+        return carry
+
+    lax.fori_loop(0, rows // tall_chunk, step, 0)
+
+
+def base_kernel(*refs):
+    ids, act_three = refs[0:2]
+    pieces = refs[2:12]
+    base, stats, norm_rows, head_all, proj_t, gathered, held, totals, sems, out_sems = refs[12:]
+    rows = act_three.shape[0]
+    lanes = pl.ds(pieces[0].shape[1] - WIDE, WIDE)
+    for copy in start_weights(ids, pieces, gathered, sems, lanes):
         copy.wait()
-    lanes = iota((1, WIDE), 1)
+    column = iota((1, WIDE), 1)
     packed = gathered[...]
-    proj_t[...] = jnp.where(lanes < C2, packed.astype(full), 0.0).astype(half)
+    proj_t[...] = jnp.where(column < C2, packed.astype(full), 0.0).astype(half)
     place = hot(iota((WIDE, 16), 0) == iota((WIDE, 16), 1) + C2)
     head_all[...] = dot(packed, place).astype(half)
     column = iota((8, WIDE), 1)
@@ -400,29 +446,18 @@
         for part in range(3)
     ]
     norm_rows[...] = pieces[0] + (pieces[1] + pieces[2])
-    stem_half = stem_pad[...].astype(half)
-    proj_a_half = proj_a[...].astype(half)
     totals[...] = jnp.zeros(totals.shape, full)
-    tall_chunk = 2 * band
-
-    def step(index, carry):
-        at = pl.ds(pl.multiple_of(index * tall_chunk, 16), tall_chunk)
-        stem = dot(patches[at], stem_half, NT)
-        stem_out[at] = stem
-        one = dot(gelu_pair(stem)[0].astype(half), proj_a_half)
-        mid_one[at] = one
-        two = dot(gelu_pair(one)[0].astype(half), proj_b_pad[...])
-        mid_two[at] = two
-        three = gelu_pair(two)[0].astype(half)
-        act_three[at] = three
-        result = dot(three, proj_t[...], NT)
-        base[at] = result
+    outputs = []
+    for part in range(QUARTERS):
+        at = quarter_rows(rows, part)
+        result = dot(act_three[at], proj_t[...], NT)
+        held[at] = result
+        outputs.append(fetch(held.at[at], base.at[at], out_sems.at[part]))
         totals[0:1] += jnp.sum(result, axis=0, keepdims=True)
         totals[1:2] += jnp.sum(result * result, axis=0, keepdims=True)
-        return carry
-
-    lax.fori_loop(0, rows // tall_chunk, step, 0)
     spread_stats(stats, [totals[0:1], totals[1:2]])
+    for copy in outputs:
+        copy.wait()
 
 
 def spread_stats(out, parts):
@@ -452,7 +487,7 @@
     return lax.fori_loop(part * step, (part + 1) * step, body, carry)
 
 
-def start_weights(ids, pieces, weights, sems):
+def start_weights(ids, pieces, weights, sems, lanes=pl.ds(0, 9 * C3)):
     rows = pieces[0].shape[0]
     low = pieces[3].shape[0]
     copies = []
@@ -465,7 +500,11 @@
                 spot = spot + low
             spot = pl.multiple_of(spot, 16)
             copies.append(
-                fetch(piece, weights.at[pl.ds(spot, piece.shape[0])], sems.at[5 * side + place])
+                fetch(
+                    piece.at[:, lanes],
+                    weights.at[pl.ds(spot, piece.shape[0])],
+                    sems.at[5 * side + place],
+                )
             )
     return copies
 
@@ -1002,6 +1041,45 @@
         copy.wait()
 
 
+def norm_kernel(sizes, *refs):
+    devices, chips, split = sizes
+    ids, one, two, small, stats_six, stats_five, stats_four, line, local, loss, norm_out = refs
+    digit = ids[3] // (chips // 4) % 4
+    inner = (digit == 1) | (digit == 2)
+
+    def walk(block, total):
+        first = one[block].astype(full)
+        second = two[block].astype(full)
+        return total + (first * first + second * second)
+
+    squares = lax.fori_loop(0, one.shape[0], walk, jnp.zeros(one.shape[1:], full))
+    squares = jnp.sum(jnp.sum(squares, axis=0, keepdims=True), axis=1, keepdims=True)
+    total = jnp.where(inner, squares / (chips // 2), 0.0)
+    tall = small.shape[0] // 2
+    value = small[...].astype(full)
+    row = iota(value.shape, 0)
+    lane = iota(value.shape, 1)
+    share = jnp.where(
+        row < tall,
+        1.0 / chips,
+        jnp.where(lane < C2 + 16, 1.0 / (chips * split), 1.0 / (2 * chips * split)),
+    )
+    value = jnp.where(inner, 2.0 * value * value * share, 0.0)
+    total = total + jnp.sum(jnp.sum(value, axis=0, keepdims=True), axis=1, keepdims=True)
+    norm_out[...] = jnp.zeros(norm_out.shape, full)
+    for place, stats in enumerate((stats_six, stats_five, stats_four)):
+        sums = jnp.sum(stats[...], axis=0)
+        norm_out[2 * place : 2 * place + 1] = sums[:, C3 : 2 * C3]
+        norm_out[2 * place + 1 : 2 * place + 2] = sums[:, 0:C3]
+        if place == 2:
+            loss[...] = sums[:, 2 * C3 : 2 * C3 + 128]
+    value = norm_out[...]
+    local[...] = pltpu.roll(value, C3 - ids[0] * (C3 // split), 1)[0:6, 0 : C3 // split]
+    value = value * value / devices
+    total = total + jnp.sum(jnp.sum(value, axis=0, keepdims=True), axis=1, keepdims=True)
+    line[...] = jnp.broadcast_to(total[None], line.shape)
+
+
 def clip_scale(squares):
     total = jnp.sum(jnp.sum(squares[...], axis=0), axis=1, keepdims=True)
     size = jnp.sqrt(total[:, 0:1] / 128.0)
@@ -1159,81 +1237,76 @@
         corners.T,
         partners.reshape(1, count),
     )
-    (own_pack,) = call(
-        pack_kernel,
-        [VMEM] * 3,
-        [(shape((2 * tall, WIDE), half), VMEM)],
-        [],
-        2,
-        1,
-    )(proj_c.T, head_w.T, norm_p, own_images)
-    packs = [own_pack] + [over_dp(own_pack, turn) for turn in range(1, split)]
     far_images = [own_images] + [over_filt(own_images, 2 * turn) for turn in range(1, chips)]
-    def start_gather(layer, after):
-        own = cast_half(ids, conv_w, layer, after)
+
+    def start_gather(own):
         return [own, over_dp(own, 1), over_dp(own, 2)]
 
     def middle_gather(pieces, after):
         rows = pieces[0].shape[0]
         return cut_rows(pieces[:0:-1], [(0, 48), (48, rows - 48)], after)
 
-    def end_gather(pieces, far):
-        pieces = [*pieces, over_dp(far[0], 1), over_dp(far[1], 2)]
+    def end_gather(pieces, far, after=()):
+        far = [over_dp(far[0], 1), over_dp(far[1], 2)]
+        if after:
+            far = cut_rows(far, [(0, piece.shape[0]) for piece in far], after)
+        pieces = [*pieces, *far]
         return pieces + [over_filt(piece, 1) for piece in pieces]
 
-    pieces = start_gather(0, packs)
+    own_one = cast_half(ids, conv_w, 0, [proj_c.T, head_w.T, norm_p], [own_images])
+    own_two = cast_half(ids, conv_w, 1, [], [own_one])
+    pieces = start_gather(own_one)
     far = middle_gather(pieces, [])
     all_images = stack(
         far_images,
         [(turn, 0, count) for turn in range(chips)],
         (chips, count, 3 * PLANE),
-        pieces[:1],
+        [own_two],
     )
 
     line = shape((devices, 1, 2 * C3))
-    (
-        patches,
-        stem_out,
-        mid_one,
-        mid_two,
-        act_three,
-        base,
-        stats,
-        norm_rows,
-        head_all,
-        proj_t,
-        facts,
-    ) = call(
+    patches, stem_out, mid_one, mid_two, act_three, facts = call(
         functools.partial(front_kernel, (per, count, groups, devices, split)),
-        [SMEM] + [VMEM] * 2 + [ANY] * split + [VMEM] * 3,
+        [SMEM] + [VMEM] * 5,
         [
             (shape((rows, 32), half), VMEM),
             (shape((rows, C0)), VMEM),
             (shape((rows, C1)), VMEM),
             (shape((rows, WIDE)), VMEM),
             (shape((rows, WIDE), half), VMEM),
-            (shape((rows, C3)), VMEM),
+            (shape((per, 128)), VMEM),
+        ],
+        [
+            pltpu.VMEM((per, 32, 128), full),
+            pltpu.VMEM((rows, 32), full),
+            pltpu.VMEM((C0, 32), full),
+            pltpu.VMEM((C1, WIDE), half),
+        ],
+        10,
+        1,
+    )(ids, all_images, over_filt(all_images, 1), stem_w.T, proj_a, proj_b, far[0])
+    kernels = [end_gather(pieces, far, [facts])]
+    base, stats, norm_rows, head_all, proj_t = call(
+        base_kernel,
+        [SMEM, VMEM] + [ANY] * 10,
+        [
+            (shape((rows, C3)), ANY),
             (line, VMEM),
             (shape((8, C3)), VMEM),
             (shape((C3, 16), half), VMEM),
             (shape((C3, WIDE), half), VMEM),
-            (shape((per, 128)), VMEM),
         ],
         [
             pltpu.VMEM((C3, WIDE), half),
-            pltpu.VMEM((per, 32, 128), full),
-            pltpu.VMEM((rows, 32), full),
-            pltpu.VMEM((C0, 32), full),
-            pltpu.VMEM((C1, WIDE), half),
+            pltpu.VMEM((rows, C3), full),
             pltpu.VMEM((8, C3), full),
-            pltpu.SemaphoreType.DMA((split,)),
+            pltpu.SemaphoreType.DMA((10,)),
+            pltpu.SemaphoreType.DMA((QUARTERS,)),
         ],
-        10,
-        1,
-    )(ids, all_images, over_filt(all_images, 1), *packs, stem_w.T, proj_a, proj_b, far[0])
-    kernels = [end_gather(pieces, far)]
+        4,
+    )(ids, act_three, *kernels[0])
     stats_one = exchange(stats)
-    pieces = start_gather(1, [stats_one])
+    pieces = start_gather(hold(own_two, stats_one))
 
     table = pltpu.VMEM((rows, C3), full)
     conv_outs = [
@@ -1259,8 +1332,9 @@
         conv_scratch,
         18,
     )(ids, base, stats_one, norm_rows, *kernels[0])
-    kernels.append(end_gather(pieces, middle_gather(pieces, [stats])))
+    far = middle_gather(pieces, [stats])
     stats_two = exchange(stats)
+    kernels.append(end_gather(pieces, far, [stats_two]))
     far_field_one = over_filt(field_one, 1)
     summed, field_two, slope_two, stats = call(
         functools.partial(conv_kernel, (per, row_total, split), 1),
@@ -1284,7 +1358,6 @@
         7,
     )(summed, stats_three, norm_rows, head_all, facts)
     stats_four = exchange(stats)
-    loss = jnp.sum(stats_four[:, 0, 2 * C3])
 
     wide_half = pltpu.VMEM((rows, WIDE), half)
     picks = pltpu.VMEM((C3, 2 * WIDE), half)
@@ -1353,10 +1426,6 @@
             flat = flat[len(parts) :]
         return result
 
-    def square_sum(value):
-        wide = value.astype(full)
-        return jnp.sum(wide * wide)
-
     def add(values):
         return sum(value.astype(full) for value in values).astype(half)
 
@@ -1384,39 +1453,57 @@
         for size in sizes:
             plan.append((size, [(source, start, 0, size) for source in range(3)]))
             start += size
-        return merge([own, over_dp(near, 1), over_dp(next_near, 2)], plan, after, 2)
-
-    def over_all_chips(value, after=()):
-        result = value
-        reach = 1
+        return merge([own, over_dp(near, 1), over_dp(next_near, 2)], plan, after, 0.1)
+
+    def gated_add(left, right, after):
+        if not after:
+            return add([left, right])
+        size = left.shape[0]
+        return merge([left, right], [(size, [(0, 0, 0, size), (1, 0, 0, size)])], after, 0.1)[0]
+
+    def chip_routes(reach):
+        routes = []
+        for move in ({0: 1, 3: 2}, {1: 2, 2: 1}, {1: 0, 2: 3}):
+            pairs = []
+            for index in range(groups):
+                here = index // 2 // reach % 4
+                if here in move:
+                    pairs.append((index, index + (move[here] - here) * 2 * reach))
+            routes.append(pairs)
+        return routes
+
+    def to_middles(value, reach, after):
+        arrived = lax.ppermute(value, "filt", chip_routes(reach)[0])
+        return gated_add(value, arrived, after)
+
+    def between_middles(value, reach, after):
+        return gated_add(value, lax.ppermute(value, "filt", chip_routes(reach)[1]), after)
+
+    def from_middles(value, reach, after=()):
+        arrived = lax.ppermute(value, "filt", chip_routes(reach)[2])
+        (result,) = call(
+            functools.partial(pick_kernel, reach),
+            [SMEM, ANY, ANY],
+            [(shape(value.shape, half), VMEM)],
+            [pltpu.SemaphoreType.DMA],
+            0.1,
+            len(after),
+        )(ids, value, arrived, *after)
+        return result
+
+    def over_more_chips(value, reach):
         while reach < chips:
-            digit = ids[3] // reach % 4
-            outer = (digit == 0) | (digit == 3)
-            moves = ({0: 1, 3: 2}, {1: 2, 2: 1}, {1: 0, 2: 3})
-            routes = []
-            for move in moves:
-                pairs = []
-                for index in range(groups):
-                    here = index // 2 // reach % 4
-                    if here in move:
-                        pairs.append((index, index + (move[here] - here) * 2 * reach))
-                routes.append(pairs)
-            arrived = lax.ppermute(result, "filt", routes[0])
-            if after:
-                size = result.shape[0]
-                plan = [(size, [(0, 0, 0, size), (1, 0, 0, size)])]
-                (result,) = merge([result, arrived], plan, after, 2)
-            else:
-                result = add([result, arrived])
-            result = add([result, lax.ppermute(result, "filt", routes[1])])
-            squares = jnp.where(outer, 0.0, square_sum(result))
-            arrived = lax.ppermute(result, "filt", routes[2])
-            result = jnp.where(outer, arrived, result)
+            value = from_middles(value, reach // 4)
+            value = to_middles(value, reach, [])
+            value = between_middles(value, reach, [])
             reach *= 4
-        return (result, squares)
+        return value
 
     chunks_two = ((0, 1, 2),)
     chunks_one = ((0, 1, 2),)
+    pairs_two = weight_grad(
+        own_half, far_half, field_two, far_field_two, chunks_two, []
+    )
     grad_one_half, own_half_one, far_half_one = call(
         functools.partial(norm_back_kernel, (row_total, split)),
         [SMEM, ANY, ANY, VMEM, VMEM, VMEM],
@@ -1432,10 +1519,8 @@
             pltpu.SemaphoreType.DMA((3 * QUARTERS,)),
         ],
         6,
-    )(ids, grad_conv_one, conv_one, stats_two, stats_five, norm_rows)
-    pairs_two = weight_grad(
-        own_half, far_half, field_two, far_field_two, chunks_two, [grad_one_half]
-    )
+        1,
+    )(ids, grad_conv_one, conv_one, stats_two, stats_five, norm_rows, pairs_two[0][0])
     pairs_one = weight_grad(
         own_half_one, far_half_one, field_one, far_field_one, chunks_one, [pairs_two[0][0]]
     )
@@ -1447,8 +1532,9 @@
         [pairs_one[0][0], begun_two[1]],
     )
     stats_six = exchange(stats)
-    (part_two,) = end_dp(begun_two, [begun_two[0].shape[0]], [stats_six])
     begun_one = start_dp(pairs_one[0], [stats_six])
+    blocks = begun_one[0].shape[0]
+    (part_two,) = end_dp(begun_two, [blocks], [stats_six])
     small = shape((split, 2 * tall, WIDE), half)
     small_mine, small_other = call(
         functools.partial(trunk_kernel, (per, row_total, split)),
@@ -1466,7 +1552,8 @@
             pltpu.VMEM((C1, WIDE), half),
             pltpu.SemaphoreType.DMA((4 * split,)),
         ],
-        13,
+        0.1,
+        2,
     )(
         ids,
         grad_base,
@@ -1484,43 +1571,45 @@
         proj_a,
         proj_b,
         grad_head,
+        begun_one[1],
+        part_two,
     )
-    blocks = begun_one[0].shape[0]
-    parts_one = end_dp(begun_one, [blocks // 2, blocks - blocks // 2], [small_mine])
-    reduced_two, squares_two = zip(over_all_chips(part_two, [small_mine]))
-    reduced_one, squares_one = zip(*[over_all_chips(part) for part in parts_one])
     crossed = over_filt(small_other, 1)
     pair = [add([small_mine[turn], crossed[turn]]) for turn in range(split)]
     small_sum = add([pair[0]] + [over_dp(pair[turn], turn) for turn in range(1, split)])
-    small_sum = add(
-        [small_sum] + [over_filt(small_sum, 2 * turn) for turn in range(1, chips)]
-    )
-    small_far = over_filt(small_sum, 1)
-
-    norm_sums = []
-    for stats in (stats_six, stats_five, stats_four):
-        sums = jnp.sum(stats[:, 0, :], axis=0)
-        norm_sums += [sums[C3 : 2 * C3], sums[0:C3]]
-    grad_norm_all = jnp.stack(norm_sums)
-    grad_norm_p = lax.dynamic_slice_in_dim(grad_norm_all, spot_d * 2 * tall, 2 * tall, axis=1)
-    squares = (
-        sum(squares_one + squares_two) / (chips // 2)
-        + square_sum(small_sum[0:tall, 0 : C2 + 16]) / chips
-        + square_sum(small_sum[tall:, 0 : C2 + 16]) / (chips * split)
-        + square_sum(small_sum[tall:, C2 + 16 :]) / (2 * chips * split)
-        + jnp.sum(grad_norm_all * grad_norm_all) / devices
-    )
-    squares = exchange(jnp.broadcast_to(squares, (devices, 1, 128)))
+    (part_one,) = end_dp(begun_one, [blocks], [small_mine])
+    half_two = to_middles(part_two, 1, [part_one])
+    half_one = to_middles(part_one, 1, [half_two, small_sum])
+    whole_two = between_middles(half_two, 1, [half_one])
+    whole_two = over_more_chips(whole_two, 4)
+    last = chips // 4
+    small_sum = between_middles(to_middles(small_sum, 1, []), 1, [])
+    small_sum = over_more_chips(small_sum, 4)
+    small_whole = from_middles(small_sum, last)
+
+    reduced_two = from_middles(whole_two, last)
+    whole_one = between_middles(half_one, 1, [reduced_two, small_sum])
+    whole_one = over_more_chips(whole_one, 4)
+    squares, grad_norm_p, loss = call(
+        functools.partial(norm_kernel, (devices, chips, split)),
+        [SMEM] + [VMEM] * 6,
+        [
+            (shape((devices, 1, 128)), VMEM),
+            (shape((6, C3 // split)), VMEM),
+            (shape((1, 128)), VMEM),
+        ],
+        [pltpu.VMEM((8, C3), full)],
+        3,
+        1,
+    )(ids, whole_one, whole_two, small_sum, stats_six, stats_five, stats_four, small_whole)
+    squares = exchange(squares)
+    reduced_one = from_middles(whole_one, last, [squares])
 
     pieces = []
     places = []
-    for owner, reduced in ((0, reduced_one), (1, reduced_two)):
-        start = 0
-        for part in reduced:
-            size = part.shape[0]
-            pieces += [part, over_filt(part, 1)]
-            places += [(owner, start, size, side) for side in range(2)]
-            start += size
+    for owner, value in enumerate((reduced_one, reduced_two)):
+        pieces += [value, over_filt(value, 1)]
+        places += [(owner, 0, blocks, side) for side in range(2)]
     whole_spec = pl.BlockSpec((1, 2 * tall, 1152), lambda layer, line: (layer, 0, line))
     conv_shape = shape(conv_w.shape)
     conv_new = pl.pallas_call(
@@ -1535,7 +1624,7 @@
             pltpu.VMEM((2, 45, 2 * tall, 128), half),
             pltpu.SemaphoreType.DMA((len(pieces),)),
         ],
-        compiler_params=pltpu.CompilerParams(vmem_limit_bytes=60 * MIB),
+        compiler_params=pltpu.CompilerParams(vmem_limit_bytes=63 * MIB),
         cost_estimate=pl.CostEstimate(
             flops=20 * conv_w.size, bytes_accessed=26 * conv_w.size, transcendentals=0
         ),
@@ -1563,7 +1652,7 @@
         [(shape(item.shape), VMEM) for item in flat] + [(shape((1, 128)), VMEM)],
         [],
         3,
-    )(ids, squares, small_sum, small_far, grad_norm_p, *flat)
+    )(ids, squares, small_whole, over_filt(small_whole, 1), grad_norm_p, *flat)
     size = small_new[18][0, 0]
     turned = [
         item.T if index // 3 in (0, 3, 4) else item for index, item in enumerate(small_new[:18])
@@ -1572,7 +1661,7 @@
         *turned[0:12],
         *conv_new,
         *turned[12:18],
-        loss,
+        loss[0, 0],
         size,
     )
 

time: 476 us -> 445 us (0.935)
  waiting for transfers between devices: 130 us -> 93.6 us
  blocking collectives: 23.7 us -> 52.7 us
  Pallas kernels: 195 us -> 218 us
  starting transfers between devices: 84 us -> 66.3 us
  local copies, waits for them, and re-layouts: 20 us -> 3.79 us
  other arithmetic: 11.1 us -> 3.05 us
    all_to_all x2 -> x4, blocking collectives: 23.7 us -> 52.7 us  [exchange(): return lax.all_to_all(stats, ('dp', 'filt'), 0, 0)]
    all_to_all x5 -> x3, waiting for transfers between devices: 38.5 us -> 15 us  [exchange(): return lax.all_to_all(stats, ('dp', 'filt'), 0, 0)]
    ppermute x22 -> x19, waiting for transfers between devices: 42.5 us -> 19.5 us  [over_dp(): return lax.ppermute(value, 'dp', xor_pairs(split, turn))]
    ppermute x26 -> x22, starting transfers between devices: 26.4 us -> 10.3 us  [over_filt(): return lax.ppermute(value, 'filt', xor_pairs(groups, turn))]
    pallas_call x3 -> x8, Pallas kernels: 7.7 us -> 22.9 us  [the longest x3 7.81 us: from_middles(): call(functools.partial(pick_kernel, reach), [SMEM, ANY, ANY], [(shape(val...]
    unnamed x98 -> x20, local copies, waits for them, and re-layouts: 18.7 us -> 3.79 us
    all_to_all x5 -> x3, starting transfers between devices: 19.8 us -> 9.57 us  [exchange(): return lax.all_to_all(stats, ('dp', 'filt'), 0, 0)]
    ppermute x9, starting transfers between devices: 14.4 us -> 24.5 us  [the longest x3 16.6 us: to_middles(): arrived = lax.ppermute(value, 'filt', chip_routes(reach)[0])]
  transfers between devices with their start and end apart: 62 -> 53, of which waited for: 17 -> 20; matrix products, arithmetic and copies ran while one was open for 3% -> 1% of each run, Pallas kernels for 30% -> 35%
where the time goes in v3:
time: 445 us; the launch traced here: 439 us
  Pallas kernels  218 us (49%)
  waiting for transfers between devices  93.6 us (21%)
  starting transfers between devices  66.3 us (15%)
  blocking collectives  52.7 us (12%)
    all_to_all x4, blocking collectives, exchange(): return lax.all_to_all(stats, ('dp', 'filt'), 0, 0)  52.7 us
    pallas_call x2, Pallas kernels, back(): call(functools.partial(back_kernel, (per, row_total, split), layer), ([SM...  40.1 us
    ppermute x3, waiting for transfers between devices, from_middles(): arrived = lax.ppermute(value, 'filt', chip_routes(reach)[2])  33.8 us
    pallas_call x2, Pallas kernels, weight_grad(): call(functools.partial(weight_grad_kernel, (chunks, split, band)), [ANY]...  26.9 us
    ppermute x19, starting transfers between devices, over_dp(): return lax.ppermute(value, 'dp', xor_pairs(split, turn))  22 us
    pallas_call x8, Pallas kernels, merge(): call(functools.partial(merge_kernel, plan, len(values)), [ANY] * len(valu...  20.7 us
    pallas_call x1, Pallas kernels, shards(): pl.pallas_call(functools.partial(conv_update_kernel, (len(pieces), places...  20.1 us
    ppermute x19, waiting for transfers between devices, over_dp(): return lax.ppermute(value, 'dp', xor_pairs(split, turn))  19.5 us
  transfers between devices with their start and end apart: 53, of which 20 were waited for; matrix products, arithmetic and copies ran while one was open for 1% of the time, Pallas kernels for 35%

profile of v3, /device:TPU:0, one launch (start us, length us, event | category | flops | bytes accessed | tf_op | source)
XLA Modules:
  0.0 438.7 jit_solution(3856601049940069234)
XLA Ops:
  0.7 2.7 shard_map.416.refs_5_.refs_0_
  3.4 3.0 collective-permute-start
  6.4 2.6 collective-permute-start.1
  9.6 3.2 shard_map.417.refs_2_.refs_4_.refs_5_
  12.9 1.8 collective-permute-start.4
  16.2 2.9 shard_map.418.refs_4_.refs_0_
  19.1 9.9 %collective-permute-done.1.refs_2_ = bf16[72,1920]{1,0:T(8,128)(2,1)} collective-permute-done((bf16[72,1920]{1,0:T(8,128)(2,1)}, bf16[72,1920]{1,0:T(8,128)(2,1)}, u32[]{:S(2)}, u32[]{:S(2)}) %collective-permute-start.1) | collective-permute-done | bytes 276512 | tf_op jit(solution)/shard_map/ppermute | solution.py:1223
  29.0 2.2 shard_map.419.refs_1_
  31.3 4.9 %collective-permute-done.4.refs_0_.refs_4_.refs_6_.refs_7_ = bf16[80,6144]{1,0:T(8,128)(2,1)} collective-permute-done((bf16[80,6144]{1,0:T(8,128)(2,1)}, bf16[80,6144]{1,0:T(8,128)(2,1)}, u32[]{:S(2)}, u32[]{:S(2)}) %collective-permute-start.4) | collective-permute-done | bytes 983072 | tf_op jit(solution)/shard_map/ppermute | solution.py:1220
  37.4 2.1 shard_map.420
  42.1 6.8 %shard_map.421 = (bf16[1152,32]{1,0:T(8,128)(2,1)}, f32[1152,16]{1,0:T(8,128)}, f32[1152,160]{1,0:T(8,128)}, f32[1152,384]{1,0:T(8,128)}, bf16[1152,384]{1,0:T(8,128)(2,1)}, /*index=5*/f32[18,128]{1,0:T(8,128)}) custom-call(s32[4]{0:T(128)} %pad_add_fusion.refs_0_, bf16[4,72,1920]{2,1,0:T(8,128)(2,1)} %shard_map.419.refs_1_, ...), custom_call_target="tpu_custom_call" | custom-call | flops 3500000000 | bytes 1 | tf_op jit(solution)/shard_map/pallas_call | solution.py:1268
  50.0 3.0 collective-permute-done.6.refs_0_
  53.0 2.1 shard_map.422
  55.8 2.4 collective-permute-done.12.refs_11_.refs_13_.refs_14_
  58.2 5.7 %shard_map.423 = (f32[1152,640]{1,0:T(8,128)}, f32[32,1,1280]{2,1,0:T(1,128)}, f32[8,640]{1,0:T(8,128)}, bf16[640,16]{1,0:T(8,128)(2,1)}, bf16[640,384]{1,0:T(8,128)(2,1)}) custom-call(s32[4]{0:T(128)} %pad_add_fusion.refs_0_, bf16[1152,384]{1,0:T(8,128)(2,1)} %get-tuple-element.106.refs_1_.refs_8_, bf16[80,6144]{1,0:T(8,128)(2,1)} %shard_map.417.refs_2_.refs_4_.refs_5_, ...), custom_call_target="tpu_custom_call" | custom-call | flops 1400000000 | bytes 1 | tf_op jit(solution)/shard_map/pallas_call | solution.py:1289
  63.9 13.7 %all_to_all.35.refs_2_.refs_1_.refs_4_ = f32[32,1,1280]{2,1,0:T(1,128)} all-to-all(f32[32,1,1280]{2,1,0:T(1,128)} %get-tuple-element.112), channel_id=1, replica_groups=mesh['dp'=4,'filt'=8] {'dp','filt'}, dimensions={0} | all-to-all | bytes 327680 | tf_op jit(solution)/shard_map/all_to_all | solution.py:1226
  79.3 18.5 %shard_map.424 = (f32[1152,640]{1,0:T(8,128)}, bf16[1152,640]{1,0:T(8,128)(2,1)}, f32[1152,640]{1,0:T(8,128)}, f32[32,1,1280]{2,1,0:T(1,128)}) custom-call(s32[4]{0:T(128)} %pad_add_fusion.refs_0_, f32[1152,640]{1,0:T(8,128)} %get-tuple-element.111.refs_1_.refs_4_.refs_2_.refs_3_, f32[32,1,1280]{2,1,0:T(1,128)} %all_to_all.35.refs_2_.refs_1_.refs_4_, ...), custom_call_target="tpu_custom_call" | custom-call | flops 6300000256 | bytes 1 | tf_op jit(solution)/shard_map/pallas_call | solution.py:1328
  97.8 3.0 collective-permute-done.13.refs_1_.refs_6_.refs_11_
  100.9 2.1 shard_map.426
  103.0 1.7 collective-permute-start.15
  105.8 13.3 %all_to_all.36.refs_2_.refs_9_.refs_3_ = f32[32,1,1280]{2,1,0:T(1,128)} all-to-all(f32[32,1,1280]{2,1,0:T(1,128)} %get-tuple-element.115.refs_2_), channel_id=1, replica_groups=mesh['dp'=4,'filt'=8] {'dp','filt'}, dimensions={0} | all-to-all | bytes 327680 | tf_op jit(solution)/shard_map/all_to_all | solution.py:1226
  119.1 2.1 shard_map.427
  121.8 2.3 collective-permute-done.21.refs_14_.refs_19_
  124.1 18.6 %shard_map.428 = (f32[1152,640]{1,0:T(8,128)}, bf16[1152,640]{1,0:T(8,128)(2,1)}, f32[1152,640]{1,0:T(8,128)}, f32[32,1,1280]{2,1,0:T(1,128)}) custom-call(s32[4]{0:T(128)} %pad_add_fusion.refs_0_, f32[1152,640]{1,0:T(8,128)} %get-tuple-element.114.refs_1_.refs_7_.refs_2_, f32[32,1,1280]{2,1,0:T(1,128)} %all_to_all.36.refs_2_.refs_9_.refs_3_, ...), custom_call_target="tpu_custom_call" | custom-call | flops 6300000256 | bytes 1 | tf_op jit(solution)/shard_map/pallas_call | solution.py:1339
  142.8 11.9 %all_to_all.37.refs_1_.refs_3_ = f32[32,1,1280]{2,1,0:T(1,128)} all-to-all(f32[32,1,1280]{2,1,0:T(1,128)} %get-tuple-element.121), channel_id=1, replica_groups=mesh['dp'=4,'filt'=8] {'dp','filt'}, dimensions={0} | all-to-all | bytes 327680 | tf_op jit(solution)/shard_map/all_to_all | solution.py:1226
  154.7 6.9 %shard_map.429 = (f32[1152,640]{1,0:T(8,128)}, f32[144,640]{1,0:T(8,128)}, f32[32,1,1408]{2,1,0:T(1,128)}, f32[640,16]{1,0:T(8,128)}) custom-call(f32[1152,640]{1,0:T(8,128)} %get-tuple-element.120.refs_0_.refs_2_, f32[32,1,1280]{2,1,0:T(1,128)} %all_to_all.37.refs_1_.refs_3_, f32[8,640]{1,0:T(8,128)} %get-tuple-element.113.refs_3_.refs_2_.refs_5_.refs_6_, ...), custom_call_target="tpu_custom_call" | custom-call | flops 2449999872 | bytes 1 | tf_op jit(solution)/shard_map/pallas_call | solution.py:1348
  161.7 3.0 all-to-all-start.3
  165.1 8.2 %all-to-all-done.3.refs_4_.refs_6_ = f32[32,1,1408]{2,1,0:T(1,128)S(1)} async-done(((f32[32,1,1408]{2,1,0:T(1,128)}), f32[32,1,1408]{2,1,0:T(1,128)S(1)}, u32[]{:S(2)}, u32[]{:S(2)}) %all-to-all-start.3) | async-done | bytes 180256 | tf_op jit(solution)/shard_map/all_to_all | solution.py:1226
  174.0 21.5 %shard_map.430 = (f32[1152,640]{1,0:T(8,128)}, f32[32,1,1280]{2,1,0:T(1,128)}, bf16[1152,384]{1,0:T(8,128)(2,1)}, bf16[1152,384]{1,0:T(8,128)(2,1)}, f32[1152,640]{1,0:T(8,128)}) custom-call(s32[4]{0:T(128)} %pad_add_fusion.refs_0_, f32[1152,640]{1,0:T(8,128)} %get-tuple-element.123.refs_1_, f32[1152,640]{1,0:T(8,128)} %get-tuple-element.120.refs_0_.refs_2_, ...), custom_call_target="tpu_custom_call" | custom-call | flops 7699999744 | bytes 1 | tf_op jit(solution)/shard_map/pallas_call | solution.py:1368
  196.3 2.8 all-to-all-start.4
  199.1 13.5 %shard_map.431 = (bf16[45,80,128]{2,1,0:T(8,128)(2,1)}, bf16[45,80,128]{2,1,0:T(8,128)(2,1)}, bf16[45,80,128]{2,1,0:T(8,128)(2,1)}, bf16[22,80,128]{2,1,0:T(8,128)(2,1)}, bf16[23,80,128]{2,1,0:T(8,128)(2,1)}) custom-call(bf16[1152,384]{1,0:T(8,128)(2,1)} %get-tuple-element.129.refs_0_, bf16[1152,384]{1,0:T(8,128)(2,1)} %collective-permute-done.22.refs_1_, ...), custom_call_target="tpu_custom_call" | custom-call | flops 4550000128 | bytes 1 | tf_op jit(solution)/shard_map/pallas_call | solution.py:1407
  213.2 6.5 %shard_map.432 = (bf16[1152,640]{1,0:T(8,128)(2,1)}, bf16[1152,384]{1,0:T(8,128)(2,1)}, bf16[1152,384]{1,0:T(8,128)(2,1)}) custom-call(s32[4]{0:T(128)} %pad_add_fusion.refs_0_, f32[1152,640]{1,0:T(8,128)} %get-tuple-element.127.refs_1_, f32[1152,640]{1,0:T(8,128)} %get-tuple-element.114.refs_1_.refs_7_.refs_2_, ...), custom_call_target="tpu_custom_call" | custom-call | flops 2100000000 | bytes 1 | tf_op jit(solution)/shard_map/pallas_call | solution.py:1507
  220.0 1.7 collective-permute-start.29
  224.1 13.5 %shard_map.433 = (bf16[45,80,128]{2,1,0:T(8,128)(2,1)}, bf16[45,80,128]{2,1,0:T(8,128)(2,1)}, bf16[45,80,128]{2,1,0:T(8,128)(2,1)}, bf16[22,80,128]{2,1,0:T(8,128)(2,1)}, bf16[23,80,128]{2,1,0:T(8,128)(2,1)}) custom-call(bf16[1152,384]{1,0:T(8,128)(2,1)} %get-tuple-element.133.refs_0_, bf16[1152,384]{1,0:T(8,128)(2,1)} %copy-done.9, ...), custom_call_target="tpu_custom_call" | custom-call | flops 4550000128 | bytes 1 | tf_op jit(solution)/shard_map/pallas_call | solution.py:1407
  237.6 2.8 shard_map.434
  244.6 18.6 %shard_map.435 = (f32[1152,640]{1,0:T(8,128)}, f32[32,1,1280]{2,1,0:T(1,128)}) custom-call(s32[4]{0:T(128)} %pad_add_fusion.refs_0_, bf16[1152,640]{1,0:T(8,128)(2,1)} %get-tuple-element.141.refs_1_, f32[1152,640]{1,0:T(8,128)} %get-tuple-element.111.refs_1_.refs_4_.refs_2_.refs_3_, f32[1152,640]{1,0:T(8,128)} %get-tuple-element.142.refs_3_, ...), custom_call_target="tpu_custom_call" | custom-call | flops 7699999744 | bytes 1 | tf_op jit(solution)/shard_map/pallas_call | solution.py:1368
  263.2 13.8 %all_to_all.38.refs_4_.refs_3_.refs_5_ = f32[32,1,1280]{2,1,0:T(1,128)} all-to-all(f32[32,1,1280]{2,1,0:T(1,128)} %get-tuple-element.148), channel_id=1, replica_groups=mesh['dp'=4,'filt'=8] {'dp','filt'}, dimensions={0} | all-to-all | bytes 327680 | tf_op jit(solution)/shard_map/all_to_all | solution.py:1226
  277.0 2.8 shard_map.436
  282.5 2.7 shard_map.437.refs_17_.refs_0_
  285.2 3.6 collective-permute-start.35
  288.8 13.0 %shard_map.438 = (bf16[4,160,384]{2,1,0:T(8,128)(2,1)}, bf16[4,160,384]{2,1,0:T(8,128)(2,1)}) custom-call(s32[4]{0:T(128)} %pad_add_fusion.refs_0_, f32[1152,640]{1,0:T(8,128)} %get-tuple-element.151.refs_1_, f32[1152,640]{1,0:T(8,128)} %get-tuple-element.152.refs_2_, f32[1152,640]{1,0:T(8,128)} %get-tuple-element.111.refs_1_.refs_4_.refs_2_.refs_3_, ...), custom_call_target="tpu_custom_call" | custom-call | flops 35000000 | bytes 1 | tf_op jit(solution)/shard_map/pallas_call | solution.py:1539
  303.2 2.8 shard_map.439.refs_2_.refs_0_
  306.0 3.5 collective-permute-start.34
  309.4 2.4 shard_map.440.refs_2_.refs_0_
  311.8 1.6 collective-permute-start.41
  317.1 2.7 collective-permute-done.37
  319.8 2.2 collective-permute-done.38
  322.7 5.5 %collective-permute-done.34.refs_1_ = bf16[45,80,128]{2,1,0:T(8,128)(2,1)} collective-permute-done((bf16[45,80,128]{2,1,0:T(8,128)(2,1)}, bf16[45,80,128]{2,1,0:T(8,128)(2,1)}, u32[]{:S(2)}, u32[]{:S(2)}) %collective-permute-start.34) | collective-permute-done | bytes 921632 | tf_op jit(solution)/shard_map/ppermute | solution.py:1476
  328.1 2.4 shard_map.441.refs_2_.refs_0_
  330.6 2.4 shard_map.442.refs_1_.refs_2_
  335.9 9.5 %collective-permute-start.43 = (bf16[160,384]{1,0:T(8,128)(2,1)}, bf16[160,384]{1,0:T(8,128)(2,1)S(1)}, u32[]{:S(2)}, u32[]{:S(2)}) collective-permute-start(bf16[160,384]{1,0:T(8,128)(2,1)} %fusion.2.refs_3_), channel_id=1, source_target_pairs={{0,2},{1,3},{6,4},{7,5},{8,10},{9,11},{14,12},{15,13},{16,18},{17,... | collective-permute-start | bytes 368648 | tf_op jit(solution)/shard_map/ppermute | solution.py:1476
  345.4 2.7 collective-permute-done.43
  350.5 7.2 %collective-permute-done.42.refs_2_ = bf16[45,80,128]{2,1,0:T(8,128)(2,1)} collective-permute-done((bf16[45,80,128]{2,1,0:T(8,128)(2,1)}, bf16[45,80,128]{2,1,0:T(8,128)(2,1)}, u32[]{:S(2)}, u32[]{:S(2)}) %collective-permute-start.42) | collective-permute-done | bytes 921632 | tf_op jit(solution)/shard_map/ppermute | solution.py:1483
  357.6 2.8 shard_map.443.refs_2_.refs_7_
  360.4 2.4 shard_map.444.refs_1_
  365.6 26.6 %collective-permute-done.45.refs_2_ = bf16[160,384]{1,0:T(8,128)(2,1)} collective-permute-done((bf16[160,384]{1,0:T(8,128)(2,1)}, bf16[160,384]{1,0:T(8,128)(2,1)}, u32[]{:S(2)}, u32[]{:S(2)}) %collective-permute-start.45) | collective-permute-done | bytes 122912 | tf_op jit(solution)/shard_map/ppermute | solution.py:1483
  392.2 2.2 shard_map.445.refs_7_.refs_2_
  394.4 3.2 shard_map.446
  397.6 3.8 all-to-all-start.6
  401.8 6.7 %all-to-all-done.6.refs_1_.refs_3_ = f32[32,1,128]{2,1,0:T(1,128)S(1)} async-done(((f32[32,1,128]{2,1,0:T(1,128)}), f32[32,1,128]{2,1,0:T(1,128)S(1)}, u32[]{:S(2)}, u32[]{:S(2)}) %all-to-all-start.6) | async-done | bytes 16416 | tf_op jit(solution)/shard_map/all_to_all | solution.py:1226
  409.1 2.8 shard_map.448.refs_5_
  412.5 2.5 collective-permute-done.46.refs_3_
  415.0 3.1 shard_map.447
  418.1 20.1 %shard_map.449 = (f32[2,160,5760]{2,1,0:T(8,128)}, f32[2,160,5760]{2,1,0:T(8,128)}, f32[2,160,5760]{2,1,0:T(8,128)}) custom-call(s32[4]{0:T(128)} %pad_add_fusion.refs_0_, f32[32,1,128]{2,1,0:T(1,128)} %copy-done.8, f32[2,160,5760]{2,1,0:T(8,128)} %refs_2_.1, f32[2,160,5760]{2,1,0:T(8,128)} %refs_3_.1, f32[2,160,5760]{2,1,0:T(8,128)} %refs_4_.5, ...), custom_call_target="tpu_custom_call" | custom-call | flops 36864000 | bytes 47923200 | tf_op jit(solution)/shard_map/pallas_call | solution.py:1615
  (105 shorter events, 38.4 us)
Async XLA Ops:
  3.4 15.7 %collective-permute-start = (bf16[72,1920]{1,0:T(8,128)(2,1)}, bf16[72,1920]{1,0:T(8,128)(2,1)}, u32[]{:S(2)}, u32[]{:S(2)}) collective-permute-start(bf16[72,1920]{1,0:T(8,128)(2,1)} %shard_map.416.refs_5_.refs_0_), channel_id=1, source_target_pairs={{0,2},{1,3},{2,0},{3,1},{4,6},{5,7},{6,4},{7,5},{8,10},{9,11},{10,... | collective-permute-start | bytes 829448 | tf_op jit(solution)/shard_map/ppermute | solution.py:1223
  6.4 22.6 %collective-permute-start.1 = (bf16[72,1920]{1,0:T(8,128)(2,1)}, bf16[72,1920]{1,0:T(8,128)(2,1)}, u32[]{:S(2)}, u32[]{:S(2)}) collective-permute-start(bf16[72,1920]{1,0:T(8,128)(2,1)} %shard_map.416.refs_5_.refs_0_), channel_id=1, source_target_pairs={{0,4},{1,5},{2,6},{3,7},{4,0},{5,1},{6,2},{7,3},{8,12},{9,13},{10,... | collective-permute-start | bytes 829448 | tf_op jit(solution)/shard_map/ppermute | solution.py:1223
  9.0 20.0 %collective-permute-start.2 = (bf16[72,1920]{1,0:T(8,128)(2,1)}, bf16[72,1920]{1,0:T(8,128)(2,1)}, u32[]{:S(2)}, u32[]{:S(2)}) collective-permute-start(bf16[72,1920]{1,0:T(8,128)(2,1)} %shard_map.416.refs_5_.refs_0_), channel_id=1, source_target_pairs={{0,6},{1,7},{2,4},{3,5},{4,2},{5,3},{6,0},{7,1},{8,14},{9,15},{10,... | collective-permute-start | bytes 829448 | tf_op jit(solution)/shard_map/ppermute | solution.py:1223
  12.9 23.3 %collective-permute-start.4 = (bf16[80,6144]{1,0:T(8,128)(2,1)}, bf16[80,6144]{1,0:T(8,128)(2,1)}, u32[]{:S(2)}, u32[]{:S(2)}) collective-permute-start(bf16[80,6144]{1,0:T(8,128)(2,1)} %shard_map.417.refs_2_.refs_4_.refs_5_), channel_id=1, source_target_pairs={{0,16},{8,24},{16,0},{24,8},{1,17},{9,25},{17,1},{25,9},{2,18},{10... | collective-permute-start | bytes 2949128 | tf_op jit(solution)/shard_map/ppermute | solution.py:1220
  14.7 22.8 %collective-permute-start.5 = (bf16[80,6144]{1,0:T(8,128)(2,1)}, bf16[80,6144]{1,0:T(8,128)(2,1)}, u32[]{:S(2)}, u32[]{:S(2)}) collective-permute-start(bf16[80,6144]{1,0:T(8,128)(2,1)} %shard_map.417.refs_2_.refs_4_.refs_5_), channel_id=1, source_target_pairs={{0,8},{8,0},{16,24},{24,16},{1,9},{9,1},{17,25},{25,17},{2,10},{10... | collective-permute-start | bytes 2949128 | tf_op jit(solution)/shard_map/ppermute | solution.py:1220
  19.1 22.6 %copy-start = (bf16[80,6144]{1,0:T(8,128)(2,1)S(1)}, bf16[80,6144]{1,0:T(8,128)(2,1)}, u32[]{:S(2)}) copy-start(bf16[80,6144]{1,0:T(8,128)(2,1)} %shard_map.417.refs_2_.refs_4_.refs_5_) | copy-start | bytes 2949124
  31.3 10.9 %collective-permute-start.3 = (bf16[4,72,1920]{2,1,0:T(8,128)(2,1)}, bf16[4,72,1920]{2,1,0:T(8,128)(2,1)}, u32[]{:S(2)}, u32[]{:S(2)}) collective-permute-start(bf16[4,72,1920]{2,1,0:T(8,128)(2,1)} %shard_map.419.refs_1_), channel_id=1, source_target_pairs={{0,1},{1,0},{2,3},{3,2},{4,5},{5,4},{6,7},{7,6},{8,9},{9,8},{10,11... | collective-permute-start | bytes 3317768 | tf_op jit(solution)/shard_map/ppermute | solution.py:1223
  39.6 13.5 %collective-permute-start.6 = (bf16[48,6144]{1,0:T(8,128)(2,1)}, bf16[48,6144]{1,0:T(8,128)(2,1)}, u32[]{:S(2)}, u32[]{:S(2)}) collective-permute-start(bf16[48,6144]{1,0:T(8,128)(2,1)} %get-tuple-element.105.refs_6_), channel_id=1, source_target_pairs={{0,8},{8,0},{16,24},{24,16},{1,9},{9,1},{17,25},{25,17},{2,10},{10... | collective-permute-start | bytes 1769480 | tf_op jit(solution)/shard_map/ppermute | solution.py:1220
  41.1 8.9 %collective-permute-start.7 = (bf16[32,6144]{1,0:T(8,128)(2,1)}, bf16[32,6144]{1,0:T(8,128)(2,1)}, u32[]{:S(2)}, u32[]{:S(2)}) collective-permute-start(bf16[32,6144]{1,0:T(8,128)(2,1)} %get-tuple-element.107), channel_id=1, source_target_pairs={{0,16},{8,24},{16,0},{24,8},{1,17},{9,25},{17,1},{25,9},{2,18},{10... | collective-permute-start | bytes 1179656 | tf_op jit(solution)/shard_map/ppermute | solution.py:1220
  41.6 14.1 %collective-permute-start.8 = (bf16[80,6144]{1,0:T(8,128)(2,1)S(1)}, bf16[80,6144]{1,0:T(8,128)(2,1)}, u32[]{:S(2)}, u32[]{:S(2)}) collective-permute-start(bf16[80,6144]{1,0:T(8,128)(2,1)S(1)} %copy-done), channel_id=1, source_target_pairs={{0,1},{1,0},{2,3},{3,2},{4,5},{5,4},{6,7},{7,6},{8,9},{9,8},{10,11... | collective-permute-start | bytes 2949128 | tf_op jit(solution)/shard_map/ppermute | solution.py:1223
  41.6 16.5 %collective-permute-start.10 = (bf16[80,6144]{1,0:T(8,128)(2,1)}, bf16[80,6144]{1,0:T(8,128)(2,1)}, u32[]{:S(2)}, u32[]{:S(2)}) collective-permute-start(bf16[80,6144]{1,0:T(8,128)(2,1)} %collective-permute-done.4.refs_0_.refs_4_.refs_6_.refs_7_), channel_id=1, source_target_pairs={{0,1},{1,0},{2,3},{3,2},{4,5},{5,4},{6,7},{7,6},{8,9},{9,8},{10,11... | collective-permute-start | bytes 2949128 | tf_op jit(solution)/shard_map/ppermute | solution.py:1223
  42.1 16.0 %collective-permute-start.9 = (bf16[80,6144]{1,0:T(8,128)(2,1)}, bf16[80,6144]{1,0:T(8,128)(2,1)}, u32[]{:S(2)}, u32[]{:S(2)}) collective-permute-start(bf16[80,6144]{1,0:T(8,128)(2,1)} %collective-permute-done.5.refs_1_.refs_3_.refs_5_.refs_6_), channel_id=1, source_target_pairs={{0,1},{1,0},{2,3},{3,2},{4,5},{5,4},{6,7},{7,6},{8,9},{9,8},{10,11... | collective-permute-start | bytes 2949128 | tf_op jit(solution)/shard_map/ppermute | solution.py:1223
  55.2 3.0 collective-permute-start.11
  55.3 2.9 collective-permute-start.12
  77.6 23.2 %collective-permute-start.13 = (bf16[80,5760]{1,0:T(8,128)(2,1)}, bf16[80,5760]{1,0:T(8,128)(2,1)}, u32[]{:S(2)}, u32[]{:S(2)}) collective-permute-start(bf16[80,5760]{1,0:T(8,128)(2,1)} %shard_map.425.refs_5_.refs_10_), channel_id=1, source_target_pairs={{0,8},{8,0},{16,24},{24,16},{1,9},{9,1},{17,25},{25,17},{2,10},{10... | collective-permute-start | bytes 2764808 | tf_op jit(solution)/shard_map/ppermute | solution.py:1220
  78.6 22.4 %collective-permute-start.14 = (bf16[80,5760]{1,0:T(8,128)(2,1)}, bf16[80,5760]{1,0:T(8,128)(2,1)}, u32[]{:S(2)}, u32[]{:S(2)}) collective-permute-start(bf16[80,5760]{1,0:T(8,128)(2,1)} %shard_map.425.refs_5_.refs_10_), channel_id=1, source_target_pairs={{0,16},{8,24},{16,0},{24,8},{1,17},{9,25},{17,1},{25,9},{2,18},{10... | collective-permute-start | bytes 2764808 | tf_op jit(solution)/shard_map/ppermute | solution.py:1220
  79.3 25.9 %copy-start.3 = (bf16[80,5760]{1,0:T(8,128)(2,1)S(1)}, bf16[80,5760]{1,0:T(8,128)(2,1)}, u32[]{:S(2)}) copy-start(bf16[80,5760]{1,0:T(8,128)(2,1)} %shard_map.425.refs_5_.refs_10_) | copy-start | bytes 2764804
  103.0 16.1 %collective-permute-start.15 = (bf16[48,5760]{1,0:T(8,128)(2,1)}, bf16[48,5760]{1,0:T(8,128)(2,1)}, u32[]{:S(2)}, u32[]{:S(2)}) collective-permute-start(bf16[48,5760]{1,0:T(8,128)(2,1)} %get-tuple-element.116), channel_id=1, source_target_pairs={{0,8},{8,0},{16,24},{24,16},{1,9},{9,1},{17,25},{25,17},{2,10},{10... | collective-permute-start | bytes 1658888 | tf_op jit(solution)/shard_map/ppermute | solution.py:1220
  104.7 14.4 %collective-permute-start.16 = (bf16[32,5760]{1,0:T(8,128)(2,1)}, bf16[32,5760]{1,0:T(8,128)(2,1)}, u32[]{:S(2)}, u32[]{:S(2)}) collective-permute-start(bf16[32,5760]{1,0:T(8,128)(2,1)} %get-tuple-element.117), channel_id=1, source_target_pairs={{0,16},{8,24},{16,0},{24,8},{1,17},{9,25},{17,1},{25,9},{2,18},{10... | collective-permute-start | bytes 1105928 | tf_op jit(solution)/shard_map/ppermute | solution.py:1220
  105.2 16.6 %collective-permute-start.17 = (bf16[80,5760]{1,0:T(8,128)(2,1)S(1)}, bf16[80,5760]{1,0:T(8,128)(2,1)}, u32[]{:S(2)}, u32[]{:S(2)}) collective-permute-start(bf16[80,5760]{1,0:T(8,128)(2,1)S(1)} %copy-done.3), channel_id=1, source_target_pairs={{0,1},{1,0},{2,3},{3,2},{4,5},{5,4},{6,7},{7,6},{8,9},{9,8},{10,11... | collective-permute-start | bytes 2764808 | tf_op jit(solution)/shard_map/ppermute | solution.py:1223
  105.2 18.9 %collective-permute-start.18 = (bf16[80,5760]{1,0:T(8,128)(2,1)}, bf16[80,5760]{1,0:T(8,128)(2,1)}, u32[]{:S(2)}, u32[]{:S(2)}) collective-permute-start(bf16[80,5760]{1,0:T(8,128)(2,1)} %collective-permute-done.13.refs_1_.refs_6_.refs_11_), channel_id=1, source_target_pairs={{0,1},{1,0},{2,3},{3,2},{4,5},{5,4},{6,7},{7,6},{8,9},{9,8},{10,11... | collective-permute-start | bytes 2764808 | tf_op jit(solution)/shard_map/ppermute | solution.py:1223
  105.8 18.4 %collective-permute-start.19 = (bf16[80,5760]{1,0:T(8,128)(2,1)}, bf16[80,5760]{1,0:T(8,128)(2,1)}, u32[]{:S(2)}, u32[]{:S(2)}) collective-permute-start(bf16[80,5760]{1,0:T(8,128)(2,1)} %collective-permute-done.14.refs_0_.refs_7_.refs_12_), channel_id=1, source_target_pairs={{0,1},{1,0},{2,3},{3,2},{4,5},{5,4},{6,7},{7,6},{8,9},{9,8},{10,11... | collective-permute-start | bytes 2764808 | tf_op jit(solution)/shard_map/ppermute | solution.py:1223
  121.2 2.9 collective-permute-start.20
  121.4 2.7 collective-permute-start.21
  161.7 11.6 %all-to-all-start.3 = ((f32[32,1,1408]{2,1,0:T(1,128)}), f32[32,1,1408]{2,1,0:T(1,128)S(1)}, u32[]{:S(2)}, u32[]{:S(2)}) async-start(f32[32,1,1408]{2,1,0:T(1,128)} %get-tuple-element.124), calls=%async_computation.3 | async-start | bytes 360448 | tf_op jit(solution)/shard_map/all_to_all | solution.py:1226
  164.7 34.3 %collective-permute-start.23 = (bf16[1152,640]{1,0:T(8,128)(2,1)}, bf16[1152,640]{1,0:T(8,128)(2,1)}, u32[]{:S(2)}, u32[]{:S(2)}) collective-permute-start(bf16[1152,640]{1,0:T(8,128)(2,1)} %get-tuple-element.131.refs_2_), channel_id=1, source_target_pairs={{0,1},{1,0},{2,3},{3,2},{4,5},{5,4},{6,7},{7,6},{8,9},{9,8},{10,11... | collective-permute-start | bytes 4423688 | tf_op jit(solution)/shard_map/ppermute | solution.py:1223
  173.3 0.7 copy-start.6
  195.5 3.6 collective-permute-start.22
  196.2 27.0 %collective-permute-start.25 = (bf16[1152,640]{1,0:T(8,128)(2,1)}, bf16[1152,640]{1,0:T(8,128)(2,1)}, u32[]{:S(2)}, u32[]{:S(2)}) collective-permute-start(bf16[1152,640]{1,0:T(8,128)(2,1)} %get-tuple-element.135.refs_2_), channel_id=1, source_target_pairs={{0,1},{1,0},{2,3},{3,2},{4,5},{5,4},{6,7},{7,6},{8,9},{9,8},{10,11... | collective-permute-start | bytes 4423688 | tf_op jit(solution)/shard_map/ppermute | solution.py:1223
  196.3 16.3 %all-to-all-start.4 = ((f32[32,1,1280]{2,1,0:T(1,128)}), f32[32,1,1280]{2,1,0:T(1,128)S(1)}, u32[]{:S(2)}, u32[]{:S(2)}) async-start(f32[32,1,1280]{2,1,0:T(1,128)} %get-tuple-element.128), calls=%async_computation.4 | async-start | bytes 327680 | tf_op jit(solution)/shard_map/all_to_all | solution.py:1226
  212.5 0.7 copy-start.7
  219.7 3.5 collective-permute-start.24
  220.0 17.6 %collective-permute-start.29 = (bf16[23,80,128]{2,1,0:T(8,128)(2,1)}, bf16[23,80,128]{2,1,0:T(8,128)(2,1)}, u32[]{:S(2)}, u32[]{:S(2)}) collective-permute-start(bf16[23,80,128]{2,1,0:T(8,128)(2,1)} %get-tuple-element.146), channel_id=1, source_target_pairs={{0,16},{8,24},{16,0},{24,8},{1,17},{9,25},{17,1},{25,9},{2,18},{10... | collective-permute-start | bytes 1413128 | tf_op jit(solution)/shard_map/ppermute | solution.py:1220
  221.7 15.9 %collective-permute-start.28 = (bf16[22,80,128]{2,1,0:T(8,128)(2,1)}, bf16[22,80,128]{2,1,0:T(8,128)(2,1)}, u32[]{:S(2)}, u32[]{:S(2)}) collective-permute-start(bf16[22,80,128]{2,1,0:T(8,128)(2,1)} %get-tuple-element.145), channel_id=1, source_target_pairs={{0,8},{8,0},{16,24},{24,16},{1,9},{9,1},{17,25},{25,17},{2,10},{10... | collective-permute-start | bytes 1351688 | tf_op jit(solution)/shard_map/ppermute | solution.py:1220
  223.2 0.9 copy-start.9
  240.5 41.1 %collective-permute-start.32 = (bf16[45,80,128]{2,1,0:T(8,128)(2,1)}, bf16[45,80,128]{2,1,0:T(8,128)(2,1)S(1)}, u32[]{:S(2)}, u32[]{:S(2)}) collective-permute-start(bf16[45,80,128]{2,1,0:T(8,128)(2,1)} %get-tuple-element.147.refs_16_), channel_id=1, source_target_pairs={{0,8},{8,0},{16,24},{24,16},{1,9},{9,1},{17,25},{25,17},{2,10},{10... | collective-permute-start | bytes 2764808 | tf_op jit(solution)/shard_map/ppermute | solution.py:1220
  241.5 40.1 %collective-permute-start.33 = (bf16[45,80,128]{2,1,0:T(8,128)(2,1)}, bf16[45,80,128]{2,1,0:T(8,128)(2,1)}, u32[]{:S(2)}, u32[]{:S(2)}) collective-permute-start(bf16[45,80,128]{2,1,0:T(8,128)(2,1)} %get-tuple-element.159), channel_id=1, source_target_pairs={{0,16},{8,24},{16,0},{24,8},{1,17},{9,25},{17,1},{25,9},{2,18},{10... | collective-permute-start | bytes 2764808 | tf_op jit(solution)/shard_map/ppermute | solution.py:1220
  243.0 34.0 %collective-permute-start.27 = (bf16[23,80,128]{2,1,0:T(8,128)(2,1)}, bf16[23,80,128]{2,1,0:T(8,128)(2,1)}, u32[]{:S(2)}, u32[]{:S(2)}) collective-permute-start(bf16[23,80,128]{2,1,0:T(8,128)(2,1)} %get-tuple-element.140), channel_id=1, source_target_pairs={{0,16},{8,24},{16,0},{24,8},{1,17},{9,25},{17,1},{25,9},{2,18},{10... | collective-permute-start | bytes 1413128 | tf_op jit(solution)/shard_map/ppermute | solution.py:1220
  243.5 33.4 %collective-permute-start.26 = (bf16[22,80,128]{2,1,0:T(8,128)(2,1)}, bf16[22,80,128]{2,1,0:T(8,128)(2,1)}, u32[]{:S(2)}, u32[]{:S(2)}) collective-permute-start(bf16[22,80,128]{2,1,0:T(8,128)(2,1)} %get-tuple-element.139), channel_id=1, source_target_pairs={{0,8},{8,0},{16,24},{24,16},{1,9},{9,1},{17,25},{25,17},{2,10},{10... | collective-permute-start | bytes 1351688 | tf_op jit(solution)/shard_map/ppermute | solution.py:1220
  279.8 23.3 %collective-permute-start.30 = (bf16[45,80,128]{2,1,0:T(8,128)(2,1)}, bf16[45,80,128]{2,1,0:T(8,128)(2,1)}, u32[]{:S(2)}, u32[]{:S(2)}) collective-permute-start(bf16[45,80,128]{2,1,0:T(8,128)(2,1)} %get-tuple-element.149.refs_16_), channel_id=1, source_target_pairs={{0,8},{8,0},{16,24},{24,16},{1,9},{9,1},{17,25},{25,17},{2,10},{10... | collective-permute-start | bytes 2764808 | tf_op jit(solution)/shard_map/ppermute | solution.py:1220
  280.8 22.4 %collective-permute-start.31 = (bf16[45,80,128]{2,1,0:T(8,128)(2,1)}, bf16[45,80,128]{2,1,0:T(8,128)(2,1)}, u32[]{:S(2)}, u32[]{:S(2)}) collective-permute-start(bf16[45,80,128]{2,1,0:T(8,128)(2,1)} %get-tuple-element.150), channel_id=1, source_target_pairs={{0,16},{8,24},{16,0},{24,8},{1,17},{9,25},{17,1},{25,9},{2,18},{10... | collective-permute-start | bytes 2764808 | tf_op jit(solution)/shard_map/ppermute | solution.py:1220
  281.6 0.9 copy-start.5
  285.2 24.2 %collective-permute-start.35 = (bf16[45,80,128]{2,1,0:T(8,128)(2,1)}, bf16[45,80,128]{2,1,0:T(8,128)(2,1)}, u32[]{:S(2)}, u32[]{:S(2)}) collective-permute-start(bf16[45,80,128]{2,1,0:T(8,128)(2,1)} %shard_map.437.refs_17_.refs_0_), channel_id=1, source_target_pairs={{0,2},{1,3},{6,4},{7,5},{8,10},{9,11},{14,12},{15,13},{16,18},{17,... | collective-permute-start | bytes 2764808 | tf_op jit(solution)/shard_map/ppermute | solution.py:1476
  301.8 11.6 %collective-permute-start.36 = (bf16[4,160,384]{2,1,0:T(8,128)(2,1)}, bf16[4,160,384]{2,1,0:T(8,128)(2,1)S(1)}, u32[]{:S(2)}, u32[]{:S(2)}) collective-permute-start(bf16[4,160,384]{2,1,0:T(8,128)(2,1)} %get-tuple-element.161), channel_id=1, source_target_pairs={{0,1},{1,0},{2,3},{3,2},{4,5},{5,4},{6,7},{7,6},{8,9},{9,8},{10,11... | collective-permute-start | bytes 1474568 | tf_op jit(solution)/shard_map/ppermute | solution.py:1223
  303.2 10.2 %copy-start.4 = (bf16[4,160,384]{2,1,0:T(8,128)(2,1)S(1)}, bf16[4,160,384]{2,1,0:T(8,128)(2,1)}, u32[]{:S(2)}) copy-start(bf16[4,160,384]{2,1,0:T(8,128)(2,1)} %get-tuple-element.160.refs_3_) | copy-start | bytes 1474564
  306.0 22.2 %collective-permute-start.34 = (bf16[45,80,128]{2,1,0:T(8,128)(2,1)}, bf16[45,80,128]{2,1,0:T(8,128)(2,1)}, u32[]{:S(2)}, u32[]{:S(2)}) collective-permute-start(bf16[45,80,128]{2,1,0:T(8,128)(2,1)} %shard_map.439.refs_2_.refs_0_), channel_id=1, source_target_pairs={{0,2},{1,3},{6,4},{7,5},{8,10},{9,11},{14,12},{15,13},{16,18},{17,... | collective-permute-start | bytes 2764808 | tf_op jit(solution)/shard_map/ppermute | solution.py:1476
  311.8 18.7 %collective-permute-start.41 = (bf16[45,80,128]{2,1,0:T(8,128)(2,1)}, bf16[45,80,128]{2,1,0:T(8,128)(2,1)}, u32[]{:S(2)}, u32[]{:S(2)}) collective-permute-start(bf16[45,80,128]{2,1,0:T(8,128)(2,1)} %shard_map.440.refs_2_.refs_0_), channel_id=1, source_target_pairs={{2,4},{3,5},{4,2},{5,3},{10,12},{11,13},{12,10},{13,11},{18,20},{1... | collective-permute-start | bytes 2764808 | tf_op jit(solution)/shard_map/ppermute | solution.py:1480
  313.5 6.2 %collective-permute-start.37 = (bf16[160,384]{1,0:T(8,128)(2,1)S(1)}, bf16[160,384]{1,0:T(8,128)(2,1)S(1)}, u32[]{:S(2)}, u32[]{:S(2)}) collective-permute-start(bf16[160,384]{1,0:T(8,128)(2,1)S(1)} %get-tuple-element.187), channel_id=1, source_target_pairs={{0,8},{8,0},{16,24},{24,16},{1,9},{9,1},{17,25},{25,17},{2,10},{10... | collective-permute-start | bytes 368648 | tf_op jit(solution)/shard_map/ppermute | solution.py:1220
  314.9 7.0 %collective-permute-start.38 = (bf16[160,384]{1,0:T(8,128)(2,1)S(1)}, bf16[160,384]{1,0:T(8,128)(2,1)S(1)}, u32[]{:S(2)}, u32[]{:S(2)}) collective-permute-start(bf16[160,384]{1,0:T(8,128)(2,1)S(1)} %get-tuple-element.189), channel_id=1, source_target_pairs={{0,16},{8,24},{16,0},{24,8},{1,17},{9,25},{17,1},{25,9},{2,18},{10... | collective-permute-start | bytes 368648 | tf_op jit(solution)/shard_map/ppermute | solution.py:1220
  316.0 6.0 %collective-permute-start.39 = (bf16[160,384]{1,0:T(8,128)(2,1)S(1)}, bf16[160,384]{1,0:T(8,128)(2,1)S(1)}, u32[]{:S(2)}, u32[]{:S(2)}) collective-permute-start(bf16[160,384]{1,0:T(8,128)(2,1)S(1)} %get-tuple-element.188), channel_id=1, source_target_pairs={{0,24},{8,16},{16,8},{24,0},{1,25},{9,17},{17,9},{25,1},{2,26},{10... | collective-permute-start | bytes 368648 | tf_op jit(solution)/shard_map/ppermute | solution.py:1220
  330.5 3.8 copy-start.1
  333.0 24.6 %collective-permute-start.42 = (bf16[45,80,128]{2,1,0:T(8,128)(2,1)}, bf16[45,80,128]{2,1,0:T(8,128)(2,1)}, u32[]{:S(2)}, u32[]{:S(2)}) collective-permute-start(bf16[45,80,128]{2,1,0:T(8,128)(2,1)} %shard_map.442.refs_1_.refs_2_), channel_id=1, source_target_pairs={{2,0},{3,1},{4,6},{5,7},{10,8},{11,9},{12,14},{13,15},{18,16},{19,... | collective-permute-start | bytes 2764808 | tf_op jit(solution)/shard_map/ppermute | solution.py:1483
  334.3 26.1 %collective-permute-start.40 = (bf16[45,80,128]{2,1,0:T(8,128)(2,1)S(1)}, bf16[45,80,128]{2,1,0:T(8,128)(2,1)}, u32[]{:S(2)}, u32[]{:S(2)}) collective-permute-start(bf16[45,80,128]{2,1,0:T(8,128)(2,1)S(1)} %copy-done.1), channel_id=1, source_target_pairs={{2,4},{3,5},{4,2},{5,3},{10,12},{11,13},{12,10},{13,11},{18,20},{1... | collective-permute-start | bytes 2764808 | tf_op jit(solution)/shard_map/ppermute | solution.py:1480
  335.9 12.2 %collective-permute-start.43 = (bf16[160,384]{1,0:T(8,128)(2,1)}, bf16[160,384]{1,0:T(8,128)(2,1)S(1)}, u32[]{:S(2)}, u32[]{:S(2)}) collective-permute-start(bf16[160,384]{1,0:T(8,128)(2,1)} %fusion.2.refs_3_), channel_id=1, source_target_pairs={{0,2},{1,3},{6,4},{7,5},{8,10},{9,11},{14,12},{15,13},{16,18},{17,... | collective-permute-start | bytes 368648 | tf_op jit(solution)/shard_map/ppermute | solution.py:1476
  349.1 0.7 collective-permute-start.44
  362.8 38.6 %copy-start.2 = (bf16[45,80,128]{2,1,0:T(8,128)(2,1)S(1)}, bf16[45,80,128]{2,1,0:T(8,128)(2,1)}, u32[]{:S(2)}) copy-start(bf16[45,80,128]{2,1,0:T(8,128)(2,1)} %shard_map.443.refs_2_.refs_7_) | copy-start | bytes 2764804
  362.8 45.7 %collective-permute-start.47 = (bf16[45,80,128]{2,1,0:T(8,128)(2,1)}, bf16[45,80,128]{2,1,0:T(8,128)(2,1)}, u32[]{:S(2)}, u32[]{:S(2)}) collective-permute-start(bf16[45,80,128]{2,1,0:T(8,128)(2,1)} %shard_map.444.refs_1_), channel_id=1, source_target_pairs={{2,0},{3,1},{4,6},{5,7},{10,8},{11,9},{12,14},{13,15},{18,16},{19,... | collective-permute-start | bytes 2764808 | tf_op jit(solution)/shard_map/ppermute | solution.py:1483
  364.3 27.9 %collective-permute-start.45 = (bf16[160,384]{1,0:T(8,128)(2,1)}, bf16[160,384]{1,0:T(8,128)(2,1)}, u32[]{:S(2)}, u32[]{:S(2)}) collective-permute-start(bf16[160,384]{1,0:T(8,128)(2,1)} %add_convert_fusion.refs_3_.refs_1_), channel_id=1, source_target_pairs={{2,0},{3,1},{4,6},{5,7},{10,8},{11,9},{12,14},{13,15},{18,16},{19,... | collective-permute-start | bytes 368648 | tf_op jit(solution)/shard_map/ppermute | solution.py:1483
  397.6 10.9 %all-to-all-start.6 = ((f32[32,1,128]{2,1,0:T(1,128)}), f32[32,1,128]{2,1,0:T(1,128)S(1)}, u32[]{:S(2)}, u32[]{:S(2)}) async-start(f32[32,1,128]{2,1,0:T(1,128)} %get-tuple-element.162), calls=%async_computation.6 | async-start | bytes 32768 | tf_op jit(solution)/shard_map/all_to_all | solution.py:1226
  401.4 16.7 %collective-permute-start.49 = (bf16[45,80,128]{2,1,0:T(8,128)(2,1)S(1)}, bf16[45,80,128]{2,1,0:T(8,128)(2,1)}, u32[]{:S(2)}, u32[]{:S(2)}) collective-permute-start(bf16[45,80,128]{2,1,0:T(8,128)(2,1)S(1)} %copy-done.2), channel_id=1, source_target_pairs={{0,1},{1,0},{2,3},{3,2},{4,5},{5,4},{6,7},{7,6},{8,9},{9,8},{10,11... | collective-permute-start | bytes 2764808 | tf_op jit(solution)/shard_map/ppermute | solution.py:1223
  408.5 0.6 copy-start.8
  411.9 6.2 %collective-permute-start.48 = (bf16[45,80,128]{2,1,0:T(8,128)(2,1)}, bf16[45,80,128]{2,1,0:T(8,128)(2,1)}, u32[]{:S(2)}, u32[]{:S(2)}) collective-permute-start(bf16[45,80,128]{2,1,0:T(8,128)(2,1)} %shard_map.448.refs_5_), channel_id=1, source_target_pairs={{0,1},{1,0},{2,3},{3,2},{4,5},{5,4},{6,7},{7,6},{8,9},{9,8},{10,11... | collective-permute-start | bytes 2764808 | tf_op jit(solution)/shard_map/ppermute | solution.py:1223
  412.0 3.0 collective-permute-start.46

commit v4 on v3

--- a/solution.py
+++ b/solution.py
@@ -596,19 +596,24 @@
     rows = per * 64
     band = per * 8
     (
-        summed,
+        source,
         stats_in,
         norm_rows,
         head_all,
         facts,
-        slope,
+        slope_out,
         spread,
         stats,
         grad_head,
         sum_value,
         sum_slope,
         sum_cross,
+        summed,
+        slope,
+        in_sems,
+        out_sems,
     ) = refs
+    inputs = [fetch_quarter(source, summed, in_sems.at[part], part) for part in range(QUARTERS)]
     mean, rstd = moments(stats_in, row_total)
     gain = norm_rows[4:5]
     bias = norm_rows[5:6]
@@ -628,7 +633,11 @@
             sum_cross[here] += gradient * unit
         return carry
 
-    lax.fori_loop(0, 8, walk, 0)
+    outputs = []
+    for part in range(QUARTERS):
+        inputs[part].wait()
+        lax.fori_loop(2 * part, 2 * part + 2, walk, 0)
+        outputs.append(fetch_quarter(slope, slope_out, out_sems.at[part], part))
 
     def by_image(ref):
         return jnp.sum(ref[...].reshape(per, 8, C3), axis=1)
@@ -654,6 +663,8 @@
     bias_sum = jnp.sum(pull * by_image(sum_slope), axis=0, keepdims=True)
     gain_sum = jnp.sum(pull * by_image(sum_cross), axis=0, keepdims=True)
     spread_stats(stats, [bias_sum, gain_sum, jnp.broadcast_to(loss, (1, 128))])
+    for copy in outputs:
+        copy.wait()
 
 
 def grad_moments(stats, row_total):
@@ -1024,26 +1035,30 @@
         for side, target in ((0, mine), (1, other)):
             place = pl.multiple_of((ids[2] ^ side) * tall, 16)
             spot = pl.multiple_of((ids[0] ^ turn) * (2 * tall) + (ids[2] ^ side) * tall, 16)
-            number = 2 * (2 * turn + side)
-            copy = pltpu.make_async_copy(
-                split_part.at[pl.ds(spot, tall)], target.at[turn, 0:tall], sems.at[number]
-            )
-            copy.start()
-            copies.append(copy)
-            copy = pltpu.make_async_copy(
-                shared_part.at[pl.ds(place, tall)],
-                target.at[turn, tall : 2 * tall],
-                sems.at[number + 1],
-            )
-            copy.start()
-            copies.append(copy)
+            for block in range(3):
+                lanes = pl.ds(block * 128, 128)
+                number = 6 * (2 * turn + side) + block
+                copies.append(
+                    fetch(
+                        split_part.at[pl.ds(spot, tall), lanes],
+                        target.at[turn, block],
+                        sems.at[number],
+                    )
+                )
+                copies.append(
+                    fetch(
+                        shared_part.at[pl.ds(place, tall), lanes],
+                        target.at[turn, 3 + block],
+                        sems.at[number + 3],
+                    )
+                )
     for copy in copies:
         copy.wait()
 
 
 def norm_kernel(sizes, *refs):
     devices, chips, split = sizes
-    ids, one, two, small, stats_six, stats_five, stats_four, line, local, loss, norm_out = refs
+    ids, one, two, stats_six, stats_five, stats_four, line, local, loss, norm_out = refs
     digit = ids[3] // (chips // 4) % 4
     inner = (digit == 1) | (digit == 2)
 
@@ -1052,19 +1067,21 @@
         second = two[block].astype(full)
         return total + (first * first + second * second)
 
-    squares = lax.fori_loop(0, one.shape[0], walk, jnp.zeros(one.shape[1:], full))
+    blocks = two.shape[0]
+    squares = lax.fori_loop(0, blocks, walk, jnp.zeros(one.shape[1:], full))
     squares = jnp.sum(jnp.sum(squares, axis=0, keepdims=True), axis=1, keepdims=True)
     total = jnp.where(inner, squares / (chips // 2), 0.0)
-    tall = small.shape[0] // 2
-    value = small[...].astype(full)
-    row = iota(value.shape, 0)
-    lane = iota(value.shape, 1)
-    share = jnp.where(
-        row < tall,
-        1.0 / chips,
-        jnp.where(lane < C2 + 16, 1.0 / (chips * split), 1.0 / (2 * chips * split)),
-    )
-    value = jnp.where(inner, 2.0 * value * value * share, 0.0)
+    value = jnp.zeros(one.shape[1:], full)
+    for block in range(6):
+        lane = iota(value.shape, 1) + block % 3 * 128
+        share = 1.0 / chips
+        if block >= 3:
+            share = jnp.where(
+                lane < C2 + 16, 1.0 / (chips * split), 1.0 / (2 * chips * split)
+            )
+        part = one[blocks + block].astype(full)
+        value = value + part * part * share
+    value = jnp.where(inner, 2.0 * value, 0.0)
     total = total + jnp.sum(jnp.sum(value, axis=0, keepdims=True), axis=1, keepdims=True)
     norm_out[...] = jnp.zeros(norm_out.shape, full)
     for place, stats in enumerate((stats_six, stats_five, stats_four)):
@@ -1087,11 +1104,14 @@
 
 
 def conv_update_kernel(sizes, *refs):
-    pieces_count, places, step_rate = sizes
+    pieces_count, places, step_rate, rates = sizes
     ids = refs[0]
     squares, weight, first, second = refs[1:5]
-    pieces = refs[5 : 5 + pieces_count]
-    (first_new, second_new, weight_new, held, sems) = refs[5 + pieces_count :]
+    small_in = refs[5:24]
+    pieces = refs[24 : 24 + pieces_count]
+    first_new, second_new, weight_new = refs[24 + pieces_count : 27 + pieces_count]
+    small_out = refs[27 + pieces_count : 46 + pieces_count]
+    held, small_held, sems, small_sems = refs[46 + pieces_count :]
     layer = pl.program_id(0)
     line = pl.program_id(1)
 
@@ -1104,17 +1124,32 @@
             row = pl.multiple_of((ids[2] ^ side) * tall, 16)
             made.append(
                 pltpu.make_async_copy(
-                    pieces[number],
+                    pieces[number].at[0:size],
                     held.at[owner, start : start + size, pl.ds(row, tall), :],
                     sems.at[number],
                 )
             )
         return made
 
+    def small_copies():
+        blocks = held.shape[1]
+        return [
+            pltpu.make_async_copy(
+                pieces[side].at[blocks : blocks + 6], small_held.at[side], small_sems.at[side]
+            )
+            for side in range(2)
+        ]
+
     @pl.when((layer == 0) & (line == 0))
     def _():
-        for copy in copies((0, 1)):
+        for copy in small_copies() + copies((0, 1)):
             copy.start()
+
+    @pl.when((layer == 0) & (line == 1))
+    def _():
+        for copy in small_copies():
+            copy.wait()
+        small_update(rates, ids, squares, small_held, small_in, small_out)
 
     for owner in range(2):
 
@@ -1136,21 +1171,26 @@
         weight_new[0, :, lanes] = results[2]
 
 
-def small_update_kernel(rates, *refs):
-    ids, squares, mine, other, grad_norm_p = refs[0:5]
-    states = refs[5:23]
-    outs = refs[23:41]
-    size_out = refs[41]
+def small_update(rates, ids, squares, blocks, refs, outs):
+    grad_norm_p = refs[0]
+    states = refs[1:19]
+    size_out = outs[18]
     size, scale = clip_scale(squares)
     size_out[...] = jnp.broadcast_to(size, size_out.shape)
     first_core = ids[2] == 0
-    tall = mine.shape[0] // 2
-    here = mine[...].astype(full)
-    there = other[...].astype(full)
-    even = jnp.where(first_core, here, there)
-    odd = jnp.where(first_core, there, here)
-    split_part = jnp.concatenate([even[0:tall], odd[0:tall]], axis=0).astype(half)
-    shared = jnp.concatenate([even[tall:], odd[tall:]], axis=0).astype(half)
+    here = blocks[0].astype(full)
+    there = blocks[1].astype(full)
+    cores = (jnp.where(first_core, here, there), jnp.where(first_core, there, here))
+    split_part, shared = [
+        jnp.concatenate(
+            [
+                jnp.concatenate([core[first], core[first + 1], core[first + 2]], axis=1)
+                for core in cores
+            ],
+            axis=0,
+        ).astype(half)
+        for first in (0, 3)
+    ]
     grad_c = split_part[:, 0:C2].astype(full)
     classes = states[12].shape[0]
     pick = hot(iota((classes, WIDE), 0) + C2 == iota((classes, WIDE), 1))
@@ -1347,14 +1387,16 @@
     far_field_two = over_filt(field_two, 1)
     slope_three, spread, stats, grad_head = call(
         functools.partial(head_kernel, (per, row_total, image_total, head_w.shape[1])),
-        [VMEM] * 5,
+        [ANY] + [VMEM] * 4,
         [
-            (shape((rows, C3)), VMEM),
+            (shape((rows, C3)), ANY),
             (shape((band, C3)), VMEM),
             (shape((devices, 1, 2 * C3 + 128)), VMEM),
             (shape((C3, 16)), VMEM),
         ],
-        [pltpu.VMEM((band, C3), full)] * 3,
+        [pltpu.VMEM((band, C3), full)] * 3
+        + [table, table]
+        + [pltpu.SemaphoreType.DMA((QUARTERS,)), pltpu.SemaphoreType.DMA((QUARTERS,))],
         7,
     )(summed, stats_three, norm_rows, head_all, facts)
     stats_four = exchange(stats)
@@ -1479,8 +1521,12 @@
     def between_middles(value, reach, after):
         return gated_add(value, lax.ppermute(value, "filt", chip_routes(reach)[1]), after)
 
-    def from_middles(value, reach, after=()):
-        arrived = lax.ppermute(value, "filt", chip_routes(reach)[2])
+    def outward(value, reach):
+        return lax.ppermute(value, "filt", chip_routes(reach)[2])
+
+    def from_middles(value, reach, after=(), arrived=None):
+        if arrived is None:
+            arrived = outward(value, reach)
         (result,) = call(
             functools.partial(pick_kernel, reach),
             [SMEM, ANY, ANY],
@@ -1535,7 +1581,7 @@
     begun_one = start_dp(pairs_one[0], [stats_six])
     blocks = begun_one[0].shape[0]
     (part_two,) = end_dp(begun_two, [blocks], [stats_six])
-    small = shape((split, 2 * tall, WIDE), half)
+    small = shape((split, 6, tall, 128), half)
     small_mine, small_other = call(
         functools.partial(trunk_kernel, (per, row_total, split)),
         [SMEM] + [VMEM] * 15,
@@ -1550,7 +1596,7 @@
             pltpu.VMEM((C1, WIDE), half),
             pltpu.VMEM((C3, WIDE), half),
             pltpu.VMEM((C1, WIDE), half),
-            pltpu.SemaphoreType.DMA((4 * split,)),
+            pltpu.SemaphoreType.DMA((12 * split,)),
         ],
         0.1,
         2,
@@ -1585,14 +1631,19 @@
     last = chips // 4
     small_sum = between_middles(to_middles(small_sum, 1, []), 1, [])
     small_sum = over_more_chips(small_sum, 4)
-    small_whole = from_middles(small_sum, last)
-
-    reduced_two = from_middles(whole_two, last)
-    whole_one = between_middles(half_one, 1, [reduced_two, small_sum])
-    whole_one = over_more_chips(whole_one, 4)
+
+    arrived_two = outward(whole_two, last)
+    terms = [half_one, lax.ppermute(half_one, "filt", chip_routes(1)[1])]
+    if chips > 4:
+        terms = [over_more_chips(add(terms), 4)]
+    plan = [(place, 0, 0, blocks) for place in range(len(terms))]
+    plan.append((len(terms), 0, blocks, 6))
+    (whole_one,) = merge([*terms, small_sum], [(blocks + 6, plan)], [arrived_two], 0.1)
+    reduced_two = from_middles(whole_two, last, [whole_one], arrived_two)
+    far_two = over_filt(reduced_two, 1)
     squares, grad_norm_p, loss = call(
         functools.partial(norm_kernel, (devices, chips, split)),
-        [SMEM] + [VMEM] * 6,
+        [SMEM] + [VMEM] * 5,
         [
             (shape((devices, 1, 128)), VMEM),
             (shape((6, C3 // split)), VMEM),
@@ -1601,34 +1652,18 @@
         [pltpu.VMEM((8, C3), full)],
         3,
         1,
-    )(ids, whole_one, whole_two, small_sum, stats_six, stats_five, stats_four, small_whole)
+    )(ids, whole_one, whole_two, stats_six, stats_five, stats_four, far_two)
     squares = exchange(squares)
     reduced_one = from_middles(whole_one, last, [squares])
 
     pieces = []
     places = []
-    for owner, value in enumerate((reduced_one, reduced_two)):
-        pieces += [value, over_filt(value, 1)]
+    far_one = over_filt(reduced_one, 1)
+    for owner, both in enumerate(((reduced_one, far_one), (reduced_two, far_two))):
+        pieces += both
         places += [(owner, 0, blocks, side) for side in range(2)]
     whole_spec = pl.BlockSpec((1, 2 * tall, 1152), lambda layer, line: (layer, 0, line))
     conv_shape = shape(conv_w.shape)
-    conv_new = pl.pallas_call(
-        functools.partial(
-            conv_update_kernel, (len(pieces), places, 0.7 / math.sqrt(9.0 * C3))
-        ),
-        grid=(2, 5),
-        in_specs=[SMEM, VMEM, whole_spec, whole_spec, whole_spec] + [ANY] * len(pieces),
-        out_specs=[whole_spec] * 3,
-        out_shape=[conv_shape] * 3,
-        scratch_shapes=[
-            pltpu.VMEM((2, 45, 2 * tall, 128), half),
-            pltpu.SemaphoreType.DMA((len(pieces),)),
-        ],
-        compiler_params=pltpu.CompilerParams(vmem_limit_bytes=63 * MIB),
-        cost_estimate=pl.CostEstimate(
-            flops=20 * conv_w.size, bytes_accessed=26 * conv_w.size, transcendentals=0
-        ),
-    )(ids, squares, conv_w, conv_w_m, conv_w_v, *pieces)
     states = (
         (stem_w.T, stem_w_m.T, stem_w_v.T),
         (proj_a, proj_a_m, proj_a_v),
@@ -1646,13 +1681,37 @@
         0.8,
     )
     flat = [item for group in states for item in group]
-    small_new = call(
-        functools.partial(small_update_kernel, rates),
-        [SMEM] + [VMEM] * 22,
-        [(shape(item.shape), VMEM) for item in flat] + [(shape((1, 128)), VMEM)],
-        [],
-        3,
-    )(ids, squares, small_whole, over_filt(small_whole, 1), grad_norm_p, *flat)
+    updated = pl.pallas_call(
+        functools.partial(
+            conv_update_kernel, (len(pieces), places, 0.7 / math.sqrt(9.0 * C3), rates)
+        ),
+        grid=(2, 5),
+        in_specs=[SMEM, VMEM, whole_spec, whole_spec, whole_spec]
+        + [VMEM] * 19
+        + [ANY] * len(pieces),
+        out_specs=[whole_spec] * 3 + [VMEM] * 19,
+        out_shape=[conv_shape] * 3 + [shape(item.shape) for item in flat] + [shape((1, 128))],
+        scratch_shapes=[
+            pltpu.VMEM((2, 45, 2 * tall, 128), half),
+            pltpu.VMEM((2, 6, tall, 128), half),
+            pltpu.SemaphoreType.DMA((len(pieces),)),
+            pltpu.SemaphoreType.DMA((2,)),
+        ],
+        compiler_params=pltpu.CompilerParams(vmem_limit_bytes=63 * MIB),
+        cost_estimate=pl.CostEstimate(
+            flops=20 * conv_w.size, bytes_accessed=26 * conv_w.size, transcendentals=0
+        ),
+    )(
+        ids,
+        squares,
+        conv_w,
+        conv_w_m,
+        conv_w_v,
+        grad_norm_p,
+        *flat,
+        *pieces,
+    )
+    conv_new, small_new = updated[0:3], updated[3:]
     size = small_new[18][0, 0]
     turned = [
         item.T if index // 3 in (0, 3, 4) else item for index, item in enumerate(small_new[:18])

time: 445 us -> 427 us (0.960)
  waiting for transfers between devices: 93.6 us -> 66.2 us
  blocking collectives: 52.7 us -> 75.2 us
  starting transfers between devices: 66.3 us -> 56.4 us
    all_to_all x4 -> x5, blocking collectives: 52.7 us -> 75.2 us  [exchange(): return lax.all_to_all(stats, ('dp', 'filt'), 0, 0)]
    ppermute x3, waiting for transfers between devices: 33.8 us -> 11.7 us  [the longest x2 11.7 us: outward(): return lax.ppermute(value, 'filt', chip_routes(reach)[2])]
    all_to_all x3 -> x2, waiting for transfers between devices: 15 us -> 8.24 us  [exchange(): return lax.all_to_all(stats, ('dp', 'filt'), 0, 0)]
    all_to_all x3 -> x2, starting transfers between devices: 9.57 us -> 5.87 us  [exchange(): return lax.all_to_all(stats, ('dp', 'filt'), 0, 0)]
    ppermute x22 -> x21, waiting for transfers between devices: 17.2 us -> 19.1 us  [over_filt(): return lax.ppermute(value, 'filt', xor_pairs(groups, turn))]
    ppermute x22 -> x21, starting transfers between devices: 10.3 us -> 9.54 us  [over_filt(): return lax.ppermute(value, 'filt', xor_pairs(groups, turn))]
  transfers between devices with their start and end apart: 53 -> 50, of which waited for: 20 -> 19; matrix products, arithmetic and copies ran while one was open for 1% -> 1% of each run, Pallas kernels for 35% -> 35%
where the time goes in v4:
time: 427 us; the launch traced here: 421 us
  Pallas kernels  214 us (50%)
  blocking collectives  75.2 us (18%)
  waiting for transfers between devices  66.2 us (16%)
  starting transfers between devices  56.4 us (13%)
  local copies, waits for them, and re-layouts  5.04 us (1%)
    all_to_all x5, blocking collectives, exchange(): return lax.all_to_all(stats, ('dp', 'filt'), 0, 0)  75.2 us
    pallas_call x2, Pallas kernels, back(): call(functools.partial(back_kernel, (per, row_total, split), layer), ([SM...  40.1 us
    pallas_call x2, Pallas kernels, weight_grad(): call(functools.partial(weight_grad_kernel, (chunks, split, band)), [ANY]...  27 us
    ppermute x19, starting transfers between devices, over_dp(): return lax.ppermute(value, 'dp', xor_pairs(split, turn))  22 us
    pallas_call x1, Pallas kernels, shards(): pl.pallas_call(functools.partial(conv_update_kernel, (len(pieces), places...  20.8 us
    pallas_call x8, Pallas kernels, merge(): call(functools.partial(merge_kernel, plan, len(values)), [ANY] * len(valu...  20.7 us
    ppermute x21, waiting for transfers between devices, over_filt(): return lax.ppermute(value, 'filt', xor_pairs(groups, turn))  19.1 us
    ppermute x19, waiting for transfers between devices, over_dp(): return lax.ppermute(value, 'dp', xor_pairs(split, turn))  19.1 us
  transfers between devices with their start and end apart: 50, of which 19 were waited for; matrix products, arithmetic and copies ran while one was open for 1% of the time, Pallas kernels for 35%

profile of v4, /device:TPU:0, one launch (start us, length us, event | category | flops | bytes accessed | tf_op | source)
XLA Modules:
  0.0 421.0 jit_solution(12265588971985339736)
XLA Ops:
  0.7 2.7 shard_map.416.refs_5_.refs_0_
  3.4 3.0 collective-permute-start
  6.4 2.6 collective-permute-start.1
  9.6 3.3 shard_map.417.refs_2_.refs_4_.refs_5_
  12.8 1.8 collective-permute-start.4
  14.6 1.5 collective-permute-start.5
  16.1 2.9 shard_map.418.refs_4_.refs_0_
  19.1 10.0 %collective-permute-done.1.refs_2_ = bf16[72,1920]{1,0:T(8,128)(2,1)} collective-permute-done((bf16[72,1920]{1,0:T(8,128)(2,1)}, bf16[72,1920]{1,0:T(8,128)(2,1)}, u32[]{:S(2)}, u32[]{:S(2)}) %collective-permute-start.1) | collective-permute-done | bytes 276512 | tf_op jit(solution)/shard_map/ppermute | solution.py:1263
  29.0 2.2 shard_map.419.refs_1_
  31.3 4.8 %collective-permute-done.4.refs_0_.refs_4_.refs_6_.refs_7_ = bf16[80,6144]{1,0:T(8,128)(2,1)} collective-permute-done((bf16[80,6144]{1,0:T(8,128)(2,1)}, bf16[80,6144]{1,0:T(8,128)(2,1)}, u32[]{:S(2)}, u32[]{:S(2)}) %collective-permute-start.4) | collective-permute-done | bytes 983072 | tf_op jit(solution)/shard_map/ppermute | solution.py:1260
  37.4 2.1 shard_map.420
  39.5 1.6 collective-permute-start.6
  42.1 6.8 %shard_map.421 = (bf16[1152,32]{1,0:T(8,128)(2,1)}, f32[1152,16]{1,0:T(8,128)}, f32[1152,160]{1,0:T(8,128)}, f32[1152,384]{1,0:T(8,128)}, bf16[1152,384]{1,0:T(8,128)(2,1)}, /*index=5*/f32[18,128]{1,0:T(8,128)}) custom-call(s32[4]{0:T(128)} %pad_add_fusion.refs_0_, bf16[4,72,1920]{2,1,0:T(8,128)(2,1)} %shard_map.419.refs_1_, ...), custom_call_target="tpu_custom_call" | custom-call | flops 3500000000 | bytes 1 | tf_op jit(solution)/shard_map/pallas_call | solution.py:1308
  50.0 3.0 collective-permute-done.6.refs_0_
  53.0 2.2 shard_map.422
  55.8 2.4 collective-permute-done.12.refs_11_.refs_13_.refs_14_
  58.2 5.8 %shard_map.423 = (f32[1152,640]{1,0:T(8,128)}, f32[32,1,1280]{2,1,0:T(1,128)}, f32[8,640]{1,0:T(8,128)}, bf16[640,16]{1,0:T(8,128)(2,1)}, bf16[640,384]{1,0:T(8,128)(2,1)}) custom-call(s32[4]{0:T(128)} %pad_add_fusion.refs_0_, bf16[1152,384]{1,0:T(8,128)(2,1)} %get-tuple-element.106.refs_1_.refs_8_, bf16[80,6144]{1,0:T(8,128)(2,1)} %shard_map.417.refs_2_.refs_4_.refs_5_, ...), custom_call_target="tpu_custom_call" | custom-call | flops 1400000000 | bytes 1 | tf_op jit(solution)/shard_map/pallas_call | solution.py:1329
  63.9 13.7 %all_to_all.35.refs_2_.refs_1_.refs_4_ = f32[32,1,1280]{2,1,0:T(1,128)} all-to-all(f32[32,1,1280]{2,1,0:T(1,128)} %get-tuple-element.112), channel_id=1, replica_groups=mesh['dp'=4,'filt'=8] {'dp','filt'}, dimensions={0} | all-to-all | bytes 327680 | tf_op jit(solution)/shard_map/all_to_all | solution.py:1266
  79.4 18.5 %shard_map.424 = (f32[1152,640]{1,0:T(8,128)}, bf16[1152,640]{1,0:T(8,128)(2,1)}, f32[1152,640]{1,0:T(8,128)}, f32[32,1,1280]{2,1,0:T(1,128)}) custom-call(s32[4]{0:T(128)} %pad_add_fusion.refs_0_, f32[1152,640]{1,0:T(8,128)} %get-tuple-element.111.refs_1_.refs_4_.refs_2_.refs_3_, f32[32,1,1280]{2,1,0:T(1,128)} %all_to_all.35.refs_2_.refs_1_.refs_4_, ...), custom_call_target="tpu_custom_call" | custom-call | flops 6300000256 | bytes 1 | tf_op jit(solution)/shard_map/pallas_call | solution.py:1368
  97.9 3.0 collective-permute-done.13.refs_1_.refs_6_.refs_11_
  101.0 2.1 shard_map.426
  103.1 1.7 collective-permute-start.15
  105.8 13.3 %all_to_all.36.refs_2_.refs_9_.refs_3_ = f32[32,1,1280]{2,1,0:T(1,128)} all-to-all(f32[32,1,1280]{2,1,0:T(1,128)} %get-tuple-element.115.refs_2_), channel_id=1, replica_groups=mesh['dp'=4,'filt'=8] {'dp','filt'}, dimensions={0} | all-to-all | bytes 327680 | tf_op jit(solution)/shard_map/all_to_all | solution.py:1266
  119.2 2.1 shard_map.427
  121.8 2.3 collective-permute-done.21.refs_14_.refs_19_
  124.2 18.6 %shard_map.428 = (f32[1152,640]{1,0:T(8,128)}, bf16[1152,640]{1,0:T(8,128)(2,1)}, f32[1152,640]{1,0:T(8,128)}, f32[32,1,1280]{2,1,0:T(1,128)}) custom-call(s32[4]{0:T(128)} %pad_add_fusion.refs_0_, f32[1152,640]{1,0:T(8,128)} %get-tuple-element.114.refs_1_.refs_7_.refs_2_, f32[32,1,1280]{2,1,0:T(1,128)} %all_to_all.36.refs_2_.refs_9_.refs_3_, ...), custom_call_target="tpu_custom_call" | custom-call | flops 6300000256 | bytes 1 | tf_op jit(solution)/shard_map/pallas_call | solution.py:1379
  142.8 11.9 %all_to_all.37.refs_1_.refs_3_ = f32[32,1,1280]{2,1,0:T(1,128)} all-to-all(f32[32,1,1280]{2,1,0:T(1,128)} %get-tuple-element.121), channel_id=1, replica_groups=mesh['dp'=4,'filt'=8] {'dp','filt'}, dimensions={0} | all-to-all | bytes 327680 | tf_op jit(solution)/shard_map/all_to_all | solution.py:1266
  154.7 7.1 %shard_map.429 = (f32[1152,640]{1,0:T(8,128)}, f32[144,640]{1,0:T(8,128)}, f32[32,1,1408]{2,1,0:T(1,128)}, f32[640,16]{1,0:T(8,128)}) custom-call(f32[1152,640]{1,0:T(8,128)} %get-tuple-element.120.refs_0_.refs_2_, f32[32,1,1280]{2,1,0:T(1,128)} %all_to_all.37.refs_1_.refs_3_, f32[8,640]{1,0:T(8,128)} %get-tuple-element.113.refs_3_.refs_2_.refs_5_.refs_6_, ...), custom_call_target="tpu_custom_call" | custom-call | flops 2449999872 | bytes 1 | tf_op jit(solution)/shard_map/pallas_call | solution.py:1388
  161.8 3.1 all-to-all-start.3
  165.3 8.2 %all-to-all-done.3.refs_4_.refs_5_ = f32[32,1,1408]{2,1,0:T(1,128)S(1)} async-done(((f32[32,1,1408]{2,1,0:T(1,128)}), f32[32,1,1408]{2,1,0:T(1,128)S(1)}, u32[]{:S(2)}, u32[]{:S(2)}) %all-to-all-start.3) | async-done | bytes 180256 | tf_op jit(solution)/shard_map/all_to_all | solution.py:1266
  174.2 21.5 %shard_map.430 = (f32[1152,640]{1,0:T(8,128)}, f32[32,1,1280]{2,1,0:T(1,128)}, bf16[1152,384]{1,0:T(8,128)(2,1)}, bf16[1152,384]{1,0:T(8,128)(2,1)}, f32[1152,640]{1,0:T(8,128)}) custom-call(s32[4]{0:T(128)} %pad_add_fusion.refs_0_, f32[1152,640]{1,0:T(8,128)} %get-tuple-element.123.refs_1_, f32[1152,640]{1,0:T(8,128)} %get-tuple-element.120.refs_0_.refs_2_, ...), custom_call_target="tpu_custom_call" | custom-call | flops 7699999744 | bytes 1 | tf_op jit(solution)/shard_map/pallas_call | solution.py:1410
  196.5 2.8 all-to-all-start.4
  199.3 13.5 %shard_map.431 = (bf16[45,80,128]{2,1,0:T(8,128)(2,1)}, bf16[45,80,128]{2,1,0:T(8,128)(2,1)}, bf16[45,80,128]{2,1,0:T(8,128)(2,1)}, bf16[22,80,128]{2,1,0:T(8,128)(2,1)}, bf16[23,80,128]{2,1,0:T(8,128)(2,1)}) custom-call(bf16[1152,384]{1,0:T(8,128)(2,1)} %get-tuple-element.129.refs_0_, bf16[1152,384]{1,0:T(8,128)(2,1)} %collective-permute-done.22.refs_1_, ...), custom_call_target="tpu_custom_call" | custom-call | flops 4550000128 | bytes 1 | tf_op jit(solution)/shard_map/pallas_call | solution.py:1449
  213.4 6.5 %shard_map.432 = (bf16[1152,640]{1,0:T(8,128)(2,1)}, bf16[1152,384]{1,0:T(8,128)(2,1)}, bf16[1152,384]{1,0:T(8,128)(2,1)}) custom-call(s32[4]{0:T(128)} %pad_add_fusion.refs_0_, f32[1152,640]{1,0:T(8,128)} %get-tuple-element.127.refs_1_, f32[1152,640]{1,0:T(8,128)} %get-tuple-element.114.refs_1_.refs_7_.refs_2_, ...), custom_call_target="tpu_custom_call" | custom-call | flops 2100000000 | bytes 1 | tf_op jit(solution)/shard_map/pallas_call | solution.py:1553
  220.3 1.7 collective-permute-start.29
  224.3 13.5 %shard_map.433 = (bf16[45,80,128]{2,1,0:T(8,128)(2,1)}, bf16[45,80,128]{2,1,0:T(8,128)(2,1)}, bf16[45,80,128]{2,1,0:T(8,128)(2,1)}, bf16[22,80,128]{2,1,0:T(8,128)(2,1)}, bf16[23,80,128]{2,1,0:T(8,128)(2,1)}) custom-call(bf16[1152,384]{1,0:T(8,128)(2,1)} %get-tuple-element.133.refs_0_, bf16[1152,384]{1,0:T(8,128)(2,1)} %copy-done.8, ...), custom_call_target="tpu_custom_call" | custom-call | flops 4550000128 | bytes 1 | tf_op jit(solution)/shard_map/pallas_call | solution.py:1449
  237.9 2.9 shard_map.434
  241.8 1.5 collective-permute-start.33
  244.9 18.6 %shard_map.435 = (f32[1152,640]{1,0:T(8,128)}, f32[32,1,1280]{2,1,0:T(1,128)}) custom-call(s32[4]{0:T(128)} %pad_add_fusion.refs_0_, bf16[1152,640]{1,0:T(8,128)(2,1)} %get-tuple-element.141.refs_1_, f32[1152,640]{1,0:T(8,128)} %get-tuple-element.111.refs_1_.refs_4_.refs_2_.refs_3_, f32[1152,640]{1,0:T(8,128)} %get-tuple-element.142.refs_3_, ...), custom_call_target="tpu_custom_call" | custom-call | flops 7699999744 | bytes 1 | tf_op jit(solution)/shard_map/pallas_call | solution.py:1410
  263.5 13.8 %all_to_all.38.refs_4_.refs_3_.refs_5_ = f32[32,1,1280]{2,1,0:T(1,128)} all-to-all(f32[32,1,1280]{2,1,0:T(1,128)} %get-tuple-element.148), channel_id=1, replica_groups=mesh['dp'=4,'filt'=8] {'dp','filt'}, dimensions={0} | all-to-all | bytes 327680 | tf_op jit(solution)/shard_map/all_to_all | solution.py:1266
  277.3 2.8 shard_map.436
  282.8 2.7 shard_map.437.refs_17_.refs_0_
  285.5 3.6 collective-permute-start.35
  289.1 13.3 %shard_map.438 = (bf16[4,6,80,128]{3,2,1,0:T(8,128)(2,1)}, bf16[4,6,80,128]{3,2,1,0:T(8,128)(2,1)}) custom-call(s32[4]{0:T(128)} %pad_add_fusion.refs_0_, f32[1152,640]{1,0:T(8,128)} %get-tuple-element.151.refs_1_, f32[1152,640]{1,0:T(8,128)} %get-tuple-element.152.refs_2_, f32[1152,640]{1,0:T(8,128)} %get-tuple-element.111.refs_1_.refs_4_.refs_2_.refs_3_, ...), custom_call_target="tpu_custom_call" | custom-call | flops 35000000 | bytes 1 | tf_op jit(solution)/shard_map/pallas_call | solution.py:1585
  303.5 2.8 shard_map.439.refs_2_.refs_0_
  306.2 3.5 collective-permute-start.34
  309.7 2.4 shard_map.440.refs_2_.refs_0_
  312.1 1.6 collective-permute-start.43
  317.4 2.7 collective-permute-done.37
  320.1 2.2 collective-permute-done.38
  323.0 5.4 %collective-permute-done.34.refs_1_ = bf16[45,80,128]{2,1,0:T(8,128)(2,1)} collective-permute-done((bf16[45,80,128]{2,1,0:T(8,128)(2,1)}, bf16[45,80,128]{2,1,0:T(8,128)(2,1)}, u32[]{:S(2)}, u32[]{:S(2)}) %collective-permute-start.34) | collective-permute-done | bytes 921632 | tf_op jit(solution)/shard_map/ppermute | solution.py:1518
  328.4 2.4 shard_map.441.refs_2_.refs_0_
  330.8 1.6 collective-permute-start.40
  332.4 2.4 shard_map.442.refs_1_.refs_2_
  336.1 5.4 %collective-permute-start.41 = (bf16[6,80,128]{2,1,0:T(8,128)(2,1)}, bf16[6,80,128]{2,1,0:T(8,128)(2,1)S(1)}, u32[]{:S(2)}, u32[]{:S(2)}) collective-permute-start(bf16[6,80,128]{2,1,0:T(8,128)(2,1)} %fusion.2.refs_3_), channel_id=1, source_target_pairs={{0,2},{1,3},{6,4},{7,5},{8,10},{9,11},{14,12},{15,13},{16,18},{17,... | collective-permute-start | bytes 368648 | tf_op jit(solution)/shard_map/ppermute | solution.py:1518
  341.5 2.7 collective-permute-done.41
  346.6 11.7 %collective-permute-done.44.refs_3_.refs_2_ = bf16[45,80,128]{2,1,0:T(8,128)(2,1)S(1)} collective-permute-done((bf16[45,80,128]{2,1,0:T(8,128)(2,1)}, bf16[45,80,128]{2,1,0:T(8,128)(2,1)S(1)}, u32[]{:S(2)}, u32[]{:S(2)}) %collective-permute-start.44) | collective-permute-done | bytes 921632 | tf_op jit(solution)/shard_map/ppermute | solution.py:1525
  359.2 2.4 shard_map.443.refs_3_.refs_1_
  361.6 2.8 shard_map.444.refs_26_
  368.1 3.2 shard_map.445
  371.3 22.5 %all_to_all.39.refs_3_.refs_1_ = f32[32,1,128]{2,1,0:T(1,128)} all-to-all(f32[32,1,128]{2,1,0:T(1,128)} %get-tuple-element.162), channel_id=1, replica_groups=mesh['dp'=4,'filt'=8] {'dp','filt'}, dimensions={0} | all-to-all | bytes 32768 | tf_op jit(solution)/shard_map/all_to_all | solution.py:1266
  393.8 2.9 shard_map.446.refs_24_
  396.8 3.0 collective-permute-done.47.refs_25_
  399.7 20.8 %shard_map.447 = (f32[2,160,5760]{2,1,0:T(8,128)}, f32[2,160,5760]{2,1,0:T(8,128)}, f32[2,160,5760]{2,1,0:T(8,128)}, f32[16,27]{1,0:T(8,128)}, f32[16,27]{1,0:T(...) custom-call(s32[4]{0:T(128)} %pad_add_fusion.refs_0_, ...), custom_call_target="tpu_custom_call" | custom-call | flops 36864000 | bytes 47923200 | tf_op jit(solution)/shard_map/pallas_call | solution.py:1684
  (96 shorter events, 32.3 us)
Async XLA Ops:
  3.4 15.7 %collective-permute-start = (bf16[72,1920]{1,0:T(8,128)(2,1)}, bf16[72,1920]{1,0:T(8,128)(2,1)}, u32[]{:S(2)}, u32[]{:S(2)}) collective-permute-start(bf16[72,1920]{1,0:T(8,128)(2,1)} %shard_map.416.refs_5_.refs_0_), channel_id=1, source_target_pairs={{0,2},{1,3},{2,0},{3,1},{4,6},{5,7},{6,4},{7,5},{8,10},{9,11},{10,... | collective-permute-start | bytes 829448 | tf_op jit(solution)/shard_map/ppermute | solution.py:1263
  6.4 22.6 %collective-permute-start.1 = (bf16[72,1920]{1,0:T(8,128)(2,1)}, bf16[72,1920]{1,0:T(8,128)(2,1)}, u32[]{:S(2)}, u32[]{:S(2)}) collective-permute-start(bf16[72,1920]{1,0:T(8,128)(2,1)} %shard_map.416.refs_5_.refs_0_), channel_id=1, source_target_pairs={{0,4},{1,5},{2,6},{3,7},{4,0},{5,1},{6,2},{7,3},{8,12},{9,13},{10,... | collective-permute-start | bytes 829448 | tf_op jit(solution)/shard_map/ppermute | solution.py:1263
  9.0 20.0 %collective-permute-start.2 = (bf16[72,1920]{1,0:T(8,128)(2,1)}, bf16[72,1920]{1,0:T(8,128)(2,1)}, u32[]{:S(2)}, u32[]{:S(2)}) collective-permute-start(bf16[72,1920]{1,0:T(8,128)(2,1)} %shard_map.416.refs_5_.refs_0_), channel_id=1, source_target_pairs={{0,6},{1,7},{2,4},{3,5},{4,2},{5,3},{6,0},{7,1},{8,14},{9,15},{10,... | collective-permute-start | bytes 829448 | tf_op jit(solution)/shard_map/ppermute | solution.py:1263
  12.8 23.3 %collective-permute-start.4 = (bf16[80,6144]{1,0:T(8,128)(2,1)}, bf16[80,6144]{1,0:T(8,128)(2,1)}, u32[]{:S(2)}, u32[]{:S(2)}) collective-permute-start(bf16[80,6144]{1,0:T(8,128)(2,1)} %shard_map.417.refs_2_.refs_4_.refs_5_), channel_id=1, source_target_pairs={{0,16},{8,24},{16,0},{24,8},{1,17},{9,25},{17,1},{25,9},{2,18},{10... | collective-permute-start | bytes 2949128 | tf_op jit(solution)/shard_map/ppermute | solution.py:1260
  14.6 22.8 %collective-permute-start.5 = (bf16[80,6144]{1,0:T(8,128)(2,1)}, bf16[80,6144]{1,0:T(8,128)(2,1)}, u32[]{:S(2)}, u32[]{:S(2)}) collective-permute-start(bf16[80,6144]{1,0:T(8,128)(2,1)} %shard_map.417.refs_2_.refs_4_.refs_5_), channel_id=1, source_target_pairs={{0,8},{8,0},{16,24},{24,16},{1,9},{9,1},{17,25},{25,17},{2,10},{10... | collective-permute-start | bytes 2949128 | tf_op jit(solution)/shard_map/ppermute | solution.py:1260
  19.0 22.6 %copy-start = (bf16[80,6144]{1,0:T(8,128)(2,1)S(1)}, bf16[80,6144]{1,0:T(8,128)(2,1)}, u32[]{:S(2)}) copy-start(bf16[80,6144]{1,0:T(8,128)(2,1)} %shard_map.417.refs_2_.refs_4_.refs_5_) | copy-start | bytes 2949124
  31.3 10.9 %collective-permute-start.3 = (bf16[4,72,1920]{2,1,0:T(8,128)(2,1)}, bf16[4,72,1920]{2,1,0:T(8,128)(2,1)}, u32[]{:S(2)}, u32[]{:S(2)}) collective-permute-start(bf16[4,72,1920]{2,1,0:T(8,128)(2,1)} %shard_map.419.refs_1_), channel_id=1, source_target_pairs={{0,1},{1,0},{2,3},{3,2},{4,5},{5,4},{6,7},{7,6},{8,9},{9,8},{10,11... | collective-permute-start | bytes 3317768 | tf_op jit(solution)/shard_map/ppermute | solution.py:1263
  39.5 13.5 %collective-permute-start.6 = (bf16[48,6144]{1,0:T(8,128)(2,1)}, bf16[48,6144]{1,0:T(8,128)(2,1)}, u32[]{:S(2)}, u32[]{:S(2)}) collective-permute-start(bf16[48,6144]{1,0:T(8,128)(2,1)} %get-tuple-element.105.refs_6_), channel_id=1, source_target_pairs={{0,8},{8,0},{16,24},{24,16},{1,9},{9,1},{17,25},{25,17},{2,10},{10... | collective-permute-start | bytes 1769480 | tf_op jit(solution)/shard_map/ppermute | solution.py:1260
  41.1 8.9 %collective-permute-start.7 = (bf16[32,6144]{1,0:T(8,128)(2,1)}, bf16[32,6144]{1,0:T(8,128)(2,1)}, u32[]{:S(2)}, u32[]{:S(2)}) collective-permute-start(bf16[32,6144]{1,0:T(8,128)(2,1)} %get-tuple-element.107), channel_id=1, source_target_pairs={{0,16},{8,24},{16,0},{24,8},{1,17},{9,25},{17,1},{25,9},{2,18},{10... | collective-permute-start | bytes 1179656 | tf_op jit(solution)/shard_map/ppermute | solution.py:1260
  41.6 14.2 %collective-permute-start.8 = (bf16[80,6144]{1,0:T(8,128)(2,1)S(1)}, bf16[80,6144]{1,0:T(8,128)(2,1)}, u32[]{:S(2)}, u32[]{:S(2)}) collective-permute-start(bf16[80,6144]{1,0:T(8,128)(2,1)S(1)} %copy-done), channel_id=1, source_target_pairs={{0,1},{1,0},{2,3},{3,2},{4,5},{5,4},{6,7},{7,6},{8,9},{9,8},{10,11... | collective-permute-start | bytes 2949128 | tf_op jit(solution)/shard_map/ppermute | solution.py:1263
  41.6 16.5 %collective-permute-start.10 = (bf16[80,6144]{1,0:T(8,128)(2,1)}, bf16[80,6144]{1,0:T(8,128)(2,1)}, u32[]{:S(2)}, u32[]{:S(2)}) collective-permute-start(bf16[80,6144]{1,0:T(8,128)(2,1)} %collective-permute-done.4.refs_0_.refs_4_.refs_6_.refs_7_), channel_id=1, source_target_pairs={{0,1},{1,0},{2,3},{3,2},{4,5},{5,4},{6,7},{7,6},{8,9},{9,8},{10,11... | collective-permute-start | bytes 2949128 | tf_op jit(solution)/shard_map/ppermute | solution.py:1263
  42.1 16.0 %collective-permute-start.9 = (bf16[80,6144]{1,0:T(8,128)(2,1)}, bf16[80,6144]{1,0:T(8,128)(2,1)}, u32[]{:S(2)}, u32[]{:S(2)}) collective-permute-start(bf16[80,6144]{1,0:T(8,128)(2,1)} %collective-permute-done.5.refs_1_.refs_3_.refs_5_.refs_6_), channel_id=1, source_target_pairs={{0,1},{1,0},{2,3},{3,2},{4,5},{5,4},{6,7},{7,6},{8,9},{9,8},{10,11... | collective-permute-start | bytes 2949128 | tf_op jit(solution)/shard_map/ppermute | solution.py:1263
  55.2 3.0 collective-permute-start.11
  55.3 2.9 collective-permute-start.12
  77.6 23.2 %collective-permute-start.13 = (bf16[80,5760]{1,0:T(8,128)(2,1)}, bf16[80,5760]{1,0:T(8,128)(2,1)}, u32[]{:S(2)}, u32[]{:S(2)}) collective-permute-start(bf16[80,5760]{1,0:T(8,128)(2,1)} %shard_map.425.refs_5_.refs_10_), channel_id=1, source_target_pairs={{0,8},{8,0},{16,24},{24,16},{1,9},{9,1},{17,25},{25,17},{2,10},{10... | collective-permute-start | bytes 2764808 | tf_op jit(solution)/shard_map/ppermute | solution.py:1260
  78.6 22.4 %collective-permute-start.14 = (bf16[80,5760]{1,0:T(8,128)(2,1)}, bf16[80,5760]{1,0:T(8,128)(2,1)}, u32[]{:S(2)}, u32[]{:S(2)}) collective-permute-start(bf16[80,5760]{1,0:T(8,128)(2,1)} %shard_map.425.refs_5_.refs_10_), channel_id=1, source_target_pairs={{0,16},{8,24},{16,0},{24,8},{1,17},{9,25},{17,1},{25,9},{2,18},{10... | collective-permute-start | bytes 2764808 | tf_op jit(solution)/shard_map/ppermute | solution.py:1260
  79.4 25.9 %copy-start.1 = (bf16[80,5760]{1,0:T(8,128)(2,1)S(1)}, bf16[80,5760]{1,0:T(8,128)(2,1)}, u32[]{:S(2)}) copy-start(bf16[80,5760]{1,0:T(8,128)(2,1)} %shard_map.425.refs_5_.refs_10_) | copy-start | bytes 2764804
  103.1 16.1 %collective-permute-start.15 = (bf16[48,5760]{1,0:T(8,128)(2,1)}, bf16[48,5760]{1,0:T(8,128)(2,1)}, u32[]{:S(2)}, u32[]{:S(2)}) collective-permute-start(bf16[48,5760]{1,0:T(8,128)(2,1)} %get-tuple-element.116), channel_id=1, source_target_pairs={{0,8},{8,0},{16,24},{24,16},{1,9},{9,1},{17,25},{25,17},{2,10},{10... | collective-permute-start | bytes 1658888 | tf_op jit(solution)/shard_map/ppermute | solution.py:1260
  104.8 14.4 %collective-permute-start.16 = (bf16[32,5760]{1,0:T(8,128)(2,1)}, bf16[32,5760]{1,0:T(8,128)(2,1)}, u32[]{:S(2)}, u32[]{:S(2)}) collective-permute-start(bf16[32,5760]{1,0:T(8,128)(2,1)} %get-tuple-element.117), channel_id=1, source_target_pairs={{0,16},{8,24},{16,0},{24,8},{1,17},{9,25},{17,1},{25,9},{2,18},{10... | collective-permute-start | bytes 1105928 | tf_op jit(solution)/shard_map/ppermute | solution.py:1260
  105.3 16.5 %collective-permute-start.17 = (bf16[80,5760]{1,0:T(8,128)(2,1)S(1)}, bf16[80,5760]{1,0:T(8,128)(2,1)}, u32[]{:S(2)}, u32[]{:S(2)}) collective-permute-start(bf16[80,5760]{1,0:T(8,128)(2,1)S(1)} %copy-done.1), channel_id=1, source_target_pairs={{0,1},{1,0},{2,3},{3,2},{4,5},{5,4},{6,7},{7,6},{8,9},{9,8},{10,11... | collective-permute-start | bytes 2764808 | tf_op jit(solution)/shard_map/ppermute | solution.py:1263
  105.3 18.8 %collective-permute-start.18 = (bf16[80,5760]{1,0:T(8,128)(2,1)}, bf16[80,5760]{1,0:T(8,128)(2,1)}, u32[]{:S(2)}, u32[]{:S(2)}) collective-permute-start(bf16[80,5760]{1,0:T(8,128)(2,1)} %collective-permute-done.13.refs_1_.refs_6_.refs_11_), channel_id=1, source_target_pairs={{0,1},{1,0},{2,3},{3,2},{4,5},{5,4},{6,7},{7,6},{8,9},{9,8},{10,11... | collective-permute-start | bytes 2764808 | tf_op jit(solution)/shard_map/ppermute | solution.py:1263
  105.8 18.3 %collective-permute-start.19 = (bf16[80,5760]{1,0:T(8,128)(2,1)}, bf16[80,5760]{1,0:T(8,128)(2,1)}, u32[]{:S(2)}, u32[]{:S(2)}) collective-permute-start(bf16[80,5760]{1,0:T(8,128)(2,1)} %collective-permute-done.14.refs_0_.refs_7_.refs_12_), channel_id=1, source_target_pairs={{0,1},{1,0},{2,3},{3,2},{4,5},{5,4},{6,7},{7,6},{8,9},{9,8},{10,11... | collective-permute-start | bytes 2764808 | tf_op jit(solution)/shard_map/ppermute | solution.py:1263
  121.3 2.9 collective-permute-start.20
  121.4 2.7 collective-permute-start.21
  161.8 11.7 %all-to-all-start.3 = ((f32[32,1,1408]{2,1,0:T(1,128)}), f32[32,1,1408]{2,1,0:T(1,128)S(1)}, u32[]{:S(2)}, u32[]{:S(2)}) async-start(f32[32,1,1408]{2,1,0:T(1,128)} %get-tuple-element.124), calls=%async_computation.3 | async-start | bytes 360448 | tf_op jit(solution)/shard_map/all_to_all | solution.py:1266
  164.9 34.3 %collective-permute-start.23 = (bf16[1152,640]{1,0:T(8,128)(2,1)}, bf16[1152,640]{1,0:T(8,128)(2,1)}, u32[]{:S(2)}, u32[]{:S(2)}) collective-permute-start(bf16[1152,640]{1,0:T(8,128)(2,1)} %get-tuple-element.131.refs_2_), channel_id=1, source_target_pairs={{0,1},{1,0},{2,3},{3,2},{4,5},{5,4},{6,7},{7,6},{8,9},{9,8},{10,11... | collective-permute-start | bytes 4423688 | tf_op jit(solution)/shard_map/ppermute | solution.py:1263
  173.5 0.7 copy-start.6
  195.7 3.6 collective-permute-start.22
  196.4 27.0 %collective-permute-start.25 = (bf16[1152,640]{1,0:T(8,128)(2,1)}, bf16[1152,640]{1,0:T(8,128)(2,1)}, u32[]{:S(2)}, u32[]{:S(2)}) collective-permute-start(bf16[1152,640]{1,0:T(8,128)(2,1)} %get-tuple-element.135.refs_2_), channel_id=1, source_target_pairs={{0,1},{1,0},{2,3},{3,2},{4,5},{5,4},{6,7},{7,6},{8,9},{9,8},{10,11... | collective-permute-start | bytes 4423688 | tf_op jit(solution)/shard_map/ppermute | solution.py:1263
  196.5 16.2 %all-to-all-start.4 = ((f32[32,1,1280]{2,1,0:T(1,128)}), f32[32,1,1280]{2,1,0:T(1,128)S(1)}, u32[]{:S(2)}, u32[]{:S(2)}) async-start(f32[32,1,1280]{2,1,0:T(1,128)} %get-tuple-element.128), calls=%async_computation.4 | async-start | bytes 327680 | tf_op jit(solution)/shard_map/all_to_all | solution.py:1266
  212.7 0.7 copy-start.7
  220.0 3.5 collective-permute-start.24
  220.3 17.6 %collective-permute-start.29 = (bf16[23,80,128]{2,1,0:T(8,128)(2,1)}, bf16[23,80,128]{2,1,0:T(8,128)(2,1)}, u32[]{:S(2)}, u32[]{:S(2)}) collective-permute-start(bf16[23,80,128]{2,1,0:T(8,128)(2,1)} %get-tuple-element.146), channel_id=1, source_target_pairs={{0,16},{8,24},{16,0},{24,8},{1,17},{9,25},{17,1},{25,9},{2,18},{10... | collective-permute-start | bytes 1413128 | tf_op jit(solution)/shard_map/ppermute | solution.py:1260
  222.0 15.9 %collective-permute-start.28 = (bf16[22,80,128]{2,1,0:T(8,128)(2,1)}, bf16[22,80,128]{2,1,0:T(8,128)(2,1)}, u32[]{:S(2)}, u32[]{:S(2)}) collective-permute-start(bf16[22,80,128]{2,1,0:T(8,128)(2,1)} %get-tuple-element.145), channel_id=1, source_target_pairs={{0,8},{8,0},{16,24},{24,16},{1,9},{9,1},{17,25},{25,17},{2,10},{10... | collective-permute-start | bytes 1351688 | tf_op jit(solution)/shard_map/ppermute | solution.py:1260
  223.4 0.9 copy-start.8
  240.8 41.1 %collective-permute-start.32 = (bf16[45,80,128]{2,1,0:T(8,128)(2,1)}, bf16[45,80,128]{2,1,0:T(8,128)(2,1)S(1)}, u32[]{:S(2)}, u32[]{:S(2)}) collective-permute-start(bf16[45,80,128]{2,1,0:T(8,128)(2,1)} %get-tuple-element.147.refs_16_), channel_id=1, source_target_pairs={{0,8},{8,0},{16,24},{24,16},{1,9},{9,1},{17,25},{25,17},{2,10},{10... | collective-permute-start | bytes 2764808 | tf_op jit(solution)/shard_map/ppermute | solution.py:1260
  241.8 40.1 %collective-permute-start.33 = (bf16[45,80,128]{2,1,0:T(8,128)(2,1)}, bf16[45,80,128]{2,1,0:T(8,128)(2,1)}, u32[]{:S(2)}, u32[]{:S(2)}) collective-permute-start(bf16[45,80,128]{2,1,0:T(8,128)(2,1)} %get-tuple-element.159), channel_id=1, source_target_pairs={{0,16},{8,24},{16,0},{24,8},{1,17},{9,25},{17,1},{25,9},{2,18},{10... | collective-permute-start | bytes 2764808 | tf_op jit(solution)/shard_map/ppermute | solution.py:1260
  243.3 34.0 %collective-permute-start.27 = (bf16[23,80,128]{2,1,0:T(8,128)(2,1)}, bf16[23,80,128]{2,1,0:T(8,128)(2,1)}, u32[]{:S(2)}, u32[]{:S(2)}) collective-permute-start(bf16[23,80,128]{2,1,0:T(8,128)(2,1)} %get-tuple-element.140), channel_id=1, source_target_pairs={{0,16},{8,24},{16,0},{24,8},{1,17},{9,25},{17,1},{25,9},{2,18},{10... | collective-permute-start | bytes 1413128 | tf_op jit(solution)/shard_map/ppermute | solution.py:1260
  243.8 33.4 %collective-permute-start.26 = (bf16[22,80,128]{2,1,0:T(8,128)(2,1)}, bf16[22,80,128]{2,1,0:T(8,128)(2,1)}, u32[]{:S(2)}, u32[]{:S(2)}) collective-permute-start(bf16[22,80,128]{2,1,0:T(8,128)(2,1)} %get-tuple-element.139), channel_id=1, source_target_pairs={{0,8},{8,0},{16,24},{24,16},{1,9},{9,1},{17,25},{25,17},{2,10},{10... | collective-permute-start | bytes 1351688 | tf_op jit(solution)/shard_map/ppermute | solution.py:1260
  280.0 23.3 %collective-permute-start.30 = (bf16[45,80,128]{2,1,0:T(8,128)(2,1)}, bf16[45,80,128]{2,1,0:T(8,128)(2,1)}, u32[]{:S(2)}, u32[]{:S(2)}) collective-permute-start(bf16[45,80,128]{2,1,0:T(8,128)(2,1)} %get-tuple-element.149.refs_16_), channel_id=1, source_target_pairs={{0,8},{8,0},{16,24},{24,16},{1,9},{9,1},{17,25},{25,17},{2,10},{10... | collective-permute-start | bytes 2764808 | tf_op jit(solution)/shard_map/ppermute | solution.py:1260
  281.1 22.4 %collective-permute-start.31 = (bf16[45,80,128]{2,1,0:T(8,128)(2,1)}, bf16[45,80,128]{2,1,0:T(8,128)(2,1)}, u32[]{:S(2)}, u32[]{:S(2)}) collective-permute-start(bf16[45,80,128]{2,1,0:T(8,128)(2,1)} %get-tuple-element.150), channel_id=1, source_target_pairs={{0,16},{8,24},{16,0},{24,8},{1,17},{9,25},{17,1},{25,9},{2,18},{10... | collective-permute-start | bytes 2764808 | tf_op jit(solution)/shard_map/ppermute | solution.py:1260
  281.9 0.9 copy-start.4
  285.5 24.2 %collective-permute-start.35 = (bf16[45,80,128]{2,1,0:T(8,128)(2,1)}, bf16[45,80,128]{2,1,0:T(8,128)(2,1)}, u32[]{:S(2)}, u32[]{:S(2)}) collective-permute-start(bf16[45,80,128]{2,1,0:T(8,128)(2,1)} %shard_map.437.refs_17_.refs_0_), channel_id=1, source_target_pairs={{0,2},{1,3},{6,4},{7,5},{8,10},{9,11},{14,12},{15,13},{16,18},{17,... | collective-permute-start | bytes 2764808 | tf_op jit(solution)/shard_map/ppermute | solution.py:1518
  302.4 11.3 %collective-permute-start.36 = (bf16[4,6,80,128]{3,2,1,0:T(8,128)(2,1)}, bf16[4,6,80,128]{3,2,1,0:T(8,128)(2,1)S(1)}, u32[]{:S(2)}, u32[]{:S(2)}) collective-permute-start(bf16[4,6,80,128]{3,2,1,0:T(8,128)(2,1)} %get-tuple-element.161), channel_id=1, source_target_pairs={{0,1},{1,0},{2,3},{3,2},{4,5},{5,4},{6,7},{7,6},{8,9},{9,8},{10,11... | collective-permute-start | bytes 1474568 | tf_op jit(solution)/shard_map/ppermute | solution.py:1263
  303.5 10.3 %copy-start.3 = (bf16[4,6,80,128]{3,2,1,0:T(8,128)(2,1)S(1)}, bf16[4,6,80,128]{3,2,1,0:T(8,128)(2,1)}, u32[]{:S(2)}) copy-start(bf16[4,6,80,128]{3,2,1,0:T(8,128)(2,1)} %get-tuple-element.160.refs_3_) | copy-start | bytes 1474564
  306.2 22.2 %collective-permute-start.34 = (bf16[45,80,128]{2,1,0:T(8,128)(2,1)}, bf16[45,80,128]{2,1,0:T(8,128)(2,1)}, u32[]{:S(2)}, u32[]{:S(2)}) collective-permute-start(bf16[45,80,128]{2,1,0:T(8,128)(2,1)} %shard_map.439.refs_2_.refs_0_), channel_id=1, source_target_pairs={{0,2},{1,3},{6,4},{7,5},{8,10},{9,11},{14,12},{15,13},{16,18},{17,... | collective-permute-start | bytes 2764808 | tf_op jit(solution)/shard_map/ppermute | solution.py:1518
  312.1 20.3 %collective-permute-start.43 = (bf16[45,80,128]{2,1,0:T(8,128)(2,1)}, bf16[45,80,128]{2,1,0:T(8,128)(2,1)}, u32[]{:S(2)}, u32[]{:S(2)}) collective-permute-start(bf16[45,80,128]{2,1,0:T(8,128)(2,1)} %shard_map.440.refs_2_.refs_0_), channel_id=1, source_target_pairs={{2,4},{3,5},{4,2},{5,3},{10,12},{11,13},{12,10},{13,11},{18,20},{1... | collective-permute-start | bytes 2764808 | tf_op jit(solution)/shard_map/ppermute | solution.py:1522
  313.9 6.2 %collective-permute-start.37 = (bf16[6,80,128]{2,1,0:T(8,128)(2,1)S(1)}, bf16[6,80,128]{2,1,0:T(8,128)(2,1)S(1)}, u32[]{:S(2)}, u32[]{:S(2)}) collective-permute-start(bf16[6,80,128]{2,1,0:T(8,128)(2,1)S(1)} %get-tuple-element.187), channel_id=1, source_target_pairs={{0,8},{8,0},{16,24},{24,16},{1,9},{9,1},{17,25},{25,17},{2,10},{10... | collective-permute-start | bytes 368648 | tf_op jit(solution)/shard_map/ppermute | solution.py:1260
  315.3 7.0 %collective-permute-start.38 = (bf16[6,80,128]{2,1,0:T(8,128)(2,1)S(1)}, bf16[6,80,128]{2,1,0:T(8,128)(2,1)S(1)}, u32[]{:S(2)}, u32[]{:S(2)}) collective-permute-start(bf16[6,80,128]{2,1,0:T(8,128)(2,1)S(1)} %get-tuple-element.189), channel_id=1, source_target_pairs={{0,16},{8,24},{16,0},{24,8},{1,17},{9,25},{17,1},{25,9},{2,18},{10... | collective-permute-start | bytes 368648 | tf_op jit(solution)/shard_map/ppermute | solution.py:1260
  316.3 6.0 %collective-permute-start.39 = (bf16[6,80,128]{2,1,0:T(8,128)(2,1)S(1)}, bf16[6,80,128]{2,1,0:T(8,128)(2,1)S(1)}, u32[]{:S(2)}, u32[]{:S(2)}) collective-permute-start(bf16[6,80,128]{2,1,0:T(8,128)(2,1)S(1)} %get-tuple-element.188), channel_id=1, source_target_pairs={{0,24},{8,16},{16,8},{24,0},{1,25},{9,17},{17,9},{25,1},{2,26},{10... | collective-permute-start | bytes 368648 | tf_op jit(solution)/shard_map/ppermute | solution.py:1260
  330.8 15.8 %collective-permute-start.40 = (bf16[45,80,128]{2,1,0:T(8,128)(2,1)}, bf16[45,80,128]{2,1,0:T(8,128)(2,1)}, u32[]{:S(2)}, u32[]{:S(2)}) collective-permute-start(bf16[45,80,128]{2,1,0:T(8,128)(2,1)} %shard_map.441.refs_2_.refs_0_), channel_id=1, source_target_pairs={{2,4},{3,5},{4,2},{5,3},{10,12},{11,13},{12,10},{13,11},{18,20},{1... | collective-permute-start | bytes 2764808 | tf_op jit(solution)/shard_map/ppermute | solution.py:1636
  334.8 23.5 %collective-permute-start.44 = (bf16[45,80,128]{2,1,0:T(8,128)(2,1)}, bf16[45,80,128]{2,1,0:T(8,128)(2,1)S(1)}, u32[]{:S(2)}, u32[]{:S(2)}) collective-permute-start(bf16[45,80,128]{2,1,0:T(8,128)(2,1)} %shard_map.442.refs_1_.refs_2_), channel_id=1, source_target_pairs={{2,0},{3,1},{4,6},{5,7},{10,8},{11,9},{12,14},{13,15},{18,16},{19,... | collective-permute-start | bytes 2764808 | tf_op jit(solution)/shard_map/ppermute | solution.py:1525
  336.1 8.2 %collective-permute-start.41 = (bf16[6,80,128]{2,1,0:T(8,128)(2,1)}, bf16[6,80,128]{2,1,0:T(8,128)(2,1)S(1)}, u32[]{:S(2)}, u32[]{:S(2)}) collective-permute-start(bf16[6,80,128]{2,1,0:T(8,128)(2,1)} %fusion.2.refs_3_), channel_id=1, source_target_pairs={{0,2},{1,3},{6,4},{7,5},{8,10},{9,11},{14,12},{15,13},{16,18},{17,... | collective-permute-start | bytes 368648 | tf_op jit(solution)/shard_map/ppermute | solution.py:1518
  345.2 0.7 collective-permute-start.42
  358.3 0.9 copy-start.2
  364.4 2.8 collective-permute-start.45
  364.5 29.3 %collective-permute-start.46 = (bf16[51,80,128]{2,1,0:T(8,128)(2,1)}, bf16[51,80,128]{2,1,0:T(8,128)(2,1)}, u32[]{:S(2)}, u32[]{:S(2)}) collective-permute-start(bf16[51,80,128]{2,1,0:T(8,128)(2,1)} %shard_map.443.refs_3_.refs_1_), channel_id=1, source_target_pairs={{2,0},{3,1},{4,6},{5,7},{10,8},{11,9},{12,14},{13,15},{18,16},{19,... | collective-permute-start | bytes 3133448 | tf_op jit(solution)/shard_map/ppermute | solution.py:1525
  367.2 0.9 copy-start.5
  396.7 3.1 collective-permute-start.47

commit v5 on v4

--- a/solution.py
+++ b/solution.py
@@ -145,7 +145,8 @@
 
 def cast_kernel(layer, *refs):
     ids, weights = refs[0:2]
-    out, wide, narrow, in_sems, out_sems = refs[-5:]
+    wide, narrow, in_sems, out_sems = refs[-4:]
+    out = refs[5] if layer == 0 else refs[2]
     rows = out.shape[0]
     cols = wide.shape[1]
     parts = rows // 16
@@ -163,6 +164,7 @@
         total = pack_lanes(*refs[2:5])
         mine = jnp.where(ids[2] == 0, total[0:rows], total[rows : 2 * rows])
         narrow[:, cols : cols + WIDE] = mine.astype(half)
+        refs[6][...] = total.astype(half)
     outputs = []
     for part in range(parts):
         here = slice(part * 16, part * 16 + 16)
@@ -177,10 +179,11 @@
     rows = conv_w.shape[1] // 2
     cols = conv_w.shape[2]
     total = cols + WIDE if layer == 0 else cols
-    (result,) = call(
+    return call(
         functools.partial(cast_kernel, layer),
         [SMEM, ANY] + [VMEM] * len(packed),
-        [(shape((rows, total), half), ANY)],
+        [(shape((rows, total), half), ANY)]
+        + ([(shape((2 * rows, WIDE), half), VMEM)] if layer == 0 else []),
         [
             pltpu.VMEM((rows, cols), full),
             pltpu.VMEM((rows, total), half),
@@ -190,7 +193,6 @@
         3,
         len(after),
     )(ids, conv_w, *packed, *after)
-    return result
 
 
 def hold_kernel(*refs):
@@ -299,14 +301,16 @@
     copies = []
     for index, (start, size) in enumerate(places):
         copies.append(
-            fetch(refs[index].at[start : start + size], outs[index], sems.at[index])
+            fetch(
+                refs[index].at[start : start + size, 0 : 9 * C3], outs[index], sems.at[index]
+            )
         )
     for copy in copies:
         copy.wait()
 
 
 def cut_rows(values, places, after):
-    cols = values[0].shape[1]
+    cols = 9 * C3
     return call(
         functools.partial(cut_kernel, places),
         [ANY] * len(values),
@@ -428,11 +432,26 @@
 
 def base_kernel(*refs):
     ids, act_three = refs[0:2]
-    pieces = refs[2:12]
-    base, stats, norm_rows, head_all, proj_t, gathered, held, totals, sems, out_sems = refs[12:]
+    pieces = refs[2:8]
+    far_pack = refs[8]
+    base, stats, norm_rows, head_all, proj_t, gathered, held, totals, sems, out_sems = refs[9:]
     rows = act_three.shape[0]
-    lanes = pl.ds(pieces[0].shape[1] - WIDE, WIDE)
-    for copy in start_weights(ids, pieces, gathered, sems, lanes):
+    tall = pieces[0].shape[0]
+    spot = pl.multiple_of((ids[0] ^ 3) * (2 * tall), 16)
+    copies = [fetch(far_pack, gathered.at[pl.ds(spot, 2 * tall)], sems.at[6])]
+    for side in range(2):
+        for turn in range(3):
+            piece = pieces[3 * side + turn]
+            lanes = pl.ds(piece.shape[1] - WIDE, WIDE)
+            spot = (ids[0] ^ turn) * (2 * tall) + (ids[2] ^ side) * tall
+            copies.append(
+                fetch(
+                    piece.at[:, lanes],
+                    gathered.at[pl.ds(pl.multiple_of(spot, 16), tall)],
+                    sems.at[3 * side + turn],
+                )
+            )
+    for copy in copies:
         copy.wait()
     column = iota((1, WIDE), 1)
     packed = gathered[...]
@@ -487,7 +506,7 @@
     return lax.fori_loop(part * step, (part + 1) * step, body, carry)
 
 
-def start_weights(ids, pieces, weights, sems, lanes=pl.ds(0, 9 * C3)):
+def start_weights(ids, pieces, weights, sems):
     rows = pieces[0].shape[0]
     low = pieces[3].shape[0]
     copies = []
@@ -501,7 +520,7 @@
             spot = pl.multiple_of(spot, 16)
             copies.append(
                 fetch(
-                    piece.at[:, lanes],
+                    piece.at[:, 0 : 9 * C3],
                     weights.at[pl.ds(spot, piece.shape[0])],
                     sems.at[5 * side + place],
                 )
@@ -1286,15 +1305,17 @@
         rows = pieces[0].shape[0]
         return cut_rows(pieces[:0:-1], [(0, 48), (48, rows - 48)], after)
 
-    def end_gather(pieces, far, after=()):
+    def cross(pieces):
+        return [over_filt(piece, 1) for piece in pieces]
+
+    def end_gather(pieces, crossed, far, after):
         far = [over_dp(far[0], 1), over_dp(far[1], 2)]
-        if after:
-            far = cut_rows(far, [(0, piece.shape[0]) for piece in far], after)
-        pieces = [*pieces, *far]
-        return pieces + [over_filt(piece, 1) for piece in pieces]
-
-    own_one = cast_half(ids, conv_w, 0, [proj_c.T, head_w.T, norm_p], [own_images])
-    own_two = cast_half(ids, conv_w, 1, [], [own_one])
+        far = cut_rows(far, [(0, piece.shape[0]) for piece in far], after)
+        return [*pieces, *far, *crossed, *cross(far)]
+
+    own_one, own_pack = cast_half(ids, conv_w, 0, [proj_c.T, head_w.T, norm_p], [own_images])
+    (own_two,) = cast_half(ids, conv_w, 1, [], [own_one])
+    far_pack = over_dp(own_pack, 3)
     pieces = start_gather(own_one)
     far = middle_gather(pieces, [])
     all_images = stack(
@@ -1325,10 +1346,10 @@
         10,
         1,
     )(ids, all_images, over_filt(all_images, 1), stem_w.T, proj_a, proj_b, far[0])
-    kernels = [end_gather(pieces, far, [facts])]
+    crossed = cross(pieces)
     base, stats, norm_rows, head_all, proj_t = call(
         base_kernel,
-        [SMEM, VMEM] + [ANY] * 10,
+        [SMEM, VMEM] + [ANY] * 7,
         [
             (shape((rows, C3)), ANY),
             (line, VMEM),
@@ -1344,7 +1365,8 @@
             pltpu.SemaphoreType.DMA((QUARTERS,)),
         ],
         4,
-    )(ids, act_three, *kernels[0])
+    )(ids, act_three, *pieces, *crossed, far_pack)
+    kernels = [end_gather(pieces, crossed, far, [stats])]
     stats_one = exchange(stats)
     pieces = start_gather(hold(own_two, stats_one))
 
@@ -1374,7 +1396,7 @@
     )(ids, base, stats_one, norm_rows, *kernels[0])
     far = middle_gather(pieces, [stats])
     stats_two = exchange(stats)
-    kernels.append(end_gather(pieces, far, [stats_two]))
+    kernels.append(end_gather(pieces, cross(pieces), far, [stats_two]))
     far_field_one = over_filt(field_one, 1)
     summed, field_two, slope_two, stats = call(
         functools.partial(conv_kernel, (per, row_total, split), 1),
@@ -1639,8 +1661,7 @@
     plan = [(place, 0, 0, blocks) for place in range(len(terms))]
     plan.append((len(terms), 0, blocks, 6))
     (whole_one,) = merge([*terms, small_sum], [(blocks + 6, plan)], [arrived_two], 0.1)
-    reduced_two = from_middles(whole_two, last, [whole_one], arrived_two)
-    far_two = over_filt(reduced_two, 1)
+    arrived_one = outward(whole_one, last)
     squares, grad_norm_p, loss = call(
         functools.partial(norm_kernel, (devices, chips, split)),
         [SMEM] + [VMEM] * 5,
@@ -1651,10 +1672,11 @@
         ],
         [pltpu.VMEM((8, C3), full)],
         3,
-        1,
-    )(ids, whole_one, whole_two, stats_six, stats_five, stats_four, far_two)
+    )(ids, whole_one, whole_two, stats_six, stats_five, stats_four)
+    reduced_two = from_middles(whole_two, last, [squares], arrived_two)
+    far_two = over_filt(reduced_two, 1)
     squares = exchange(squares)
-    reduced_one = from_middles(whole_one, last, [squares])
+    reduced_one = from_middles(whole_one, last, [squares, far_two], arrived_one)
 
     pieces = []
     places = []

time: 427 us -> 421 us (0.986)
  blocking collectives: 75.2 us -> 57.3 us
  starting transfers between devices: 56.4 us -> 64.2 us
    all_to_all x5 -> x4, blocking collectives: 75.2 us -> 57.3 us  [exchange(): return lax.all_to_all(stats, ('dp', 'filt'), 0, 0)]
    all_to_all x2 -> x3, starting transfers between devices: 5.87 us -> 13.8 us  [exchange(): return lax.all_to_all(stats, ('dp', 'filt'), 0, 0)]
    ppermute x19 -> x20, waiting for transfers between devices: 19.1 us -> 12 us  [over_dp(): return lax.ppermute(value, 'dp', xor_pairs(split, turn))]
    all_to_all x2 -> x3, waiting for transfers between devices: 8.24 us -> 14 us  [exchange(): return lax.all_to_all(stats, ('dp', 'filt'), 0, 0)]
    ppermute x19 -> x20, starting transfers between devices: 22 us -> 22.6 us  [over_dp(): return lax.ppermute(value, 'dp', xor_pairs(split, turn))]
  transfers between devices with their start and end apart: 50 -> 52, of which waited for: 19 -> 16; matrix products, arithmetic and copies ran while one was open for 1% -> 1% of each run, Pallas kernels for 35% -> 36%
where the time goes in v5:
time: 421 us; the launch traced here: 415 us
  Pallas kernels  214 us (51%)
  waiting for transfers between devices  68.2 us (16%)
  starting transfers between devices  64.2 us (15%)
  blocking collectives  57.3 us (14%)
  local copies, waits for them, and re-layouts  6.6 us (2%)
    all_to_all x4, blocking collectives, exchange(): return lax.all_to_all(stats, ('dp', 'filt'), 0, 0)  57.3 us
    pallas_call x2, Pallas kernels, back(): call(functools.partial(back_kernel, (per, row_total, split), layer), ([SM...  40.1 us
    pallas_call x2, Pallas kernels, weight_grad(): call(functools.partial(weight_grad_kernel, (chunks, split, band)), [ANY]...  27 us
    ppermute x20, starting transfers between devices, over_dp(): return lax.ppermute(value, 'dp', xor_pairs(split, turn))  22.6 us
    ppermute x21, waiting for transfers between devices, over_filt(): return lax.ppermute(value, 'filt', xor_pairs(groups, turn))  22.2 us
    pallas_call x1, Pallas kernels, shards(): pl.pallas_call(functools.partial(conv_update_kernel, (len(pieces), places...  20.8 us
    pallas_call x8, Pallas kernels, merge(): call(functools.partial(merge_kernel, plan, len(values)), [ANY] * len(valu...  20.7 us
    pallas_call x1, Pallas kernels, shards(): call(functools.partial(conv_kernel, (per, row_total, split), 1), [SMEM, A...  18.6 us
  transfers between devices with their start and end apart: 52, of which 16 were waited for; matrix products, arithmetic and copies ran while one was open for 1% of the time, Pallas kernels for 36%

profile of v5, /device:TPU:0, one launch (start us, length us, event | category | flops | bytes accessed | tf_op | source)
XLA Modules:
  0.0 415.1 jit_solution(8701732999910686397)
XLA Ops:
  1.3 2.7 shard_map.416.refs_5_.refs_0_
  4.1 3.9 shard_map.417
  8.0 3.0 collective-permute-start.5
  11.0 1.5 collective-permute-start.4
  12.5 1.6 collective-permute-start
  14.1 2.6 collective-permute-start.1
  16.9 2.9 shard_map.418.refs_4_.refs_0_
  19.8 5.7 %collective-permute-done.refs_1_ = bf16[72,1920]{1,0:T(8,128)(2,1)} collective-permute-done((bf16[72,1920]{1,0:T(8,128)(2,1)}, bf16[72,1920]{1,0:T(8,128)(2,1)}, u32[]{:S(2)}, u32[]{:S(2)}) %collective-permute-start) | collective-permute-done | bytes 276512 | tf_op jit(solution)/shard_map/ppermute | solution.py:1282
  25.5 11.2 %collective-permute-done.1.refs_2_ = bf16[72,1920]{1,0:T(8,128)(2,1)} collective-permute-done((bf16[72,1920]{1,0:T(8,128)(2,1)}, bf16[72,1920]{1,0:T(8,128)(2,1)}, u32[]{:S(2)}, u32[]{:S(2)}) %collective-permute-start.1) | collective-permute-done | bytes 276512 | tf_op jit(solution)/shard_map/ppermute | solution.py:1282
  36.7 2.2 shard_map.419.refs_1_
  40.5 2.1 shard_map.420
  42.6 4.0 collective-permute-done.9.refs_8_
  47.6 6.8 %shard_map.421 = (bf16[1152,32]{1,0:T(8,128)(2,1)}, f32[1152,16]{1,0:T(8,128)}, f32[1152,160]{1,0:T(8,128)}, f32[1152,384]{1,0:T(8,128)}, bf16[1152,384]{1,0:T(8,128)(2,1)}, /*index=5*/f32[18,128]{1,0:T(8,128)}) custom-call(s32[4]{0:T(128)} %pad_add_fusion.refs_0_, bf16[4,72,1920]{2,1,0:T(8,128)(2,1)} %shard_map.419.refs_1_, ...), custom_call_target="tpu_custom_call" | custom-call | flops 3500000000 | bytes 1 | tf_op jit(solution)/shard_map/pallas_call | solution.py:1329
  54.4 5.8 %shard_map.422 = (f32[1152,640]{1,0:T(8,128)}, f32[32,1,1280]{2,1,0:T(1,128)}, f32[8,640]{1,0:T(8,128)}, bf16[640,16]{1,0:T(8,128)(2,1)}, bf16[640,384]{1,0:T(8,128)(2,1)}) custom-call(s32[4]{0:T(128)} %pad_add_fusion.refs_0_, bf16[1152,384]{1,0:T(8,128)(2,1)} %get-tuple-element.109.refs_1_.refs_8_, ...), custom_call_target="tpu_custom_call" | custom-call | flops 1400000000 | bytes 1 | tf_op jit(solution)/shard_map/pallas_call | solution.py:1350
  60.2 8.0 %all-to-all-start = ((f32[32,1,1280]{2,1,0:T(1,128)}), f32[32,1,1280]{2,1,0:T(1,128)S(1)}, u32[]{:S(2)}, u32[]{:S(2)}) async-start(f32[32,1,1280]{2,1,0:T(1,128)} %get-tuple-element.112.refs_2_), calls=%async_computation | async-start | bytes 327680 | tf_op jit(solution)/shard_map/all_to_all | solution.py:1285
  68.2 2.1 shard_map.423
  70.9 5.7 %all-to-all-done.refs_2_.refs_1_.refs_4_ = f32[32,1,1280]{2,1,0:T(1,128)S(1)} async-done(((f32[32,1,1280]{2,1,0:T(1,128)}), f32[32,1,1280]{2,1,0:T(1,128)S(1)}, u32[]{:S(2)}, u32[]{:S(2)}) %all-to-all-start) | async-done | bytes 163872 | tf_op jit(solution)/shard_map/all_to_all | solution.py:1285
  79.9 18.5 %shard_map.424 = (f32[1152,640]{1,0:T(8,128)}, bf16[1152,640]{1,0:T(8,128)(2,1)}, f32[1152,640]{1,0:T(8,128)}, f32[32,1,1280]{2,1,0:T(1,128)}) custom-call(s32[4]{0:T(128)} %pad_add_fusion.refs_0_, f32[1152,640]{1,0:T(8,128)} %get-tuple-element.111.refs_1_.refs_4_.refs_2_.refs_3_, f32[32,1,1280]{2,1,0:T(1,128)} %copy-done.5, ...), custom_call_target="tpu_custom_call" | custom-call | flops 6300000256 | bytes 1 | tf_op jit(solution)/shard_map/pallas_call | solution.py:1390
  98.4 2.0 collective-permute-done.14.refs_1_.refs_6_.refs_11_
  100.6 2.1 shard_map.426
  102.7 1.7 collective-permute-start.16
  105.4 13.3 %all_to_all.35.refs_2_.refs_9_.refs_3_ = f32[32,1,1280]{2,1,0:T(1,128)} all-to-all(f32[32,1,1280]{2,1,0:T(1,128)} %get-tuple-element.118.refs_2_), channel_id=1, replica_groups=mesh['dp'=4,'filt'=8] {'dp','filt'}, dimensions={0} | all-to-all | bytes 327680 | tf_op jit(solution)/shard_map/all_to_all | solution.py:1285
  118.8 2.1 shard_map.427
  121.4 2.3 collective-permute-done.22.refs_14_.refs_19_
  123.8 18.6 %shard_map.428 = (f32[1152,640]{1,0:T(8,128)}, bf16[1152,640]{1,0:T(8,128)(2,1)}, f32[1152,640]{1,0:T(8,128)}, f32[32,1,1280]{2,1,0:T(1,128)}) custom-call(s32[4]{0:T(128)} %pad_add_fusion.refs_0_, f32[1152,640]{1,0:T(8,128)} %get-tuple-element.117.refs_1_.refs_7_.refs_2_, f32[32,1,1280]{2,1,0:T(1,128)} %all_to_all.35.refs_2_.refs_9_.refs_3_, ...), custom_call_target="tpu_custom_call" | custom-call | flops 6300000256 | bytes 1 | tf_op jit(solution)/shard_map/pallas_call | solution.py:1401
  142.4 11.9 %all_to_all.36.refs_1_.refs_3_ = f32[32,1,1280]{2,1,0:T(1,128)} all-to-all(f32[32,1,1280]{2,1,0:T(1,128)} %get-tuple-element.124), channel_id=1, replica_groups=mesh['dp'=4,'filt'=8] {'dp','filt'}, dimensions={0} | all-to-all | bytes 327680 | tf_op jit(solution)/shard_map/all_to_all | solution.py:1285
  154.4 7.1 %shard_map.429 = (f32[1152,640]{1,0:T(8,128)}, f32[144,640]{1,0:T(8,128)}, f32[32,1,1408]{2,1,0:T(1,128)}, f32[640,16]{1,0:T(8,128)}) custom-call(f32[1152,640]{1,0:T(8,128)} %get-tuple-element.123.refs_0_.refs_2_, f32[32,1,1280]{2,1,0:T(1,128)} %all_to_all.36.refs_1_.refs_3_, f32[8,640]{1,0:T(8,128)} %get-tuple-element.113.refs_3_.refs_2_.refs_5_.refs_6_, ...), custom_call_target="tpu_custom_call" | custom-call | flops 2449999872 | bytes 1 | tf_op jit(solution)/shard_map/pallas_call | solution.py:1410
  161.4 3.1 all-to-all-start.3
  164.9 8.2 %all-to-all-done.3.refs_4_.refs_5_ = f32[32,1,1408]{2,1,0:T(1,128)S(1)} async-done(((f32[32,1,1408]{2,1,0:T(1,128)}), f32[32,1,1408]{2,1,0:T(1,128)S(1)}, u32[]{:S(2)}, u32[]{:S(2)}) %all-to-all-start.3) | async-done | bytes 180256 | tf_op jit(solution)/shard_map/all_to_all | solution.py:1285
  173.8 21.5 %shard_map.430 = (f32[1152,640]{1,0:T(8,128)}, f32[32,1,1280]{2,1,0:T(1,128)}, bf16[1152,384]{1,0:T(8,128)(2,1)}, bf16[1152,384]{1,0:T(8,128)(2,1)}, f32[1152,640]{1,0:T(8,128)}) custom-call(s32[4]{0:T(128)} %pad_add_fusion.refs_0_, f32[1152,640]{1,0:T(8,128)} %get-tuple-element.127.refs_1_, f32[1152,640]{1,0:T(8,128)} %get-tuple-element.123.refs_0_.refs_2_, ...), custom_call_target="tpu_custom_call" | custom-call | flops 7699999744 | bytes 1 | tf_op jit(solution)/shard_map/pallas_call | solution.py:1432
  196.2 2.8 all-to-all-start.4
  199.0 13.5 %shard_map.431 = (bf16[45,80,128]{2,1,0:T(8,128)(2,1)}, bf16[45,80,128]{2,1,0:T(8,128)(2,1)}, bf16[45,80,128]{2,1,0:T(8,128)(2,1)}, bf16[22,80,128]{2,1,0:T(8,128)(2,1)}, bf16[23,80,128]{2,1,0:T(8,128)(2,1)}) custom-call(bf16[1152,384]{1,0:T(8,128)(2,1)} %get-tuple-element.133.refs_0_, bf16[1152,384]{1,0:T(8,128)(2,1)} %collective-permute-done.23.refs_1_, ...), custom_call_target="tpu_custom_call" | custom-call | flops 4550000128 | bytes 1 | tf_op jit(solution)/shard_map/pallas_call | solution.py:1471
  213.1 6.5 %shard_map.432 = (bf16[1152,640]{1,0:T(8,128)(2,1)}, bf16[1152,384]{1,0:T(8,128)(2,1)}, bf16[1152,384]{1,0:T(8,128)(2,1)}) custom-call(s32[4]{0:T(128)} %pad_add_fusion.refs_0_, f32[1152,640]{1,0:T(8,128)} %get-tuple-element.131.refs_1_, f32[1152,640]{1,0:T(8,128)} %get-tuple-element.117.refs_1_.refs_7_.refs_2_, ...), custom_call_target="tpu_custom_call" | custom-call | flops 2100000000 | bytes 1 | tf_op jit(solution)/shard_map/pallas_call | solution.py:1575
  220.0 1.7 collective-permute-start.30
  221.7 1.5 collective-permute-start.29
  224.1 13.5 %shard_map.433 = (bf16[45,80,128]{2,1,0:T(8,128)(2,1)}, bf16[45,80,128]{2,1,0:T(8,128)(2,1)}, bf16[45,80,128]{2,1,0:T(8,128)(2,1)}, bf16[22,80,128]{2,1,0:T(8,128)(2,1)}, bf16[23,80,128]{2,1,0:T(8,128)(2,1)}) custom-call(bf16[1152,384]{1,0:T(8,128)(2,1)} %get-tuple-element.137.refs_0_, bf16[1152,384]{1,0:T(8,128)(2,1)} %copy-done.9, ...), custom_call_target="tpu_custom_call" | custom-call | flops 4550000128 | bytes 1 | tf_op jit(solution)/shard_map/pallas_call | solution.py:1471
  237.6 2.8 shard_map.434
  241.4 1.5 collective-permute-start.34
  244.5 18.6 %shard_map.435 = (f32[1152,640]{1,0:T(8,128)}, f32[32,1,1280]{2,1,0:T(1,128)}) custom-call(s32[4]{0:T(128)} %pad_add_fusion.refs_0_, bf16[1152,640]{1,0:T(8,128)(2,1)} %get-tuple-element.145.refs_1_, f32[1152,640]{1,0:T(8,128)} %get-tuple-element.111.refs_1_.refs_4_.refs_2_.refs_3_, f32[1152,640]{1,0:T(8,128)} %get-tuple-element.146.refs_3_, ...), custom_call_target="tpu_custom_call" | custom-call | flops 7699999744 | bytes 1 | tf_op jit(solution)/shard_map/pallas_call | solution.py:1432
  263.1 13.8 %all_to_all.37.refs_4_.refs_3_.refs_5_ = f32[32,1,1280]{2,1,0:T(1,128)} all-to-all(f32[32,1,1280]{2,1,0:T(1,128)} %get-tuple-element.152), channel_id=1, replica_groups=mesh['dp'=4,'filt'=8] {'dp','filt'}, dimensions={0} | all-to-all | bytes 327680 | tf_op jit(solution)/shard_map/all_to_all | solution.py:1285
  276.9 2.8 shard_map.436
  282.5 2.7 shard_map.437.refs_17_.refs_0_
  285.2 3.6 collective-permute-start.36
  288.8 13.3 %shard_map.438 = (bf16[4,6,80,128]{3,2,1,0:T(8,128)(2,1)}, bf16[4,6,80,128]{3,2,1,0:T(8,128)(2,1)}) custom-call(s32[4]{0:T(128)} %pad_add_fusion.refs_0_, f32[1152,640]{1,0:T(8,128)} %get-tuple-element.155.refs_1_, f32[1152,640]{1,0:T(8,128)} %get-tuple-element.156.refs_2_, f32[1152,640]{1,0:T(8,128)} %get-tuple-element.111.refs_1_.refs_4_.refs_2_.refs_3_, ...), custom_call_target="tpu_custom_call" | custom-call | flops 35000000 | bytes 1 | tf_op jit(solution)/shard_map/pallas_call | solution.py:1607
  303.1 2.8 shard_map.439.refs_2_.refs_0_
  305.9 3.5 collective-permute-start.35
  309.4 2.4 shard_map.440.refs_2_.refs_0_
  311.8 1.6 collective-permute-start.44
  317.0 2.7 collective-permute-done.38
  319.7 2.2 collective-permute-done.39
  322.6 5.5 %collective-permute-done.35.refs_1_ = bf16[45,80,128]{2,1,0:T(8,128)(2,1)} collective-permute-done((bf16[45,80,128]{2,1,0:T(8,128)(2,1)}, bf16[45,80,128]{2,1,0:T(8,128)(2,1)}, u32[]{:S(2)}, u32[]{:S(2)}) %collective-permute-start.35) | collective-permute-done | bytes 921632 | tf_op jit(solution)/shard_map/ppermute | solution.py:1540
  328.1 2.4 shard_map.441.refs_2_.refs_0_
  330.5 1.6 collective-permute-start.41
  332.1 2.4 shard_map.442.refs_2_.refs_1_
  335.8 5.4 %collective-permute-start.42 = (bf16[6,80,128]{2,1,0:T(8,128)(2,1)}, bf16[6,80,128]{2,1,0:T(8,128)(2,1)S(1)}, u32[]{:S(2)}, u32[]{:S(2)}) collective-permute-start(bf16[6,80,128]{2,1,0:T(8,128)(2,1)} %fusion.2.refs_3_), channel_id=1, source_target_pairs={{0,2},{1,3},{6,4},{7,5},{8,10},{9,11},{14,12},{15,13},{16,18},{17,... | collective-permute-start | bytes 368648 | tf_op jit(solution)/shard_map/ppermute | solution.py:1540
  341.2 2.7 collective-permute-done.42
  346.2 11.7 %collective-permute-done.45.refs_3_.refs_2_ = bf16[45,80,128]{2,1,0:T(8,128)(2,1)S(1)} collective-permute-done((bf16[45,80,128]{2,1,0:T(8,128)(2,1)}, bf16[45,80,128]{2,1,0:T(8,128)(2,1)S(1)}, u32[]{:S(2)}, u32[]{:S(2)}) %collective-permute-start.45) | collective-permute-done | bytes 921632 | tf_op jit(solution)/shard_map/ppermute | solution.py:1547
  358.9 2.4 shard_map.443.refs_1_
  362.6 3.2 shard_map.444
  365.8 2.8 shard_map.445.refs_26_
  368.7 18.3 %all_to_all.38.refs_3_.refs_1_ = f32[32,1,128]{2,1,0:T(1,128)} all-to-all(f32[32,1,128]{2,1,0:T(1,128)} %get-tuple-element.166.refs_3_), channel_id=1, replica_groups=mesh['dp'=4,'filt'=8] {'dp','filt'}, dimensions={0} | all-to-all | bytes 32768 | tf_op jit(solution)/shard_map/all_to_all | solution.py:1285
  387.9 2.9 shard_map.446.refs_24_
  390.9 3.0 collective-permute-done.48.refs_25_
  393.8 20.8 %shard_map.447 = (f32[2,160,5760]{2,1,0:T(8,128)}, f32[2,160,5760]{2,1,0:T(8,128)}, f32[2,160,5760]{2,1,0:T(8,128)}, f32[16,27]{1,0:T(8,128)}, f32[16,27]{1,0:T(...) custom-call(s32[4]{0:T(128)} %pad_add_fusion.refs_0_, ...), custom_call_target="tpu_custom_call" | custom-call | flops 36864000 | bytes 47923200 | tf_op jit(solution)/shard_map/pallas_call | solution.py:1706
  (105 shorter events, 30.6 us)
Async XLA Ops:
  8.0 31.5 %collective-permute-start.5 = (bf16[80,6144]{1,0:T(8,128)(2,1)}, bf16[80,6144]{1,0:T(8,128)(2,1)}, u32[]{:S(2)}, u32[]{:S(2)}) collective-permute-start(bf16[80,6144]{1,0:T(8,128)(2,1)} %get-tuple-element.107.refs_2_.refs_4_.refs_5_), channel_id=1, source_target_pairs={{0,8},{8,0},{16,24},{24,16},{1,9},{9,1},{17,25},{25,17},{2,10},{10... | collective-permute-start | bytes 2949128 | tf_op jit(solution)/shard_map/ppermute | solution.py:1279
  11.0 28.6 %collective-permute-start.4 = (bf16[80,6144]{1,0:T(8,128)(2,1)}, bf16[80,6144]{1,0:T(8,128)(2,1)}, u32[]{:S(2)}, u32[]{:S(2)}) collective-permute-start(bf16[80,6144]{1,0:T(8,128)(2,1)} %get-tuple-element.107.refs_2_.refs_4_.refs_5_), channel_id=1, source_target_pairs={{0,16},{8,24},{16,0},{24,8},{1,17},{9,25},{17,1},{25,9},{2,18},{10... | collective-permute-start | bytes 2949128 | tf_op jit(solution)/shard_map/ppermute | solution.py:1279
  12.5 13.0 %collective-permute-start = (bf16[72,1920]{1,0:T(8,128)(2,1)}, bf16[72,1920]{1,0:T(8,128)(2,1)}, u32[]{:S(2)}, u32[]{:S(2)}) collective-permute-start(bf16[72,1920]{1,0:T(8,128)(2,1)} %shard_map.416.refs_5_.refs_0_), channel_id=1, source_target_pairs={{0,2},{1,3},{2,0},{3,1},{4,6},{5,7},{6,4},{7,5},{8,10},{9,11},{10,... | collective-permute-start | bytes 829448 | tf_op jit(solution)/shard_map/ppermute | solution.py:1282
  14.1 22.6 %collective-permute-start.1 = (bf16[72,1920]{1,0:T(8,128)(2,1)}, bf16[72,1920]{1,0:T(8,128)(2,1)}, u32[]{:S(2)}, u32[]{:S(2)}) collective-permute-start(bf16[72,1920]{1,0:T(8,128)(2,1)} %shard_map.416.refs_5_.refs_0_), channel_id=1, source_target_pairs={{0,4},{1,5},{2,6},{3,7},{4,0},{5,1},{6,2},{7,3},{8,12},{9,13},{10,... | collective-permute-start | bytes 829448 | tf_op jit(solution)/shard_map/ppermute | solution.py:1282
  16.7 20.0 %collective-permute-start.2 = (bf16[72,1920]{1,0:T(8,128)(2,1)}, bf16[72,1920]{1,0:T(8,128)(2,1)}, u32[]{:S(2)}, u32[]{:S(2)}) collective-permute-start(bf16[72,1920]{1,0:T(8,128)(2,1)} %shard_map.416.refs_5_.refs_0_), channel_id=1, source_target_pairs={{0,6},{1,7},{2,4},{3,5},{4,2},{5,3},{6,0},{7,1},{8,14},{9,15},{10,... | collective-permute-start | bytes 829448 | tf_op jit(solution)/shard_map/ppermute | solution.py:1282
  19.8 19.2 %copy-start = (bf16[80,6144]{1,0:T(8,128)(2,1)S(1)}, bf16[80,6144]{1,0:T(8,128)(2,1)}, u32[]{:S(2)}) copy-start(bf16[80,6144]{1,0:T(8,128)(2,1)} %get-tuple-element.107.refs_2_.refs_4_.refs_5_) | copy-start | bytes 2949124
  38.9 8.2 %collective-permute-start.3 = (bf16[4,72,1920]{2,1,0:T(8,128)(2,1)}, bf16[4,72,1920]{2,1,0:T(8,128)(2,1)}, u32[]{:S(2)}, u32[]{:S(2)}) collective-permute-start(bf16[4,72,1920]{2,1,0:T(8,128)(2,1)} %shard_map.419.refs_1_), channel_id=1, source_target_pairs={{0,1},{1,0},{2,3},{3,2},{4,5},{5,4},{6,7},{7,6},{8,9},{9,8},{10,11... | collective-permute-start | bytes 3317768 | tf_op jit(solution)/shard_map/ppermute | solution.py:1282
  39.0 15.4 %collective-permute-start.6 = (bf16[80,6144]{1,0:T(8,128)(2,1)S(1)}, bf16[80,6144]{1,0:T(8,128)(2,1)}, u32[]{:S(2)}, u32[]{:S(2)}) collective-permute-start(bf16[80,6144]{1,0:T(8,128)(2,1)S(1)} %copy-done), channel_id=1, source_target_pairs={{0,1},{1,0},{2,3},{3,2},{4,5},{5,4},{6,7},{7,6},{8,9},{9,8},{10,11... | collective-permute-start | bytes 2949128 | tf_op jit(solution)/shard_map/ppermute | solution.py:1282
  39.5 14.9 %collective-permute-start.7 = (bf16[80,6144]{1,0:T(8,128)(2,1)}, bf16[80,6144]{1,0:T(8,128)(2,1)}, u32[]{:S(2)}, u32[]{:S(2)}) collective-permute-start(bf16[80,6144]{1,0:T(8,128)(2,1)} %collective-permute-done.5.refs_1_.refs_3_.refs_5_.refs_6_), channel_id=1, source_target_pairs={{0,1},{1,0},{2,3},{3,2},{4,5},{5,4},{6,7},{7,6},{8,9},{9,8},{10,11... | collective-permute-start | bytes 2949128 | tf_op jit(solution)/shard_map/ppermute | solution.py:1282
  39.6 14.8 %collective-permute-start.8 = (bf16[80,6144]{1,0:T(8,128)(2,1)}, bf16[80,6144]{1,0:T(8,128)(2,1)}, u32[]{:S(2)}, u32[]{:S(2)}) collective-permute-start(bf16[80,6144]{1,0:T(8,128)(2,1)} %collective-permute-done.4.refs_0_.refs_4_.refs_6_.refs_7_), channel_id=1, source_target_pairs={{0,1},{1,0},{2,3},{3,2},{4,5},{5,4},{6,7},{7,6},{8,9},{9,8},{10,11... | collective-permute-start | bytes 2949128 | tf_op jit(solution)/shard_map/ppermute | solution.py:1282
  40.0 6.5 %collective-permute-start.9 = (bf16[160,384]{1,0:T(8,128)(2,1)}, bf16[160,384]{1,0:T(8,128)(2,1)}, u32[]{:S(2)}, u32[]{:S(2)}) collective-permute-start(bf16[160,384]{1,0:T(8,128)(2,1)} %get-tuple-element.110), channel_id=1, source_target_pairs={{0,24},{8,16},{16,8},{24,0},{1,25},{9,17},{17,9},{25,1},{2,26},{10... | collective-permute-start | bytes 368648 | tf_op jit(solution)/shard_map/ppermute | solution.py:1279
  46.6 21.6 %collective-permute-start.10 = (bf16[48,5760]{1,0:T(8,128)(2,1)}, bf16[48,5760]{1,0:T(8,128)(2,1)}, u32[]{:S(2)}, u32[]{:S(2)}) collective-permute-start(bf16[48,5760]{1,0:T(8,128)(2,1)} %get-tuple-element.108.refs_6_), channel_id=1, source_target_pairs={{0,8},{8,0},{16,24},{24,16},{1,9},{9,1},{17,25},{25,17},{2,10},{10... | collective-permute-start | bytes 1658888 | tf_op jit(solution)/shard_map/ppermute | solution.py:1279
  47.1 21.1 %collective-permute-start.11 = (bf16[32,5760]{1,0:T(8,128)(2,1)}, bf16[32,5760]{1,0:T(8,128)(2,1)}, u32[]{:S(2)}, u32[]{:S(2)}) collective-permute-start(bf16[32,5760]{1,0:T(8,128)(2,1)} %get-tuple-element.114), channel_id=1, source_target_pairs={{0,16},{8,24},{16,0},{24,8},{1,17},{9,25},{17,1},{25,9},{2,18},{10... | collective-permute-start | bytes 1105928 | tf_op jit(solution)/shard_map/ppermute | solution.py:1279
  60.2 16.4 %all-to-all-start = ((f32[32,1,1280]{2,1,0:T(1,128)}), f32[32,1,1280]{2,1,0:T(1,128)S(1)}, u32[]{:S(2)}, u32[]{:S(2)}) async-start(f32[32,1,1280]{2,1,0:T(1,128)} %get-tuple-element.112.refs_2_), calls=%async_computation | async-start | bytes 327680 | tf_op jit(solution)/shard_map/all_to_all | solution.py:1285
  70.3 8.7 %collective-permute-start.12 = (bf16[48,5760]{1,0:T(8,128)(2,1)}, bf16[48,5760]{1,0:T(8,128)(2,1)S(1)}, u32[]{:S(2)}, u32[]{:S(2)}) collective-permute-start(bf16[48,5760]{1,0:T(8,128)(2,1)} %get-tuple-element.115.refs_7_.refs_8_), channel_id=1, source_target_pairs={{0,1},{1,0},{2,3},{3,2},{4,5},{5,4},{6,7},{7,6},{8,9},{9,8},{10,11... | collective-permute-start | bytes 1658888 | tf_op jit(solution)/shard_map/ppermute | solution.py:1282
  70.7 8.3 %collective-permute-start.13 = (bf16[32,5760]{1,0:T(8,128)(2,1)}, bf16[32,5760]{1,0:T(8,128)(2,1)S(1)}, u32[]{:S(2)}, u32[]{:S(2)}) collective-permute-start(bf16[32,5760]{1,0:T(8,128)(2,1)} %get-tuple-element.116.refs_8_.refs_9_), channel_id=1, source_target_pairs={{0,1},{1,0},{2,3},{3,2},{4,5},{5,4},{6,7},{7,6},{8,9},{9,8},{10,11... | collective-permute-start | bytes 1105928 | tf_op jit(solution)/shard_map/ppermute | solution.py:1282
  76.6 0.7 copy-start.5
  77.3 23.2 %collective-permute-start.14 = (bf16[80,5760]{1,0:T(8,128)(2,1)}, bf16[80,5760]{1,0:T(8,128)(2,1)}, u32[]{:S(2)}, u32[]{:S(2)}) collective-permute-start(bf16[80,5760]{1,0:T(8,128)(2,1)} %shard_map.425.refs_5_.refs_10_), channel_id=1, source_target_pairs={{0,8},{8,0},{16,24},{24,16},{1,9},{9,1},{17,25},{25,17},{2,10},{10... | collective-permute-start | bytes 2764808 | tf_op jit(solution)/shard_map/ppermute | solution.py:1279
  78.3 22.4 %collective-permute-start.15 = (bf16[80,5760]{1,0:T(8,128)(2,1)}, bf16[80,5760]{1,0:T(8,128)(2,1)}, u32[]{:S(2)}, u32[]{:S(2)}) collective-permute-start(bf16[80,5760]{1,0:T(8,128)(2,1)} %shard_map.425.refs_5_.refs_10_), channel_id=1, source_target_pairs={{0,16},{8,24},{16,0},{24,8},{1,17},{9,25},{17,1},{25,9},{2,18},{10... | collective-permute-start | bytes 2764808 | tf_op jit(solution)/shard_map/ppermute | solution.py:1279
  79.0 0.7 copy-start.11
  79.0 0.9 copy-start.10
  79.9 25.0 %copy-start.1 = (bf16[80,5760]{1,0:T(8,128)(2,1)S(1)}, bf16[80,5760]{1,0:T(8,128)(2,1)}, u32[]{:S(2)}) copy-start(bf16[80,5760]{1,0:T(8,128)(2,1)} %shard_map.425.refs_5_.refs_10_) | copy-start | bytes 2764804
  102.7 16.1 %collective-permute-start.16 = (bf16[48,5760]{1,0:T(8,128)(2,1)}, bf16[48,5760]{1,0:T(8,128)(2,1)}, u32[]{:S(2)}, u32[]{:S(2)}) collective-permute-start(bf16[48,5760]{1,0:T(8,128)(2,1)} %get-tuple-element.119), channel_id=1, source_target_pairs={{0,8},{8,0},{16,24},{24,16},{1,9},{9,1},{17,25},{25,17},{2,10},{10... | collective-permute-start | bytes 1658888 | tf_op jit(solution)/shard_map/ppermute | solution.py:1279
  104.4 14.4 %collective-permute-start.17 = (bf16[32,5760]{1,0:T(8,128)(2,1)}, bf16[32,5760]{1,0:T(8,128)(2,1)}, u32[]{:S(2)}, u32[]{:S(2)}) collective-permute-start(bf16[32,5760]{1,0:T(8,128)(2,1)} %get-tuple-element.120), channel_id=1, source_target_pairs={{0,16},{8,24},{16,0},{24,8},{1,17},{9,25},{17,1},{25,9},{2,18},{10... | collective-permute-start | bytes 1105928 | tf_op jit(solution)/shard_map/ppermute | solution.py:1279
  104.9 16.5 %collective-permute-start.18 = (bf16[80,5760]{1,0:T(8,128)(2,1)S(1)}, bf16[80,5760]{1,0:T(8,128)(2,1)}, u32[]{:S(2)}, u32[]{:S(2)}) collective-permute-start(bf16[80,5760]{1,0:T(8,128)(2,1)S(1)} %copy-done.1), channel_id=1, source_target_pairs={{0,1},{1,0},{2,3},{3,2},{4,5},{5,4},{6,7},{7,6},{8,9},{9,8},{10,11... | collective-permute-start | bytes 2764808 | tf_op jit(solution)/shard_map/ppermute | solution.py:1282
  104.9 18.8 %collective-permute-start.19 = (bf16[80,5760]{1,0:T(8,128)(2,1)}, bf16[80,5760]{1,0:T(8,128)(2,1)}, u32[]{:S(2)}, u32[]{:S(2)}) collective-permute-start(bf16[80,5760]{1,0:T(8,128)(2,1)} %collective-permute-done.14.refs_1_.refs_6_.refs_11_), channel_id=1, source_target_pairs={{0,1},{1,0},{2,3},{3,2},{4,5},{5,4},{6,7},{7,6},{8,9},{9,8},{10,11... | collective-permute-start | bytes 2764808 | tf_op jit(solution)/shard_map/ppermute | solution.py:1282
  105.4 18.3 %collective-permute-start.20 = (bf16[80,5760]{1,0:T(8,128)(2,1)}, bf16[80,5760]{1,0:T(8,128)(2,1)}, u32[]{:S(2)}, u32[]{:S(2)}) collective-permute-start(bf16[80,5760]{1,0:T(8,128)(2,1)} %collective-permute-done.15.refs_0_.refs_7_.refs_12_), channel_id=1, source_target_pairs={{0,1},{1,0},{2,3},{3,2},{4,5},{5,4},{6,7},{7,6},{8,9},{9,8},{10,11... | collective-permute-start | bytes 2764808 | tf_op jit(solution)/shard_map/ppermute | solution.py:1282
  120.9 2.9 collective-permute-start.21
  121.0 2.7 collective-permute-start.22
  161.4 11.7 %all-to-all-start.3 = ((f32[32,1,1408]{2,1,0:T(1,128)}), f32[32,1,1408]{2,1,0:T(1,128)S(1)}, u32[]{:S(2)}, u32[]{:S(2)}) async-start(f32[32,1,1408]{2,1,0:T(1,128)} %get-tuple-element.128), calls=%async_computation.3 | async-start | bytes 360448 | tf_op jit(solution)/shard_map/all_to_all | solution.py:1285
  164.6 34.4 %collective-permute-start.24 = (bf16[1152,640]{1,0:T(8,128)(2,1)}, bf16[1152,640]{1,0:T(8,128)(2,1)}, u32[]{:S(2)}, u32[]{:S(2)}) collective-permute-start(bf16[1152,640]{1,0:T(8,128)(2,1)} %get-tuple-element.135.refs_2_), channel_id=1, source_target_pairs={{0,1},{1,0},{2,3},{3,2},{4,5},{5,4},{6,7},{7,6},{8,9},{9,8},{10,11... | collective-permute-start | bytes 4423688 | tf_op jit(solution)/shard_map/ppermute | solution.py:1282
  173.2 0.7 copy-start.7
  195.4 3.6 collective-permute-start.23
  196.1 27.0 %collective-permute-start.26 = (bf16[1152,640]{1,0:T(8,128)(2,1)}, bf16[1152,640]{1,0:T(8,128)(2,1)}, u32[]{:S(2)}, u32[]{:S(2)}) collective-permute-start(bf16[1152,640]{1,0:T(8,128)(2,1)} %get-tuple-element.139.refs_2_), channel_id=1, source_target_pairs={{0,1},{1,0},{2,3},{3,2},{4,5},{5,4},{6,7},{7,6},{8,9},{9,8},{10,11... | collective-permute-start | bytes 4423688 | tf_op jit(solution)/shard_map/ppermute | solution.py:1282
  196.2 16.3 %all-to-all-start.4 = ((f32[32,1,1280]{2,1,0:T(1,128)}), f32[32,1,1280]{2,1,0:T(1,128)S(1)}, u32[]{:S(2)}, u32[]{:S(2)}) async-start(f32[32,1,1280]{2,1,0:T(1,128)} %get-tuple-element.132), calls=%async_computation.4 | async-start | bytes 327680 | tf_op jit(solution)/shard_map/all_to_all | solution.py:1285
  212.5 0.7 copy-start.8
  219.7 3.5 collective-permute-start.25
  220.0 17.6 %collective-permute-start.30 = (bf16[23,80,128]{2,1,0:T(8,128)(2,1)}, bf16[23,80,128]{2,1,0:T(8,128)(2,1)}, u32[]{:S(2)}, u32[]{:S(2)}) collective-permute-start(bf16[23,80,128]{2,1,0:T(8,128)(2,1)} %get-tuple-element.150), channel_id=1, source_target_pairs={{0,16},{8,24},{16,0},{24,8},{1,17},{9,25},{17,1},{25,9},{2,18},{10... | collective-permute-start | bytes 1413128 | tf_op jit(solution)/shard_map/ppermute | solution.py:1279
  221.7 15.9 %collective-permute-start.29 = (bf16[22,80,128]{2,1,0:T(8,128)(2,1)}, bf16[22,80,128]{2,1,0:T(8,128)(2,1)}, u32[]{:S(2)}, u32[]{:S(2)}) collective-permute-start(bf16[22,80,128]{2,1,0:T(8,128)(2,1)} %get-tuple-element.149), channel_id=1, source_target_pairs={{0,8},{8,0},{16,24},{24,16},{1,9},{9,1},{17,25},{25,17},{2,10},{10... | collective-permute-start | bytes 1351688 | tf_op jit(solution)/shard_map/ppermute | solution.py:1279
  223.1 0.9 copy-start.9
  240.4 41.1 %collective-permute-start.33 = (bf16[45,80,128]{2,1,0:T(8,128)(2,1)}, bf16[45,80,128]{2,1,0:T(8,128)(2,1)S(1)}, u32[]{:S(2)}, u32[]{:S(2)}) collective-permute-start(bf16[45,80,128]{2,1,0:T(8,128)(2,1)} %get-tuple-element.151.refs_16_), channel_id=1, source_target_pairs={{0,8},{8,0},{16,24},{24,16},{1,9},{9,1},{17,25},{25,17},{2,10},{10... | collective-permute-start | bytes 2764808 | tf_op jit(solution)/shard_map/ppermute | solution.py:1279
  241.4 40.1 %collective-permute-start.34 = (bf16[45,80,128]{2,1,0:T(8,128)(2,1)}, bf16[45,80,128]{2,1,0:T(8,128)(2,1)}, u32[]{:S(2)}, u32[]{:S(2)}) collective-permute-start(bf16[45,80,128]{2,1,0:T(8,128)(2,1)} %get-tuple-element.163), channel_id=1, source_target_pairs={{0,16},{8,24},{16,0},{24,8},{1,17},{9,25},{17,1},{25,9},{2,18},{10... | collective-permute-start | bytes 2764808 | tf_op jit(solution)/shard_map/ppermute | solution.py:1279
  242.9 34.0 %collective-permute-start.28 = (bf16[23,80,128]{2,1,0:T(8,128)(2,1)}, bf16[23,80,128]{2,1,0:T(8,128)(2,1)}, u32[]{:S(2)}, u32[]{:S(2)}) collective-permute-start(bf16[23,80,128]{2,1,0:T(8,128)(2,1)} %get-tuple-element.144), channel_id=1, source_target_pairs={{0,16},{8,24},{16,0},{24,8},{1,17},{9,25},{17,1},{25,9},{2,18},{10... | collective-permute-start | bytes 1413128 | tf_op jit(solution)/shard_map/ppermute | solution.py:1279
  243.5 33.4 %collective-permute-start.27 = (bf16[22,80,128]{2,1,0:T(8,128)(2,1)}, bf16[22,80,128]{2,1,0:T(8,128)(2,1)}, u32[]{:S(2)}, u32[]{:S(2)}) collective-permute-start(bf16[22,80,128]{2,1,0:T(8,128)(2,1)} %get-tuple-element.143), channel_id=1, source_target_pairs={{0,8},{8,0},{16,24},{24,16},{1,9},{9,1},{17,25},{25,17},{2,10},{10... | collective-permute-start | bytes 1351688 | tf_op jit(solution)/shard_map/ppermute | solution.py:1279
  279.7 23.3 %collective-permute-start.31 = (bf16[45,80,128]{2,1,0:T(8,128)(2,1)}, bf16[45,80,128]{2,1,0:T(8,128)(2,1)}, u32[]{:S(2)}, u32[]{:S(2)}) collective-permute-start(bf16[45,80,128]{2,1,0:T(8,128)(2,1)} %get-tuple-element.153.refs_16_), channel_id=1, source_target_pairs={{0,8},{8,0},{16,24},{24,16},{1,9},{9,1},{17,25},{25,17},{2,10},{10... | collective-permute-start | bytes 2764808 | tf_op jit(solution)/shard_map/ppermute | solution.py:1279
  280.8 22.4 %collective-permute-start.32 = (bf16[45,80,128]{2,1,0:T(8,128)(2,1)}, bf16[45,80,128]{2,1,0:T(8,128)(2,1)}, u32[]{:S(2)}, u32[]{:S(2)}) collective-permute-start(bf16[45,80,128]{2,1,0:T(8,128)(2,1)} %get-tuple-element.154), channel_id=1, source_target_pairs={{0,16},{8,24},{16,0},{24,8},{1,17},{9,25},{17,1},{25,9},{2,18},{10... | collective-permute-start | bytes 2764808 | tf_op jit(solution)/shard_map/ppermute | solution.py:1279
  281.5 0.9 copy-start.6
  285.2 24.2 %collective-permute-start.36 = (bf16[45,80,128]{2,1,0:T(8,128)(2,1)}, bf16[45,80,128]{2,1,0:T(8,128)(2,1)}, u32[]{:S(2)}, u32[]{:S(2)}) collective-permute-start(bf16[45,80,128]{2,1,0:T(8,128)(2,1)} %shard_map.437.refs_17_.refs_0_), channel_id=1, source_target_pairs={{0,2},{1,3},{6,4},{7,5},{8,10},{9,11},{14,12},{15,13},{16,18},{17,... | collective-permute-start | bytes 2764808 | tf_op jit(solution)/shard_map/ppermute | solution.py:1540
  302.0 11.3 %collective-permute-start.37 = (bf16[4,6,80,128]{3,2,1,0:T(8,128)(2,1)}, bf16[4,6,80,128]{3,2,1,0:T(8,128)(2,1)S(1)}, u32[]{:S(2)}, u32[]{:S(2)}) collective-permute-start(bf16[4,6,80,128]{3,2,1,0:T(8,128)(2,1)} %get-tuple-element.165), channel_id=1, source_target_pairs={{0,1},{1,0},{2,3},{3,2},{4,5},{5,4},{6,7},{7,6},{8,9},{9,8},{10,11... | collective-permute-start | bytes 1474568 | tf_op jit(solution)/shard_map/ppermute | solution.py:1282
  303.1 10.3 %copy-start.4 = (bf16[4,6,80,128]{3,2,1,0:T(8,128)(2,1)S(1)}, bf16[4,6,80,128]{3,2,1,0:T(8,128)(2,1)}, u32[]{:S(2)}) copy-start(bf16[4,6,80,128]{3,2,1,0:T(8,128)(2,1)} %get-tuple-element.164.refs_3_) | copy-start | bytes 1474564
  305.9 22.2 %collective-permute-start.35 = (bf16[45,80,128]{2,1,0:T(8,128)(2,1)}, bf16[45,80,128]{2,1,0:T(8,128)(2,1)}, u32[]{:S(2)}, u32[]{:S(2)}) collective-permute-start(bf16[45,80,128]{2,1,0:T(8,128)(2,1)} %shard_map.439.refs_2_.refs_0_), channel_id=1, source_target_pairs={{0,2},{1,3},{6,4},{7,5},{8,10},{9,11},{14,12},{15,13},{16,18},{17,... | collective-permute-start | bytes 2764808 | tf_op jit(solution)/shard_map/ppermute | solution.py:1540
  311.8 20.3 %collective-permute-start.44 = (bf16[45,80,128]{2,1,0:T(8,128)(2,1)}, bf16[45,80,128]{2,1,0:T(8,128)(2,1)}, u32[]{:S(2)}, u32[]{:S(2)}) collective-permute-start(bf16[45,80,128]{2,1,0:T(8,128)(2,1)} %shard_map.440.refs_2_.refs_0_), channel_id=1, source_target_pairs={{2,4},{3,5},{4,2},{5,3},{10,12},{11,13},{12,10},{13,11},{18,20},{1... | collective-permute-start | bytes 2764808 | tf_op jit(solution)/shard_map/ppermute | solution.py:1544
  313.5 6.2 %collective-permute-start.38 = (bf16[6,80,128]{2,1,0:T(8,128)(2,1)S(1)}, bf16[6,80,128]{2,1,0:T(8,128)(2,1)S(1)}, u32[]{:S(2)}, u32[]{:S(2)}) collective-permute-start(bf16[6,80,128]{2,1,0:T(8,128)(2,1)S(1)} %get-tuple-element.191), channel_id=1, source_target_pairs={{0,8},{8,0},{16,24},{24,16},{1,9},{9,1},{17,25},{25,17},{2,10},{10... | collective-permute-start | bytes 368648 | tf_op jit(solution)/shard_map/ppermute | solution.py:1279
  314.9 7.0 %collective-permute-start.39 = (bf16[6,80,128]{2,1,0:T(8,128)(2,1)S(1)}, bf16[6,80,128]{2,1,0:T(8,128)(2,1)S(1)}, u32[]{:S(2)}, u32[]{:S(2)}) collective-permute-start(bf16[6,80,128]{2,1,0:T(8,128)(2,1)S(1)} %get-tuple-element.193), channel_id=1, source_target_pairs={{0,16},{8,24},{16,0},{24,8},{1,17},{9,25},{17,1},{25,9},{2,18},{10... | collective-permute-start | bytes 368648 | tf_op jit(solution)/shard_map/ppermute | solution.py:1279
  315.9 6.0 %collective-permute-start.40 = (bf16[6,80,128]{2,1,0:T(8,128)(2,1)S(1)}, bf16[6,80,128]{2,1,0:T(8,128)(2,1)S(1)}, u32[]{:S(2)}, u32[]{:S(2)}) collective-permute-start(bf16[6,80,128]{2,1,0:T(8,128)(2,1)S(1)} %get-tuple-element.192), channel_id=1, source_target_pairs={{0,24},{8,16},{16,8},{24,0},{1,25},{9,17},{17,9},{25,1},{2,26},{10... | collective-permute-start | bytes 368648 | tf_op jit(solution)/shard_map/ppermute | solution.py:1279
  330.5 15.8 %collective-permute-start.41 = (bf16[45,80,128]{2,1,0:T(8,128)(2,1)}, bf16[45,80,128]{2,1,0:T(8,128)(2,1)}, u32[]{:S(2)}, u32[]{:S(2)}) collective-permute-start(bf16[45,80,128]{2,1,0:T(8,128)(2,1)} %shard_map.441.refs_2_.refs_0_), channel_id=1, source_target_pairs={{2,4},{3,5},{4,2},{5,3},{10,12},{11,13},{12,10},{13,11},{18,20},{1... | collective-permute-start | bytes 2764808 | tf_op jit(solution)/shard_map/ppermute | solution.py:1658
  334.5 23.5 %collective-permute-start.45 = (bf16[45,80,128]{2,1,0:T(8,128)(2,1)}, bf16[45,80,128]{2,1,0:T(8,128)(2,1)S(1)}, u32[]{:S(2)}, u32[]{:S(2)}) collective-permute-start(bf16[45,80,128]{2,1,0:T(8,128)(2,1)} %shard_map.442.refs_2_.refs_1_), channel_id=1, source_target_pairs={{2,0},{3,1},{4,6},{5,7},{10,8},{11,9},{12,14},{13,15},{18,16},{19,... | collective-permute-start | bytes 2764808 | tf_op jit(solution)/shard_map/ppermute | solution.py:1547
  335.8 8.1 %collective-permute-start.42 = (bf16[6,80,128]{2,1,0:T(8,128)(2,1)}, bf16[6,80,128]{2,1,0:T(8,128)(2,1)S(1)}, u32[]{:S(2)}, u32[]{:S(2)}) collective-permute-start(bf16[6,80,128]{2,1,0:T(8,128)(2,1)} %fusion.2.refs_3_), channel_id=1, source_target_pairs={{0,2},{1,3},{6,4},{7,5},{8,10},{9,11},{14,12},{15,13},{16,18},{17,... | collective-permute-start | bytes 368648 | tf_op jit(solution)/shard_map/ppermute | solution.py:1540
  344.9 0.7 collective-permute-start.43
  358.0 0.9 copy-start.3
  361.3 25.6 %collective-permute-start.46 = (bf16[51,80,128]{2,1,0:T(8,128)(2,1)}, bf16[51,80,128]{2,1,0:T(8,128)(2,1)}, u32[]{:S(2)}, u32[]{:S(2)}) collective-permute-start(bf16[51,80,128]{2,1,0:T(8,128)(2,1)} %shard_map.443.refs_1_), channel_id=1, source_target_pairs={{2,0},{3,1},{4,6},{5,7},{10,8},{11,9},{12,14},{13,15},{18,16},{19,... | collective-permute-start | bytes 3133448 | tf_op jit(solution)/shard_map/ppermute | solution.py:1547
  368.6 18.3 %collective-permute-start.47 = (bf16[45,80,128]{2,1,0:T(8,128)(2,1)}, bf16[45,80,128]{2,1,0:T(8,128)(2,1)S(1)}, u32[]{:S(2)}, u32[]{:S(2)}) collective-permute-start(bf16[45,80,128]{2,1,0:T(8,128)(2,1)} %shard_map.445.refs_26_), channel_id=1, source_target_pairs={{0,1},{1,0},{2,3},{3,2},{4,5},{5,4},{6,7},{7,6},{8,9},{9,8},{10,11... | collective-permute-start | bytes 2764808 | tf_op jit(solution)/shard_map/ppermute | solution.py:1282
  387.0 0.9 copy-start.2
  390.8 3.1 collective-permute-start.48

commit v6 on v5

--- a/solution.py
+++ b/solution.py
@@ -190,7 +190,7 @@
             pltpu.SemaphoreType.DMA((rows // 16,)),
             pltpu.SemaphoreType.DMA((rows // 16,)),
         ],
-        3,
+        0.1,
         len(after),
     )(ids, conv_w, *packed, *after)
 
@@ -1660,7 +1660,7 @@
         terms = [over_more_chips(add(terms), 4)]
     plan = [(place, 0, 0, blocks) for place in range(len(terms))]
     plan.append((len(terms), 0, blocks, 6))
-    (whole_one,) = merge([*terms, small_sum], [(blocks + 6, plan)], [arrived_two], 0.1)
+    (whole_one,) = merge([*terms, small_sum], [(blocks + 6, plan)], [], 0.1)
     arrived_one = outward(whole_one, last)
     squares, grad_norm_p, loss = call(
         functools.partial(norm_kernel, (devices, chips, split)),

time: 421 us -> 419 us (level)
  waiting for transfers between devices: 68.2 us -> 61.4 us
  blocking collectives: 57.3 us -> 63.4 us
    ppermute x2, waiting for transfers between devices: 11.7 us -> 5.27 us  [outward(): return lax.ppermute(value, 'filt', chip_routes(reach)[2])]
    all_to_all x4, blocking collectives: 57.3 us -> 63.4 us  [exchange(): return lax.all_to_all(stats, ('dp', 'filt'), 0, 0)]
  transfers between devices with their start and end apart: 52 -> 52, of which waited for: 16 -> 16; matrix products, arithmetic and copies ran while one was open for 1% -> 0% of each run, Pallas kernels for 36% -> 37%
where the time goes in v6:
time: 419 us; the launch traced here: 413 us
  Pallas kernels  214 us (51%)
  starting transfers between devices  65 us (16%)
  blocking collectives  63.4 us (15%)
  waiting for transfers between devices  61.4 us (15%)
  local copies, waits for them, and re-layouts  5.69 us (1%)
    all_to_all x4, blocking collectives, exchange(): return lax.all_to_all(stats, ('dp', 'filt'), 0, 0)  63.4 us
    pallas_call x2, Pallas kernels, back(): call(functools.partial(back_kernel, (per, row_total, split), layer), ([SM...  40.1 us
    pallas_call x2, Pallas kernels, weight_grad(): call(functools.partial(weight_grad_kernel, (chunks, split, band)), [ANY]...  27 us
    ppermute x20, starting transfers between devices, over_dp(): return lax.ppermute(value, 'dp', xor_pairs(split, turn))  22.6 us
    ppermute x21, waiting for transfers between devices, over_filt(): return lax.ppermute(value, 'filt', xor_pairs(groups, turn))  22.2 us
    pallas_call x1, Pallas kernels, shards(): pl.pallas_call(functools.partial(conv_update_kernel, (len(pieces), places...  20.8 us
    pallas_call x8, Pallas kernels, merge(): call(functools.partial(merge_kernel, plan, len(values)), [ANY] * len(valu...  20.7 us
    pallas_call x1, Pallas kernels, shards(): call(functools.partial(conv_kernel, (per, row_total, split), 1), [SMEM, A...  18.6 us
  transfers between devices with their start and end apart: 52, of which 16 were waited for; matrix products, arithmetic and copies ran while one was open for 0% of the time, Pallas kernels for 37%

profile of v6, /device:TPU:0, one launch (start us, length us, event | category | flops | bytes accessed | tf_op | source)
XLA Modules:
  0.0 413.5 jit_solution(14684862910783041234)
XLA Ops:
  1.3 2.7 shard_map.416.refs_5_.refs_0_
  4.1 3.9 shard_map.417
  8.0 3.0 collective-permute-start.5
  11.0 1.5 collective-permute-start.4
  12.5 1.6 collective-permute-start
  14.1 2.6 collective-permute-start.1
  16.9 2.9 shard_map.418.refs_4_.refs_0_
  19.8 5.7 %collective-permute-done.refs_1_ = bf16[72,1920]{1,0:T(8,128)(2,1)} collective-permute-done((bf16[72,1920]{1,0:T(8,128)(2,1)}, bf16[72,1920]{1,0:T(8,128)(2,1)}, u32[]{:S(2)}, u32[]{:S(2)}) %collective-permute-start) | collective-permute-done | bytes 276512 | tf_op jit(solution)/shard_map/ppermute | solution.py:1282
  25.5 11.2 %collective-permute-done.1.refs_2_ = bf16[72,1920]{1,0:T(8,128)(2,1)} collective-permute-done((bf16[72,1920]{1,0:T(8,128)(2,1)}, bf16[72,1920]{1,0:T(8,128)(2,1)}, u32[]{:S(2)}, u32[]{:S(2)}) %collective-permute-start.1) | collective-permute-done | bytes 276512 | tf_op jit(solution)/shard_map/ppermute | solution.py:1282
  36.7 2.2 shard_map.419.refs_1_
  40.5 2.1 shard_map.420
  42.6 4.0 collective-permute-done.9.refs_8_
  47.6 6.8 %shard_map.421 = (bf16[1152,32]{1,0:T(8,128)(2,1)}, f32[1152,16]{1,0:T(8,128)}, f32[1152,160]{1,0:T(8,128)}, f32[1152,384]{1,0:T(8,128)}, bf16[1152,384]{1,0:T(8,128)(2,1)}, /*index=5*/f32[18,128]{1,0:T(8,128)}) custom-call(s32[4]{0:T(128)} %pad_add_fusion.refs_0_, bf16[4,72,1920]{2,1,0:T(8,128)(2,1)} %shard_map.419.refs_1_, ...), custom_call_target="tpu_custom_call" | custom-call | flops 3500000000 | bytes 1 | tf_op jit(solution)/shard_map/pallas_call | solution.py:1329
  54.4 5.8 %shard_map.422 = (f32[1152,640]{1,0:T(8,128)}, f32[32,1,1280]{2,1,0:T(1,128)}, f32[8,640]{1,0:T(8,128)}, bf16[640,16]{1,0:T(8,128)(2,1)}, bf16[640,384]{1,0:T(8,128)(2,1)}) custom-call(s32[4]{0:T(128)} %pad_add_fusion.refs_0_, bf16[1152,384]{1,0:T(8,128)(2,1)} %get-tuple-element.109.refs_1_.refs_8_, ...), custom_call_target="tpu_custom_call" | custom-call | flops 1400000000 | bytes 1 | tf_op jit(solution)/shard_map/pallas_call | solution.py:1350
  60.2 8.0 %all-to-all-start = ((f32[32,1,1280]{2,1,0:T(1,128)}), f32[32,1,1280]{2,1,0:T(1,128)S(1)}, u32[]{:S(2)}, u32[]{:S(2)}) async-start(f32[32,1,1280]{2,1,0:T(1,128)} %get-tuple-element.112.refs_2_), calls=%async_computation | async-start | bytes 327680 | tf_op jit(solution)/shard_map/all_to_all | solution.py:1285
  68.2 2.1 shard_map.423
  70.9 5.7 %all-to-all-done.refs_2_.refs_1_.refs_4_ = f32[32,1,1280]{2,1,0:T(1,128)S(1)} async-done(((f32[32,1,1280]{2,1,0:T(1,128)}), f32[32,1,1280]{2,1,0:T(1,128)S(1)}, u32[]{:S(2)}, u32[]{:S(2)}) %all-to-all-start) | async-done | bytes 163872 | tf_op jit(solution)/shard_map/all_to_all | solution.py:1285
  79.9 18.5 %shard_map.424 = (f32[1152,640]{1,0:T(8,128)}, bf16[1152,640]{1,0:T(8,128)(2,1)}, f32[1152,640]{1,0:T(8,128)}, f32[32,1,1280]{2,1,0:T(1,128)}) custom-call(s32[4]{0:T(128)} %pad_add_fusion.refs_0_, f32[1152,640]{1,0:T(8,128)} %get-tuple-element.111.refs_1_.refs_4_.refs_2_.refs_3_, f32[32,1,1280]{2,1,0:T(1,128)} %copy-done.4, ...), custom_call_target="tpu_custom_call" | custom-call | flops 6300000256 | bytes 1 | tf_op jit(solution)/shard_map/pallas_call | solution.py:1390
  98.4 2.0 collective-permute-done.14.refs_1_.refs_6_.refs_11_
  100.6 2.1 shard_map.426
  102.7 1.7 collective-permute-start.16
  105.4 13.3 %all_to_all.35.refs_2_.refs_9_.refs_3_ = f32[32,1,1280]{2,1,0:T(1,128)} all-to-all(f32[32,1,1280]{2,1,0:T(1,128)} %get-tuple-element.118.refs_2_), channel_id=1, replica_groups=mesh['dp'=4,'filt'=8] {'dp','filt'}, dimensions={0} | all-to-all | bytes 327680 | tf_op jit(solution)/shard_map/all_to_all | solution.py:1285
  118.8 2.1 shard_map.427
  121.4 2.3 collective-permute-done.22.refs_14_.refs_19_
  123.8 18.6 %shard_map.428 = (f32[1152,640]{1,0:T(8,128)}, bf16[1152,640]{1,0:T(8,128)(2,1)}, f32[1152,640]{1,0:T(8,128)}, f32[32,1,1280]{2,1,0:T(1,128)}) custom-call(s32[4]{0:T(128)} %pad_add_fusion.refs_0_, f32[1152,640]{1,0:T(8,128)} %get-tuple-element.117.refs_1_.refs_7_.refs_2_, f32[32,1,1280]{2,1,0:T(1,128)} %all_to_all.35.refs_2_.refs_9_.refs_3_, ...), custom_call_target="tpu_custom_call" | custom-call | flops 6300000256 | bytes 1 | tf_op jit(solution)/shard_map/pallas_call | solution.py:1401
  142.4 11.9 %all_to_all.36.refs_1_.refs_3_ = f32[32,1,1280]{2,1,0:T(1,128)} all-to-all(f32[32,1,1280]{2,1,0:T(1,128)} %get-tuple-element.124), channel_id=1, replica_groups=mesh['dp'=4,'filt'=8] {'dp','filt'}, dimensions={0} | all-to-all | bytes 327680 | tf_op jit(solution)/shard_map/all_to_all | solution.py:1285
  154.4 7.1 %shard_map.429 = (f32[1152,640]{1,0:T(8,128)}, f32[144,640]{1,0:T(8,128)}, f32[32,1,1408]{2,1,0:T(1,128)}, f32[640,16]{1,0:T(8,128)}) custom-call(f32[1152,640]{1,0:T(8,128)} %get-tuple-element.123.refs_0_.refs_2_, f32[32,1,1280]{2,1,0:T(1,128)} %all_to_all.36.refs_1_.refs_3_, f32[8,640]{1,0:T(8,128)} %get-tuple-element.113.refs_3_.refs_2_.refs_5_.refs_6_, ...), custom_call_target="tpu_custom_call" | custom-call | flops 2449999872 | bytes 1 | tf_op jit(solution)/shard_map/pallas_call | solution.py:1410
  161.4 3.1 all-to-all-start.3
  164.9 8.2 %all-to-all-done.3.refs_4_.refs_5_ = f32[32,1,1408]{2,1,0:T(1,128)S(1)} async-done(((f32[32,1,1408]{2,1,0:T(1,128)}), f32[32,1,1408]{2,1,0:T(1,128)S(1)}, u32[]{:S(2)}, u32[]{:S(2)}) %all-to-all-start.3) | async-done | bytes 180256 | tf_op jit(solution)/shard_map/all_to_all | solution.py:1285
  173.8 21.5 %shard_map.430 = (f32[1152,640]{1,0:T(8,128)}, f32[32,1,1280]{2,1,0:T(1,128)}, bf16[1152,384]{1,0:T(8,128)(2,1)}, bf16[1152,384]{1,0:T(8,128)(2,1)}, f32[1152,640]{1,0:T(8,128)}) custom-call(s32[4]{0:T(128)} %pad_add_fusion.refs_0_, f32[1152,640]{1,0:T(8,128)} %get-tuple-element.127.refs_1_, f32[1152,640]{1,0:T(8,128)} %get-tuple-element.123.refs_0_.refs_2_, ...), custom_call_target="tpu_custom_call" | custom-call | flops 7699999744 | bytes 1 | tf_op jit(solution)/shard_map/pallas_call | solution.py:1432
  196.2 2.8 all-to-all-start.4
  199.0 13.5 %shard_map.431 = (bf16[45,80,128]{2,1,0:T(8,128)(2,1)}, bf16[45,80,128]{2,1,0:T(8,128)(2,1)}, bf16[45,80,128]{2,1,0:T(8,128)(2,1)}, bf16[22,80,128]{2,1,0:T(8,128)(2,1)}, bf16[23,80,128]{2,1,0:T(8,128)(2,1)}) custom-call(bf16[1152,384]{1,0:T(8,128)(2,1)} %get-tuple-element.133.refs_0_, bf16[1152,384]{1,0:T(8,128)(2,1)} %collective-permute-done.23.refs_1_, ...), custom_call_target="tpu_custom_call" | custom-call | flops 4550000128 | bytes 1 | tf_op jit(solution)/shard_map/pallas_call | solution.py:1471
  213.1 6.5 %shard_map.432 = (bf16[1152,640]{1,0:T(8,128)(2,1)}, bf16[1152,384]{1,0:T(8,128)(2,1)}, bf16[1152,384]{1,0:T(8,128)(2,1)}) custom-call(s32[4]{0:T(128)} %pad_add_fusion.refs_0_, f32[1152,640]{1,0:T(8,128)} %get-tuple-element.131.refs_1_, f32[1152,640]{1,0:T(8,128)} %get-tuple-element.117.refs_1_.refs_7_.refs_2_, ...), custom_call_target="tpu_custom_call" | custom-call | flops 2100000000 | bytes 1 | tf_op jit(solution)/shard_map/pallas_call | solution.py:1575
  220.0 1.7 collective-permute-start.30
  221.7 1.5 collective-permute-start.29
  224.1 13.5 %shard_map.433 = (bf16[45,80,128]{2,1,0:T(8,128)(2,1)}, bf16[45,80,128]{2,1,0:T(8,128)(2,1)}, bf16[45,80,128]{2,1,0:T(8,128)(2,1)}, bf16[22,80,128]{2,1,0:T(8,128)(2,1)}, bf16[23,80,128]{2,1,0:T(8,128)(2,1)}) custom-call(bf16[1152,384]{1,0:T(8,128)(2,1)} %get-tuple-element.137.refs_0_, bf16[1152,384]{1,0:T(8,128)(2,1)} %copy-done.9, ...), custom_call_target="tpu_custom_call" | custom-call | flops 4550000128 | bytes 1 | tf_op jit(solution)/shard_map/pallas_call | solution.py:1471
  237.6 2.8 shard_map.434
  241.4 1.5 collective-permute-start.34
  244.5 18.6 %shard_map.435 = (f32[1152,640]{1,0:T(8,128)}, f32[32,1,1280]{2,1,0:T(1,128)}) custom-call(s32[4]{0:T(128)} %pad_add_fusion.refs_0_, bf16[1152,640]{1,0:T(8,128)(2,1)} %get-tuple-element.145.refs_1_, f32[1152,640]{1,0:T(8,128)} %get-tuple-element.111.refs_1_.refs_4_.refs_2_.refs_3_, f32[1152,640]{1,0:T(8,128)} %get-tuple-element.146.refs_3_, ...), custom_call_target="tpu_custom_call" | custom-call | flops 7699999744 | bytes 1 | tf_op jit(solution)/shard_map/pallas_call | solution.py:1432
  263.1 13.8 %all_to_all.37.refs_4_.refs_3_.refs_5_ = f32[32,1,1280]{2,1,0:T(1,128)} all-to-all(f32[32,1,1280]{2,1,0:T(1,128)} %get-tuple-element.152), channel_id=1, replica_groups=mesh['dp'=4,'filt'=8] {'dp','filt'}, dimensions={0} | all-to-all | bytes 327680 | tf_op jit(solution)/shard_map/all_to_all | solution.py:1285
  276.9 2.8 shard_map.436
  282.5 2.7 shard_map.437.refs_17_.refs_0_
  285.2 3.6 collective-permute-start.36
  288.8 13.3 %shard_map.438 = (bf16[4,6,80,128]{3,2,1,0:T(8,128)(2,1)}, bf16[4,6,80,128]{3,2,1,0:T(8,128)(2,1)}) custom-call(s32[4]{0:T(128)} %pad_add_fusion.refs_0_, f32[1152,640]{1,0:T(8,128)} %get-tuple-element.155.refs_1_, f32[1152,640]{1,0:T(8,128)} %get-tuple-element.156.refs_2_, f32[1152,640]{1,0:T(8,128)} %get-tuple-element.111.refs_1_.refs_4_.refs_2_.refs_3_, ...), custom_call_target="tpu_custom_call" | custom-call | flops 35000000 | bytes 1 | tf_op jit(solution)/shard_map/pallas_call | solution.py:1607
  303.1 2.8 shard_map.439.refs_2_.refs_0_
  305.9 3.5 collective-permute-start.35
  309.4 2.4 shard_map.440.refs_2_.refs_0_
  311.8 1.6 collective-permute-start.44
  317.0 2.7 collective-permute-done.38
  319.7 2.2 collective-permute-done.39
  322.6 5.5 %collective-permute-done.35.refs_1_ = bf16[45,80,128]{2,1,0:T(8,128)(2,1)} collective-permute-done((bf16[45,80,128]{2,1,0:T(8,128)(2,1)}, bf16[45,80,128]{2,1,0:T(8,128)(2,1)}, u32[]{:S(2)}, u32[]{:S(2)}) %collective-permute-start.35) | collective-permute-done | bytes 921632 | tf_op jit(solution)/shard_map/ppermute | solution.py:1540
  328.1 2.4 shard_map.441.refs_0_.refs_2_
  330.5 1.6 collective-permute-start.41
  332.1 2.4 shard_map.443.refs_2_.refs_1_
  335.8 6.2 %collective-permute-start.42 = (bf16[6,80,128]{2,1,0:T(8,128)(2,1)S(1)}, bf16[6,80,128]{2,1,0:T(8,128)(2,1)S(1)}, u32[]{:S(2)}, u32[]{:S(2)}) collective-permute-start(bf16[6,80,128]{2,1,0:T(8,128)(2,1)S(1)} %copy-done.5), channel_id=1, source_target_pairs={{0,2},{1,3},{6,4},{7,5},{8,10},{9,11},{14,12},{15,13},{16,18},{17,... | collective-permute-start | bytes 368648 | tf_op jit(solution)/shard_map/ppermute | solution.py:1540
  342.0 2.4 collective-permute-done.42
  345.9 2.4 shard_map.442.refs_1_
  349.6 3.2 shard_map.444
  352.8 5.3 %collective-permute-done.46.refs_2_ = bf16[45,80,128]{2,1,0:T(8,128)(2,1)} collective-permute-done((bf16[45,80,128]{2,1,0:T(8,128)(2,1)}, bf16[45,80,128]{2,1,0:T(8,128)(2,1)}, u32[]{:S(2)}, u32[]{:S(2)}) %collective-permute-start.46) | collective-permute-done | bytes 921632 | tf_op jit(solution)/shard_map/ppermute | solution.py:1547
  358.1 2.8 shard_map.445.refs_26_
  361.0 24.4 %all_to_all.38.refs_3_.refs_1_ = f32[32,1,128]{2,1,0:T(1,128)} all-to-all(f32[32,1,128]{2,1,0:T(1,128)} %get-tuple-element.166.refs_3_), channel_id=1, replica_groups=mesh['dp'=4,'filt'=8] {'dp','filt'}, dimensions={0} | all-to-all | bytes 32768 | tf_op jit(solution)/shard_map/all_to_all | solution.py:1285
  386.3 2.9 shard_map.446.refs_24_
  389.2 3.0 collective-permute-done.48.refs_25_
  392.2 20.8 %shard_map.447 = (f32[2,160,5760]{2,1,0:T(8,128)}, f32[2,160,5760]{2,1,0:T(8,128)}, f32[2,160,5760]{2,1,0:T(8,128)}, f32[16,27]{1,0:T(8,128)}, f32[16,27]{1,0:T(...) custom-call(s32[4]{0:T(128)} %pad_add_fusion.refs_0_, ...), custom_call_target="tpu_custom_call" | custom-call | flops 36864000 | bytes 47923200 | tf_op jit(solution)/shard_map/pallas_call | solution.py:1706
  (105 shorter events, 28.8 us)
Async XLA Ops:
  8.0 31.5 %collective-permute-start.5 = (bf16[80,6144]{1,0:T(8,128)(2,1)}, bf16[80,6144]{1,0:T(8,128)(2,1)}, u32[]{:S(2)}, u32[]{:S(2)}) collective-permute-start(bf16[80,6144]{1,0:T(8,128)(2,1)} %get-tuple-element.107.refs_2_.refs_4_.refs_5_), channel_id=1, source_target_pairs={{0,8},{8,0},{16,24},{24,16},{1,9},{9,1},{17,25},{25,17},{2,10},{10... | collective-permute-start | bytes 2949128 | tf_op jit(solution)/shard_map/ppermute | solution.py:1279
  11.0 28.6 %collective-permute-start.4 = (bf16[80,6144]{1,0:T(8,128)(2,1)}, bf16[80,6144]{1,0:T(8,128)(2,1)}, u32[]{:S(2)}, u32[]{:S(2)}) collective-permute-start(bf16[80,6144]{1,0:T(8,128)(2,1)} %get-tuple-element.107.refs_2_.refs_4_.refs_5_), channel_id=1, source_target_pairs={{0,16},{8,24},{16,0},{24,8},{1,17},{9,25},{17,1},{25,9},{2,18},{10... | collective-permute-start | bytes 2949128 | tf_op jit(solution)/shard_map/ppermute | solution.py:1279
  12.5 13.0 %collective-permute-start = (bf16[72,1920]{1,0:T(8,128)(2,1)}, bf16[72,1920]{1,0:T(8,128)(2,1)}, u32[]{:S(2)}, u32[]{:S(2)}) collective-permute-start(bf16[72,1920]{1,0:T(8,128)(2,1)} %shard_map.416.refs_5_.refs_0_), channel_id=1, source_target_pairs={{0,2},{1,3},{2,0},{3,1},{4,6},{5,7},{6,4},{7,5},{8,10},{9,11},{10,... | collective-permute-start | bytes 829448 | tf_op jit(solution)/shard_map/ppermute | solution.py:1282
  14.1 22.6 %collective-permute-start.1 = (bf16[72,1920]{1,0:T(8,128)(2,1)}, bf16[72,1920]{1,0:T(8,128)(2,1)}, u32[]{:S(2)}, u32[]{:S(2)}) collective-permute-start(bf16[72,1920]{1,0:T(8,128)(2,1)} %shard_map.416.refs_5_.refs_0_), channel_id=1, source_target_pairs={{0,4},{1,5},{2,6},{3,7},{4,0},{5,1},{6,2},{7,3},{8,12},{9,13},{10,... | collective-permute-start | bytes 829448 | tf_op jit(solution)/shard_map/ppermute | solution.py:1282
  16.7 20.0 %collective-permute-start.2 = (bf16[72,1920]{1,0:T(8,128)(2,1)}, bf16[72,1920]{1,0:T(8,128)(2,1)}, u32[]{:S(2)}, u32[]{:S(2)}) collective-permute-start(bf16[72,1920]{1,0:T(8,128)(2,1)} %shard_map.416.refs_5_.refs_0_), channel_id=1, source_target_pairs={{0,6},{1,7},{2,4},{3,5},{4,2},{5,3},{6,0},{7,1},{8,14},{9,15},{10,... | collective-permute-start | bytes 829448 | tf_op jit(solution)/shard_map/ppermute | solution.py:1282
  19.8 19.2 %copy-start = (bf16[80,6144]{1,0:T(8,128)(2,1)S(1)}, bf16[80,6144]{1,0:T(8,128)(2,1)}, u32[]{:S(2)}) copy-start(bf16[80,6144]{1,0:T(8,128)(2,1)} %get-tuple-element.107.refs_2_.refs_4_.refs_5_) | copy-start | bytes 2949124
  38.9 8.2 %collective-permute-start.3 = (bf16[4,72,1920]{2,1,0:T(8,128)(2,1)}, bf16[4,72,1920]{2,1,0:T(8,128)(2,1)}, u32[]{:S(2)}, u32[]{:S(2)}) collective-permute-start(bf16[4,72,1920]{2,1,0:T(8,128)(2,1)} %shard_map.419.refs_1_), channel_id=1, source_target_pairs={{0,1},{1,0},{2,3},{3,2},{4,5},{5,4},{6,7},{7,6},{8,9},{9,8},{10,11... | collective-permute-start | bytes 3317768 | tf_op jit(solution)/shard_map/ppermute | solution.py:1282
  39.0 15.4 %collective-permute-start.6 = (bf16[80,6144]{1,0:T(8,128)(2,1)S(1)}, bf16[80,6144]{1,0:T(8,128)(2,1)}, u32[]{:S(2)}, u32[]{:S(2)}) collective-permute-start(bf16[80,6144]{1,0:T(8,128)(2,1)S(1)} %copy-done), channel_id=1, source_target_pairs={{0,1},{1,0},{2,3},{3,2},{4,5},{5,4},{6,7},{7,6},{8,9},{9,8},{10,11... | collective-permute-start | bytes 2949128 | tf_op jit(solution)/shard_map/ppermute | solution.py:1282
  39.5 14.9 %collective-permute-start.7 = (bf16[80,6144]{1,0:T(8,128)(2,1)}, bf16[80,6144]{1,0:T(8,128)(2,1)}, u32[]{:S(2)}, u32[]{:S(2)}) collective-permute-start(bf16[80,6144]{1,0:T(8,128)(2,1)} %collective-permute-done.5.refs_1_.refs_3_.refs_5_.refs_6_), channel_id=1, source_target_pairs={{0,1},{1,0},{2,3},{3,2},{4,5},{5,4},{6,7},{7,6},{8,9},{9,8},{10,11... | collective-permute-start | bytes 2949128 | tf_op jit(solution)/shard_map/ppermute | solution.py:1282
  39.6 14.8 %collective-permute-start.8 = (bf16[80,6144]{1,0:T(8,128)(2,1)}, bf16[80,6144]{1,0:T(8,128)(2,1)}, u32[]{:S(2)}, u32[]{:S(2)}) collective-permute-start(bf16[80,6144]{1,0:T(8,128)(2,1)} %collective-permute-done.4.refs_0_.refs_4_.refs_6_.refs_7_), channel_id=1, source_target_pairs={{0,1},{1,0},{2,3},{3,2},{4,5},{5,4},{6,7},{7,6},{8,9},{9,8},{10,11... | collective-permute-start | bytes 2949128 | tf_op jit(solution)/shard_map/ppermute | solution.py:1282
  40.0 6.5 %collective-permute-start.9 = (bf16[160,384]{1,0:T(8,128)(2,1)}, bf16[160,384]{1,0:T(8,128)(2,1)}, u32[]{:S(2)}, u32[]{:S(2)}) collective-permute-start(bf16[160,384]{1,0:T(8,128)(2,1)} %get-tuple-element.110), channel_id=1, source_target_pairs={{0,24},{8,16},{16,8},{24,0},{1,25},{9,17},{17,9},{25,1},{2,26},{10... | collective-permute-start | bytes 368648 | tf_op jit(solution)/shard_map/ppermute | solution.py:1279
  46.6 21.6 %collective-permute-start.10 = (bf16[48,5760]{1,0:T(8,128)(2,1)}, bf16[48,5760]{1,0:T(8,128)(2,1)}, u32[]{:S(2)}, u32[]{:S(2)}) collective-permute-start(bf16[48,5760]{1,0:T(8,128)(2,1)} %get-tuple-element.108.refs_6_), channel_id=1, source_target_pairs={{0,8},{8,0},{16,24},{24,16},{1,9},{9,1},{17,25},{25,17},{2,10},{10... | collective-permute-start | bytes 1658888 | tf_op jit(solution)/shard_map/ppermute | solution.py:1279
  47.1 21.1 %collective-permute-start.11 = (bf16[32,5760]{1,0:T(8,128)(2,1)}, bf16[32,5760]{1,0:T(8,128)(2,1)}, u32[]{:S(2)}, u32[]{:S(2)}) collective-permute-start(bf16[32,5760]{1,0:T(8,128)(2,1)} %get-tuple-element.114), channel_id=1, source_target_pairs={{0,16},{8,24},{16,0},{24,8},{1,17},{9,25},{17,1},{25,9},{2,18},{10... | collective-permute-start | bytes 1105928 | tf_op jit(solution)/shard_map/ppermute | solution.py:1279
  60.2 16.4 %all-to-all-start = ((f32[32,1,1280]{2,1,0:T(1,128)}), f32[32,1,1280]{2,1,0:T(1,128)S(1)}, u32[]{:S(2)}, u32[]{:S(2)}) async-start(f32[32,1,1280]{2,1,0:T(1,128)} %get-tuple-element.112.refs_2_), calls=%async_computation | async-start | bytes 327680 | tf_op jit(solution)/shard_map/all_to_all | solution.py:1285
  70.3 8.7 %collective-permute-start.12 = (bf16[48,5760]{1,0:T(8,128)(2,1)}, bf16[48,5760]{1,0:T(8,128)(2,1)S(1)}, u32[]{:S(2)}, u32[]{:S(2)}) collective-permute-start(bf16[48,5760]{1,0:T(8,128)(2,1)} %get-tuple-element.115.refs_7_.refs_8_), channel_id=1, source_target_pairs={{0,1},{1,0},{2,3},{3,2},{4,5},{5,4},{6,7},{7,6},{8,9},{9,8},{10,11... | collective-permute-start | bytes 1658888 | tf_op jit(solution)/shard_map/ppermute | solution.py:1282
  70.7 8.3 %collective-permute-start.13 = (bf16[32,5760]{1,0:T(8,128)(2,1)}, bf16[32,5760]{1,0:T(8,128)(2,1)S(1)}, u32[]{:S(2)}, u32[]{:S(2)}) collective-permute-start(bf16[32,5760]{1,0:T(8,128)(2,1)} %get-tuple-element.116.refs_8_.refs_9_), channel_id=1, source_target_pairs={{0,1},{1,0},{2,3},{3,2},{4,5},{5,4},{6,7},{7,6},{8,9},{9,8},{10,11... | collective-permute-start | bytes 1105928 | tf_op jit(solution)/shard_map/ppermute | solution.py:1282
  76.6 0.7 copy-start.4
  77.3 23.2 %collective-permute-start.14 = (bf16[80,5760]{1,0:T(8,128)(2,1)}, bf16[80,5760]{1,0:T(8,128)(2,1)}, u32[]{:S(2)}, u32[]{:S(2)}) collective-permute-start(bf16[80,5760]{1,0:T(8,128)(2,1)} %shard_map.425.refs_5_.refs_10_), channel_id=1, source_target_pairs={{0,8},{8,0},{16,24},{24,16},{1,9},{9,1},{17,25},{25,17},{2,10},{10... | collective-permute-start | bytes 2764808 | tf_op jit(solution)/shard_map/ppermute | solution.py:1279
  78.3 22.4 %collective-permute-start.15 = (bf16[80,5760]{1,0:T(8,128)(2,1)}, bf16[80,5760]{1,0:T(8,128)(2,1)}, u32[]{:S(2)}, u32[]{:S(2)}) collective-permute-start(bf16[80,5760]{1,0:T(8,128)(2,1)} %shard_map.425.refs_5_.refs_10_), channel_id=1, source_target_pairs={{0,16},{8,24},{16,0},{24,8},{1,17},{9,25},{17,1},{25,9},{2,18},{10... | collective-permute-start | bytes 2764808 | tf_op jit(solution)/shard_map/ppermute | solution.py:1279
  79.0 0.7 copy-start.11
  79.0 0.9 copy-start.10
  79.9 25.0 %copy-start.1 = (bf16[80,5760]{1,0:T(8,128)(2,1)S(1)}, bf16[80,5760]{1,0:T(8,128)(2,1)}, u32[]{:S(2)}) copy-start(bf16[80,5760]{1,0:T(8,128)(2,1)} %shard_map.425.refs_5_.refs_10_) | copy-start | bytes 2764804
  102.7 16.1 %collective-permute-start.16 = (bf16[48,5760]{1,0:T(8,128)(2,1)}, bf16[48,5760]{1,0:T(8,128)(2,1)}, u32[]{:S(2)}, u32[]{:S(2)}) collective-permute-start(bf16[48,5760]{1,0:T(8,128)(2,1)} %get-tuple-element.119), channel_id=1, source_target_pairs={{0,8},{8,0},{16,24},{24,16},{1,9},{9,1},{17,25},{25,17},{2,10},{10... | collective-permute-start | bytes 1658888 | tf_op jit(solution)/shard_map/ppermute | solution.py:1279
  104.4 14.4 %collective-permute-start.17 = (bf16[32,5760]{1,0:T(8,128)(2,1)}, bf16[32,5760]{1,0:T(8,128)(2,1)}, u32[]{:S(2)}, u32[]{:S(2)}) collective-permute-start(bf16[32,5760]{1,0:T(8,128)(2,1)} %get-tuple-element.120), channel_id=1, source_target_pairs={{0,16},{8,24},{16,0},{24,8},{1,17},{9,25},{17,1},{25,9},{2,18},{10... | collective-permute-start | bytes 1105928 | tf_op jit(solution)/shard_map/ppermute | solution.py:1279
  104.9 16.5 %collective-permute-start.18 = (bf16[80,5760]{1,0:T(8,128)(2,1)S(1)}, bf16[80,5760]{1,0:T(8,128)(2,1)}, u32[]{:S(2)}, u32[]{:S(2)}) collective-permute-start(bf16[80,5760]{1,0:T(8,128)(2,1)S(1)} %copy-done.1), channel_id=1, source_target_pairs={{0,1},{1,0},{2,3},{3,2},{4,5},{5,4},{6,7},{7,6},{8,9},{9,8},{10,11... | collective-permute-start | bytes 2764808 | tf_op jit(solution)/shard_map/ppermute | solution.py:1282
  104.9 18.8 %collective-permute-start.19 = (bf16[80,5760]{1,0:T(8,128)(2,1)}, bf16[80,5760]{1,0:T(8,128)(2,1)}, u32[]{:S(2)}, u32[]{:S(2)}) collective-permute-start(bf16[80,5760]{1,0:T(8,128)(2,1)} %collective-permute-done.14.refs_1_.refs_6_.refs_11_), channel_id=1, source_target_pairs={{0,1},{1,0},{2,3},{3,2},{4,5},{5,4},{6,7},{7,6},{8,9},{9,8},{10,11... | collective-permute-start | bytes 2764808 | tf_op jit(solution)/shard_map/ppermute | solution.py:1282
  105.4 18.3 %collective-permute-start.20 = (bf16[80,5760]{1,0:T(8,128)(2,1)}, bf16[80,5760]{1,0:T(8,128)(2,1)}, u32[]{:S(2)}, u32[]{:S(2)}) collective-permute-start(bf16[80,5760]{1,0:T(8,128)(2,1)} %collective-permute-done.15.refs_0_.refs_7_.refs_12_), channel_id=1, source_target_pairs={{0,1},{1,0},{2,3},{3,2},{4,5},{5,4},{6,7},{7,6},{8,9},{9,8},{10,11... | collective-permute-start | bytes 2764808 | tf_op jit(solution)/shard_map/ppermute | solution.py:1282
  120.9 2.9 collective-permute-start.21
  121.0 2.7 collective-permute-start.22
  161.4 11.7 %all-to-all-start.3 = ((f32[32,1,1408]{2,1,0:T(1,128)}), f32[32,1,1408]{2,1,0:T(1,128)S(1)}, u32[]{:S(2)}, u32[]{:S(2)}) async-start(f32[32,1,1408]{2,1,0:T(1,128)} %get-tuple-element.128), calls=%async_computation.3 | async-start | bytes 360448 | tf_op jit(solution)/shard_map/all_to_all | solution.py:1285
  164.6 34.4 %collective-permute-start.24 = (bf16[1152,640]{1,0:T(8,128)(2,1)}, bf16[1152,640]{1,0:T(8,128)(2,1)}, u32[]{:S(2)}, u32[]{:S(2)}) collective-permute-start(bf16[1152,640]{1,0:T(8,128)(2,1)} %get-tuple-element.135.refs_2_), channel_id=1, source_target_pairs={{0,1},{1,0},{2,3},{3,2},{4,5},{5,4},{6,7},{7,6},{8,9},{9,8},{10,11... | collective-permute-start | bytes 4423688 | tf_op jit(solution)/shard_map/ppermute | solution.py:1282
  173.2 0.7 copy-start.7
  195.4 3.6 collective-permute-start.23
  196.1 27.0 %collective-permute-start.26 = (bf16[1152,640]{1,0:T(8,128)(2,1)}, bf16[1152,640]{1,0:T(8,128)(2,1)}, u32[]{:S(2)}, u32[]{:S(2)}) collective-permute-start(bf16[1152,640]{1,0:T(8,128)(2,1)} %get-tuple-element.139.refs_2_), channel_id=1, source_target_pairs={{0,1},{1,0},{2,3},{3,2},{4,5},{5,4},{6,7},{7,6},{8,9},{9,8},{10,11... | collective-permute-start | bytes 4423688 | tf_op jit(solution)/shard_map/ppermute | solution.py:1282
  196.2 16.3 %all-to-all-start.4 = ((f32[32,1,1280]{2,1,0:T(1,128)}), f32[32,1,1280]{2,1,0:T(1,128)S(1)}, u32[]{:S(2)}, u32[]{:S(2)}) async-start(f32[32,1,1280]{2,1,0:T(1,128)} %get-tuple-element.132), calls=%async_computation.4 | async-start | bytes 327680 | tf_op jit(solution)/shard_map/all_to_all | solution.py:1285
  212.5 0.7 copy-start.8
  219.7 3.5 collective-permute-start.25
  220.0 17.6 %collective-permute-start.30 = (bf16[23,80,128]{2,1,0:T(8,128)(2,1)}, bf16[23,80,128]{2,1,0:T(8,128)(2,1)}, u32[]{:S(2)}, u32[]{:S(2)}) collective-permute-start(bf16[23,80,128]{2,1,0:T(8,128)(2,1)} %get-tuple-element.150), channel_id=1, source_target_pairs={{0,16},{8,24},{16,0},{24,8},{1,17},{9,25},{17,1},{25,9},{2,18},{10... | collective-permute-start | bytes 1413128 | tf_op jit(solution)/shard_map/ppermute | solution.py:1279
  221.7 15.9 %collective-permute-start.29 = (bf16[22,80,128]{2,1,0:T(8,128)(2,1)}, bf16[22,80,128]{2,1,0:T(8,128)(2,1)}, u32[]{:S(2)}, u32[]{:S(2)}) collective-permute-start(bf16[22,80,128]{2,1,0:T(8,128)(2,1)} %get-tuple-element.149), channel_id=1, source_target_pairs={{0,8},{8,0},{16,24},{24,16},{1,9},{9,1},{17,25},{25,17},{2,10},{10... | collective-permute-start | bytes 1351688 | tf_op jit(solution)/shard_map/ppermute | solution.py:1279
  223.1 0.9 copy-start.9
  240.4 41.1 %collective-permute-start.33 = (bf16[45,80,128]{2,1,0:T(8,128)(2,1)}, bf16[45,80,128]{2,1,0:T(8,128)(2,1)S(1)}, u32[]{:S(2)}, u32[]{:S(2)}) collective-permute-start(bf16[45,80,128]{2,1,0:T(8,128)(2,1)} %get-tuple-element.151.refs_16_), channel_id=1, source_target_pairs={{0,8},{8,0},{16,24},{24,16},{1,9},{9,1},{17,25},{25,17},{2,10},{10... | collective-permute-start | bytes 2764808 | tf_op jit(solution)/shard_map/ppermute | solution.py:1279
  241.4 40.1 %collective-permute-start.34 = (bf16[45,80,128]{2,1,0:T(8,128)(2,1)}, bf16[45,80,128]{2,1,0:T(8,128)(2,1)}, u32[]{:S(2)}, u32[]{:S(2)}) collective-permute-start(bf16[45,80,128]{2,1,0:T(8,128)(2,1)} %get-tuple-element.163), channel_id=1, source_target_pairs={{0,16},{8,24},{16,0},{24,8},{1,17},{9,25},{17,1},{25,9},{2,18},{10... | collective-permute-start | bytes 2764808 | tf_op jit(solution)/shard_map/ppermute | solution.py:1279
  242.9 34.0 %collective-permute-start.28 = (bf16[23,80,128]{2,1,0:T(8,128)(2,1)}, bf16[23,80,128]{2,1,0:T(8,128)(2,1)}, u32[]{:S(2)}, u32[]{:S(2)}) collective-permute-start(bf16[23,80,128]{2,1,0:T(8,128)(2,1)} %get-tuple-element.144), channel_id=1, source_target_pairs={{0,16},{8,24},{16,0},{24,8},{1,17},{9,25},{17,1},{25,9},{2,18},{10... | collective-permute-start | bytes 1413128 | tf_op jit(solution)/shard_map/ppermute | solution.py:1279
  243.5 33.4 %collective-permute-start.27 = (bf16[22,80,128]{2,1,0:T(8,128)(2,1)}, bf16[22,80,128]{2,1,0:T(8,128)(2,1)}, u32[]{:S(2)}, u32[]{:S(2)}) collective-permute-start(bf16[22,80,128]{2,1,0:T(8,128)(2,1)} %get-tuple-element.143), channel_id=1, source_target_pairs={{0,8},{8,0},{16,24},{24,16},{1,9},{9,1},{17,25},{25,17},{2,10},{10... | collective-permute-start | bytes 1351688 | tf_op jit(solution)/shard_map/ppermute | solution.py:1279
  279.7 23.3 %collective-permute-start.31 = (bf16[45,80,128]{2,1,0:T(8,128)(2,1)}, bf16[45,80,128]{2,1,0:T(8,128)(2,1)}, u32[]{:S(2)}, u32[]{:S(2)}) collective-permute-start(bf16[45,80,128]{2,1,0:T(8,128)(2,1)} %get-tuple-element.153.refs_16_), channel_id=1, source_target_pairs={{0,8},{8,0},{16,24},{24,16},{1,9},{9,1},{17,25},{25,17},{2,10},{10... | collective-permute-start | bytes 2764808 | tf_op jit(solution)/shard_map/ppermute | solution.py:1279
  280.8 22.4 %collective-permute-start.32 = (bf16[45,80,128]{2,1,0:T(8,128)(2,1)}, bf16[45,80,128]{2,1,0:T(8,128)(2,1)}, u32[]{:S(2)}, u32[]{:S(2)}) collective-permute-start(bf16[45,80,128]{2,1,0:T(8,128)(2,1)} %get-tuple-element.154), channel_id=1, source_target_pairs={{0,16},{8,24},{16,0},{24,8},{1,17},{9,25},{17,1},{25,9},{2,18},{10... | collective-permute-start | bytes 2764808 | tf_op jit(solution)/shard_map/ppermute | solution.py:1279
  281.5 0.9 copy-start.6
  285.2 24.2 %collective-permute-start.36 = (bf16[45,80,128]{2,1,0:T(8,128)(2,1)}, bf16[45,80,128]{2,1,0:T(8,128)(2,1)}, u32[]{:S(2)}, u32[]{:S(2)}) collective-permute-start(bf16[45,80,128]{2,1,0:T(8,128)(2,1)} %shard_map.437.refs_17_.refs_0_), channel_id=1, source_target_pairs={{0,2},{1,3},{6,4},{7,5},{8,10},{9,11},{14,12},{15,13},{16,18},{17,... | collective-permute-start | bytes 2764808 | tf_op jit(solution)/shard_map/ppermute | solution.py:1540
  302.0 11.3 %collective-permute-start.37 = (bf16[4,6,80,128]{3,2,1,0:T(8,128)(2,1)}, bf16[4,6,80,128]{3,2,1,0:T(8,128)(2,1)S(1)}, u32[]{:S(2)}, u32[]{:S(2)}) collective-permute-start(bf16[4,6,80,128]{3,2,1,0:T(8,128)(2,1)} %get-tuple-element.165), channel_id=1, source_target_pairs={{0,1},{1,0},{2,3},{3,2},{4,5},{5,4},{6,7},{7,6},{8,9},{9,8},{10,11... | collective-permute-start | bytes 1474568 | tf_op jit(solution)/shard_map/ppermute | solution.py:1282
  303.1 10.3 %copy-start.3 = (bf16[4,6,80,128]{3,2,1,0:T(8,128)(2,1)S(1)}, bf16[4,6,80,128]{3,2,1,0:T(8,128)(2,1)}, u32[]{:S(2)}) copy-start(bf16[4,6,80,128]{3,2,1,0:T(8,128)(2,1)} %get-tuple-element.164.refs_3_) | copy-start | bytes 1474564
  305.9 22.2 %collective-permute-start.35 = (bf16[45,80,128]{2,1,0:T(8,128)(2,1)}, bf16[45,80,128]{2,1,0:T(8,128)(2,1)}, u32[]{:S(2)}, u32[]{:S(2)}) collective-permute-start(bf16[45,80,128]{2,1,0:T(8,128)(2,1)} %shard_map.439.refs_2_.refs_0_), channel_id=1, source_target_pairs={{0,2},{1,3},{6,4},{7,5},{8,10},{9,11},{14,12},{15,13},{16,18},{17,... | collective-permute-start | bytes 2764808 | tf_op jit(solution)/shard_map/ppermute | solution.py:1540
  311.8 20.3 %collective-permute-start.44 = (bf16[45,80,128]{2,1,0:T(8,128)(2,1)}, bf16[45,80,128]{2,1,0:T(8,128)(2,1)}, u32[]{:S(2)}, u32[]{:S(2)}) collective-permute-start(bf16[45,80,128]{2,1,0:T(8,128)(2,1)} %shard_map.440.refs_2_.refs_0_), channel_id=1, source_target_pairs={{2,4},{3,5},{4,2},{5,3},{10,12},{11,13},{12,10},{13,11},{18,20},{1... | collective-permute-start | bytes 2764808 | tf_op jit(solution)/shard_map/ppermute | solution.py:1544
  313.5 6.2 %collective-permute-start.38 = (bf16[6,80,128]{2,1,0:T(8,128)(2,1)S(1)}, bf16[6,80,128]{2,1,0:T(8,128)(2,1)S(1)}, u32[]{:S(2)}, u32[]{:S(2)}) collective-permute-start(bf16[6,80,128]{2,1,0:T(8,128)(2,1)S(1)} %get-tuple-element.191), channel_id=1, source_target_pairs={{0,8},{8,0},{16,24},{24,16},{1,9},{9,1},{17,25},{25,17},{2,10},{10... | collective-permute-start | bytes 368648 | tf_op jit(solution)/shard_map/ppermute | solution.py:1279
  314.9 7.0 %collective-permute-start.39 = (bf16[6,80,128]{2,1,0:T(8,128)(2,1)S(1)}, bf16[6,80,128]{2,1,0:T(8,128)(2,1)S(1)}, u32[]{:S(2)}, u32[]{:S(2)}) collective-permute-start(bf16[6,80,128]{2,1,0:T(8,128)(2,1)S(1)} %get-tuple-element.193), channel_id=1, source_target_pairs={{0,16},{8,24},{16,0},{24,8},{1,17},{9,25},{17,1},{25,9},{2,18},{10... | collective-permute-start | bytes 368648 | tf_op jit(solution)/shard_map/ppermute | solution.py:1279
  315.9 6.0 %collective-permute-start.40 = (bf16[6,80,128]{2,1,0:T(8,128)(2,1)S(1)}, bf16[6,80,128]{2,1,0:T(8,128)(2,1)S(1)}, u32[]{:S(2)}, u32[]{:S(2)}) collective-permute-start(bf16[6,80,128]{2,1,0:T(8,128)(2,1)S(1)} %get-tuple-element.192), channel_id=1, source_target_pairs={{0,24},{8,16},{16,8},{24,0},{1,25},{9,17},{17,9},{25,1},{2,26},{10... | collective-permute-start | bytes 368648 | tf_op jit(solution)/shard_map/ppermute | solution.py:1279
  322.6 13.2 %copy-start.5 = (bf16[6,80,128]{2,1,0:T(8,128)(2,1)S(1)}, bf16[6,80,128]{2,1,0:T(8,128)(2,1)}, u32[]{:S(2)}) copy-start(bf16[6,80,128]{2,1,0:T(8,128)(2,1)} %fusion.2.refs_3_) | copy-start | bytes 368644
  330.5 15.4 %collective-permute-start.41 = (bf16[45,80,128]{2,1,0:T(8,128)(2,1)}, bf16[45,80,128]{2,1,0:T(8,128)(2,1)}, u32[]{:S(2)}, u32[]{:S(2)}) collective-permute-start(bf16[45,80,128]{2,1,0:T(8,128)(2,1)} %shard_map.441.refs_0_.refs_2_), channel_id=1, source_target_pairs={{2,4},{3,5},{4,2},{5,3},{10,12},{11,13},{12,10},{13,11},{18,20},{1... | collective-permute-start | bytes 2764808 | tf_op jit(solution)/shard_map/ppermute | solution.py:1658
  334.5 23.6 %collective-permute-start.46 = (bf16[45,80,128]{2,1,0:T(8,128)(2,1)}, bf16[45,80,128]{2,1,0:T(8,128)(2,1)}, u32[]{:S(2)}, u32[]{:S(2)}) collective-permute-start(bf16[45,80,128]{2,1,0:T(8,128)(2,1)} %shard_map.443.refs_2_.refs_1_), channel_id=1, source_target_pairs={{2,0},{3,1},{4,6},{5,7},{10,8},{11,9},{12,14},{13,15},{18,16},{19,... | collective-permute-start | bytes 2764808 | tf_op jit(solution)/shard_map/ppermute | solution.py:1547
  335.8 8.6 %collective-permute-start.42 = (bf16[6,80,128]{2,1,0:T(8,128)(2,1)S(1)}, bf16[6,80,128]{2,1,0:T(8,128)(2,1)S(1)}, u32[]{:S(2)}, u32[]{:S(2)}) collective-permute-start(bf16[6,80,128]{2,1,0:T(8,128)(2,1)S(1)} %copy-done.5), channel_id=1, source_target_pairs={{0,2},{1,3},{6,4},{7,5},{8,10},{9,11},{14,12},{15,13},{16,18},{17,... | collective-permute-start | bytes 368648 | tf_op jit(solution)/shard_map/ppermute | solution.py:1540
  344.5 0.7 collective-permute-start.43
  348.3 37.0 %collective-permute-start.45 = (bf16[51,80,128]{2,1,0:T(8,128)(2,1)}, bf16[51,80,128]{2,1,0:T(8,128)(2,1)}, u32[]{:S(2)}, u32[]{:S(2)}) collective-permute-start(bf16[51,80,128]{2,1,0:T(8,128)(2,1)} %shard_map.442.refs_1_), channel_id=1, source_target_pairs={{2,0},{3,1},{4,6},{5,7},{10,8},{11,9},{12,14},{13,15},{18,16},{19,... | collective-permute-start | bytes 3133448 | tf_op jit(solution)/shard_map/ppermute | solution.py:1547
  360.9 24.5 %collective-permute-start.47 = (bf16[45,80,128]{2,1,0:T(8,128)(2,1)}, bf16[45,80,128]{2,1,0:T(8,128)(2,1)S(1)}, u32[]{:S(2)}, u32[]{:S(2)}) collective-permute-start(bf16[45,80,128]{2,1,0:T(8,128)(2,1)} %shard_map.445.refs_26_), channel_id=1, source_target_pairs={{0,1},{1,0},{2,3},{3,2},{4,5},{5,4},{6,7},{7,6},{8,9},{9,8},{10,11... | collective-permute-start | bytes 2764808 | tf_op jit(solution)/shard_map/ppermute | solution.py:1282
  385.3 0.9 copy-start.2
  389.2 3.1 collective-permute-start.48
